TPU v7x, 256 devices: a whole 4x4x8 slice. The times are simulated.
256 devices in a mesh: blk: 16 (over y_hi, x, core), col: 16 (over z, y_lo).
Axes of the slice: x: 4, y: 4 (y_hi: 2, y_lo: 2; y = y_hi * 2 + y_lo), z: 8, core: 2. Of those that a mesh axis runs over, the one named last changes fastest.
Arguments:
- queries: bfloat16 [128, 256, 1152], P('blk', 'col'), may hold values from -200 to 200
- key_states: bfloat16 [32, 64, 1152], P('blk', 'col'), may hold values from -6 to 6
- values: bfloat16 [32, 64, 1152], P('blk', 'col'), may hold values from -6 to 6
- saved_out: bfloat16 [128, 256, 1152], P('blk', 'col'), may hold values from -6 to 6
- grad_out: bfloat16 [128, 256, 1152], P('blk', 'col'), may hold values from -96 to 96
- w_qkv: bfloat16 [1152, 3456], replicated, may hold values from -0.1875 to 0.1875
- w_patch: bfloat16 [256, 1152], replicated, may hold values from -0.375 to 0.375
Outputs:
- grad_image: float32 [1024, 2048], P('blk', 'col')
All inputs are finite; a program needn't handle non-finite values.
Results may differ from a plain program's by a relative error of at most 0.0055.
Values may be sent and summed in bfloat16 or wider, within the bound.
No kernel may reach another device: no remote copies, remote signals or barrier semaphores. Data moves between devices by JAX's collectives and lax.ppermute only.
A program may use at most 64 MiB of HBM per device.

v0:
```python
import jax
import jax.numpy as jnp
from jax import lax
from jax.sharding import PartitionSpec as P

D = 1152
HEADS = 16
POOL = 4


def for_sending(x):

    def short(part):
        return part.astype(jnp.bfloat16) if part.dtype == jnp.float32 else part

    return jax.tree.map(short, x)


def shifted(x, axis, by):
    peers = lax.axis_size(axis)
    return lax.ppermute(x, axis, [(i, (i + by) % peers) for i in range(peers)])


def padded(block, sides, width):
    for axis, dim in sides:
        count = lax.axis_size(axis)
        forward = [(i, i + 1) for i in range(count - 1)]
        backward = [(target, source) for source, target in forward]
        low = lax.ppermute(
            lax.slice_in_dim(block, block.shape[dim] - width, None, axis=dim), axis, forward
        )
        high = lax.ppermute(lax.slice_in_dim(block, 0, width, axis=dim), axis, backward)
        block = jnp.concatenate([low, block, high], axis=dim)
    return block


def score_block(queries_h, key_block, score_scale):
    return score_scale * jnp.einsum(
        "qhd,khd->hqk", queries_h, key_block, preferred_element_type=jnp.float32
    )


def norm_update(carry_max, carry_total, scores):
    new_max = jnp.maximum(carry_max, jnp.max(scores, axis=2))
    new_total = carry_total * jnp.exp(carry_max - new_max) + jnp.sum(
        jnp.exp(scores - new_max[:, :, None]), axis=2
    )
    return (new_max, new_total)


def block_terms(queries_h, grads_h, log_norms, out_dots, key_block, value_block, score_scale):
    scores = score_block(queries_h, key_block, score_scale)
    probs = jnp.exp(scores - log_norms[:, :, None])
    prob_half = probs.astype(jnp.bfloat16)
    grad_probs = jnp.einsum(
        "qhd,khd->hqk", grads_h, value_block, preferred_element_type=jnp.float32
    )
    grad_scores = (probs * (grad_probs - out_dots[:, :, None])).astype(jnp.bfloat16)
    query_term = jnp.einsum(
        "hqk,khd->qhd", grad_scores, key_block, preferred_element_type=jnp.float32
    )
    key_term = jnp.einsum(
        "hqk,qhd->khd", grad_scores, queries_h, preferred_element_type=jnp.float32
    )
    value_term = jnp.einsum("hqk,qhd->khd", prob_half, grads_h, preferred_element_type=jnp.float32)
    return (query_term, key_term, value_term)


def rotate(moving):
    return jax.tree.map(
        lambda part, own: part.astype(own.dtype), shifted(for_sending(moving), "blk", 1), moving
    )


def expand_pooled(pooled):
    spread = jnp.repeat(jnp.repeat(pooled, POOL, axis=0), POOL, axis=1)
    return spread * (1.0 / (POOL * POOL))


def fold_blocks(padded_patch, row_count, col_count):
    total = None
    for row_step in (0, 1):
        for col_step in (0, 1):
            piece = padded_patch[
                1 - row_step : row_count + 2 - row_step,
                1 - col_step : col_count + 2 - col_step,
                row_step,
                :,
                col_step,
                :,
            ]
            total = piece if total is None else total + piece
    return total.transpose(0, 2, 1, 3).reshape(8 * (row_count + 1), 8 * (col_count + 1))


def on_device(queries, key_states, values, saved_out, grad_out, w_qkv, w_patch):
    row_count, col_count, width = queries.shape
    band_count = lax.axis_size("blk")
    local_heads = HEADS // lax.axis_size("col")
    head_dim = D // HEADS
    score_scale = head_dim ** (-0.5)
    moved = (
        lax.all_to_all(queries, "col", split_axis=2, concat_axis=1, tiled=True),
        lax.all_to_all(key_states, "col", split_axis=2, concat_axis=1, tiled=True),
        lax.all_to_all(values, "col", split_axis=2, concat_axis=1, tiled=True),
        lax.all_to_all(saved_out, "col", split_axis=2, concat_axis=1, tiled=True),
        lax.all_to_all(grad_out, "col", split_axis=2, concat_axis=1, tiled=True),
    )
    band_cols = moved[0].shape[1]
    band_tokens = row_count * band_cols
    pooled_rows = moved[1].shape[0]
    pooled_cols = moved[1].shape[1]
    band_keys = pooled_rows * pooled_cols
    queries_h = moved[0].reshape(band_tokens, local_heads, head_dim)
    keys_h = moved[1].reshape(band_keys, local_heads, head_dim)
    values_h = moved[2].reshape(band_keys, local_heads, head_dim)
    outs_h = moved[3].reshape(band_tokens, local_heads, head_dim)
    grads_h = moved[4].reshape(band_tokens, local_heads, head_dim)
    out_dots = jnp.sum(grads_h.astype(jnp.float32) * outs_h.astype(jnp.float32), axis=2).T
    start_max = jnp.full((local_heads, band_tokens), -1e30, jnp.float32)
    start_total = jnp.zeros((local_heads, band_tokens), jnp.float32)
    zeros_query = jnp.zeros((band_tokens, local_heads, head_dim), jnp.float32)
    zeros_key = jnp.zeros((band_keys, local_heads, head_dim), jnp.float32)

    def norm_turn(turn_index, carry):
        key_block, run_max, run_total = carry
        run_max, run_total = norm_update(
            run_max, run_total, score_block(queries_h, key_block, score_scale)
        )
        return (rotate(key_block), run_max, run_total)

    unused, run_max, run_total = lax.fori_loop(
        0, band_count, norm_turn, (keys_h, start_max, start_total)
    )
    log_norms = run_max + jnp.log(run_total)

    def grad_turn(turn_index, carry):
        key_block, value_block, key_sum, value_sum, query_sum = carry
        query_term, key_term, value_term = block_terms(
            queries_h, grads_h, log_norms, out_dots, key_block, value_block, score_scale
        )
        key_block, value_block = rotate((key_block, value_block))
        key_sum, value_sum = shifted((key_sum + key_term, value_sum + value_term), "blk", 1)
        return (key_block, value_block, key_sum, value_sum, query_sum + query_term)

    carry = lax.fori_loop(
        0, band_count, grad_turn, (keys_h, values_h, zeros_key, zeros_key, zeros_query)
    )
    key_sum, value_sum, query_sum = (carry[2], carry[3], carry[4])
    grad_query = (
        (score_scale * query_sum)
        .astype(jnp.bfloat16)
        .reshape(row_count, band_cols, local_heads * head_dim)
    )
    grad_key = (
        (score_scale * key_sum)
        .astype(jnp.bfloat16)
        .reshape(pooled_rows, pooled_cols, local_heads * head_dim)
    )
    grad_value = value_sum.astype(jnp.bfloat16).reshape(
        pooled_rows, pooled_cols, local_heads * head_dim
    )
    back_q, back_k, back_v = (
        lax.all_to_all(grad_query, "col", split_axis=1, concat_axis=2, tiled=True),
        lax.all_to_all(grad_key, "col", split_axis=1, concat_axis=2, tiled=True),
        lax.all_to_all(grad_value, "col", split_axis=1, concat_axis=2, tiled=True),
    )
    joined = jnp.concatenate([back_q, expand_pooled(back_k), expand_pooled(back_v)], axis=2)
    grad_embed = lax.dot_general(
        joined, w_qkv, (((2,), (1,)), ((), ())), preferred_element_type=jnp.float32
    ).astype(jnp.bfloat16)
    framed = padded(grad_embed, (("blk", 0), ("col", 1)), 1)
    framed_patch = lax.dot_general(
        framed, w_patch, (((2,), (1,)), ((), ())), preferred_element_type=jnp.float32
    )
    framed_patch = framed_patch.reshape(row_count + 2, col_count + 2, 2, 8, 2, 8)
    canvas = fold_blocks(framed_patch, row_count, col_count)
    return canvas[4:-4, 4:-4]


def solution(mesh):
    placed = (
        P("blk", "col", None),
        P("blk", "col", None),
        P("blk", "col", None),
        P("blk", "col", None),
        P("blk", "col", None),
        P(),
        P(),
    )
    return jax.shard_map(
        on_device, mesh=mesh, in_specs=placed, out_specs=P("blk", "col"), check_vma=False
    )
```

profile of v0, /device:TPU:15, one launch (start us, length us, event | category | flops | bytes accessed | tf_op | source)
XLA Modules:
  0.0 422.4 jit_solution(11424630946194480548)
XLA Ops:
  2.6 9.4 %all-to-all-start = ((bf16[16,2,288]{2,1,0:T(2,128)(2,1)}), bf16[16,2,288]{2,1,0:T(2,128)(2,1)S(1)}, u32[]{:S(2)}, u32[]{:S(2)}) async-start(bf16[16,2,288]{2,1,0:T(2,128)(2,1)} %reshape.140), calls=%async_computation | async-start | bytes 49152 | tf_op jit(solution)/shard_map/all_to_all | solution.py:104
  19.1 4.3 %all-to-all-start.1 = ((bf16[16,2,288]{2,1,0:T(2,128)(2,1)}), bf16[16,2,288]{2,1,0:T(2,128)(2,1)S(1)}, u32[]{:S(2)}, u32[]{:S(2)}) async-start(bf16[16,2,288]{2,1,0:T(2,128)(2,1)} %reshape.142), calls=%async_computation.1 | async-start | bytes 49152 | tf_op jit(solution)/shard_map/all_to_all | solution.py:105
  30.6 7.2 %all-to-all-start.2 = ((bf16[16,2,4608]{2,1,0:T(2,128)(2,1)}), bf16[16,2,4608]{2,1,0:T(2,128)(2,1)S(1)}, u32[]{:S(2)}, u32[]{:S(2)}) async-start(bf16[16,2,4608]{2,1,0:T(2,128)(2,1)} %reshape.144), calls=%async_computation.2 | async-start | bytes 589824 | tf_op jit(solution)/shard_map/all_to_all | solution.py:103
  46.6 4.6 %all-to-all-start.3 = ((bf16[16,2,4608]{2,1,0:T(2,128)(2,1)}), bf16[16,2,4608]{2,1,0:T(2,128)(2,1)S(1)}, u32[]{:S(2)}, u32[]{:S(2)}) async-start(bf16[16,2,4608]{2,1,0:T(2,128)(2,1)} %reshape.146), calls=%async_computation.3 | async-start | bytes 589824 | tf_op jit(solution)/shard_map/all_to_all | solution.py:107
  60.4 4.9 %all-to-all-start.4 = ((bf16[16,2,4608]{2,1,0:T(2,128)(2,1)}), bf16[16,2,4608]{2,1,0:T(2,128)(2,1)}, u32[]{:S(2)}, u32[]{:S(2)}) async-start(bf16[16,2,4608]{2,1,0:T(2,128)(2,1)} %reshape.138), calls=%async_computation.4 | async-start | bytes 589824 | tf_op jit(solution)/shard_map/all_to_all | solution.py:106
  90.5 110.1 %while.34 = (s32[]{:T(128)}, bf16[128,1,72]{0,2,1:T(8,128)(2,1)S(1)}, f32[1,2048]{1,0:T(1,128)S(1)}, f32[1,2048]{1,0:T(1,128)S(1)}, bf16[2048,1,72]{0,2,1:T(8,128)(2,1)S(1)}, /*index=5*/s32[]{:T(128)}, s32[]{:T(128)}) while((s32[]{:T(128)}, bf16[128,1,72]{0,2,1:T(8,128)(2,1)S(1)}, f32[1,2048]{1,0:T(1,128)S(1)}, ...), condition=%wide.region_3.4_spmd.clone, body=%wide.region_0.3_spmd.clone.sunk | while | flops 38807552 | bytes 2627712 | solution.py:132
  90.5 7.2 %collective-permute-start = (bf16[128,1,72]{0,2,1:T(8,128)(2,1)S(1)}, bf16[128,1,72]{0,2,1:T(8,128)(2,1)S(1)}, u32[]{:S(2)}, u32[]{:S(2)}) collective-permute-start(bf16[128,1,72]{0,2,1:T(8,128)(2,1)S(1)} %copy.96), channel_id=1, source_target_pairs={{0,16},{16,32},{32,48},{48,64},{64,80},{80,96},{96,112},{112,128},... | collective-permute-start | bytes 55304 | tf_op jit(solution)/shard_map/while/body/eval_jaxpr/ppermute | solution.py:21
  98.5 5.9 %collective-permute-start = (bf16[128,1,72]{0,2,1:T(8,128)(2,1)S(1)}, bf16[128,1,72]{0,2,1:T(8,128)(2,1)S(1)}, u32[]{:S(2)}, u32[]{:S(2)}) collective-permute-start(bf16[128,1,72]{0,2,1:T(8,128)(2,1)S(1)} %copy.96), channel_id=1, source_target_pairs={{0,16},{16,32},{32,48},{48,64},{64,80},{80,96},{96,112},{112,128},... | collective-permute-start | bytes 55304 | tf_op jit(solution)/shard_map/while/body/eval_jaxpr/ppermute | solution.py:21
  105.3 5.9 %collective-permute-start = (bf16[128,1,72]{0,2,1:T(8,128)(2,1)S(1)}, bf16[128,1,72]{0,2,1:T(8,128)(2,1)S(1)}, u32[]{:S(2)}, u32[]{:S(2)}) collective-permute-start(bf16[128,1,72]{0,2,1:T(8,128)(2,1)S(1)} %copy.96), channel_id=1, source_target_pairs={{0,16},{16,32},{32,48},{48,64},{64,80},{80,96},{96,112},{112,128},... | collective-permute-start | bytes 55304 | tf_op jit(solution)/shard_map/while/body/eval_jaxpr/ppermute | solution.py:21
  112.1 5.9 %collective-permute-start = (bf16[128,1,72]{0,2,1:T(8,128)(2,1)S(1)}, bf16[128,1,72]{0,2,1:T(8,128)(2,1)S(1)}, u32[]{:S(2)}, u32[]{:S(2)}) collective-permute-start(bf16[128,1,72]{0,2,1:T(8,128)(2,1)S(1)} %copy.96), channel_id=1, source_target_pairs={{0,16},{16,32},{32,48},{48,64},{64,80},{80,96},{96,112},{112,128},... | collective-permute-start | bytes 55304 | tf_op jit(solution)/shard_map/while/body/eval_jaxpr/ppermute | solution.py:21
  118.9 5.9 %collective-permute-start = (bf16[128,1,72]{0,2,1:T(8,128)(2,1)S(1)}, bf16[128,1,72]{0,2,1:T(8,128)(2,1)S(1)}, u32[]{:S(2)}, u32[]{:S(2)}) collective-permute-start(bf16[128,1,72]{0,2,1:T(8,128)(2,1)S(1)} %copy.96), channel_id=1, source_target_pairs={{0,16},{16,32},{32,48},{48,64},{64,80},{80,96},{96,112},{112,128},... | collective-permute-start | bytes 55304 | tf_op jit(solution)/shard_map/while/body/eval_jaxpr/ppermute | solution.py:21
  125.7 5.9 %collective-permute-start = (bf16[128,1,72]{0,2,1:T(8,128)(2,1)S(1)}, bf16[128,1,72]{0,2,1:T(8,128)(2,1)S(1)}, u32[]{:S(2)}, u32[]{:S(2)}) collective-permute-start(bf16[128,1,72]{0,2,1:T(8,128)(2,1)S(1)} %copy.96), channel_id=1, source_target_pairs={{0,16},{16,32},{32,48},{48,64},{64,80},{80,96},{96,112},{112,128},... | collective-permute-start | bytes 55304 | tf_op jit(solution)/shard_map/while/body/eval_jaxpr/ppermute | solution.py:21
  132.5 5.9 %collective-permute-start = (bf16[128,1,72]{0,2,1:T(8,128)(2,1)S(1)}, bf16[128,1,72]{0,2,1:T(8,128)(2,1)S(1)}, u32[]{:S(2)}, u32[]{:S(2)}) collective-permute-start(bf16[128,1,72]{0,2,1:T(8,128)(2,1)S(1)} %copy.96), channel_id=1, source_target_pairs={{0,16},{16,32},{32,48},{48,64},{64,80},{80,96},{96,112},{112,128},... | collective-permute-start | bytes 55304 | tf_op jit(solution)/shard_map/while/body/eval_jaxpr/ppermute | solution.py:21
  139.3 5.9 %collective-permute-start = (bf16[128,1,72]{0,2,1:T(8,128)(2,1)S(1)}, bf16[128,1,72]{0,2,1:T(8,128)(2,1)S(1)}, u32[]{:S(2)}, u32[]{:S(2)}) collective-permute-start(bf16[128,1,72]{0,2,1:T(8,128)(2,1)S(1)} %copy.96), channel_id=1, source_target_pairs={{0,16},{16,32},{32,48},{48,64},{64,80},{80,96},{96,112},{112,128},... | collective-permute-start | bytes 55304 | tf_op jit(solution)/shard_map/while/body/eval_jaxpr/ppermute | solution.py:21
  146.1 5.9 %collective-permute-start = (bf16[128,1,72]{0,2,1:T(8,128)(2,1)S(1)}, bf16[128,1,72]{0,2,1:T(8,128)(2,1)S(1)}, u32[]{:S(2)}, u32[]{:S(2)}) collective-permute-start(bf16[128,1,72]{0,2,1:T(8,128)(2,1)S(1)} %copy.96), channel_id=1, source_target_pairs={{0,16},{16,32},{32,48},{48,64},{64,80},{80,96},{96,112},{112,128},... | collective-permute-start | bytes 55304 | tf_op jit(solution)/shard_map/while/body/eval_jaxpr/ppermute | solution.py:21
  153.0 5.9 %collective-permute-start = (bf16[128,1,72]{0,2,1:T(8,128)(2,1)S(1)}, bf16[128,1,72]{0,2,1:T(8,128)(2,1)S(1)}, u32[]{:S(2)}, u32[]{:S(2)}) collective-permute-start(bf16[128,1,72]{0,2,1:T(8,128)(2,1)S(1)} %copy.96), channel_id=1, source_target_pairs={{0,16},{16,32},{32,48},{48,64},{64,80},{80,96},{96,112},{112,128},... | collective-permute-start | bytes 55304 | tf_op jit(solution)/shard_map/while/body/eval_jaxpr/ppermute | solution.py:21
  159.8 5.9 %collective-permute-start = (bf16[128,1,72]{0,2,1:T(8,128)(2,1)S(1)}, bf16[128,1,72]{0,2,1:T(8,128)(2,1)S(1)}, u32[]{:S(2)}, u32[]{:S(2)}) collective-permute-start(bf16[128,1,72]{0,2,1:T(8,128)(2,1)S(1)} %copy.96), channel_id=1, source_target_pairs={{0,16},{16,32},{32,48},{48,64},{64,80},{80,96},{96,112},{112,128},... | collective-permute-start | bytes 55304 | tf_op jit(solution)/shard_map/while/body/eval_jaxpr/ppermute | solution.py:21
  166.6 5.9 %collective-permute-start = (bf16[128,1,72]{0,2,1:T(8,128)(2,1)S(1)}, bf16[128,1,72]{0,2,1:T(8,128)(2,1)S(1)}, u32[]{:S(2)}, u32[]{:S(2)}) collective-permute-start(bf16[128,1,72]{0,2,1:T(8,128)(2,1)S(1)} %copy.96), channel_id=1, source_target_pairs={{0,16},{16,32},{32,48},{48,64},{64,80},{80,96},{96,112},{112,128},... | collective-permute-start | bytes 55304 | tf_op jit(solution)/shard_map/while/body/eval_jaxpr/ppermute | solution.py:21
  173.4 5.9 %collective-permute-start = (bf16[128,1,72]{0,2,1:T(8,128)(2,1)S(1)}, bf16[128,1,72]{0,2,1:T(8,128)(2,1)S(1)}, u32[]{:S(2)}, u32[]{:S(2)}) collective-permute-start(bf16[128,1,72]{0,2,1:T(8,128)(2,1)S(1)} %copy.96), channel_id=1, source_target_pairs={{0,16},{16,32},{32,48},{48,64},{64,80},{80,96},{96,112},{112,128},... | collective-permute-start | bytes 55304 | tf_op jit(solution)/shard_map/while/body/eval_jaxpr/ppermute | solution.py:21
  180.2 5.9 %collective-permute-start = (bf16[128,1,72]{0,2,1:T(8,128)(2,1)S(1)}, bf16[128,1,72]{0,2,1:T(8,128)(2,1)S(1)}, u32[]{:S(2)}, u32[]{:S(2)}) collective-permute-start(bf16[128,1,72]{0,2,1:T(8,128)(2,1)S(1)} %copy.96), channel_id=1, source_target_pairs={{0,16},{16,32},{32,48},{48,64},{64,80},{80,96},{96,112},{112,128},... | collective-permute-start | bytes 55304 | tf_op jit(solution)/shard_map/while/body/eval_jaxpr/ppermute | solution.py:21
  187.0 5.9 %collective-permute-start = (bf16[128,1,72]{0,2,1:T(8,128)(2,1)S(1)}, bf16[128,1,72]{0,2,1:T(8,128)(2,1)S(1)}, u32[]{:S(2)}, u32[]{:S(2)}) collective-permute-start(bf16[128,1,72]{0,2,1:T(8,128)(2,1)S(1)} %copy.96), channel_id=1, source_target_pairs={{0,16},{16,32},{32,48},{48,64},{64,80},{80,96},{96,112},{112,128},... | collective-permute-start | bytes 55304 | tf_op jit(solution)/shard_map/while/body/eval_jaxpr/ppermute | solution.py:21
  193.8 5.9 %collective-permute-start = (bf16[128,1,72]{0,2,1:T(8,128)(2,1)S(1)}, bf16[128,1,72]{0,2,1:T(8,128)(2,1)S(1)}, u32[]{:S(2)}, u32[]{:S(2)}) collective-permute-start(bf16[128,1,72]{0,2,1:T(8,128)(2,1)S(1)} %copy.96), channel_id=1, source_target_pairs={{0,16},{16,32},{32,48},{48,64},{64,80},{80,96},{96,112},{112,128},... | collective-permute-start | bytes 55304 | tf_op jit(solution)/shard_map/while/body/eval_jaxpr/ppermute | solution.py:21
  200.6 141.2 %while.35 = (s32[]{:T(128)}, bf16[128,1,72]{0,2,1:T(8,128)(2,1)S(1)}, bf16[128,1,72]{0,2,1:T(8,128)(2,1)S(1)}, f32[128,1,72]{0,2,1:T(8,128)S(1)}, f32[128,1,72]{...) while((s32[]{:T(128)}, ...), condition=%wide.region_6.0_spmd.clone, body=%wide.region_5.0_spmd.clone.sunk | while | flops 190629888 | bytes 7813407 | solution.py:146
  200.9 6.0 %collective-permute-start.1 = (bf16[128,1,72]{0,2,1:T(8,128)(2,1)S(1)}, bf16[128,1,72]{0,2,1:T(8,128)(2,1)S(1)}, u32[]{:S(2)}, u32[]{:S(2)}) collective-permute-start(bf16[128,1,72]{0,2,1:T(8,128)(2,1)S(1)} %copy.110), channel_id=1, source_target_pairs={{0,16},{16,32},{32,48},{48,64},{64,80},{80,96},{96,112},{112,128},... | collective-permute-start | bytes 55304 | tf_op jit(solution)/shard_map/while/body/eval_jaxpr/ppermute | solution.py:21
  209.8 5.9 %collective-permute-start.1 = (bf16[128,1,72]{0,2,1:T(8,128)(2,1)S(1)}, bf16[128,1,72]{0,2,1:T(8,128)(2,1)S(1)}, u32[]{:S(2)}, u32[]{:S(2)}) collective-permute-start(bf16[128,1,72]{0,2,1:T(8,128)(2,1)S(1)} %copy.110), channel_id=1, source_target_pairs={{0,16},{16,32},{32,48},{48,64},{64,80},{80,96},{96,112},{112,128},... | collective-permute-start | bytes 55304 | tf_op jit(solution)/shard_map/while/body/eval_jaxpr/ppermute | solution.py:21
  218.6 5.9 %collective-permute-start.1 = (bf16[128,1,72]{0,2,1:T(8,128)(2,1)S(1)}, bf16[128,1,72]{0,2,1:T(8,128)(2,1)S(1)}, u32[]{:S(2)}, u32[]{:S(2)}) collective-permute-start(bf16[128,1,72]{0,2,1:T(8,128)(2,1)S(1)} %copy.110), channel_id=1, source_target_pairs={{0,16},{16,32},{32,48},{48,64},{64,80},{80,96},{96,112},{112,128},... | collective-permute-start | bytes 55304 | tf_op jit(solution)/shard_map/while/body/eval_jaxpr/ppermute | solution.py:21
  227.4 5.9 %collective-permute-start.1 = (bf16[128,1,72]{0,2,1:T(8,128)(2,1)S(1)}, bf16[128,1,72]{0,2,1:T(8,128)(2,1)S(1)}, u32[]{:S(2)}, u32[]{:S(2)}) collective-permute-start(bf16[128,1,72]{0,2,1:T(8,128)(2,1)S(1)} %copy.110), channel_id=1, source_target_pairs={{0,16},{16,32},{32,48},{48,64},{64,80},{80,96},{96,112},{112,128},... | collective-permute-start | bytes 55304 | tf_op jit(solution)/shard_map/while/body/eval_jaxpr/ppermute | solution.py:21
  236.2 5.9 %collective-permute-start.1 = (bf16[128,1,72]{0,2,1:T(8,128)(2,1)S(1)}, bf16[128,1,72]{0,2,1:T(8,128)(2,1)S(1)}, u32[]{:S(2)}, u32[]{:S(2)}) collective-permute-start(bf16[128,1,72]{0,2,1:T(8,128)(2,1)S(1)} %copy.110), channel_id=1, source_target_pairs={{0,16},{16,32},{32,48},{48,64},{64,80},{80,96},{96,112},{112,128},... | collective-permute-start | bytes 55304 | tf_op jit(solution)/shard_map/while/body/eval_jaxpr/ppermute | solution.py:21
  245.0 5.9 %collective-permute-start.1 = (bf16[128,1,72]{0,2,1:T(8,128)(2,1)S(1)}, bf16[128,1,72]{0,2,1:T(8,128)(2,1)S(1)}, u32[]{:S(2)}, u32[]{:S(2)}) collective-permute-start(bf16[128,1,72]{0,2,1:T(8,128)(2,1)S(1)} %copy.110), channel_id=1, source_target_pairs={{0,16},{16,32},{32,48},{48,64},{64,80},{80,96},{96,112},{112,128},... | collective-permute-start | bytes 55304 | tf_op jit(solution)/shard_map/while/body/eval_jaxpr/ppermute | solution.py:21
  253.8 5.9 %collective-permute-start.1 = (bf16[128,1,72]{0,2,1:T(8,128)(2,1)S(1)}, bf16[128,1,72]{0,2,1:T(8,128)(2,1)S(1)}, u32[]{:S(2)}, u32[]{:S(2)}) collective-permute-start(bf16[128,1,72]{0,2,1:T(8,128)(2,1)S(1)} %copy.110), channel_id=1, source_target_pairs={{0,16},{16,32},{32,48},{48,64},{64,80},{80,96},{96,112},{112,128},... | collective-permute-start | bytes 55304 | tf_op jit(solution)/shard_map/while/body/eval_jaxpr/ppermute | solution.py:21
  262.6 5.9 %collective-permute-start.1 = (bf16[128,1,72]{0,2,1:T(8,128)(2,1)S(1)}, bf16[128,1,72]{0,2,1:T(8,128)(2,1)S(1)}, u32[]{:S(2)}, u32[]{:S(2)}) collective-permute-start(bf16[128,1,72]{0,2,1:T(8,128)(2,1)S(1)} %copy.110), channel_id=1, source_target_pairs={{0,16},{16,32},{32,48},{48,64},{64,80},{80,96},{96,112},{112,128},... | collective-permute-start | bytes 55304 | tf_op jit(solution)/shard_map/while/body/eval_jaxpr/ppermute | solution.py:21
  271.4 5.9 %collective-permute-start.1 = (bf16[128,1,72]{0,2,1:T(8,128)(2,1)S(1)}, bf16[128,1,72]{0,2,1:T(8,128)(2,1)S(1)}, u32[]{:S(2)}, u32[]{:S(2)}) collective-permute-start(bf16[128,1,72]{0,2,1:T(8,128)(2,1)S(1)} %copy.110), channel_id=1, source_target_pairs={{0,16},{16,32},{32,48},{48,64},{64,80},{80,96},{96,112},{112,128},... | collective-permute-start | bytes 55304 | tf_op jit(solution)/shard_map/while/body/eval_jaxpr/ppermute | solution.py:21
  280.2 5.9 %collective-permute-start.1 = (bf16[128,1,72]{0,2,1:T(8,128)(2,1)S(1)}, bf16[128,1,72]{0,2,1:T(8,128)(2,1)S(1)}, u32[]{:S(2)}, u32[]{:S(2)}) collective-permute-start(bf16[128,1,72]{0,2,1:T(8,128)(2,1)S(1)} %copy.110), channel_id=1, source_target_pairs={{0,16},{16,32},{32,48},{48,64},{64,80},{80,96},{96,112},{112,128},... | collective-permute-start | bytes 55304 | tf_op jit(solution)/shard_map/while/body/eval_jaxpr/ppermute | solution.py:21
  289.0 5.9 %collective-permute-start.1 = (bf16[128,1,72]{0,2,1:T(8,128)(2,1)S(1)}, bf16[128,1,72]{0,2,1:T(8,128)(2,1)S(1)}, u32[]{:S(2)}, u32[]{:S(2)}) collective-permute-start(bf16[128,1,72]{0,2,1:T(8,128)(2,1)S(1)} %copy.110), channel_id=1, source_target_pairs={{0,16},{16,32},{32,48},{48,64},{64,80},{80,96},{96,112},{112,128},... | collective-permute-start | bytes 55304 | tf_op jit(solution)/shard_map/while/body/eval_jaxpr/ppermute | solution.py:21
  297.8 5.9 %collective-permute-start.1 = (bf16[128,1,72]{0,2,1:T(8,128)(2,1)S(1)}, bf16[128,1,72]{0,2,1:T(8,128)(2,1)S(1)}, u32[]{:S(2)}, u32[]{:S(2)}) collective-permute-start(bf16[128,1,72]{0,2,1:T(8,128)(2,1)S(1)} %copy.110), channel_id=1, source_target_pairs={{0,16},{16,32},{32,48},{48,64},{64,80},{80,96},{96,112},{112,128},... | collective-permute-start | bytes 55304 | tf_op jit(solution)/shard_map/while/body/eval_jaxpr/ppermute | solution.py:21
  306.6 5.9 %collective-permute-start.1 = (bf16[128,1,72]{0,2,1:T(8,128)(2,1)S(1)}, bf16[128,1,72]{0,2,1:T(8,128)(2,1)S(1)}, u32[]{:S(2)}, u32[]{:S(2)}) collective-permute-start(bf16[128,1,72]{0,2,1:T(8,128)(2,1)S(1)} %copy.110), channel_id=1, source_target_pairs={{0,16},{16,32},{32,48},{48,64},{64,80},{80,96},{96,112},{112,128},... | collective-permute-start | bytes 55304 | tf_op jit(solution)/shard_map/while/body/eval_jaxpr/ppermute | solution.py:21
  315.4 5.9 %collective-permute-start.1 = (bf16[128,1,72]{0,2,1:T(8,128)(2,1)S(1)}, bf16[128,1,72]{0,2,1:T(8,128)(2,1)S(1)}, u32[]{:S(2)}, u32[]{:S(2)}) collective-permute-start(bf16[128,1,72]{0,2,1:T(8,128)(2,1)S(1)} %copy.110), channel_id=1, source_target_pairs={{0,16},{16,32},{32,48},{48,64},{64,80},{80,96},{96,112},{112,128},... | collective-permute-start | bytes 55304 | tf_op jit(solution)/shard_map/while/body/eval_jaxpr/ppermute | solution.py:21
  324.2 5.9 %collective-permute-start.1 = (bf16[128,1,72]{0,2,1:T(8,128)(2,1)S(1)}, bf16[128,1,72]{0,2,1:T(8,128)(2,1)S(1)}, u32[]{:S(2)}, u32[]{:S(2)}) collective-permute-start(bf16[128,1,72]{0,2,1:T(8,128)(2,1)S(1)} %copy.110), channel_id=1, source_target_pairs={{0,16},{16,32},{32,48},{48,64},{64,80},{80,96},{96,112},{112,128},... | collective-permute-start | bytes 55304 | tf_op jit(solution)/shard_map/while/body/eval_jaxpr/ppermute | solution.py:21
  333.0 5.9 %collective-permute-start.1 = (bf16[128,1,72]{0,2,1:T(8,128)(2,1)S(1)}, bf16[128,1,72]{0,2,1:T(8,128)(2,1)S(1)}, u32[]{:S(2)}, u32[]{:S(2)}) collective-permute-start(bf16[128,1,72]{0,2,1:T(8,128)(2,1)S(1)} %copy.110), channel_id=1, source_target_pairs={{0,16},{16,32},{32,48},{48,64},{64,80},{80,96},{96,112},{112,128},... | collective-permute-start | bytes 55304 | tf_op jit(solution)/shard_map/while/body/eval_jaxpr/ppermute | solution.py:21
  342.6 7.6 %all-to-all-start.6 = ((bf16[2,64,72]{2,0,1:T(2,128)(2,1)}), bf16[2,64,72]{2,0,1:T(2,128)(2,1)S(1)}, u32[]{:S(2)}, u32[]{:S(2)}) async-start(bf16[2,64,72]{2,0,1:T(2,128)(2,1)} %copy.78), calls=%async_computation.6 | async-start | bytes 65536 | tf_op jit(solution)/shard_map/all_to_all | solution.py:165
  351.1 5.8 %all-to-all-done.6 = bf16[2,64,72]{2,0,1:T(2,128)(2,1)S(1)} async-done(((bf16[2,64,72]{2,0,1:T(2,128)(2,1)}), bf16[2,64,72]{2,0,1:T(2,128)(2,1)S(1)}, u32[]{:S(2)}, u32[]{:S(2)}) %all-to-all-start.6) | async-done | bytes 18464 | tf_op jit(solution)/shard_map/all_to_all | solution.py:165
  356.8 4.4 %all-to-all-start.7 = ((bf16[2,64,72]{2,0,1:T(2,128)(2,1)}), bf16[2,64,72]{2,0,1:T(2,128)(2,1)S(1)}, u32[]{:S(2)}, u32[]{:S(2)}) async-start(bf16[2,64,72]{2,0,1:T(2,128)(2,1)} %copy.81), calls=%async_computation.7 | async-start | bytes 65536 | tf_op jit(solution)/shard_map/all_to_all | solution.py:166
  362.6 5.3 %all-to-all-done.7 = bf16[2,64,72]{2,0,1:T(2,128)(2,1)S(1)} async-done(((bf16[2,64,72]{2,0,1:T(2,128)(2,1)}), bf16[2,64,72]{2,0,1:T(2,128)(2,1)S(1)}, u32[]{:S(2)}, u32[]{:S(2)}) %all-to-all-start.7) | async-done | bytes 18464 | tf_op jit(solution)/shard_map/all_to_all | solution.py:166
  367.9 4.5 %all-to-all-start.5 = ((bf16[8,256,72]{2,0,1:T(8,128)(2,1)}), bf16[8,256,72]{2,0,1:T(8,128)(2,1)S(1)}, u32[]{:S(2)}, u32[]{:S(2)}) async-start(bf16[8,256,72]{2,0,1:T(8,128)(2,1)} %copy.75), calls=%async_computation.5 | async-start | bytes 1048576 | tf_op jit(solution)/shard_map/all_to_all | solution.py:164
  373.1 10.2 %all-to-all-done.5 = bf16[8,256,72]{2,0,1:T(8,128)(2,1)S(1)} async-done(((bf16[8,256,72]{2,0,1:T(8,128)(2,1)}), bf16[8,256,72]{2,0,1:T(8,128)(2,1)S(1)}, u32[]{:S(2)}, u32[]{:S(2)}) %all-to-all-start.5) | async-done | bytes 294944 | tf_op jit(solution)/shard_map/all_to_all | solution.py:164
  384.1 5.7 %fusion.22 = bf16[8,16,1152]{2,1,0:T(8,128)(2,1)S(1)} fusion(bf16[1152,3456]{1,0:T(8,128)(2,1)} %param.16, bf16[8,16,1152]{2,1,0:T(8,128)(2,1)S(1)} %mul.81, bf16[8,16,1152]{2,1,0:T(8,128)(2,1)S(1)} %mul.76, bf16[8,16,1152]{2,1,0:T(8,128)(2,1)S(1)} %all_to_all.98), kind=kOutput, calls=%fused_computation.31 | convolution fusion | flops 1022017536 | bytes 9142272 | tf_op jit(solution)/shard_map/dot_general | solution.py:169
  389.9 11.3 %collective-permute-start.5 = (bf16[1,16,1152]{2,1,0:T(8,128)(2,1)S(1)}, bf16[1,16,1152]{2,1,0:T(8,128)(2,1)S(1)}, u32[]{:S(2)}, u32[]{:S(2)}) collective-permute-start(bf16[1,16,1152]{2,1,0:T(8,128)(2,1)S(1)} %get-tuple-element.222), channel_id=1, source_target_pairs={{0,16},{16,32},{32,48},{48,64},{64,80},{80,96},{96,112},{112,128},... | collective-permute-start | bytes 110600 | tf_op jit(solution)/shard_map/ppermute | solution.py:29
  403.2 7.0 %collective-permute-done.6 = bf16[1,16,1152]{2,1,0:T(8,128)(2,1)S(1)} collective-permute-done((bf16[1,16,1152]{2,1,0:T(8,128)(2,1)S(1)}, bf16[1,16,1152]{2,1,0:T(8,128)(2,1)S(1)}, u32[]{:S(2)}, u32[]{:S(2)}) %collective-permute-start.6) | collective-permute-done | bytes 36896 | tf_op jit(solution)/shard_map/ppermute | solution.py:32
  (432 shorter events, 138.3 us)
Async XLA Ops:
  2.6 15.9 %all-to-all-start = ((bf16[16,2,288]{2,1,0:T(2,128)(2,1)}), bf16[16,2,288]{2,1,0:T(2,128)(2,1)S(1)}, u32[]{:S(2)}, u32[]{:S(2)}) async-start(bf16[16,2,288]{2,1,0:T(2,128)(2,1)} %reshape.140), calls=%async_computation | async-start | bytes 49152 | tf_op jit(solution)/shard_map/all_to_all | solution.py:104
  19.1 10.9 %all-to-all-start.1 = ((bf16[16,2,288]{2,1,0:T(2,128)(2,1)}), bf16[16,2,288]{2,1,0:T(2,128)(2,1)S(1)}, u32[]{:S(2)}, u32[]{:S(2)}) async-start(bf16[16,2,288]{2,1,0:T(2,128)(2,1)} %reshape.142), calls=%async_computation.1 | async-start | bytes 49152 | tf_op jit(solution)/shard_map/all_to_all | solution.py:105
  30.6 16.0 %all-to-all-start.2 = ((bf16[16,2,4608]{2,1,0:T(2,128)(2,1)}), bf16[16,2,4608]{2,1,0:T(2,128)(2,1)S(1)}, u32[]{:S(2)}, u32[]{:S(2)}) async-start(bf16[16,2,4608]{2,1,0:T(2,128)(2,1)} %reshape.144), calls=%async_computation.2 | async-start | bytes 589824 | tf_op jit(solution)/shard_map/all_to_all | solution.py:103
  46.6 13.8 %all-to-all-start.3 = ((bf16[16,2,4608]{2,1,0:T(2,128)(2,1)}), bf16[16,2,4608]{2,1,0:T(2,128)(2,1)S(1)}, u32[]{:S(2)}, u32[]{:S(2)}) async-start(bf16[16,2,4608]{2,1,0:T(2,128)(2,1)} %reshape.146), calls=%async_computation.3 | async-start | bytes 589824 | tf_op jit(solution)/shard_map/all_to_all | solution.py:107
  60.4 22.6 %all-to-all-start.4 = ((bf16[16,2,4608]{2,1,0:T(2,128)(2,1)}), bf16[16,2,4608]{2,1,0:T(2,128)(2,1)}, u32[]{:S(2)}, u32[]{:S(2)}) async-start(bf16[16,2,4608]{2,1,0:T(2,128)(2,1)} %reshape.138), calls=%async_computation.4 | async-start | bytes 589824 | tf_op jit(solution)/shard_map/all_to_all | solution.py:106
  90.5 8.0 %collective-permute-start = (bf16[128,1,72]{0,2,1:T(8,128)(2,1)S(1)}, bf16[128,1,72]{0,2,1:T(8,128)(2,1)S(1)}, u32[]{:S(2)}, u32[]{:S(2)}) collective-permute-start(bf16[128,1,72]{0,2,1:T(8,128)(2,1)S(1)} %copy.96), channel_id=1, source_target_pairs={{0,16},{16,32},{32,48},{48,64},{64,80},{80,96},{96,112},{112,128},... | collective-permute-start | bytes 55304 | tf_op jit(solution)/shard_map/while/body/eval_jaxpr/ppermute | solution.py:21
  98.5 6.8 %collective-permute-start = (bf16[128,1,72]{0,2,1:T(8,128)(2,1)S(1)}, bf16[128,1,72]{0,2,1:T(8,128)(2,1)S(1)}, u32[]{:S(2)}, u32[]{:S(2)}) collective-permute-start(bf16[128,1,72]{0,2,1:T(8,128)(2,1)S(1)} %copy.96), channel_id=1, source_target_pairs={{0,16},{16,32},{32,48},{48,64},{64,80},{80,96},{96,112},{112,128},... | collective-permute-start | bytes 55304 | tf_op jit(solution)/shard_map/while/body/eval_jaxpr/ppermute | solution.py:21
  105.3 6.8 %collective-permute-start = (bf16[128,1,72]{0,2,1:T(8,128)(2,1)S(1)}, bf16[128,1,72]{0,2,1:T(8,128)(2,1)S(1)}, u32[]{:S(2)}, u32[]{:S(2)}) collective-permute-start(bf16[128,1,72]{0,2,1:T(8,128)(2,1)S(1)} %copy.96), channel_id=1, source_target_pairs={{0,16},{16,32},{32,48},{48,64},{64,80},{80,96},{96,112},{112,128},... | collective-permute-start | bytes 55304 | tf_op jit(solution)/shard_map/while/body/eval_jaxpr/ppermute | solution.py:21
  112.1 6.8 %collective-permute-start = (bf16[128,1,72]{0,2,1:T(8,128)(2,1)S(1)}, bf16[128,1,72]{0,2,1:T(8,128)(2,1)S(1)}, u32[]{:S(2)}, u32[]{:S(2)}) collective-permute-start(bf16[128,1,72]{0,2,1:T(8,128)(2,1)S(1)} %copy.96), channel_id=1, source_target_pairs={{0,16},{16,32},{32,48},{48,64},{64,80},{80,96},{96,112},{112,128},... | collective-permute-start | bytes 55304 | tf_op jit(solution)/shard_map/while/body/eval_jaxpr/ppermute | solution.py:21
  118.9 6.8 %collective-permute-start = (bf16[128,1,72]{0,2,1:T(8,128)(2,1)S(1)}, bf16[128,1,72]{0,2,1:T(8,128)(2,1)S(1)}, u32[]{:S(2)}, u32[]{:S(2)}) collective-permute-start(bf16[128,1,72]{0,2,1:T(8,128)(2,1)S(1)} %copy.96), channel_id=1, source_target_pairs={{0,16},{16,32},{32,48},{48,64},{64,80},{80,96},{96,112},{112,128},... | collective-permute-start | bytes 55304 | tf_op jit(solution)/shard_map/while/body/eval_jaxpr/ppermute | solution.py:21
  125.7 6.8 %collective-permute-start = (bf16[128,1,72]{0,2,1:T(8,128)(2,1)S(1)}, bf16[128,1,72]{0,2,1:T(8,128)(2,1)S(1)}, u32[]{:S(2)}, u32[]{:S(2)}) collective-permute-start(bf16[128,1,72]{0,2,1:T(8,128)(2,1)S(1)} %copy.96), channel_id=1, source_target_pairs={{0,16},{16,32},{32,48},{48,64},{64,80},{80,96},{96,112},{112,128},... | collective-permute-start | bytes 55304 | tf_op jit(solution)/shard_map/while/body/eval_jaxpr/ppermute | solution.py:21
  132.5 6.8 %collective-permute-start = (bf16[128,1,72]{0,2,1:T(8,128)(2,1)S(1)}, bf16[128,1,72]{0,2,1:T(8,128)(2,1)S(1)}, u32[]{:S(2)}, u32[]{:S(2)}) collective-permute-start(bf16[128,1,72]{0,2,1:T(8,128)(2,1)S(1)} %copy.96), channel_id=1, source_target_pairs={{0,16},{16,32},{32,48},{48,64},{64,80},{80,96},{96,112},{112,128},... | collective-permute-start | bytes 55304 | tf_op jit(solution)/shard_map/while/body/eval_jaxpr/ppermute | solution.py:21
  139.3 6.8 %collective-permute-start = (bf16[128,1,72]{0,2,1:T(8,128)(2,1)S(1)}, bf16[128,1,72]{0,2,1:T(8,128)(2,1)S(1)}, u32[]{:S(2)}, u32[]{:S(2)}) collective-permute-start(bf16[128,1,72]{0,2,1:T(8,128)(2,1)S(1)} %copy.96), channel_id=1, source_target_pairs={{0,16},{16,32},{32,48},{48,64},{64,80},{80,96},{96,112},{112,128},... | collective-permute-start | bytes 55304 | tf_op jit(solution)/shard_map/while/body/eval_jaxpr/ppermute | solution.py:21
  146.1 6.8 %collective-permute-start = (bf16[128,1,72]{0,2,1:T(8,128)(2,1)S(1)}, bf16[128,1,72]{0,2,1:T(8,128)(2,1)S(1)}, u32[]{:S(2)}, u32[]{:S(2)}) collective-permute-start(bf16[128,1,72]{0,2,1:T(8,128)(2,1)S(1)} %copy.96), channel_id=1, source_target_pairs={{0,16},{16,32},{32,48},{48,64},{64,80},{80,96},{96,112},{112,128},... | collective-permute-start | bytes 55304 | tf_op jit(solution)/shard_map/while/body/eval_jaxpr/ppermute | solution.py:21
  153.0 6.8 %collective-permute-start = (bf16[128,1,72]{0,2,1:T(8,128)(2,1)S(1)}, bf16[128,1,72]{0,2,1:T(8,128)(2,1)S(1)}, u32[]{:S(2)}, u32[]{:S(2)}) collective-permute-start(bf16[128,1,72]{0,2,1:T(8,128)(2,1)S(1)} %copy.96), channel_id=1, source_target_pairs={{0,16},{16,32},{32,48},{48,64},{64,80},{80,96},{96,112},{112,128},... | collective-permute-start | bytes 55304 | tf_op jit(solution)/shard_map/while/body/eval_jaxpr/ppermute | solution.py:21
  159.8 6.8 %collective-permute-start = (bf16[128,1,72]{0,2,1:T(8,128)(2,1)S(1)}, bf16[128,1,72]{0,2,1:T(8,128)(2,1)S(1)}, u32[]{:S(2)}, u32[]{:S(2)}) collective-permute-start(bf16[128,1,72]{0,2,1:T(8,128)(2,1)S(1)} %copy.96), channel_id=1, source_target_pairs={{0,16},{16,32},{32,48},{48,64},{64,80},{80,96},{96,112},{112,128},... | collective-permute-start | bytes 55304 | tf_op jit(solution)/shard_map/while/body/eval_jaxpr/ppermute | solution.py:21
  166.6 6.8 %collective-permute-start = (bf16[128,1,72]{0,2,1:T(8,128)(2,1)S(1)}, bf16[128,1,72]{0,2,1:T(8,128)(2,1)S(1)}, u32[]{:S(2)}, u32[]{:S(2)}) collective-permute-start(bf16[128,1,72]{0,2,1:T(8,128)(2,1)S(1)} %copy.96), channel_id=1, source_target_pairs={{0,16},{16,32},{32,48},{48,64},{64,80},{80,96},{96,112},{112,128},... | collective-permute-start | bytes 55304 | tf_op jit(solution)/shard_map/while/body/eval_jaxpr/ppermute | solution.py:21
  173.4 6.8 %collective-permute-start = (bf16[128,1,72]{0,2,1:T(8,128)(2,1)S(1)}, bf16[128,1,72]{0,2,1:T(8,128)(2,1)S(1)}, u32[]{:S(2)}, u32[]{:S(2)}) collective-permute-start(bf16[128,1,72]{0,2,1:T(8,128)(2,1)S(1)} %copy.96), channel_id=1, source_target_pairs={{0,16},{16,32},{32,48},{48,64},{64,80},{80,96},{96,112},{112,128},... | collective-permute-start | bytes 55304 | tf_op jit(solution)/shard_map/while/body/eval_jaxpr/ppermute | solution.py:21
  180.2 6.8 %collective-permute-start = (bf16[128,1,72]{0,2,1:T(8,128)(2,1)S(1)}, bf16[128,1,72]{0,2,1:T(8,128)(2,1)S(1)}, u32[]{:S(2)}, u32[]{:S(2)}) collective-permute-start(bf16[128,1,72]{0,2,1:T(8,128)(2,1)S(1)} %copy.96), channel_id=1, source_target_pairs={{0,16},{16,32},{32,48},{48,64},{64,80},{80,96},{96,112},{112,128},... | collective-permute-start | bytes 55304 | tf_op jit(solution)/shard_map/while/body/eval_jaxpr/ppermute | solution.py:21
  187.0 6.8 %collective-permute-start = (bf16[128,1,72]{0,2,1:T(8,128)(2,1)S(1)}, bf16[128,1,72]{0,2,1:T(8,128)(2,1)S(1)}, u32[]{:S(2)}, u32[]{:S(2)}) collective-permute-start(bf16[128,1,72]{0,2,1:T(8,128)(2,1)S(1)} %copy.96), channel_id=1, source_target_pairs={{0,16},{16,32},{32,48},{48,64},{64,80},{80,96},{96,112},{112,128},... | collective-permute-start | bytes 55304 | tf_op jit(solution)/shard_map/while/body/eval_jaxpr/ppermute | solution.py:21
  193.8 6.8 %collective-permute-start = (bf16[128,1,72]{0,2,1:T(8,128)(2,1)S(1)}, bf16[128,1,72]{0,2,1:T(8,128)(2,1)S(1)}, u32[]{:S(2)}, u32[]{:S(2)}) collective-permute-start(bf16[128,1,72]{0,2,1:T(8,128)(2,1)S(1)} %copy.96), channel_id=1, source_target_pairs={{0,16},{16,32},{32,48},{48,64},{64,80},{80,96},{96,112},{112,128},... | collective-permute-start | bytes 55304 | tf_op jit(solution)/shard_map/while/body/eval_jaxpr/ppermute | solution.py:21
  200.9 8.2 %collective-permute-start.1 = (bf16[128,1,72]{0,2,1:T(8,128)(2,1)S(1)}, bf16[128,1,72]{0,2,1:T(8,128)(2,1)S(1)}, u32[]{:S(2)}, u32[]{:S(2)}) collective-permute-start(bf16[128,1,72]{0,2,1:T(8,128)(2,1)S(1)} %copy.110), channel_id=1, source_target_pairs={{0,16},{16,32},{32,48},{48,64},{64,80},{80,96},{96,112},{112,128},... | collective-permute-start | bytes 55304 | tf_op jit(solution)/shard_map/while/body/eval_jaxpr/ppermute | solution.py:21
  206.9 2.2 collective-permute-start.2
  209.8 8.1 %collective-permute-start.1 = (bf16[128,1,72]{0,2,1:T(8,128)(2,1)S(1)}, bf16[128,1,72]{0,2,1:T(8,128)(2,1)S(1)}, u32[]{:S(2)}, u32[]{:S(2)}) collective-permute-start(bf16[128,1,72]{0,2,1:T(8,128)(2,1)S(1)} %copy.110), channel_id=1, source_target_pairs={{0,16},{16,32},{32,48},{48,64},{64,80},{80,96},{96,112},{112,128},... | collective-permute-start | bytes 55304 | tf_op jit(solution)/shard_map/while/body/eval_jaxpr/ppermute | solution.py:21
  218.6 8.1 %collective-permute-start.1 = (bf16[128,1,72]{0,2,1:T(8,128)(2,1)S(1)}, bf16[128,1,72]{0,2,1:T(8,128)(2,1)S(1)}, u32[]{:S(2)}, u32[]{:S(2)}) collective-permute-start(bf16[128,1,72]{0,2,1:T(8,128)(2,1)S(1)} %copy.110), channel_id=1, source_target_pairs={{0,16},{16,32},{32,48},{48,64},{64,80},{80,96},{96,112},{112,128},... | collective-permute-start | bytes 55304 | tf_op jit(solution)/shard_map/while/body/eval_jaxpr/ppermute | solution.py:21
  224.5 2.2 collective-permute-start.2
  227.4 8.1 %collective-permute-start.1 = (bf16[128,1,72]{0,2,1:T(8,128)(2,1)S(1)}, bf16[128,1,72]{0,2,1:T(8,128)(2,1)S(1)}, u32[]{:S(2)}, u32[]{:S(2)}) collective-permute-start(bf16[128,1,72]{0,2,1:T(8,128)(2,1)S(1)} %copy.110), channel_id=1, source_target_pairs={{0,16},{16,32},{32,48},{48,64},{64,80},{80,96},{96,112},{112,128},... | collective-permute-start | bytes 55304 | tf_op jit(solution)/shard_map/while/body/eval_jaxpr/ppermute | solution.py:21
  236.2 8.1 %collective-permute-start.1 = (bf16[128,1,72]{0,2,1:T(8,128)(2,1)S(1)}, bf16[128,1,72]{0,2,1:T(8,128)(2,1)S(1)}, u32[]{:S(2)}, u32[]{:S(2)}) collective-permute-start(bf16[128,1,72]{0,2,1:T(8,128)(2,1)S(1)} %copy.110), channel_id=1, source_target_pairs={{0,16},{16,32},{32,48},{48,64},{64,80},{80,96},{96,112},{112,128},... | collective-permute-start | bytes 55304 | tf_op jit(solution)/shard_map/while/body/eval_jaxpr/ppermute | solution.py:21
  245.0 8.1 %collective-permute-start.1 = (bf16[128,1,72]{0,2,1:T(8,128)(2,1)S(1)}, bf16[128,1,72]{0,2,1:T(8,128)(2,1)S(1)}, u32[]{:S(2)}, u32[]{:S(2)}) collective-permute-start(bf16[128,1,72]{0,2,1:T(8,128)(2,1)S(1)} %copy.110), channel_id=1, source_target_pairs={{0,16},{16,32},{32,48},{48,64},{64,80},{80,96},{96,112},{112,128},... | collective-permute-start | bytes 55304 | tf_op jit(solution)/shard_map/while/body/eval_jaxpr/ppermute | solution.py:21
  250.9 2.2 collective-permute-start.2
  253.8 8.1 %collective-permute-start.1 = (bf16[128,1,72]{0,2,1:T(8,128)(2,1)S(1)}, bf16[128,1,72]{0,2,1:T(8,128)(2,1)S(1)}, u32[]{:S(2)}, u32[]{:S(2)}) collective-permute-start(bf16[128,1,72]{0,2,1:T(8,128)(2,1)S(1)} %copy.110), channel_id=1, source_target_pairs={{0,16},{16,32},{32,48},{48,64},{64,80},{80,96},{96,112},{112,128},... | collective-permute-start | bytes 55304 | tf_op jit(solution)/shard_map/while/body/eval_jaxpr/ppermute | solution.py:21
  262.6 8.1 %collective-permute-start.1 = (bf16[128,1,72]{0,2,1:T(8,128)(2,1)S(1)}, bf16[128,1,72]{0,2,1:T(8,128)(2,1)S(1)}, u32[]{:S(2)}, u32[]{:S(2)}) collective-permute-start(bf16[128,1,72]{0,2,1:T(8,128)(2,1)S(1)} %copy.110), channel_id=1, source_target_pairs={{0,16},{16,32},{32,48},{48,64},{64,80},{80,96},{96,112},{112,128},... | collective-permute-start | bytes 55304 | tf_op jit(solution)/shard_map/while/body/eval_jaxpr/ppermute | solution.py:21
  271.4 8.1 %collective-permute-start.1 = (bf16[128,1,72]{0,2,1:T(8,128)(2,1)S(1)}, bf16[128,1,72]{0,2,1:T(8,128)(2,1)S(1)}, u32[]{:S(2)}, u32[]{:S(2)}) collective-permute-start(bf16[128,1,72]{0,2,1:T(8,128)(2,1)S(1)} %copy.110), channel_id=1, source_target_pairs={{0,16},{16,32},{32,48},{48,64},{64,80},{80,96},{96,112},{112,128},... | collective-permute-start | bytes 55304 | tf_op jit(solution)/shard_map/while/body/eval_jaxpr/ppermute | solution.py:21
  277.3 2.2 collective-permute-start.2
  280.2 8.1 %collective-permute-start.1 = (bf16[128,1,72]{0,2,1:T(8,128)(2,1)S(1)}, bf16[128,1,72]{0,2,1:T(8,128)(2,1)S(1)}, u32[]{:S(2)}, u32[]{:S(2)}) collective-permute-start(bf16[128,1,72]{0,2,1:T(8,128)(2,1)S(1)} %copy.110), channel_id=1, source_target_pairs={{0,16},{16,32},{32,48},{48,64},{64,80},{80,96},{96,112},{112,128},... | collective-permute-start | bytes 55304 | tf_op jit(solution)/shard_map/while/body/eval_jaxpr/ppermute | solution.py:21
  289.0 8.1 %collective-permute-start.1 = (bf16[128,1,72]{0,2,1:T(8,128)(2,1)S(1)}, bf16[128,1,72]{0,2,1:T(8,128)(2,1)S(1)}, u32[]{:S(2)}, u32[]{:S(2)}) collective-permute-start(bf16[128,1,72]{0,2,1:T(8,128)(2,1)S(1)} %copy.110), channel_id=1, source_target_pairs={{0,16},{16,32},{32,48},{48,64},{64,80},{80,96},{96,112},{112,128},... | collective-permute-start | bytes 55304 | tf_op jit(solution)/shard_map/while/body/eval_jaxpr/ppermute | solution.py:21
  297.8 8.1 %collective-permute-start.1 = (bf16[128,1,72]{0,2,1:T(8,128)(2,1)S(1)}, bf16[128,1,72]{0,2,1:T(8,128)(2,1)S(1)}, u32[]{:S(2)}, u32[]{:S(2)}) collective-permute-start(bf16[128,1,72]{0,2,1:T(8,128)(2,1)S(1)} %copy.110), channel_id=1, source_target_pairs={{0,16},{16,32},{32,48},{48,64},{64,80},{80,96},{96,112},{112,128},... | collective-permute-start | bytes 55304 | tf_op jit(solution)/shard_map/while/body/eval_jaxpr/ppermute | solution.py:21
  306.6 8.1 %collective-permute-start.1 = (bf16[128,1,72]{0,2,1:T(8,128)(2,1)S(1)}, bf16[128,1,72]{0,2,1:T(8,128)(2,1)S(1)}, u32[]{:S(2)}, u32[]{:S(2)}) collective-permute-start(bf16[128,1,72]{0,2,1:T(8,128)(2,1)S(1)} %copy.110), channel_id=1, source_target_pairs={{0,16},{16,32},{32,48},{48,64},{64,80},{80,96},{96,112},{112,128},... | collective-permute-start | bytes 55304 | tf_op jit(solution)/shard_map/while/body/eval_jaxpr/ppermute | solution.py:21
  315.4 8.1 %collective-permute-start.1 = (bf16[128,1,72]{0,2,1:T(8,128)(2,1)S(1)}, bf16[128,1,72]{0,2,1:T(8,128)(2,1)S(1)}, u32[]{:S(2)}, u32[]{:S(2)}) collective-permute-start(bf16[128,1,72]{0,2,1:T(8,128)(2,1)S(1)} %copy.110), channel_id=1, source_target_pairs={{0,16},{16,32},{32,48},{48,64},{64,80},{80,96},{96,112},{112,128},... | collective-permute-start | bytes 55304 | tf_op jit(solution)/shard_map/while/body/eval_jaxpr/ppermute | solution.py:21
  324.2 8.1 %collective-permute-start.1 = (bf16[128,1,72]{0,2,1:T(8,128)(2,1)S(1)}, bf16[128,1,72]{0,2,1:T(8,128)(2,1)S(1)}, u32[]{:S(2)}, u32[]{:S(2)}) collective-permute-start(bf16[128,1,72]{0,2,1:T(8,128)(2,1)S(1)} %copy.110), channel_id=1, source_target_pairs={{0,16},{16,32},{32,48},{48,64},{64,80},{80,96},{96,112},{112,128},... | collective-permute-start | bytes 55304 | tf_op jit(solution)/shard_map/while/body/eval_jaxpr/ppermute | solution.py:21
  333.0 8.1 %collective-permute-start.1 = (bf16[128,1,72]{0,2,1:T(8,128)(2,1)S(1)}, bf16[128,1,72]{0,2,1:T(8,128)(2,1)S(1)}, u32[]{:S(2)}, u32[]{:S(2)}) collective-permute-start(bf16[128,1,72]{0,2,1:T(8,128)(2,1)S(1)} %copy.110), channel_id=1, source_target_pairs={{0,16},{16,32},{32,48},{48,64},{64,80},{80,96},{96,112},{112,128},... | collective-permute-start | bytes 55304 | tf_op jit(solution)/shard_map/while/body/eval_jaxpr/ppermute | solution.py:21
  342.6 14.2 %all-to-all-start.6 = ((bf16[2,64,72]{2,0,1:T(2,128)(2,1)}), bf16[2,64,72]{2,0,1:T(2,128)(2,1)S(1)}, u32[]{:S(2)}, u32[]{:S(2)}) async-start(bf16[2,64,72]{2,0,1:T(2,128)(2,1)} %copy.78), calls=%async_computation.6 | async-start | bytes 65536 | tf_op jit(solution)/shard_map/all_to_all | solution.py:165
  356.8 11.1 %all-to-all-start.7 = ((bf16[2,64,72]{2,0,1:T(2,128)(2,1)}), bf16[2,64,72]{2,0,1:T(2,128)(2,1)S(1)}, u32[]{:S(2)}, u32[]{:S(2)}) async-start(bf16[2,64,72]{2,0,1:T(2,128)(2,1)} %copy.81), calls=%async_computation.7 | async-start | bytes 65536 | tf_op jit(solution)/shard_map/all_to_all | solution.py:166
  367.9 15.4 %all-to-all-start.5 = ((bf16[8,256,72]{2,0,1:T(8,128)(2,1)}), bf16[8,256,72]{2,0,1:T(8,128)(2,1)S(1)}, u32[]{:S(2)}, u32[]{:S(2)}) async-start(bf16[8,256,72]{2,0,1:T(8,128)(2,1)} %copy.75), calls=%async_computation.5 | async-start | bytes 1048576 | tf_op jit(solution)/shard_map/all_to_all | solution.py:164
  389.9 13.3 %collective-permute-start.5 = (bf16[1,16,1152]{2,1,0:T(8,128)(2,1)S(1)}, bf16[1,16,1152]{2,1,0:T(8,128)(2,1)S(1)}, u32[]{:S(2)}, u32[]{:S(2)}) collective-permute-start(bf16[1,16,1152]{2,1,0:T(8,128)(2,1)S(1)} %get-tuple-element.222), channel_id=1, source_target_pairs={{0,16},{16,32},{32,48},{48,64},{64,80},{80,96},{96,112},{112,128},... | collective-permute-start | bytes 110600 | tf_op jit(solution)/shard_map/ppermute | solution.py:29
  401.3 8.9 %collective-permute-start.6 = (bf16[1,16,1152]{2,1,0:T(8,128)(2,1)S(1)}, bf16[1,16,1152]{2,1,0:T(8,128)(2,1)S(1)}, u32[]{:S(2)}, u32[]{:S(2)}) collective-permute-start(bf16[1,16,1152]{2,1,0:T(8,128)(2,1)S(1)} %get-tuple-element.223), channel_id=1, source_target_pairs={{16,0},{32,16},{48,32},{64,48},{80,64},{96,80},{112,96},{128,112},... | collective-permute-start | bytes 110600 | tf_op jit(solution)/shard_map/ppermute | solution.py:32
  410.2 5.7 %collective-permute-start.7 = (bf16[10,1,1152]{2,1,0:T(2,128)(2,1)S(1)}, bf16[10,1,1152]{2,1,0:T(2,128)(2,1)S(1)}, u32[]{:S(2)}, u32[]{:S(2)}) collective-permute-start(bf16[10,1,1152]{2,1,0:T(2,128)(2,1)S(1)} %get-tuple-element.220), channel_id=1, source_target_pairs={{0,1},{1,2},{2,3},{3,4},{4,5},{5,6},{6,7},{7,8},{8,9},{9,10},{10,1... | collective-permute-start | bytes 69128 | tf_op jit(solution)/shard_map/ppermute | solution.py:29
  414.0 5.7 %collective-permute-start.8 = (bf16[10,1,1152]{2,1,0:T(2,128)(2,1)S(1)}, bf16[10,1,1152]{2,1,0:T(2,128)(2,1)S(1)}, u32[]{:S(2)}, u32[]{:S(2)}) collective-permute-start(bf16[10,1,1152]{2,1,0:T(2,128)(2,1)S(1)} %get-tuple-element.221), channel_id=1, source_target_pairs={{1,0},{2,1},{3,2},{4,3},{5,4},{6,5},{7,6},{8,7},{9,8},{10,9},{11,1... | collective-permute-start | bytes 69128 | tf_op jit(solution)/shard_map/ppermute | solution.py:32
  (55 other events, 748.5 us)
where the time goes:
time: 424 us; the launch traced here: 422 us
  starting transfers between devices  260 us (61%)
  waiting for transfers between devices  58.8 us (14%)
  local copies, waits for them, and re-layouts  54.6 us (13%)
  matrix products  42.7 us (10%)
    ppermute x80, starting transfers between devices, shifted(): return lax.ppermute(x, axis, [(i, (i + by) % peers) for i in range(peers)])  194 us
    unnamed x43, local copies, waits for them, and re-layouts  39.7 us
    ppermute x80, waiting for transfers between devices, shifted(): return lax.ppermute(x, axis, [(i, (i + by) % peers) for i in range(peers)])  15.9 us
    ppermute x2, starting transfers between devices, padded(): lax.ppermute(lax.slice_in_dim(block, block.shape[dim] - width, None, axis...  15.1 us
    dot_general x32, matrix products, score_block(): jnp.einsum('qhd,khd->hqk', queries_h, key_block, preferred_element_type=j...  13.4 us
    ppermute x2, waiting for transfers between devices, padded(): lax.ppermute(lax.slice_in_dim(block, 0, width, axis=dim), axis, backward)  10.7 us
    all_to_all x1, waiting for transfers between devices, on_device(): lax.all_to_all(grad_query, 'col', split_axis=1, concat_axis=2, tiled=True)  10.2 us
    all_to_all x1, starting transfers between devices, on_device(): lax.all_to_all(key_states, 'col', split_axis=2, concat_axis=1, tiled=True)  9.38 us
  transfers between devices with their start and end apart: 92, of which 57 were waited for; matrix products, arithmetic and copies ran while one was open for 19% of the time, Pallas kernels for 0%

commit v1 on v0

v1 whole, which is shorter than its diff:
```python
import math

import jax
import jax.numpy as jnp
from jax import lax
from jax.experimental import pallas as pl
from jax.experimental.pallas import tpu as pltpu
from jax.sharding import Mesh, PartitionSpec as P

D = 1152
HEADS = 16
DH = D // HEADS
POOL = 4
SCALE = DH**-0.5
SCALE2 = SCALE * math.log2(math.e)
ROWS, COLS = 8, 16
TOK = ROWS * COLS
CELLS = TOK // POOL**2
FPAD = 80
KEYS = 2048
HEAD_AXES = ("yh", "x", "yl")
BLK = ("yh", "x", "c")
COL = ("z", "yl")
NT = (((1,), (1,)), ((), ()))
VMEM = 48 * 2**20
bf16, f32 = jnp.bfloat16, jnp.float32


def call(kernel, shapes, scratch=()):
    return pl.pallas_call(
        kernel,
        out_shape=shapes,
        scratch_shapes=scratch,
        compiler_params=pltpu.CompilerParams(vmem_limit_bytes=VMEM),
    )


def pack_kernel(q_ref, g_ref, o_ref, k_ref, v_ref, send_ref):
    q_t = q_ref[...].astype(f32).T
    g_t = g_ref[...].astype(f32).T
    prod = g_t * o_ref[...].astype(f32).T
    keys = k_ref[...].astype(f32)
    vals = v_ref[...].astype(f32)
    row = lax.broadcasted_iota(jnp.int32, (8, TOK), 0)
    lanes = jnp.zeros((CELLS, 128 - DH), f32)
    lane = lax.broadcasted_iota(jnp.int32, (CELLS, 128 - DH), 1)
    ones = jnp.where(lane < 3, 1.0, 0.0).astype(f32)
    for h in range(HEADS):
        part = slice(h * DH, (h + 1) * DH)
        dot = -jnp.sum(prod[part], axis=0, keepdims=True)
        high = dot.astype(bf16).astype(f32)
        mid = (dot - high).astype(bf16).astype(f32)
        low = dot - high - mid
        dots = jnp.where(row == 0, high, jnp.where(row == 1, mid, jnp.where(row == 2, low, 0.0)))
        send_ref[h, 0:FPAD, :] = jnp.concatenate([q_t[part], jnp.zeros((8, TOK), f32)]).astype(bf16)
        send_ref[h, FPAD : 2 * FPAD, :] = jnp.concatenate([g_t[part], dots]).astype(bf16)
        k_h = jnp.concatenate([keys[:, part], lanes], axis=1)
        v_h = jnp.concatenate([vals[:, part], ones], axis=1)
        send_ref[h, 2 * FPAD : 2 * FPAD + 16, :] = jnp.concatenate([k_h, v_h]).astype(bf16)


def attention_kernel(
    qg_ref, kv_own, kv_other, dq_ref, own_ref, other_ref, k_s, v_s, kt_s, e_s, dk_s, dv_s
):
    half = KEYS // 2
    for at, kv_ref in ((0, kv_own), (half, kv_other)):
        kv = kv_ref[...].astype(f32).reshape(8 * HEADS, 2, CELLS, 128)
        keys = kv[:, 0].reshape(half, 128)
        k_s[at : at + half] = keys.astype(bf16)
        kt_s[:, at : at + half] = keys.T.astype(bf16)
        v_s[at : at + half] = kv[:, 1].reshape(half, 128).astype(bf16)
    dk_s[...] = jnp.zeros_like(dk_s)
    dv_s[...] = jnp.zeros_like(dv_s)
    step = 512
    blocks = [slice(at, at + step) for at in range(0, KEYS, step)]

    def tile(t, _):
        q_t = jnp.concatenate([qg_ref[2 * t, 0:FPAD], qg_ref[2 * t + 1, 0:FPAD]], axis=1)
        g_t = jnp.concatenate(
            [qg_ref[2 * t, FPAD : 2 * FPAD], qg_ref[2 * t + 1, FPAD : 2 * FPAD]], axis=1
        )
        top = jnp.full((1, 2 * TOK), -jnp.inf, f32)
        for b in blocks:
            scores = jnp.dot(k_s[b, 0:FPAD], q_t, preferred_element_type=f32)
            e_s[b] = scores
            top = jnp.maximum(top, jnp.max(scores, axis=0, keepdims=True))
        top = top * SCALE2
        total = jnp.zeros((1, 2 * TOK), f32)
        for b in blocks:
            exps = jnp.exp2(e_s[b] * SCALE2 - top)
            e_s[b] = exps
            total = total + jnp.sum(exps, axis=0, keepdims=True)
        inverse = 1.0 / total
        dq = jnp.zeros((FPAD, 2 * TOK), f32)
        for b in blocks:
            probs = e_s[b] * inverse
            half_probs = probs.astype(bf16)
            shifted = jnp.dot(v_s[b, 0:FPAD], g_t, preferred_element_type=f32)
            ds = (probs * shifted).astype(bf16)
            dk_s[b, 0:FPAD] += lax.dot_general(ds, q_t, NT, preferred_element_type=f32)
            dv_s[b, 0:FPAD] += lax.dot_general(half_probs, g_t, NT, preferred_element_type=f32)
            dq = dq + jnp.dot(kt_s[0:FPAD, b], ds, preferred_element_type=f32)
        dq = (dq * SCALE).astype(bf16)
        dq_ref[2 * t] = dq[:, 0:TOK]
        dq_ref[2 * t + 1] = dq[:, TOK:]
        return 0

    lax.fori_loop(0, HEADS // 2, tile, 0)
    dk_t = dk_s[...].T
    dv_t = dv_s[...].T
    for out, at in ((own_ref, 0), (other_ref, half)):
        for b in range(8):
            keys = slice(at + b * 128, at + (b + 1) * 128)
            out[b, 0:DH] = dk_t[0:DH, keys] * SCALE
            out[b, DH : 2 * DH] = dv_t[0:DH, keys]


def pack_back_kernel(dq_ref, mine_ref, came_ref, send_ref):
    total = mine_ref[...] + came_ref[...].astype(f32)
    lanes = jnp.zeros((128, 128 - DH), f32)
    dk = jnp.concatenate([total[0:DH].T, lanes], axis=1)
    dv = jnp.concatenate([total[DH : 2 * DH].T, lanes], axis=1)
    send_ref[:, 0:FPAD, :] = dq_ref[...]
    for a in range(HEADS):
        cells = slice(a * CELLS, (a + 1) * CELLS)
        send_ref[a, FPAD : FPAD + 16, :] = jnp.concatenate([dk[cells], dv[cells]]).astype(bf16)


def embed_kernel(back_ref, q_hi, q_lo, kv_hi, kv_lo, out_ref):
    dq_t = back_ref[:, 0:FPAD, :].reshape(HEADS * FPAD, TOK)
    rows = (((0,), (0,)), ((), ()))
    patch = lax.dot_general(dq_t, q_hi[...], rows, preferred_element_type=f32)
    patch = patch + lax.dot_general(dq_t, q_lo[...], rows, preferred_element_type=f32)
    cell = jnp.zeros((CELLS, 256), f32)
    for h in range(HEADS):
        pooled = back_ref[h, FPAD : FPAD + 16, :].astype(f32)
        for part in (0, 1):
            mine = pooled[part * CELLS : (part + 1) * CELLS].astype(bf16)
            for w in (kv_hi, kv_lo):
                cell = cell + jnp.dot(mine, w[part, h], preferred_element_type=f32)
    cell = cell * (1.0 / POOL**2)
    spread = cell.reshape(CELLS // 4, 4, 1, 256)
    spread = jnp.broadcast_to(spread, (CELLS // 4, 4, POOL, 256)).reshape(CELLS // 4, 1, COLS, 256)
    spread = jnp.broadcast_to(spread, (CELLS // 4, POOL, COLS, 256)).reshape(TOK, 256)
    out_ref[...] = patch + spread


def swapped(x, axis, by):
    peers = lax.axis_size(axis)
    return lax.ppermute(x, axis, [(i, i ^ by) for i in range(peers)])


def fold_blocks(padded_patch, row_count, col_count):
    total = None
    for row_step in (0, 1):
        for col_step in (0, 1):
            piece = padded_patch[
                1 - row_step : row_count + 2 - row_step,
                1 - col_step : col_count + 2 - col_step,
                row_step,
                :,
                col_step,
                :,
            ]
            total = piece if total is None else total + piece
    return total.transpose(0, 2, 1, 3).reshape(8 * (row_count + 1), 8 * (col_count + 1))


def edges_added(canvas, axis, dim):
    count = lax.axis_size(axis)
    size = canvas.shape[dim]
    forward = [(i, i + 1) for i in range(count - 1)]
    backward = [(target, source) for source, target in forward]
    last = lax.ppermute(lax.slice_in_dim(canvas, size - 4, size, axis=dim), axis, forward)
    first = lax.ppermute(lax.slice_in_dim(canvas, 0, 4, axis=dim), axis, backward)
    parts = [
        lax.slice_in_dim(canvas, 4, 8, axis=dim) + last,
        lax.slice_in_dim(canvas, 8, size - 8, axis=dim),
        lax.slice_in_dim(canvas, size - 8, size - 4, axis=dim) + first,
    ]
    return jnp.concatenate(parts, axis=dim)


def combined_weights(w_qkv, w_patch):
    both = lax.dot_general(w_qkv, w_patch, (((0,), (1,)), ((), ())), preferred_element_type=f32)
    both = both.reshape(3, HEADS, DH, 256)
    high = lax.reduce_precision(both, 8, 7)
    low = both - high

    def padded(x, to):
        return jnp.pad(x.astype(bf16), ((0, 0),) * (x.ndim - 2) + ((0, to - DH), (0, 0)))

    return [
        padded(high[0], FPAD).reshape(HEADS * FPAD, 256),
        padded(low[0], FPAD).reshape(HEADS * FPAD, 256),
        padded(high[1:], 128),
        padded(low[1:], 128),
    ]


def on_device(queries, key_states, values, saved_out, grad_out, w_qkv, w_patch):
    weights = combined_weights(w_qkv, w_patch)
    send = call(pack_kernel, jax.ShapeDtypeStruct((HEADS, 2 * FPAD + 16, TOK), bf16))(
        queries.reshape(TOK, D),
        grad_out.reshape(TOK, D),
        saved_out.reshape(TOK, D),
        key_states.reshape(CELLS, D),
        values.reshape(CELLS, D),
    )
    got = lax.all_to_all(send, HEAD_AXES, 0, 0, tiled=True)
    kv = got[:, 2 * FPAD :, :][None]
    for by in (1, 2, 4):
        kv = jnp.concatenate([kv, swapped(kv, "z", by)])
    kv_other = swapped(kv, "c", 1)
    grads = jax.ShapeDtypeStruct((8, 2 * DH, 128), f32)
    dq, own, other = call(
        attention_kernel,
        [jax.ShapeDtypeStruct((HEADS, FPAD, TOK), bf16), grads, grads],
        [
            pltpu.VMEM((KEYS, 128), bf16),
            pltpu.VMEM((KEYS, 128), bf16),
            pltpu.VMEM((128, KEYS), bf16),
            pltpu.VMEM((KEYS, 2 * TOK), f32),
            pltpu.VMEM((KEYS, 128), f32),
            pltpu.VMEM((KEYS, 128), f32),
        ],
    )(got, kv, kv_other)
    mine = own + swapped(other, "c", 1)
    for by in (4, 2):
        mine = mine[:by] + swapped(mine[by:].astype(bf16), "z", by).astype(f32)
    came = swapped(mine[1].astype(bf16), "z", 1)
    send = call(pack_back_kernel, jax.ShapeDtypeStruct((HEADS, FPAD + 16, TOK), bf16))(
        dq, mine[0], came
    )
    back = lax.all_to_all(send, HEAD_AXES, 0, 0, tiled=True)
    patch = call(embed_kernel, jax.ShapeDtypeStruct((TOK, 256), f32))(back, *weights)
    patch = patch.reshape(ROWS, COLS, 2, 8, 2, 8)
    patch = jnp.pad(patch, ((1, 1), (1, 1), (0, 0), (0, 0), (0, 0), (0, 0)))
    canvas = fold_blocks(patch, ROWS, COLS)
    canvas = edges_added(canvas, BLK, 0)
    return edges_added(canvas, COL, 1)


def solution(mesh):
    fine = Mesh(mesh.devices.reshape(2, 4, 2, 8, 2), ("yh", "x", "c", "z", "yl"))
    split = P(BLK, COL, None)
    return jax.shard_map(
        on_device,
        mesh=fine,
        in_specs=(split, split, split, split, split, P(), P()),
        out_specs=P(BLK, COL),
        check_vma=False,
    )
```

time: 424 us -> 149 us (0.35)
  starting transfers between devices: 260 us -> 60.9 us
  local copies, waits for them, and re-layouts: 54.6 us -> 13.2 us
  matrix products: 42.7 us -> 4.27 us
  waiting for transfers between devices: 58.8 us -> 30.8 us
  Pallas kernels: 0 us -> 19.7 us
  blocking collectives: 0 us -> 16.3 us
    ppermute x84 -> x12, starting transfers between devices: 213 us -> 48.9 us  [the longest x8 33.3 us: swapped(): return lax.ppermute(x, axis, [(i, i ^ by) for i in range(peers)])]
    dot_general x98 -> x1, matrix products: 42.7 us -> 4.27 us  [combined_weights(): lax.dot_general(w_qkv, w_patch, (((0,), (1,)), ((), ())), preferred_eleme...]
    all_to_all x8 -> x1, starting transfers between devices: 46.9 us -> 12 us  [on_device(): back = lax.all_to_all(send, HEAD_AXES, 0, 0, tiled=True)]
    unnamed x43 -> x14, local copies, waits for them, and re-layouts: 39.7 us -> 5.57 us
    all_to_all x8 -> x1, waiting for transfers between devices: 32.2 us -> 0.01 us  [on_device(): back = lax.all_to_all(send, HEAD_AXES, 0, 0, tiled=True)]
    pallas_call x0 -> x4, Pallas kernels: none -> 19.7 us  [the longest x1 16.6 us: on_device(): call(attention_kernel, [jax.ShapeDtypeStruct((HEADS, FPAD, TOK), bf16), g...]
    all_to_all x0 -> x1, blocking collectives: none -> 16.3 us  [on_device(): got = lax.all_to_all(send, HEAD_AXES, 0, 0, tiled=True)]
    all_to_all x6 -> x0, local copies, waits for them, and re-layouts: 6.9 us -> none  [the longest x1 2.75 us: on_device(): lax.all_to_all(grad_out, 'col', split_axis=2, concat_axis=1, tiled=True)]
  transfers between devices with their start and end apart: 92 -> 13, of which waited for: 57 -> 11; matrix products, arithmetic and copies ran while one was open for 19% -> 7% of each run, Pallas kernels for 0% -> 0%
where the time goes in v1:
time: 149 us
  starting transfers between devices  60.9 us (41%)
  waiting for transfers between devices  30.8 us (21%)
  Pallas kernels  19.7 us (13%)
  blocking collectives  16.3 us (11%)
  local copies, waits for them, and re-layouts  13.2 us (9%)
  matrix products  4.27 us (3%)
  other arithmetic  3.38 us (2%)
    ppermute x8, starting transfers between devices, swapped(): return lax.ppermute(x, axis, [(i, i ^ by) for i in range(peers)])  33.3 us
    ppermute x8, waiting for transfers between devices, swapped(): return lax.ppermute(x, axis, [(i, i ^ by) for i in range(peers)])  19.8 us
    pallas_call x1, Pallas kernels, on_device(): call(attention_kernel, [jax.ShapeDtypeStruct((HEADS, FPAD, TOK), bf16), g...  16.6 us
    all_to_all x1, blocking collectives, on_device(): got = lax.all_to_all(send, HEAD_AXES, 0, 0, tiled=True)  16.3 us
    all_to_all x1, starting transfers between devices, on_device(): back = lax.all_to_all(send, HEAD_AXES, 0, 0, tiled=True)  12 us
    ppermute x2, starting transfers between devices, edges_added(): lax.ppermute(lax.slice_in_dim(canvas, size - 4, size, axis=dim), axis, fo...  11.8 us
    ppermute x2, waiting for transfers between devices, edges_added(): lax.ppermute(lax.slice_in_dim(canvas, 0, 4, axis=dim), axis, backward)  9.54 us
    unnamed x14, local copies, waits for them, and re-layouts  5.57 us
  transfers between devices with their start and end apart: 13, of which 11 were waited for; matrix products, arithmetic and copies ran while one was open for 7% of the time, Pallas kernels for 0%

profile of v1, /device:TPU:15, one launch (start us, length us, event | category | flops | bytes accessed | tf_op | source)
XLA Modules:
  0.0 148.8 jit_solution(15713569336697318837)
XLA Ops:
  0.0 0.8 reshape.40.k_ref
  0.8 0.7 reshape.41.v_ref
  1.5 1.0 copy-done.3
  2.5 1.0 copy-done.4
  3.5 1.0 copy-done.5
  4.4 0.3 shard_map.73
  4.8 16.3 %all_to_all.10.qg_ref = bf16[16,176,128]{2,1,0:T(8,128)(2,1)S(1)} all-to-all(bf16[16,176,128]{2,1,0:T(8,128)(2,1)S(1)} %shard_map.73), channel_id=1, replica_groups=mesh['yh'=2,'x'=4,'c'=2,'z'=8,'yl'=2] {'yh','x','yl'}, dimensions={0} | all-to-all | bytes 1441792 | tf_op jit(solution)/shard_map/all_to_all | solution.py:210
  21.1 1.6 %collective-permute-start = (bf16[1,16,16,128]{3,2,1,0:T(8,128)(2,1)S(1)}, bf16[1,16,16,128]{3,2,1,0:T(8,128)(2,1)S(1)}, u32[]{:S(2)}, u32[]{:S(2)}) collective-permute-start(bf16[1,16,16,128]{3,2,1,0:T(8,128)(2,1)S(1)} %slice_bitcast_fusion.3), channel_id=1, source_target_pairs={{0,2},{2,0},{4,6},{6,4},{8,10},{10,8},{12,14},{14,12},{1,3},{3,1},... | collective-permute-start | bytes 196616 | tf_op jit(solution)/shard_map/ppermute | solution.py:150
  22.8 1.7 %collective-permute-done = bf16[1,16,16,128]{3,2,1,0:T(8,128)(2,1)S(1)} collective-permute-done((bf16[1,16,16,128]{3,2,1,0:T(8,128)(2,1)S(1)}, bf16[1,16,16,128]{3,2,1,0:T(8,128)(2,1)S(1)}, u32[]{:S(2)}, u32[]{:S(2)}) %collective-permute-start) | collective-permute-done | bytes 65568 | tf_op jit(solution)/shard_map/ppermute | solution.py:150
  24.4 3.1 %collective-permute-start.1 = (bf16[2,16,16,128]{3,2,1,0:T(8,128)(2,1)S(1)}, bf16[2,16,16,128]{3,2,1,0:T(8,128)(2,1)S(1)}, u32[]{:S(2)}, u32[]{:S(2)}) collective-permute-start(bf16[2,16,16,128]{3,2,1,0:T(8,128)(2,1)S(1)} %pad_maximum_fusion.2), channel_id=1, source_target_pairs={{0,4},{2,6},{4,0},{6,2},{8,12},{10,14},{12,8},{14,10},{1,5},{3,7},... | collective-permute-start | bytes 393224 | tf_op jit(solution)/shard_map/ppermute | solution.py:150
  27.5 3.8 %collective-permute-done.1 = bf16[2,16,16,128]{3,2,1,0:T(8,128)(2,1)S(1)} collective-permute-done((bf16[2,16,16,128]{3,2,1,0:T(8,128)(2,1)S(1)}, bf16[2,16,16,128]{3,2,1,0:T(8,128)(2,1)S(1)}, u32[]{:S(2)}, u32[]{:S(2)}) %collective-permute-start.1) | collective-permute-done | bytes 131104 | tf_op jit(solution)/shard_map/ppermute | solution.py:150
  31.3 6.2 %collective-permute-start.2 = (bf16[4,16,16,128]{3,2,1,0:T(8,128)(2,1)S(1)}, bf16[4,16,16,128]{3,2,1,0:T(8,128)(2,1)S(1)}, u32[]{:S(2)}, u32[]{:S(2)}) collective-permute-start(bf16[4,16,16,128]{3,2,1,0:T(8,128)(2,1)S(1)} %pad_maximum_fusion.1), channel_id=1, source_target_pairs={{0,8},{2,10},{4,12},{6,14},{8,0},{10,2},{12,4},{14,6},{1,9},{3,11}... | collective-permute-start | bytes 786440 | tf_op jit(solution)/shard_map/ppermute | solution.py:150
  37.5 4.1 %collective-permute-done.2 = bf16[4,16,16,128]{3,2,1,0:T(8,128)(2,1)S(1)} collective-permute-done((bf16[4,16,16,128]{3,2,1,0:T(8,128)(2,1)S(1)}, bf16[4,16,16,128]{3,2,1,0:T(8,128)(2,1)S(1)}, u32[]{:S(2)}, u32[]{:S(2)}) %collective-permute-start.2) | collective-permute-done | bytes 262176 | tf_op jit(solution)/shard_map/ppermute | solution.py:150
  41.6 11.8 %collective-permute-start.3 = (bf16[8,16,16,128]{3,2,1,0:T(8,128)(2,1)S(1)}, bf16[8,16,16,128]{3,2,1,0:T(8,128)(2,1)S(1)}, u32[]{:S(2)}, u32[]{:S(2)}) collective-permute-start(bf16[8,16,16,128]{3,2,1,0:T(8,128)(2,1)S(1)} %pad_maximum_fusion.kv_own), channel_id=1, source_target_pairs={{0,16},{16,0},{1,17},{17,1},{2,18},{18,2},{3,19},{19,3},{4,20},{20... | collective-permute-start | bytes 1572872 | tf_op jit(solution)/shard_map/ppermute | solution.py:150
  53.5 1.5 %collective-permute-done.3.kv_other = bf16[8,16,16,128]{3,2,1,0:T(8,128)(2,1)S(1)} collective-permute-done((bf16[8,16,16,128]{3,2,1,0:T(8,128)(2,1)S(1)}, bf16[8,16,16,128]{3,2,1,0:T(8,128)(2,1)S(1)}, u32[]{:S(2)}, u32[]{:S(2)}) %collective-permute-start.3) | collective-permute-done | bytes 524320 | tf_op jit(solution)/shard_map/ppermute | solution.py:150
  55.0 16.6 %shard_map.74 = (bf16[16,80,128]{2,1,0:T(8,128)(2,1)S(1)}, f32[8,144,128]{2,1,0:T(8,128)S(1)}, f32[8,144,128]{2,1,0:T(8,128)S(1)}) custom-call(bf16[16,176,128]{2,1,0:T(8,128)(2,1)S(1)} %all_to_all.10.qg_ref, bf16[8,16,16,128]{3,2,1,0:T(8,128)(2,1)S(1)} %pad_maximum_fusion.kv_own, bf16[8,16,16,128]{3,2,1,0:T(8,128)(2,1)S(1)} %collective-permute-done.3.kv_other), custom_call_target="tpu_custom_call" | custom-call | tf_op jit(solution)/shard_map/pallas_call | solution.py:216
  71.6 0.4 collective-permute-start.4
  72.1 1.6 %collective-permute-done.4 = f32[8,144,128]{2,1,0:T(8,128)S(1)} collective-permute-done((f32[8,144,128]{2,1,0:T(8,128)S(1)}, f32[8,144,128]{2,1,0:T(8,128)S(1)}, u32[]{:S(2)}, u32[]{:S(2)}) %collective-permute-start.4) | collective-permute-done | bytes 589856 | tf_op jit(solution)/shard_map/ppermute | solution.py:150
  73.8 4.1 %collective-permute-start.5 = (bf16[4,144,128]{2,1,0:T(8,128)(2,1)S(1)}, bf16[4,144,128]{2,1,0:T(8,128)(2,1)S(1)}, u32[]{:S(2)}, u32[]{:S(2)}) collective-permute-start(bf16[4,144,128]{2,1,0:T(8,128)(2,1)S(1)} %slice.159), channel_id=1, source_target_pairs={{0,8},{2,10},{4,12},{6,14},{8,0},{10,2},{12,4},{14,6},{1,9},{3,11}... | collective-permute-start | bytes 442376 | tf_op jit(solution)/shard_map/ppermute | solution.py:150
  78.0 5.8 %collective-permute-done.5 = bf16[4,144,128]{2,1,0:T(8,128)(2,1)S(1)} collective-permute-done((bf16[4,144,128]{2,1,0:T(8,128)(2,1)S(1)}, bf16[4,144,128]{2,1,0:T(8,128)(2,1)S(1)}, u32[]{:S(2)}, u32[]{:S(2)}) %collective-permute-start.5) | collective-permute-done | bytes 147488 | tf_op jit(solution)/shard_map/ppermute | solution.py:150
  83.9 4.3 %fusion.6 = f32[3456,256]{1,0:T(8,128)} fusion(bf16[1152,3456]{1,0:T(8,128)(2,1)S(1)} %copy-done.6, bf16[256,1152]{1,0:T(8,128)(2,1)S(1)} %copy-done), kind=kOutput, calls=%fused_computation.32 | convolution fusion | flops 2038431744 | bytes 12091392 | tf_op jit(solution)/shard_map/dot_general | solution.py:185
  88.2 5.9 %collective-permute-start.7 = (bf16[144,128]{1,0:T(8,128)(2,1)S(1)}, bf16[144,128]{1,0:T(8,128)(2,1)S(1)}, u32[]{:S(2)}, u32[]{:S(2)}) collective-permute-start(bf16[144,128]{1,0:T(8,128)(2,1)S(1)} %fusion.5), channel_id=1, source_target_pairs={{0,2},{2,0},{4,6},{6,4},{8,10},{10,8},{12,14},{14,12},{1,3},{3,1},... | collective-permute-start | bytes 110600 | tf_op jit(solution)/shard_map/ppermute | solution.py:150
  94.1 1.3 collective-permute-done.7.came_ref
  95.4 0.9 shard_map.75
  96.3 12.0 %all-to-all-start.1 = ((bf16[16,96,128]{2,1,0:T(8,128)(2,1)}), bf16[16,96,128]{2,1,0:T(8,128)(2,1)}, u32[]{:S(2)}, u32[]{:S(2)}) async-start(bf16[16,96,128]{2,1,0:T(8,128)(2,1)} %shard_map.75), calls=%async_computation.1 | async-start | bytes 786432 | tf_op jit(solution)/shard_map/all_to_all | solution.py:235
  108.3 2.5 %fusion = (bf16[3,16,72,256]{3,2,1,0:T(8,128)(2,1)S(1)}, bf16[3,16,72,256]{3,2,1,0:T(8,128)(2,1)S(1)}) fusion(f32[3,16,72,256]{3,2,1,0:T(8,128)} %bitcast.31), kind=kLoop, calls=%fused_computation.2 | loop fusion | flops 3538944 | bytes 7077888 | tf_op jit(solution)/shard_map/convert.2
  111.2 0.9 pad.18
  112.0 0.2 pad.20.kv_hi
  112.3 1.6 %pad.21.kv_lo = bf16[2,16,128,256]{3,2,1,0:T(8,128)(2,1)} pad(bf16[2,16,72,256]{3,2,1,0:T(8,128)(2,1)S(1)} %slice.121, bf16[]{:T(256)} %constant.3.clone.1), padding=0_0x0_0x0_56x0_0 | pad | bytes 3276802 | tf_op jit(solution)/shard_map/jit(_pad)/pad | solution.py:191
  113.9 1.6 %copy-done.1 = bf16[2,16,128,256]{3,2,1,0:T(8,128)(2,1)S(1)} copy-done((bf16[2,16,128,256]{3,2,1,0:T(8,128)(2,1)S(1)}, bf16[2,16,128,256]{3,2,1,0:T(8,128)(2,1)}, u32[]{:S(2)}) %copy-start.1) | copy-done | bytes 2097176
  115.5 1.1 copy-done.2
  116.6 1.9 %shard_map.76 = f32[128,256]{1,0:T(8,128)S(1)} custom-call(bf16[16,96,128]{2,1,0:T(8,128)(2,1)} %all-to-all-done.1.back_ref, bf16[1280,256]{1,0:T(8,128)(2,1)S(1)} %bitcast.27, bf16[1280,256]{1,0:T(8,128)(2,1)S(1)} %bitcast.26, bf16[2,16,128,256]{3,2,1,0:T(8,128)(2,1)S(1)} %pad.20.kv_hi, bf16[2,16,128,256]{3,2,1,0:T(8,128)(2,1)S(1)} %copy-done.1), custom_call_target="tpu_custom_call" | custom-call | tf_op jit(solution)/shard_map/pallas_call | solution.py:236
  118.5 0.3 reshape.45
  118.9 0.3 fusion.4
  119.1 0.5 copy.11
  119.7 0.2 reshape.46
  119.9 7.2 %collective-permute-start.8 = (f32[4,136]{1,0:T(4,128)S(1)}, f32[4,136]{1,0:T(4,128)S(1)}, u32[]{:S(2)}, u32[]{:S(2)}) collective-permute-start(f32[4,136]{1,0:T(4,128)S(1)} %slice.123), channel_id=1, source_target_pairs={{0,16},{16,32},{32,48},{48,64},{64,80},{80,96},{96,112},{112,128},... | collective-permute-start | bytes 6536 | tf_op jit(solution)/shard_map/ppermute | solution.py:174
  127.1 0.7 collective-permute-done.8
  127.9 1.9 %collective-permute-start.9 = (f32[4,136]{1,0:T(4,128)S(1)}, f32[4,136]{1,0:T(4,128)S(1)}, u32[]{:S(2)}, u32[]{:S(2)}) collective-permute-start(f32[4,136]{1,0:T(4,128)S(1)} %get-tuple-element.16), channel_id=1, source_target_pairs={{16,0},{32,16},{48,32},{64,48},{80,64},{96,80},{112,96},{128,112},... | collective-permute-start | bytes 6536 | tf_op jit(solution)/shard_map/ppermute | solution.py:175
  129.8 0.7 copy.12
  130.5 0.2 slice.103
  130.8 6.1 %collective-permute-done.9 = f32[4,136]{1,0:T(4,128)S(1)} collective-permute-done((f32[4,136]{1,0:T(4,128)S(1)}, f32[4,136]{1,0:T(4,128)S(1)}, u32[]{:S(2)}, u32[]{:S(2)}) %collective-permute-start.9) | collective-permute-done | bytes 2208 | tf_op jit(solution)/shard_map/ppermute | solution.py:175
  137.1 4.6 %collective-permute-start.10 = (f32[64,4]{0,1:T(4,128)S(1)}, f32[64,4]{0,1:T(4,128)S(1)}, u32[]{:S(2)}, u32[]{:S(2)}) collective-permute-start(f32[64,4]{0,1:T(4,128)S(1)} %pad_maximum_fusion.6), channel_id=1, source_target_pairs={{0,1},{1,2},{2,3},{3,4},{4,5},{5,6},{6,7},{7,8},{8,9},{9,10},{10,1... | collective-permute-start | bytes 3080 | tf_op jit(solution)/shard_map/ppermute | solution.py:174
  141.7 0.7 collective-permute-done.10
  142.5 1.9 %collective-permute-start.11 = (f32[64,4]{0,1:T(4,128)S(1)}, f32[64,4]{0,1:T(4,128)S(1)}, u32[]{:S(2)}, u32[]{:S(2)}) collective-permute-start(f32[64,4]{0,1:T(4,128)S(1)} %get-tuple-element.14), channel_id=1, source_target_pairs={{1,0},{2,1},{3,2},{4,3},{5,4},{6,5},{7,6},{8,7},{9,8},{10,9},{11,1... | collective-permute-start | bytes 3080 | tf_op jit(solution)/shard_map/ppermute | solution.py:175
  144.4 0.1 pad_maximum_fusion.3
  144.6 3.4 %collective-permute-done.11 = f32[64,4]{0,1:T(4,128)S(1)} collective-permute-done((f32[64,4]{0,1:T(4,128)S(1)}, f32[64,4]{0,1:T(4,128)S(1)}, u32[]{:S(2)}, u32[]{:S(2)}) %collective-permute-start.11) | collective-permute-done | bytes 1056 | tf_op jit(solution)/shard_map/ppermute | solution.py:175
  148.1 0.7 copy.15
  (39 shorter events, 1.2 us)
Async XLA Ops:
  0.0 83.9 %copy-start = (bf16[256,1152]{1,0:T(8,128)(2,1)S(1)}, bf16[256,1152]{1,0:T(8,128)(2,1)}, u32[]{:S(2)}) copy-start(bf16[256,1152]{1,0:T(8,128)(2,1)} %param.13) | copy-start | bytes 1769476
  1.5 1.0 copy-start.3
  2.5 1.0 copy-start.4
  3.5 1.0 copy-start.5
  4.8 79.2 %copy-start.6 = (bf16[1152,3456]{1,0:T(8,128)(2,1)S(1)}, bf16[1152,3456]{1,0:T(8,128)(2,1)}, u32[]{:S(2)}) copy-start(bf16[1152,3456]{1,0:T(8,128)(2,1)} %param.12) | copy-start | bytes 23887876
  21.1 3.3 %collective-permute-start = (bf16[1,16,16,128]{3,2,1,0:T(8,128)(2,1)S(1)}, bf16[1,16,16,128]{3,2,1,0:T(8,128)(2,1)S(1)}, u32[]{:S(2)}, u32[]{:S(2)}) collective-permute-start(bf16[1,16,16,128]{3,2,1,0:T(8,128)(2,1)S(1)} %slice_bitcast_fusion.3), channel_id=1, source_target_pairs={{0,2},{2,0},{4,6},{6,4},{8,10},{10,8},{12,14},{14,12},{1,3},{3,1},... | collective-permute-start | bytes 196616 | tf_op jit(solution)/shard_map/ppermute | solution.py:150
  24.4 6.8 %collective-permute-start.1 = (bf16[2,16,16,128]{3,2,1,0:T(8,128)(2,1)S(1)}, bf16[2,16,16,128]{3,2,1,0:T(8,128)(2,1)S(1)}, u32[]{:S(2)}, u32[]{:S(2)}) collective-permute-start(bf16[2,16,16,128]{3,2,1,0:T(8,128)(2,1)S(1)} %pad_maximum_fusion.2), channel_id=1, source_target_pairs={{0,4},{2,6},{4,0},{6,2},{8,12},{10,14},{12,8},{14,10},{1,5},{3,7},... | collective-permute-start | bytes 393224 | tf_op jit(solution)/shard_map/ppermute | solution.py:150
  31.3 10.2 %collective-permute-start.2 = (bf16[4,16,16,128]{3,2,1,0:T(8,128)(2,1)S(1)}, bf16[4,16,16,128]{3,2,1,0:T(8,128)(2,1)S(1)}, u32[]{:S(2)}, u32[]{:S(2)}) collective-permute-start(bf16[4,16,16,128]{3,2,1,0:T(8,128)(2,1)S(1)} %pad_maximum_fusion.1), channel_id=1, source_target_pairs={{0,8},{2,10},{4,12},{6,14},{8,0},{10,2},{12,4},{14,6},{1,9},{3,11}... | collective-permute-start | bytes 786440 | tf_op jit(solution)/shard_map/ppermute | solution.py:150
  41.6 13.4 %collective-permute-start.3 = (bf16[8,16,16,128]{3,2,1,0:T(8,128)(2,1)S(1)}, bf16[8,16,16,128]{3,2,1,0:T(8,128)(2,1)S(1)}, u32[]{:S(2)}, u32[]{:S(2)}) collective-permute-start(bf16[8,16,16,128]{3,2,1,0:T(8,128)(2,1)S(1)} %pad_maximum_fusion.kv_own), channel_id=1, source_target_pairs={{0,16},{16,0},{1,17},{17,1},{2,18},{18,2},{3,19},{19,3},{4,20},{20... | collective-permute-start | bytes 1572872 | tf_op jit(solution)/shard_map/ppermute | solution.py:150
  71.6 2.1 %collective-permute-start.4 = (f32[8,144,128]{2,1,0:T(8,128)S(1)}, f32[8,144,128]{2,1,0:T(8,128)S(1)}, u32[]{:S(2)}, u32[]{:S(2)}) collective-permute-start(f32[8,144,128]{2,1,0:T(8,128)S(1)} %get-tuple-element.10), channel_id=1, source_target_pairs={{0,16},{16,0},{1,17},{17,1},{2,18},{18,2},{3,19},{19,3},{4,20},{20... | collective-permute-start | bytes 1769480 | tf_op jit(solution)/shard_map/ppermute | solution.py:150
  73.8 9.9 %collective-permute-start.5 = (bf16[4,144,128]{2,1,0:T(8,128)(2,1)S(1)}, bf16[4,144,128]{2,1,0:T(8,128)(2,1)S(1)}, u32[]{:S(2)}, u32[]{:S(2)}) collective-permute-start(bf16[4,144,128]{2,1,0:T(8,128)(2,1)S(1)} %slice.159), channel_id=1, source_target_pairs={{0,8},{2,10},{4,12},{6,14},{8,0},{10,2},{12,4},{14,6},{1,9},{3,11}... | collective-permute-start | bytes 442376 | tf_op jit(solution)/shard_map/ppermute | solution.py:150
  83.8 4.4 %collective-permute-start.6 = (bf16[2,144,128]{2,1,0:T(8,128)(2,1)S(1)}, bf16[2,144,128]{2,1,0:T(8,128)(2,1)S(1)}, u32[]{:S(2)}, u32[]{:S(2)}) collective-permute-start(bf16[2,144,128]{2,1,0:T(8,128)(2,1)S(1)} %slice.160), channel_id=1, source_target_pairs={{0,4},{2,6},{4,0},{6,2},{8,12},{10,14},{12,8},{14,10},{1,5},{3,7},... | collective-permute-start | bytes 221192 | tf_op jit(solution)/shard_map/ppermute | solution.py:150
  88.2 7.2 %collective-permute-start.7 = (bf16[144,128]{1,0:T(8,128)(2,1)S(1)}, bf16[144,128]{1,0:T(8,128)(2,1)S(1)}, u32[]{:S(2)}, u32[]{:S(2)}) collective-permute-start(bf16[144,128]{1,0:T(8,128)(2,1)S(1)} %fusion.5), channel_id=1, source_target_pairs={{0,2},{2,0},{4,6},{6,4},{8,10},{10,8},{12,14},{14,12},{1,3},{3,1},... | collective-permute-start | bytes 110600 | tf_op jit(solution)/shard_map/ppermute | solution.py:150
  96.3 17.6 %all-to-all-start.1 = ((bf16[16,96,128]{2,1,0:T(8,128)(2,1)}), bf16[16,96,128]{2,1,0:T(8,128)(2,1)}, u32[]{:S(2)}, u32[]{:S(2)}) async-start(bf16[16,96,128]{2,1,0:T(8,128)(2,1)} %shard_map.75), calls=%async_computation.1 | async-start | bytes 786432 | tf_op jit(solution)/shard_map/all_to_all | solution.py:235
  113.9 1.6 %copy-start.1 = (bf16[2,16,128,256]{3,2,1,0:T(8,128)(2,1)S(1)}, bf16[2,16,128,256]{3,2,1,0:T(8,128)(2,1)}, u32[]{:S(2)}) copy-start(bf16[2,16,128,256]{3,2,1,0:T(8,128)(2,1)} %pad.21.kv_lo) | copy-start | bytes 6291460
  115.5 1.1 copy-start.2
  119.9 8.0 %collective-permute-start.8 = (f32[4,136]{1,0:T(4,128)S(1)}, f32[4,136]{1,0:T(4,128)S(1)}, u32[]{:S(2)}, u32[]{:S(2)}) collective-permute-start(f32[4,136]{1,0:T(4,128)S(1)} %slice.123), channel_id=1, source_target_pairs={{0,16},{16,32},{32,48},{48,64},{64,80},{80,96},{96,112},{112,128},... | collective-permute-start | bytes 6536 | tf_op jit(solution)/shard_map/ppermute | solution.py:174
  127.9 9.1 %collective-permute-start.9 = (f32[4,136]{1,0:T(4,128)S(1)}, f32[4,136]{1,0:T(4,128)S(1)}, u32[]{:S(2)}, u32[]{:S(2)}) collective-permute-start(f32[4,136]{1,0:T(4,128)S(1)} %get-tuple-element.16), channel_id=1, source_target_pairs={{16,0},{32,16},{48,32},{64,48},{80,64},{96,80},{112,96},{128,112},... | collective-permute-start | bytes 6536 | tf_op jit(solution)/shard_map/ppermute | solution.py:175
  137.1 5.3 %collective-permute-start.10 = (f32[64,4]{0,1:T(4,128)S(1)}, f32[64,4]{0,1:T(4,128)S(1)}, u32[]{:S(2)}, u32[]{:S(2)}) collective-permute-start(f32[64,4]{0,1:T(4,128)S(1)} %pad_maximum_fusion.6), channel_id=1, source_target_pairs={{0,1},{1,2},{2,3},{3,4},{4,5},{5,6},{6,7},{7,8},{8,9},{9,10},{10,1... | collective-permute-start | bytes 3080 | tf_op jit(solution)/shard_map/ppermute | solution.py:174
  142.5 5.5 %collective-permute-start.11 = (f32[64,4]{0,1:T(4,128)S(1)}, f32[64,4]{0,1:T(4,128)S(1)}, u32[]{:S(2)}, u32[]{:S(2)}) collective-permute-start(f32[64,4]{0,1:T(4,128)S(1)} %get-tuple-element.14), channel_id=1, source_target_pairs={{1,0},{2,1},{3,2},{4,3},{5,4},{6,5},{7,6},{8,7},{9,8},{10,9},{11,1... | collective-permute-start | bytes 3080 | tf_op jit(solution)/shard_map/ppermute | solution.py:175

commit v2 on v1

v2 whole, which is shorter than its diff:
```python
import math

import jax
import jax.numpy as jnp
import ml_dtypes
import numpy as np
from jax import lax
from jax.experimental import pallas as pl
from jax.experimental.pallas import tpu as pltpu
from jax.sharding import Mesh, PartitionSpec as P

D = 1152
HEADS = 16
DH = D // HEADS
POOL = 4
SCALE = DH**-0.5
SCALE2 = SCALE * math.log2(math.e)
ROWS, COLS = 8, 16
TOK = ROWS * COLS
CELLS = TOK // POOL**2
FPAD = 80
KEYS = 2048
HEAD_AXES = ("yh", "x", "yl")
BLK = ("yh", "x", "c")
COL = ("z", "yl")
NT = (((1,), (1,)), ((), ()))
VMEM = 48 * 2**20
bf16, f32 = jnp.bfloat16, jnp.float32


def call(kernel, shapes, scratch=()):
    return pl.pallas_call(
        kernel,
        out_shape=shapes,
        scratch_shapes=scratch,
        compiler_params=pltpu.CompilerParams(vmem_limit_bytes=VMEM),
    )


def pack_kernel(q_in, g_in, o_in, k_in, v_in, send_ref, q_ref, g_ref, o_ref, k_ref, v_ref, sems):
    copies = []
    quarter = TOK // 4
    for source, target in ((k_in, k_ref), (v_in, v_ref)):
        copies.append((source, target))
    for source, target in ((q_in, q_ref), (g_in, g_ref), (o_in, o_ref)):
        for at in range(0, TOK, quarter):
            copies.append((source.at[at : at + quarter], target.at[at : at + quarter]))
    copies = [pltpu.make_async_copy(*pair, sems.at[n]) for n, pair in enumerate(copies)]
    for copy in copies:
        copy.start()
    for copy in copies:
        copy.wait()
    q_t = q_ref[...].astype(f32).T
    g_t = g_ref[...].astype(f32).T
    prod = g_t * o_ref[...].astype(f32).T
    keys = jnp.concatenate([k_ref[0].astype(f32), k_ref[1].astype(f32)])
    vals = jnp.concatenate([v_ref[0].astype(f32), v_ref[1].astype(f32)])
    row = lax.broadcasted_iota(jnp.int32, (8, TOK), 0)
    lanes = jnp.zeros((CELLS, 128 - DH), f32)
    for h in range(HEADS):
        part = slice(h * DH, (h + 1) * DH)
        dot = -jnp.sum(prod[part], axis=0, keepdims=True)
        high = dot.astype(bf16).astype(f32)
        mid = (dot - high).astype(bf16).astype(f32)
        low = dot - high - mid
        dots = jnp.where(row == 0, high, jnp.where(row == 1, mid, jnp.where(row == 2, low, 0.0)))
        send_ref[h, 0:FPAD, :] = jnp.concatenate([q_t[part], jnp.zeros((8, TOK), f32)]).astype(bf16)
        send_ref[h, FPAD : 2 * FPAD, :] = jnp.concatenate([g_t[part], dots]).astype(bf16)
        k_h = jnp.concatenate([keys[:, part], lanes], axis=1)
        v_h = jnp.concatenate([vals[:, part], lanes], axis=1)
        send_ref[h, 2 * FPAD : 2 * FPAD + 16, :] = jnp.concatenate([k_h, v_h]).astype(bf16)


def keys_kernel(got_ref, out_ref):
    kv = got_ref[...].astype(f32).reshape(HEADS, 2, CELLS, 128)
    k_t = kv[:, 0].reshape(128, 128).T
    v_t = kv[:, 1].reshape(128, 128).T
    out_ref[...] = jnp.concatenate([k_t[0:DH], v_t[0:DH]]).astype(bf16)


def attention_kernel(
    qg_ref, kv_own, kv_other, dq_ref, own_ref, other_ref, k_s, v_s, kt_s, e_s, dk_s, dv_s
):
    half = KEYS // 2
    lane = lax.broadcasted_iota(jnp.int32, (128, 128), 1)
    pad = jnp.zeros((128 - DH, 128), f32)
    for at, kv_ref in ((0, kv_own), (half, kv_other)):
        for b in range(8):
            kv = kv_ref[b].astype(f32)
            keys = slice(at + b * 128, at + (b + 1) * 128)
            k_t = jnp.concatenate([kv[0:DH], pad])
            kt_s[:, keys] = k_t.astype(bf16)
            k_s[keys] = k_t.T.astype(bf16)
            v = jnp.concatenate([kv[DH:], pad]).T
            v_s[keys] = jnp.where((lane >= DH) & (lane < DH + 3), 1.0, v).astype(bf16)
    dk_s[...] = jnp.zeros_like(dk_s)
    dv_s[...] = jnp.zeros_like(dv_s)
    step = 512
    blocks = [slice(at, at + step) for at in range(0, KEYS, step)]

    def tile(t, _):
        q_t = jnp.concatenate([qg_ref[2 * t, 0:FPAD], qg_ref[2 * t + 1, 0:FPAD]], axis=1)
        g_t = jnp.concatenate(
            [qg_ref[2 * t, FPAD : 2 * FPAD], qg_ref[2 * t + 1, FPAD : 2 * FPAD]], axis=1
        )
        top = jnp.full((1, 2 * TOK), -jnp.inf, f32)
        for b in blocks:
            scores = jnp.dot(k_s[b, 0:FPAD], q_t, preferred_element_type=f32)
            e_s[b] = scores
            top = jnp.maximum(top, jnp.max(scores, axis=0, keepdims=True))
        top = top * SCALE2
        total = jnp.zeros((1, 2 * TOK), f32)
        for b in blocks:
            exps = jnp.exp2(e_s[b] * SCALE2 - top)
            e_s[b] = exps
            total = total + jnp.sum(exps, axis=0, keepdims=True)
        inverse = 1.0 / total
        dq = jnp.zeros((FPAD, 2 * TOK), f32)
        for b in blocks:
            probs = e_s[b] * inverse
            half_probs = probs.astype(bf16)
            shifted = jnp.dot(v_s[b, 0:FPAD], g_t, preferred_element_type=f32)
            ds = (probs * shifted).astype(bf16)
            dk_s[b, 0:FPAD] += lax.dot_general(ds, q_t, NT, preferred_element_type=f32)
            dv_s[b, 0:FPAD] += lax.dot_general(half_probs, g_t, NT, preferred_element_type=f32)
            dq = dq + jnp.dot(kt_s[0:FPAD, b], ds, preferred_element_type=f32)
        dq = (dq * SCALE).astype(bf16)
        dq_ref[2 * t] = dq[:, 0:TOK]
        dq_ref[2 * t + 1] = dq[:, TOK:]
        return 0

    lax.fori_loop(0, HEADS // 2, tile, 0)
    dk_t = dk_s[...].T
    dv_t = dv_s[...].T
    for out, at in ((own_ref, 0), (other_ref, half)):
        for b in range(8):
            keys = slice(at + b * 128, at + (b + 1) * 128)
            out[b, 0:DH] = dk_t[0:DH, keys] * SCALE
            out[b, DH : 2 * DH] = dv_t[0:DH, keys]


def pack_back_kernel(dq_ref, mine_ref, came_ref, send_ref):
    total = mine_ref[...] + came_ref[...].astype(f32)
    lanes = jnp.zeros((128, 128 - DH), f32)
    dk = jnp.concatenate([total[0:DH].T, lanes], axis=1)
    dv = jnp.concatenate([total[DH : 2 * DH].T, lanes], axis=1)
    send_ref[:, 0:FPAD, :] = dq_ref[...]
    for a in range(HEADS):
        cells = slice(a * CELLS, (a + 1) * CELLS)
        send_ref[a, FPAD : FPAD + 16, :] = jnp.concatenate([dk[cells], dv[cells]]).astype(bf16)


def weights_kernel(patch_ref, qkv_ref, high_ref, low_ref):
    both = jnp.dot(patch_ref[...], qkv_ref[...], preferred_element_type=f32)
    high = both.astype(bf16)
    high_ref[...] = high
    low_ref[...] = (both - high.astype(f32)).astype(bf16)


def embed_kernel(core_ref, back_ref, high_ref, low_ref, tile_ref, canvas_ref, core_out, chip_out, joined, sheet):
    cols = (((0,), (0,)), ((), ()))
    cell = lax.broadcasted_iota(jnp.int32, (CELLS, TOK), 0)
    token = lax.broadcasted_iota(jnp.int32, (CELLS, TOK), 1)
    holds = (token // (POOL * COLS) == cell // 4) & (token % COLS // POOL == cell % 4)
    spread = jnp.where(holds, 1.0 / POOL**2, 0.0).astype(bf16)
    for h in range(HEADS):
        mine = back_ref[h].astype(f32)
        rows = slice(h * DH, (h + 1) * DH)
        joined[rows] = mine[0:DH]
        for part in (0, 1):
            at = FPAD + part * CELLS
            pooled = mine[at : at + CELLS].astype(bf16)
            wide = lax.dot_general(pooled, spread, cols, preferred_element_type=f32)
            joined[(part + 1) * D + h * DH : (part + 1) * D + (h + 1) * DH] = wide[0:DH]
    values = joined[...].astype(bf16)
    patch = jnp.dot(high_ref[...], values, preferred_element_type=f32)
    patch = patch + jnp.dot(low_ref[...], values, preferred_element_type=f32)
    patch = jnp.concatenate([patch[0:128].T, patch[128:256].T])
    high = patch.astype(bf16)
    rest = patch - high.astype(f32)
    mid = rest.astype(bf16)
    low = (rest - mid.astype(f32)).astype(bf16)
    lane = lax.broadcasted_iota(jnp.int32, (2 * TOK, 256), 1)
    row = lax.broadcasted_iota(jnp.int32, (2 * TOK, 256), 0)
    here = lane % 128 // 8 == row % COLS
    sheet[...] = jnp.zeros_like(sheet)
    parts = jnp.concatenate([high, mid, low], axis=1)
    for pair in range(8):
        wide = jnp.dot(parts, tile_ref[:, pair * 256 : (pair + 1) * 256], preferred_element_type=f32)
        wide = jnp.where(here, wide, 0.0)
        wide = jnp.sum(wide.reshape(2 * ROWS, COLS, 256), axis=1)
        for k in (0, 1):
            u = 2 * pair + k
            for side in (0, 1):
                piece = wide[side * ROWS : (side + 1) * ROWS, k * 128 : (k + 1) * 128]
                sheet[side, pl.ds(u, ROWS, stride=8), :] += piece
    left = sheet[0]
    right = sheet[1]
    lane = lax.broadcasted_iota(jnp.int32, left.shape, 1)
    center = jnp.where(lane < 124, pltpu.roll(left, 124, 1), 0.0)
    center = center + jnp.where(lane >= 4, pltpu.roll(right, 4, 1), 0.0)
    edges = jnp.where(lane < 4, left, pltpu.roll(right, 8, 1))
    canvas = jnp.concatenate([center, jnp.where(lane < 8, edges, 0.0)], axis=1)
    canvas_ref[...] = canvas
    first = core_ref[0] == 0
    core_out[...] = jnp.where(first, canvas[68:72], canvas[0:4])
    chip_out[...] = jnp.where(first, canvas[0:4], canvas[68:72])


def rows_kernel(at_ref, canvas_ref, core_ref, chip_ref, center_ref, near_out, far_out):
    first = at_ref[0] == 0
    above = jnp.where(first, chip_ref[...], core_ref[...])
    below = jnp.where(first, core_ref[...], chip_ref[...])
    quiet = jnp.zeros((56, 256), f32)
    canvas = canvas_ref[4:68] + jnp.concatenate([above, quiet, below])
    center_ref[...] = canvas[:, 0:128]
    edges = canvas[:, 128:256].T[0:8]
    left, right = edges[0:4], edges[4:8]
    begins = at_ref[1] == 0
    near_out[...] = jnp.where(begins, right, left)
    far_out[...] = jnp.where(begins, left, right)


def cols_kernel(at_ref, center_ref, near_ref, far_ref, out_ref):
    begins = at_ref[1] == 0
    left = jnp.where(begins, far_ref[...], near_ref[...])
    right = jnp.where(begins, near_ref[...], far_ref[...])
    quiet = jnp.zeros((120, 64), f32)
    out_ref[...] = center_ref[...] + jnp.concatenate([left, quiet, right]).T


def swapped(x, axis, by):
    peers = lax.axis_size(axis)
    return lax.ppermute(x, axis, [(i, i ^ by) for i in range(peers)])


def neighbours(x, axis):
    peers = lax.axis_size(axis)
    pairs = [(i, i + 1) for i in range(1, peers - 1, 2)]
    return lax.ppermute(x, axis, pairs + [(target, source) for source, target in pairs])


def tile_matrix():
    rows = np.arange(128)[:, None]
    lanes = np.arange(2048)[None, :]
    tile = (lanes // 128 == rows // 8) & (lanes % 8 == rows % 8)
    return np.concatenate([tile] * 3).astype(ml_dtypes.bfloat16)


def combined_weights(w_qkv, w_patch):
    ordered = w_patch.reshape(16, 2, 8, D).transpose(1, 0, 2, 3).reshape(256, D)
    width = 384
    shape = jax.ShapeDtypeStruct((256, 3 * D), bf16)
    return pl.pallas_call(
        weights_kernel,
        grid=(3 * D // width,),
        in_specs=[pl.BlockSpec((256, D), lambda n: (0, 0)), pl.BlockSpec((D, width), lambda n: (0, n))],
        out_specs=[pl.BlockSpec((256, width), lambda n: (0, n))] * 2,
        out_shape=[shape, shape],
        cost_estimate=pl.CostEstimate(flops=2 * 256 * D * 3 * D, bytes_accessed=6 * D * D, transcendentals=0),
    )(ordered, w_qkv)


def on_device(queries, key_states, values, saved_out, grad_out, w_qkv, w_patch):
    weights = combined_weights(w_qkv, w_patch)
    anywhere = pl.BlockSpec(memory_space=pl.ANY)
    tokens = pltpu.VMEM((TOK, D), bf16)
    cells = pltpu.VMEM((2, 4, D), bf16)
    send = pl.pallas_call(
        pack_kernel,
        in_specs=[anywhere] * 5,
        out_shape=jax.ShapeDtypeStruct((HEADS, 2 * FPAD + 16, TOK), bf16),
        scratch_shapes=[tokens, tokens, tokens, cells, cells, pltpu.SemaphoreType.DMA((14,))],
        compiler_params=pltpu.CompilerParams(vmem_limit_bytes=VMEM),
    )(
        queries.reshape(TOK, D),
        grad_out.reshape(TOK, D),
        saved_out.reshape(TOK, D),
        key_states,
        values,
    )
    got = lax.all_to_all(send, HEAD_AXES, 0, 0, tiled=True)
    kv = pl.pallas_call(
        keys_kernel,
        grid=(1,),
        in_specs=[pl.BlockSpec((HEADS, 16, 128), lambda n: (0, 10, 0))],
        out_specs=pl.BlockSpec((2 * DH, 128), lambda n: (0, 0)),
        out_shape=jax.ShapeDtypeStruct((2 * DH, 128), bf16),
    )(got)[None]
    for by in (4, 2, 1):
        kv = jnp.concatenate([kv, swapped(kv, "z", by)])
    kv_other = swapped(kv, "c", 1)
    kv, kv_other, *weights = lax.optimization_barrier((kv, kv_other, *weights))
    grads = jax.ShapeDtypeStruct((8, 2 * DH, 128), f32)
    dq, own, other = call(
        attention_kernel,
        [jax.ShapeDtypeStruct((HEADS, FPAD, TOK), bf16), grads, grads],
        [
            pltpu.VMEM((KEYS, 128), bf16),
            pltpu.VMEM((KEYS, 128), bf16),
            pltpu.VMEM((128, KEYS), bf16),
            pltpu.VMEM((KEYS, 2 * TOK), f32),
            pltpu.VMEM((KEYS, 128), f32),
            pltpu.VMEM((KEYS, 128), f32),
        ],
    )(got, kv, kv_other)
    mine = own + swapped(other, "c", 1)
    for by, keep in ((1, 4), (2, 2)):
        mine = mine[:keep] + swapped(mine[keep:].astype(bf16), "z", by).astype(f32)
    came = swapped(mine[1].astype(bf16), "z", 4)
    send = call(pack_back_kernel, jax.ShapeDtypeStruct((HEADS, FPAD + 16, TOK), bf16))(
        dq, mine[0], came
    )
    back = lax.all_to_all(send, HEAD_AXES, 0, 0, tiled=True)
    at = jnp.stack([lax.axis_index("c"), lax.axis_index("yl")]).astype(jnp.int32)
    scalars = pl.BlockSpec(memory_space=pltpu.SMEM)
    whole = pl.BlockSpec(memory_space=pltpu.VMEM)
    strip = jax.ShapeDtypeStruct((4, 256), f32)
    canvas, to_core, to_chip = pl.pallas_call(
        embed_kernel,
        in_specs=[scalars] + [whole] * 4,
        out_shape=[jax.ShapeDtypeStruct((72, 256), f32), strip, strip],
        scratch_shapes=[pltpu.VMEM((3 * D, TOK), f32), pltpu.VMEM((2, 72, 128), f32)],
        compiler_params=pltpu.CompilerParams(vmem_limit_bytes=VMEM),
    )(at, back, *weights, tile_matrix())
    strip = jax.ShapeDtypeStruct((4, 64), f32)
    center, to_near, to_far = pl.pallas_call(
        rows_kernel,
        in_specs=[scalars] + [whole] * 3,
        out_shape=[jax.ShapeDtypeStruct((64, 128), f32), strip, strip],
    )(at, canvas, swapped(to_core, "c", 1), neighbours(to_chip, BLK))
    return pl.pallas_call(
        cols_kernel,
        in_specs=[scalars] + [whole] * 3,
        out_shape=jax.ShapeDtypeStruct((64, 128), f32),
    )(at, center, swapped(to_near, "yl", 1), neighbours(to_far, COL))


def solution(mesh):
    fine = Mesh(mesh.devices.reshape(2, 4, 2, 8, 2), ("yh", "x", "c", "z", "yl"))
    split = P(BLK, COL, None)
    return jax.shard_map(
        on_device,
        mesh=fine,
        in_specs=(split, split, split, split, split, P(), P()),
        out_specs=P(BLK, COL),
        check_vma=False,
    )
```

time: 149 us -> 141 us (0.946)
  the two profiles are of different devices: /device:TPU:15 before, /device:TPU:144 now
where the time goes in v2:
time: 141 us; the launch traced here: 140 us
  waiting for transfers between devices  55 us (39%)
  Pallas kernels  36.4 us (26%)
  blocking collectives  18.8 us (13%)
  starting transfers between devices  17.4 us (12%)
  local copies, waits for them, and re-layouts  9.2 us (7%)
  other arithmetic  2.54 us (2%)
    ppermute x10, waiting for transfers between devices, swapped(): return lax.ppermute(x, axis, [(i, i ^ by) for i in range(peers)])  38.8 us
    all_to_all x1, blocking collectives, on_device(): got = lax.all_to_all(send, HEAD_AXES, 0, 0, tiled=True)  18.8 us
    pallas_call x1, Pallas kernels, on_device(): call(attention_kernel, [jax.ShapeDtypeStruct((HEADS, FPAD, TOK), bf16), g...  16.7 us
    pallas_call x1, Pallas kernels, combined_weights(): pl.pallas_call(weights_kernel, grid=(3 * D // width,), in_specs=[pl.Block...  10.1 us
    ppermute x2, waiting for transfers between devices, neighbours(): lax.ppermute(x, axis, pairs + [(target, source) for source, target in pai...  8.95 us
    unnamed x34, local copies, waits for them, and re-layouts  8.28 us
    all_to_all x1, waiting for transfers between devices, on_device(): back = lax.all_to_all(send, HEAD_AXES, 0, 0, tiled=True)  7.22 us
    ppermute x2, starting transfers between devices, neighbours(): lax.ppermute(x, axis, pairs + [(target, source) for source, target in pai...  6.78 us
  transfers between devices with their start and end apart: 13, of which 11 were waited for; matrix products, arithmetic and copies ran while one was open for 1% of the time, Pallas kernels for 7%

profile of v2, /device:TPU:144, one launch (start us, length us, event | category | flops | bytes accessed | tf_op | source)
XLA Modules:
  0.0 139.6 jit_solution(11418357174491823817)
XLA Ops:
  0.0 1.0 copy-done.5
  1.0 1.0 copy-done.6
  1.9 1.0 copy-done.7
  2.9 0.7 copy-done.9
  3.6 0.7 copy-done.10
  4.3 1.7 %shard_map.82 = bf16[16,176,128]{2,1,0:T(8,128)(2,1)S(1)} custom-call(bf16[128,1152]{1,0:T(8,128)(2,1)S(1)} %bitcast.14, bf16[128,1152]{1,0:T(8,128)(2,1)S(1)} %bitcast.15, bf16[128,1152]{1,0:T(8,128)(2,1)S(1)} %bitcast.16, bf16[2,4,1152]{2,1,0:T(4,128)(2,1)S(1)} %copy-done.9, bf16[2,4,1152]{2,1,0:T(4,128)(2,1)S(1)} %copy-done.10), custom_call_target="tpu_custom_call" | custom-call | tf_op jit(solution)/shard_map/pallas_call | solution.py:269
  6.0 0.0 copy-start.12
  6.0 18.8 %all_to_all.10.got_ref.qg_ref = bf16[16,176,128]{2,1,0:T(8,128)(2,1)} all-to-all(bf16[16,176,128]{2,1,0:T(8,128)(2,1)S(1)} %shard_map.82), channel_id=1, replica_groups=mesh['yh'=2,'x'=4,'c'=2,'z'=8,'yl'=2] {'yh','x','yl'}, dimensions={0} | all-to-all | bytes 1441792 | tf_op jit(solution)/shard_map/all_to_all | solution.py:282
  24.8 1.5 %shard_map.83 = bf16[144,128]{1,0:T(8,128)(2,1)} custom-call(bf16[16,176,128]{2,1,0:T(8,128)(2,1)} %all_to_all.10.got_ref.qg_ref), custom_call_target="tpu_custom_call" | custom-call | tf_op jit(solution)/shard_map/pallas_call | solution.py:283
  26.4 8.1 %collective-permute-done = bf16[1,144,128]{2,1,0:T(8,128)(2,1)S(1)} collective-permute-done((bf16[1,144,128]{2,1,0:T(8,128)(2,1)}, bf16[1,144,128]{2,1,0:T(8,128)(2,1)S(1)}, u32[]{:S(2)}, u32[]{:S(2)}) %collective-permute-start) | collective-permute-done | bytes 36896 | tf_op jit(solution)/shard_map/ppermute | solution.py:234
  34.4 0.8 pad_maximum_fusion.2
  35.2 1.5 %collective-permute-start.1 = (bf16[2,144,128]{2,1,0:T(8,128)(2,1)S(1)}, bf16[2,144,128]{2,1,0:T(8,128)(2,1)S(1)}, u32[]{:S(2)}, u32[]{:S(2)}) collective-permute-start(bf16[2,144,128]{2,1,0:T(8,128)(2,1)S(1)} %pad_maximum_fusion.2), channel_id=1, source_target_pairs={{0,4},{2,6},{4,0},{6,2},{8,12},{10,14},{12,8},{14,10},{1,5},{3,7},... | collective-permute-start | bytes 221192 | tf_op jit(solution)/shard_map/ppermute | solution.py:234
  36.7 4.7 %collective-permute-done.1 = bf16[2,144,128]{2,1,0:T(8,128)(2,1)S(1)} collective-permute-done((bf16[2,144,128]{2,1,0:T(8,128)(2,1)S(1)}, bf16[2,144,128]{2,1,0:T(8,128)(2,1)S(1)}, u32[]{:S(2)}, u32[]{:S(2)}) %collective-permute-start.1) | collective-permute-done | bytes 73760 | tf_op jit(solution)/shard_map/ppermute | solution.py:234
  41.4 0.8 pad_maximum_fusion.1
  42.1 0.3 collective-permute-start.2
  42.5 4.9 %collective-permute-done.2 = bf16[4,144,128]{2,1,0:T(8,128)(2,1)S(1)} collective-permute-done((bf16[4,144,128]{2,1,0:T(8,128)(2,1)S(1)}, bf16[4,144,128]{2,1,0:T(8,128)(2,1)S(1)}, u32[]{:S(2)}, u32[]{:S(2)}) %collective-permute-start.2) | collective-permute-done | bytes 147488 | tf_op jit(solution)/shard_map/ppermute | solution.py:234
  47.4 0.8 pad_maximum_fusion.kv_own
  48.2 0.1 collective-permute-start.3
  48.3 0.9 copy.9
  49.2 10.1 %shard_map.84 = (bf16[256,3456]{1,0:T(8,128)(2,1)}, bf16[256,3456]{1,0:T(8,128)(2,1)}) custom-call(bf16[256,1152]{1,0:T(8,128)(2,1)} %bitcast.17, bf16[1152,3456]{1,0:T(8,128)(2,1)} %qkv_ref.1), custom_call_target="tpu_custom_call" | custom-call | flops 2038431744 | bytes 7962624 | tf_op jit(solution)/shard_map/pallas_call | solution.py:254
  59.2 16.7 %shard_map.85 = (bf16[16,80,128]{2,1,0:T(8,128)(2,1)S(1)}, f32[8,144,128]{2,1,0:T(8,128)S(1)}, f32[8,144,128]{2,1,0:T(8,128)S(1)}) custom-call(bf16[16,176,128]{2,1,0:T(8,128)(2,1)S(1)} %copy-done, bf16[8,144,128]{2,1,0:T(8,128)(2,1)S(1)} %pad_maximum_fusion.kv_own, bf16[8,144,128]{2,1,0:T(8,128)(2,1)S(1)} %collective-permute-done.3.kv_other), custom_call_target="tpu_custom_call" | custom-call | tf_op jit(solution)/shard_map/pallas_call | solution.py:295
  75.9 0.6 collective-permute-start.4
  76.5 1.6 %collective-permute-done.4 = f32[8,144,128]{2,1,0:T(8,128)S(1)} collective-permute-done((f32[8,144,128]{2,1,0:T(8,128)S(1)}, f32[8,144,128]{2,1,0:T(8,128)S(1)}, u32[]{:S(2)}, u32[]{:S(2)}) %collective-permute-start.4) | collective-permute-done | bytes 589856 | tf_op jit(solution)/shard_map/ppermute | solution.py:234
  78.2 0.1 add.9
  78.3 0.3 collective-permute-start.5
  78.6 5.9 %collective-permute-done.5 = bf16[4,144,128]{2,1,0:T(8,128)(2,1)S(1)} collective-permute-done((bf16[4,144,128]{2,1,0:T(8,128)(2,1)S(1)}, bf16[4,144,128]{2,1,0:T(8,128)(2,1)S(1)}, u32[]{:S(2)}, u32[]{:S(2)}) %collective-permute-start.5) | collective-permute-done | bytes 147488 | tf_op jit(solution)/shard_map/ppermute | solution.py:234
  84.5 0.9 collective-permute-start.6
  85.4 5.2 %collective-permute-done.6 = bf16[2,144,128]{2,1,0:T(8,128)(2,1)S(1)} collective-permute-done((bf16[2,144,128]{2,1,0:T(8,128)(2,1)S(1)}, bf16[2,144,128]{2,1,0:T(8,128)(2,1)S(1)}, u32[]{:S(2)}, u32[]{:S(2)}) %collective-permute-start.6) | collective-permute-done | bytes 73760 | tf_op jit(solution)/shard_map/ppermute | solution.py:234
  90.7 0.1 collective-permute-start.7
  90.8 7.8 %collective-permute-done.7.came_ref = bf16[144,128]{1,0:T(8,128)(2,1)S(1)} collective-permute-done((bf16[144,128]{1,0:T(8,128)(2,1)S(1)}, bf16[144,128]{1,0:T(8,128)(2,1)S(1)}, u32[]{:S(2)}, u32[]{:S(2)}) %collective-permute-start.7) | collective-permute-done | bytes 36896 | tf_op jit(solution)/shard_map/ppermute | solution.py:234
  98.6 0.1 shard_map.86
  98.7 0.8 copy-done.3
  99.5 5.8 %all-to-all-start.1 = ((bf16[16,96,128]{2,1,0:T(8,128)(2,1)}), bf16[16,96,128]{2,1,0:T(8,128)(2,1)}, u32[]{:S(2)}, u32[]{:S(2)}) async-start(bf16[16,96,128]{2,1,0:T(8,128)(2,1)} %copy-done.3), calls=%async_computation.1 | async-start | bytes 786432 | tf_op jit(solution)/shard_map/all_to_all | solution.py:314
  105.3 0.1 pad_add_fusion.core_ref.at_ref
  105.3 7.2 %all-to-all-done.1.back_ref = bf16[16,96,128]{2,1,0:T(8,128)(2,1)} async-done(((bf16[16,96,128]{2,1,0:T(8,128)(2,1)}), bf16[16,96,128]{2,1,0:T(8,128)(2,1)}, u32[]{:S(2)}, u32[]{:S(2)}) %all-to-all-start.1) | async-done | bytes 393248 | tf_op jit(solution)/shard_map/all_to_all | solution.py:314
  112.6 1.4 %copy-done.4 = bf16[384,2048]{1,0:T(8,128)(2,1)S(1)} copy-done((bf16[384,2048]{1,0:T(8,128)(2,1)S(1)}, bf16[384,2048]{1,0:T(8,128)(2,1)}, u32[]{:S(2)}) %copy-start.4) | copy-done | bytes 1572888
  114.0 3.3 %shard_map.87 = (f32[72,256]{1,0:T(8,128)S(1)}, f32[4,256]{1,0:T(4,128)S(1)}, f32[4,256]{1,0:T(4,128)S(1)}) custom-call(s32[2]{0:T(128)S(1)} %pad_add_fusion.core_ref.at_ref, bf16[16,96,128]{2,1,0:T(8,128)(2,1)} %all-to-all-done.1.back_ref, bf16[256,3456]{1,0:T(8,128)(2,1)S(1)} %copy-done.1, bf16[256,3456]{1,0:T(8,128)(2,1)S(1)} %copy-done.2, ...), custom_call_target="tpu_custom_call" | custom-call | tf_op jit(solution)/shard_map/pallas_call | solution.py:319
  117.3 0.6 copy-done.8
  117.9 4.7 %collective-permute-start.9 = (f32[4,256]{1,0:T(4,128)S(1)}, f32[4,256]{1,0:T(4,128)S(1)}, u32[]{:S(2)}, u32[]{:S(2)}) collective-permute-start(f32[4,256]{1,0:T(4,128)S(1)} %get-tuple-element.31), channel_id=1, source_target_pairs={{16,32},{48,64},{80,96},{112,128},{144,160},{176,192},{208,224},{3... | collective-permute-start | bytes 12296 | tf_op jit(solution)/shard_map/ppermute | solution.py:240
  122.6 3.8 %collective-permute-done.9.chip_ref = f32[4,256]{1,0:T(4,128)S(1)} collective-permute-done((f32[4,256]{1,0:T(4,128)S(1)}, f32[4,256]{1,0:T(4,128)S(1)}, u32[]{:S(2)}, u32[]{:S(2)}) %collective-permute-start.9) | collective-permute-done | bytes 4128 | tf_op jit(solution)/shard_map/ppermute | solution.py:240
  126.4 0.6 copy-done.14
  127.0 1.6 %shard_map.88 = (f32[64,128]{1,0:T(8,128)}, f32[4,64]{1,0:T(4,128)}, f32[4,64]{1,0:T(4,128)}) custom-call(s32[2]{0:T(128)} %copy-done.11, f32[72,256]{1,0:T(8,128)} %copy-done.8, f32[4,256]{1,0:T(4,128)} %copy-done.13, f32[4,256]{1,0:T(4,128)} %copy-done.14), custom_call_target="tpu_custom_call" | custom-call | tf_op jit(solution)/shard_map/pallas_call | solution.py:327
  128.6 1.1 collective-permute-start.10
  129.7 2.1 %collective-permute-start.11 = (f32[4,64]{1,0:T(4,128)}, f32[4,64]{1,0:T(4,128)S(1)}, u32[]{:S(2)}, u32[]{:S(2)}) collective-permute-start(f32[4,64]{1,0:T(4,128)} %get-tuple-element.34), channel_id=1, source_target_pairs={{1,2},{3,4},{5,6},{7,8},{9,10},{11,12},{13,14},{2,1},{4,3},{6,5},{... | collective-permute-start | bytes 3080 | tf_op jit(solution)/shard_map/ppermute | solution.py:240
  131.8 0.6 collective-permute-done.10.near_ref
  132.4 5.1 %collective-permute-done.11.far_ref = f32[4,64]{1,0:T(4,128)S(1)} collective-permute-done((f32[4,64]{1,0:T(4,128)}, f32[4,64]{1,0:T(4,128)S(1)}, u32[]{:S(2)}, u32[]{:S(2)}) %collective-permute-start.11) | collective-permute-done | bytes 1056 | tf_op jit(solution)/shard_map/ppermute | solution.py:240
  137.5 0.6 copy-done.16
  138.1 1.5 %shard_map.89 = f32[64,128]{1,0:T(8,128)} custom-call(s32[2]{0:T(128)} %copy-done.11, f32[64,128]{1,0:T(8,128)} %get-tuple-element.32.center_ref, f32[4,64]{1,0:T(4,128)} %copy-done.15, f32[4,64]{1,0:T(4,128)} %copy-done.16), custom_call_target="tpu_custom_call" | custom-call | tf_op jit(solution)/shard_map/pallas_call | solution.py:332
  (33 shorter events, 0.1 us)
Async XLA Ops:
  0.0 1.0 copy-start.5
  1.0 1.0 copy-start.6
  1.9 1.0 copy-start.7
  2.9 0.7 copy-start.9
  3.6 0.7 copy-start.10
  6.0 42.3 %copy-start.12 = (bf16[256,1152]{1,0:T(8,128)(2,1)S(1)}, bf16[256,1152]{1,0:T(8,128)(2,1)}, u32[]{:S(2)}) copy-start(bf16[256,1152]{1,0:T(8,128)(2,1)} %param.14) | copy-start | bytes 1769476
  26.4 8.1 %collective-permute-start = (bf16[1,144,128]{2,1,0:T(8,128)(2,1)}, bf16[1,144,128]{2,1,0:T(8,128)(2,1)S(1)}, u32[]{:S(2)}, u32[]{:S(2)}) collective-permute-start(bf16[1,144,128]{2,1,0:T(8,128)(2,1)} %bitcast.18), channel_id=1, source_target_pairs={{0,8},{2,10},{4,12},{6,14},{8,0},{10,2},{12,4},{14,6},{1,9},{3,11}... | collective-permute-start | bytes 110600 | tf_op jit(solution)/shard_map/ppermute | solution.py:234
  35.2 6.1 %collective-permute-start.1 = (bf16[2,144,128]{2,1,0:T(8,128)(2,1)S(1)}, bf16[2,144,128]{2,1,0:T(8,128)(2,1)S(1)}, u32[]{:S(2)}, u32[]{:S(2)}) collective-permute-start(bf16[2,144,128]{2,1,0:T(8,128)(2,1)S(1)} %pad_maximum_fusion.2), channel_id=1, source_target_pairs={{0,4},{2,6},{4,0},{6,2},{8,12},{10,14},{12,8},{14,10},{1,5},{3,7},... | collective-permute-start | bytes 221192 | tf_op jit(solution)/shard_map/ppermute | solution.py:234
  42.1 5.2 %collective-permute-start.2 = (bf16[4,144,128]{2,1,0:T(8,128)(2,1)S(1)}, bf16[4,144,128]{2,1,0:T(8,128)(2,1)S(1)}, u32[]{:S(2)}, u32[]{:S(2)}) collective-permute-start(bf16[4,144,128]{2,1,0:T(8,128)(2,1)S(1)} %pad_maximum_fusion.1), channel_id=1, source_target_pairs={{0,2},{2,0},{4,6},{6,4},{8,10},{10,8},{12,14},{14,12},{1,3},{3,1},... | collective-permute-start | bytes 442376 | tf_op jit(solution)/shard_map/ppermute | solution.py:234
  48.2 11.0 %collective-permute-start.3 = (bf16[8,144,128]{2,1,0:T(8,128)(2,1)S(1)}, bf16[8,144,128]{2,1,0:T(8,128)(2,1)S(1)}, u32[]{:S(2)}, u32[]{:S(2)}) collective-permute-start(bf16[8,144,128]{2,1,0:T(8,128)(2,1)S(1)} %pad_maximum_fusion.kv_own), channel_id=1, source_target_pairs={{0,16},{16,0},{1,17},{17,1},{2,18},{18,2},{3,19},{19,3},{4,20},{20... | collective-permute-start | bytes 884744 | tf_op jit(solution)/shard_map/ppermute | solution.py:234
  49.2 10.1 %copy-start = (bf16[16,176,128]{2,1,0:T(8,128)(2,1)S(1)}, bf16[16,176,128]{2,1,0:T(8,128)(2,1)}, u32[]{:S(2)}) copy-start(bf16[16,176,128]{2,1,0:T(8,128)(2,1)} %all_to_all.10.got_ref.qg_ref) | copy-start | bytes 2162692
  75.9 2.2 %collective-permute-start.4 = (f32[8,144,128]{2,1,0:T(8,128)S(1)}, f32[8,144,128]{2,1,0:T(8,128)S(1)}, u32[]{:S(2)}, u32[]{:S(2)}) collective-permute-start(f32[8,144,128]{2,1,0:T(8,128)S(1)} %get-tuple-element.26), channel_id=1, source_target_pairs={{0,16},{16,0},{1,17},{17,1},{2,18},{18,2},{3,19},{19,3},{4,20},{20... | collective-permute-start | bytes 1769480 | tf_op jit(solution)/shard_map/ppermute | solution.py:234
  78.2 34.4 %copy-start.2 = (bf16[256,3456]{1,0:T(8,128)(2,1)S(1)}, bf16[256,3456]{1,0:T(8,128)(2,1)}, u32[]{:S(2)}) copy-start(bf16[256,3456]{1,0:T(8,128)(2,1)} %get-tuple-element.28.low_ref) | copy-start | bytes 5308420
  78.2 34.3 %copy-start.1 = (bf16[256,3456]{1,0:T(8,128)(2,1)S(1)}, bf16[256,3456]{1,0:T(8,128)(2,1)}, u32[]{:S(2)}) copy-start(bf16[256,3456]{1,0:T(8,128)(2,1)} %get-tuple-element.27.high_ref) | copy-start | bytes 5308420
  78.3 6.2 %collective-permute-start.5 = (bf16[4,144,128]{2,1,0:T(8,128)(2,1)S(1)}, bf16[4,144,128]{2,1,0:T(8,128)(2,1)S(1)}, u32[]{:S(2)}, u32[]{:S(2)}) collective-permute-start(bf16[4,144,128]{2,1,0:T(8,128)(2,1)S(1)} %slice.41), channel_id=1, source_target_pairs={{0,2},{2,0},{4,6},{6,4},{8,10},{10,8},{12,14},{14,12},{1,3},{3,1},... | collective-permute-start | bytes 442376 | tf_op jit(solution)/shard_map/ppermute | solution.py:234
  84.5 6.1 %collective-permute-start.6 = (bf16[2,144,128]{2,1,0:T(8,128)(2,1)S(1)}, bf16[2,144,128]{2,1,0:T(8,128)(2,1)S(1)}, u32[]{:S(2)}, u32[]{:S(2)}) collective-permute-start(bf16[2,144,128]{2,1,0:T(8,128)(2,1)S(1)} %slice.42), channel_id=1, source_target_pairs={{0,4},{2,6},{4,0},{6,2},{8,12},{10,14},{12,8},{14,10},{1,5},{3,7},... | collective-permute-start | bytes 221192 | tf_op jit(solution)/shard_map/ppermute | solution.py:234
  90.7 8.0 %collective-permute-start.7 = (bf16[144,128]{1,0:T(8,128)(2,1)S(1)}, bf16[144,128]{1,0:T(8,128)(2,1)S(1)}, u32[]{:S(2)}, u32[]{:S(2)}) collective-permute-start(bf16[144,128]{1,0:T(8,128)(2,1)S(1)} %fusion), channel_id=1, source_target_pairs={{0,8},{2,10},{4,12},{6,14},{8,0},{10,2},{12,4},{14,6},{1,9},{3,11}... | collective-permute-start | bytes 110600 | tf_op jit(solution)/shard_map/ppermute | solution.py:234
  98.7 0.8 copy-start.3
  99.5 13.1 %all-to-all-start.1 = ((bf16[16,96,128]{2,1,0:T(8,128)(2,1)}), bf16[16,96,128]{2,1,0:T(8,128)(2,1)}, u32[]{:S(2)}, u32[]{:S(2)}) async-start(bf16[16,96,128]{2,1,0:T(8,128)(2,1)} %copy-done.3), calls=%async_computation.1 | async-start | bytes 786432 | tf_op jit(solution)/shard_map/all_to_all | solution.py:314
  105.3 11.9 %copy-start.11 = (s32[2]{0:T(128)}, s32[2]{0:T(128)S(1)}, u32[]{:S(2)}) copy-start(s32[2]{0:T(128)S(1)} %pad_add_fusion.core_ref.at_ref) | copy-start | bytes 28
  112.6 1.4 %copy-start.4 = (bf16[384,2048]{1,0:T(8,128)(2,1)S(1)}, bf16[384,2048]{1,0:T(8,128)(2,1)}, u32[]{:S(2)}) copy-start(bf16[384,2048]{1,0:T(8,128)(2,1)} %constant.10.clone.tile_ref) | copy-start | bytes 4718596
  117.3 0.6 copy-start.8
  117.9 4.7 %collective-permute-start.8 = (f32[4,256]{1,0:T(4,128)S(1)}, f32[4,256]{1,0:T(4,128)S(1)}, u32[]{:S(2)}, u32[]{:S(2)}) collective-permute-start(f32[4,256]{1,0:T(4,128)S(1)} %get-tuple-element.30), channel_id=1, source_target_pairs={{0,16},{16,0},{1,17},{17,1},{2,18},{18,2},{3,19},{19,3},{4,20},{20... | collective-permute-start | bytes 12296 | tf_op jit(solution)/shard_map/ppermute | solution.py:234
  117.9 8.5 %collective-permute-start.9 = (f32[4,256]{1,0:T(4,128)S(1)}, f32[4,256]{1,0:T(4,128)S(1)}, u32[]{:S(2)}, u32[]{:S(2)}) collective-permute-start(f32[4,256]{1,0:T(4,128)S(1)} %get-tuple-element.31), channel_id=1, source_target_pairs={{16,32},{48,64},{80,96},{112,128},{144,160},{176,192},{208,224},{3... | collective-permute-start | bytes 12296 | tf_op jit(solution)/shard_map/ppermute | solution.py:240
  122.6 3.8 %copy-start.13 = (f32[4,256]{1,0:T(4,128)}, f32[4,256]{1,0:T(4,128)S(1)}, u32[]{:S(2)}) copy-start(f32[4,256]{1,0:T(4,128)S(1)} %collective-permute-done.8.core_ref) | copy-start | bytes 12292
  126.4 0.6 copy-start.14
  128.6 3.8 %collective-permute-start.10 = (f32[4,64]{1,0:T(4,128)}, f32[4,64]{1,0:T(4,128)S(1)}, u32[]{:S(2)}, u32[]{:S(2)}) collective-permute-start(f32[4,64]{1,0:T(4,128)} %get-tuple-element.33), channel_id=1, source_target_pairs={{0,1},{1,0},{2,3},{3,2},{4,5},{5,4},{6,7},{7,6},{8,9},{9,8},{10,11... | collective-permute-start | bytes 3080 | tf_op jit(solution)/shard_map/ppermute | solution.py:234
  129.7 7.8 %collective-permute-start.11 = (f32[4,64]{1,0:T(4,128)}, f32[4,64]{1,0:T(4,128)S(1)}, u32[]{:S(2)}, u32[]{:S(2)}) collective-permute-start(f32[4,64]{1,0:T(4,128)} %get-tuple-element.34), channel_id=1, source_target_pairs={{1,2},{3,4},{5,6},{7,8},{9,10},{11,12},{13,14},{2,1},{4,3},{6,5},{... | collective-permute-start | bytes 3080 | tf_op jit(solution)/shard_map/ppermute | solution.py:240
  132.4 5.1 %copy-start.15 = (f32[4,64]{1,0:T(4,128)}, f32[4,64]{1,0:T(4,128)S(1)}, u32[]{:S(2)}) copy-start(f32[4,64]{1,0:T(4,128)S(1)} %collective-permute-done.10.near_ref) | copy-start | bytes 3076
  137.5 0.6 copy-start.16

commit v3 on v2

--- a/solution.py
+++ b/solution.py
@@ -1,9 +1,8 @@
+import functools
 import math
 
 import jax
 import jax.numpy as jnp
-import ml_dtypes
-import numpy as np
 from jax import lax
 from jax.experimental import pallas as pl
 from jax.experimental.pallas import tpu as pltpu
@@ -24,20 +23,24 @@
 BLK = ("yh", "x", "c")
 COL = ("z", "yl")
 NT = (((1,), (1,)), ((), ()))
-VMEM = 48 * 2**20
+WHOLE = pl.BlockSpec(memory_space=pltpu.VMEM)
+ANYWHERE = pl.BlockSpec(memory_space=pl.ANY)
 bf16, f32 = jnp.bfloat16, jnp.float32
 
 
-def call(kernel, shapes, scratch=()):
+def call(kernel, out, mib, scratch=(), specs=None, **more):
+    if specs is not None:
+        more["in_specs"] = specs
     return pl.pallas_call(
         kernel,
-        out_shape=shapes,
+        out_shape=out,
         scratch_shapes=scratch,
-        compiler_params=pltpu.CompilerParams(vmem_limit_bytes=VMEM),
-    )
-
-
-def pack_kernel(q_in, g_in, o_in, k_in, v_in, send_ref, q_ref, g_ref, o_ref, k_ref, v_ref, sems):
+        compiler_params=pltpu.CompilerParams(vmem_limit_bytes=mib * 2**20 if mib else None),
+        **more,
+    )
+
+
+def pack_kernel(q_in, g_in, o_in, k_in, v_in, out_ref, q_ref, g_ref, o_ref, k_ref, v_ref, send_ref, sems, out_sems):
     copies = []
     quarter = TOK // 4
     for source, target in ((k_in, k_ref), (v_in, v_ref)):
@@ -50,6 +53,7 @@
         copy.start()
     for copy in copies:
         copy.wait()
+    outs = []
     q_t = q_ref[...].astype(f32).T
     g_t = g_ref[...].astype(f32).T
     prod = g_t * o_ref[...].astype(f32).T
@@ -69,25 +73,35 @@
         k_h = jnp.concatenate([keys[:, part], lanes], axis=1)
         v_h = jnp.concatenate([vals[:, part], lanes], axis=1)
         send_ref[h, 2 * FPAD : 2 * FPAD + 16, :] = jnp.concatenate([k_h, v_h]).astype(bf16)
-
-
-def keys_kernel(got_ref, out_ref):
-    kv = got_ref[...].astype(f32).reshape(HEADS, 2, CELLS, 128)
+        if h % 4 == 3:
+            heads = slice(h - 3, h + 1)
+            copy = pltpu.make_async_copy(send_ref.at[heads], out_ref.at[heads], out_sems.at[h // 4])
+            copy.start()
+            outs.append(copy)
+    for copy in outs:
+        copy.wait()
+
+
+def keys_kernel(got_ref, out_ref, kv_ref, sem):
+    copy = pltpu.make_async_copy(got_ref.at[:, 2 * FPAD : 2 * FPAD + 16], kv_ref, sem)
+    copy.start()
+    copy.wait()
+    kv = kv_ref[...].astype(f32).reshape(HEADS, 2, CELLS, 128)
     k_t = kv[:, 0].reshape(128, 128).T
     v_t = kv[:, 1].reshape(128, 128).T
     out_ref[...] = jnp.concatenate([k_t[0:DH], v_t[0:DH]]).astype(bf16)
 
 
 def attention_kernel(
-    qg_ref, kv_own, kv_other, dq_ref, own_ref, other_ref, k_s, v_s, kt_s, e_s, dk_s, dv_s
+    qg_ref, kv_a, kv_b, kv_c, kv_d, dq_ref, own_ref, other_ref, k_s, v_s, kt_s, e_s, dk_s, dv_s
 ):
     half = KEYS // 2
     lane = lax.broadcasted_iota(jnp.int32, (128, 128), 1)
     pad = jnp.zeros((128 - DH, 128), f32)
-    for at, kv_ref in ((0, kv_own), (half, kv_other)):
-        for b in range(8):
+    for at, kv_ref in enumerate((kv_a, kv_b, kv_c, kv_d)):
+        for b in range(4):
             kv = kv_ref[b].astype(f32)
-            keys = slice(at + b * 128, at + (b + 1) * 128)
+            keys = slice((4 * at + b) * 128, (4 * at + b + 1) * 128)
             k_t = jnp.concatenate([kv[0:DH], pad])
             kt_s[:, keys] = k_t.astype(bf16)
             k_s[keys] = k_t.T.astype(bf16)
@@ -139,8 +153,10 @@
             out[b, DH : 2 * DH] = dv_t[0:DH, keys]
 
 
-def pack_back_kernel(dq_ref, mine_ref, came_ref, send_ref):
-    total = mine_ref[...] + came_ref[...].astype(f32)
+def pack_back_kernel(dq_ref, mine_ref, came_a, came_b, came_c, send_ref):
+    total = mine_ref[0]
+    for came in (came_a, came_b, came_c):
+        total = total + came[...].astype(f32)
     lanes = jnp.zeros((128, 128 - DH), f32)
     dk = jnp.concatenate([total[0:DH].T, lanes], axis=1)
     dv = jnp.concatenate([total[DH : 2 * DH].T, lanes], axis=1)
@@ -150,14 +166,26 @@
         send_ref[a, FPAD : FPAD + 16, :] = jnp.concatenate([dk[cells], dv[cells]]).astype(bf16)
 
 
-def weights_kernel(patch_ref, qkv_ref, high_ref, low_ref):
-    both = jnp.dot(patch_ref[...], qkv_ref[...], preferred_element_type=f32)
+def weights_kernel(part, patch_ref, qkv_ref, high_ref, low_ref, qkv_s, sems):
+    step = 128
+    copies = []
+    for n in range(D // step):
+        rows = slice(n * step, (n + 1) * step)
+        source = qkv_ref.at[rows, part * D : (part + 1) * D]
+        copies.append(pltpu.make_async_copy(source, qkv_s.at[rows], sems.at[n]))
+        copies[-1].start()
+    for copy in copies:
+        copy.wait()
+    both = jnp.dot(patch_ref[...], qkv_s[...], preferred_element_type=f32)
+    both = both.reshape(16, 2, 8, D)
+    both = jnp.concatenate([both[:, 0].reshape(128, D), both[:, 1].reshape(128, D)])
     high = both.astype(bf16)
     high_ref[...] = high
     low_ref[...] = (both - high.astype(f32)).astype(bf16)
 
 
-def embed_kernel(core_ref, back_ref, high_ref, low_ref, tile_ref, canvas_ref, core_out, chip_out, joined, sheet):
+def embed_kernel(back_ref, *refs):
+    weights, (canvas_ref, core_out, chip_out, joined, sheet) = refs[:6], refs[6:]
     cols = (((0,), (0,)), ((), ()))
     cell = lax.broadcasted_iota(jnp.int32, (CELLS, TOK), 0)
     token = lax.broadcasted_iota(jnp.int32, (CELLS, TOK), 1)
@@ -173,8 +201,10 @@
             wide = lax.dot_general(pooled, spread, cols, preferred_element_type=f32)
             joined[(part + 1) * D + h * DH : (part + 1) * D + (h + 1) * DH] = wide[0:DH]
     values = joined[...].astype(bf16)
-    patch = jnp.dot(high_ref[...], values, preferred_element_type=f32)
-    patch = patch + jnp.dot(low_ref[...], values, preferred_element_type=f32)
+    patch = jnp.zeros((256, TOK), f32)
+    for n, weight in enumerate(weights):
+        rows = slice(n // 2 * D, (n // 2 + 1) * D)
+        patch = patch + jnp.dot(weight[...], values[rows], preferred_element_type=f32)
     patch = jnp.concatenate([patch[0:128].T, patch[128:256].T])
     high = patch.astype(bf16)
     rest = patch - high.astype(f32)
@@ -185,8 +215,13 @@
     here = lane % 128 // 8 == row % COLS
     sheet[...] = jnp.zeros_like(sheet)
     parts = jnp.concatenate([high, mid, low], axis=1)
+    to = lax.broadcasted_iota(jnp.int32, (128, 256), 1)
+    at = lax.broadcasted_iota(jnp.int32, (128, 256), 0)
     for pair in range(8):
-        wide = jnp.dot(parts, tile_ref[:, pair * 256 : (pair + 1) * 256], preferred_element_type=f32)
+        tile = (to // 128 + 2 * pair == at // 8) & (to % 8 == at % 8)
+        tile = jnp.where(tile, 1.0, 0.0).astype(bf16)
+        tile = jnp.concatenate([tile] * 3)
+        wide = jnp.dot(parts, tile, preferred_element_type=f32)
         wide = jnp.where(here, wide, 0.0)
         wide = jnp.sum(wide.reshape(2 * ROWS, COLS, 256), axis=1)
         for k in (0, 1):
@@ -202,13 +237,13 @@
     edges = jnp.where(lane < 4, left, pltpu.roll(right, 8, 1))
     canvas = jnp.concatenate([center, jnp.where(lane < 8, edges, 0.0)], axis=1)
     canvas_ref[...] = canvas
-    first = core_ref[0] == 0
+    first = lax.axis_index("c") == 0
     core_out[...] = jnp.where(first, canvas[68:72], canvas[0:4])
     chip_out[...] = jnp.where(first, canvas[0:4], canvas[68:72])
 
 
-def rows_kernel(at_ref, canvas_ref, core_ref, chip_ref, center_ref, near_out, far_out):
-    first = at_ref[0] == 0
+def rows_kernel(canvas_ref, core_ref, chip_ref, center_ref, near_out, far_out):
+    first = lax.axis_index("c") == 0
     above = jnp.where(first, chip_ref[...], core_ref[...])
     below = jnp.where(first, core_ref[...], chip_ref[...])
     quiet = jnp.zeros((56, 256), f32)
@@ -216,13 +251,13 @@
     center_ref[...] = canvas[:, 0:128]
     edges = canvas[:, 128:256].T[0:8]
     left, right = edges[0:4], edges[4:8]
-    begins = at_ref[1] == 0
+    begins = lax.axis_index("yl") == 0
     near_out[...] = jnp.where(begins, right, left)
     far_out[...] = jnp.where(begins, left, right)
 
 
-def cols_kernel(at_ref, center_ref, near_ref, far_ref, out_ref):
-    begins = at_ref[1] == 0
+def cols_kernel(center_ref, near_ref, far_ref, out_ref):
+    begins = lax.axis_index("yl") == 0
     left = jnp.where(begins, far_ref[...], near_ref[...])
     right = jnp.where(begins, near_ref[...], far_ref[...])
     quiet = jnp.zeros((120, 64), f32)
@@ -240,38 +275,30 @@
     return lax.ppermute(x, axis, pairs + [(target, source) for source, target in pairs])
 
 
-def tile_matrix():
-    rows = np.arange(128)[:, None]
-    lanes = np.arange(2048)[None, :]
-    tile = (lanes // 128 == rows // 8) & (lanes % 8 == rows % 8)
-    return np.concatenate([tile] * 3).astype(ml_dtypes.bfloat16)
-
-
-def combined_weights(w_qkv, w_patch):
-    ordered = w_patch.reshape(16, 2, 8, D).transpose(1, 0, 2, 3).reshape(256, D)
-    width = 384
-    shape = jax.ShapeDtypeStruct((256, 3 * D), bf16)
-    return pl.pallas_call(
-        weights_kernel,
-        grid=(3 * D // width,),
-        in_specs=[pl.BlockSpec((256, D), lambda n: (0, 0)), pl.BlockSpec((D, width), lambda n: (0, n))],
-        out_specs=[pl.BlockSpec((256, width), lambda n: (0, n))] * 2,
-        out_shape=[shape, shape],
-        cost_estimate=pl.CostEstimate(flops=2 * 256 * D * 3 * D, bytes_accessed=6 * D * D, transcendentals=0),
-    )(ordered, w_qkv)
+def combined_weights(w_qkv, w_patch, part):
+    shape = jax.ShapeDtypeStruct((256, D), bf16)
+    return call(
+        functools.partial(weights_kernel, part),
+        [shape, shape],
+        12,
+        [pltpu.VMEM((D, D), bf16), pltpu.SemaphoreType.DMA((D // 128,))],
+        [WHOLE, ANYWHERE],
+        cost_estimate=pl.CostEstimate(flops=2 * 256 * D * D, bytes_accessed=4 * D * D, transcendentals=0),
+    )(w_patch, w_qkv)
 
 
 def on_device(queries, key_states, values, saved_out, grad_out, w_qkv, w_patch):
-    weights = combined_weights(w_qkv, w_patch)
-    anywhere = pl.BlockSpec(memory_space=pl.ANY)
     tokens = pltpu.VMEM((TOK, D), bf16)
     cells = pltpu.VMEM((2, 4, D), bf16)
-    send = pl.pallas_call(
+    packed = (HEADS, 2 * FPAD + 16, TOK)
+    dma = pltpu.SemaphoreType.DMA
+    send = call(
         pack_kernel,
-        in_specs=[anywhere] * 5,
-        out_shape=jax.ShapeDtypeStruct((HEADS, 2 * FPAD + 16, TOK), bf16),
-        scratch_shapes=[tokens, tokens, tokens, cells, cells, pltpu.SemaphoreType.DMA((14,))],
-        compiler_params=pltpu.CompilerParams(vmem_limit_bytes=VMEM),
+        jax.ShapeDtypeStruct(packed, bf16),
+        None,
+        [tokens, tokens, tokens, cells, cells, pltpu.VMEM(packed, bf16), dma((14,)), dma((4,))],
+        [ANYWHERE] * 5,
+        out_specs=ANYWHERE,
     )(
         queries.reshape(TOK, D),
         grad_out.reshape(TOK, D),
@@ -280,21 +307,28 @@
         values,
     )
     got = lax.all_to_all(send, HEAD_AXES, 0, 0, tiled=True)
-    kv = pl.pallas_call(
+    kv = call(
         keys_kernel,
-        grid=(1,),
-        in_specs=[pl.BlockSpec((HEADS, 16, 128), lambda n: (0, 10, 0))],
-        out_specs=pl.BlockSpec((2 * DH, 128), lambda n: (0, 0)),
-        out_shape=jax.ShapeDtypeStruct((2 * DH, 128), bf16),
-    )(got)[None]
-    for by in (4, 2, 1):
-        kv = jnp.concatenate([kv, swapped(kv, "z", by)])
-    kv_other = swapped(kv, "c", 1)
-    kv, kv_other, *weights = lax.optimization_barrier((kv, kv_other, *weights))
+        jax.ShapeDtypeStruct((2 * DH, 128), bf16),
+        4,
+        [pltpu.VMEM((HEADS, 16, 128), bf16), dma(())],
+        [ANYWHERE],
+    )(got)
+    came = [swapped(kv, "z", by) for by in (2, 4, 6)]
+    weights = list(combined_weights(w_qkv, w_patch, 0))
+    came, weights = lax.optimization_barrier((came, weights))
+    kv_a = jnp.stack([kv] + came)
+    kv_b = swapped(kv_a, "z", 1)
+    kv_c = swapped(kv_a, "c", 1)
+    for part in (1, 2):
+        weights += combined_weights(w_qkv, w_patch, part)
+    kv_b, kv_c, weights = lax.optimization_barrier((kv_b, kv_c, weights))
+    kv_d = swapped(kv_b, "c", 1)
     grads = jax.ShapeDtypeStruct((8, 2 * DH, 128), f32)
     dq, own, other = call(
         attention_kernel,
         [jax.ShapeDtypeStruct((HEADS, FPAD, TOK), bf16), grads, grads],
+        32,
         [
             pltpu.VMEM((KEYS, 128), bf16),
             pltpu.VMEM((KEYS, 128), bf16),
@@ -303,37 +337,28 @@
             pltpu.VMEM((KEYS, 128), f32),
             pltpu.VMEM((KEYS, 128), f32),
         ],
-    )(got, kv, kv_other)
+    )(got, kv_a, kv_b, kv_c, kv_d)
     mine = own + swapped(other, "c", 1)
-    for by, keep in ((1, 4), (2, 2)):
-        mine = mine[:keep] + swapped(mine[keep:].astype(bf16), "z", by).astype(f32)
-    came = swapped(mine[1].astype(bf16), "z", 4)
-    send = call(pack_back_kernel, jax.ShapeDtypeStruct((HEADS, FPAD + 16, TOK), bf16))(
-        dq, mine[0], came
+    mine = mine[:4] + swapped(mine[4:].astype(bf16), "z", 1).astype(f32)
+    came = [swapped(mine[n].astype(bf16), "z", 2 * n) for n in (1, 2, 3)]
+    send = call(pack_back_kernel, jax.ShapeDtypeStruct((HEADS, FPAD + 16, TOK), bf16), 8)(
+        dq, mine[0:1], *came
     )
     back = lax.all_to_all(send, HEAD_AXES, 0, 0, tiled=True)
-    at = jnp.stack([lax.axis_index("c"), lax.axis_index("yl")]).astype(jnp.int32)
-    scalars = pl.BlockSpec(memory_space=pltpu.SMEM)
-    whole = pl.BlockSpec(memory_space=pltpu.VMEM)
     strip = jax.ShapeDtypeStruct((4, 256), f32)
-    canvas, to_core, to_chip = pl.pallas_call(
+    canvas, to_core, to_chip = call(
         embed_kernel,
-        in_specs=[scalars] + [whole] * 4,
-        out_shape=[jax.ShapeDtypeStruct((72, 256), f32), strip, strip],
-        scratch_shapes=[pltpu.VMEM((3 * D, TOK), f32), pltpu.VMEM((2, 72, 128), f32)],
-        compiler_params=pltpu.CompilerParams(vmem_limit_bytes=VMEM),
-    )(at, back, *weights, tile_matrix())
+        [jax.ShapeDtypeStruct((72, 256), f32), strip, strip],
+        24,
+        [pltpu.VMEM((3 * D, TOK), f32), pltpu.VMEM((2, 72, 128), f32)],
+    )(back, *weights)
     strip = jax.ShapeDtypeStruct((4, 64), f32)
-    center, to_near, to_far = pl.pallas_call(
-        rows_kernel,
-        in_specs=[scalars] + [whole] * 3,
-        out_shape=[jax.ShapeDtypeStruct((64, 128), f32), strip, strip],
-    )(at, canvas, swapped(to_core, "c", 1), neighbours(to_chip, BLK))
-    return pl.pallas_call(
-        cols_kernel,
-        in_specs=[scalars] + [whole] * 3,
-        out_shape=jax.ShapeDtypeStruct((64, 128), f32),
-    )(at, center, swapped(to_near, "yl", 1), neighbours(to_far, COL))
+    center, to_near, to_far = call(
+        rows_kernel, [jax.ShapeDtypeStruct((64, 128), f32), strip, strip], 4
+    )(canvas, swapped(to_core, "c", 1), neighbours(to_chip, BLK))
+    return call(cols_kernel, jax.ShapeDtypeStruct((64, 128), f32), 4)(
+        center, swapped(to_near, "yl", 1), neighbours(to_far, COL)
+    )
 
 
 def solution(mesh):

time: 141 us -> 113 us (0.80)
  the two profiles are of different devices: /device:TPU:144 before, /device:TPU:24 now
where the time goes in v3:
time: 113 us
  blocking collectives  31.1 us (28%)
  starting transfers between devices  26.9 us (24%)
  Pallas kernels  26.6 us (24%)
  waiting for transfers between devices  23.3 us (21%)
  local copies, waits for them, and re-layouts  4.36 us (4%)
    ppermute x13, starting transfers between devices, swapped(): return lax.ppermute(x, axis, [(i, i ^ by) for i in range(peers)])  19.1 us
    all_to_all x1, blocking collectives, on_device(): got = lax.all_to_all(send, HEAD_AXES, 0, 0, tiled=True)  18.5 us
    pallas_call x1, Pallas kernels, on_device(): call(attention_kernel, [jax.ShapeDtypeStruct((HEADS, FPAD, TOK), bf16), g...  16.7 us
    ppermute x13, waiting for transfers between devices, swapped(): return lax.ppermute(x, axis, [(i, i ^ by) for i in range(peers)])  16.3 us
    all_to_all x1, blocking collectives, on_device(): back = lax.all_to_all(send, HEAD_AXES, 0, 0, tiled=True)  12.6 us
    ppermute x2, starting transfers between devices, neighbours(): lax.ppermute(x, axis, pairs + [(target, source) for source, target in pai...  7.79 us
    ppermute x2, waiting for transfers between devices, neighbours(): lax.ppermute(x, axis, pairs + [(target, source) for source, target in pai...  7.08 us
    unnamed x4, local copies, waits for them, and re-layouts  4.32 us
  transfers between devices with their start and end apart: 15, of which 7 were waited for; matrix products, arithmetic and copies ran while one was open for 0% of the time, Pallas kernels for 3%

profile of v3, /device:TPU:24, one launch (start us, length us, event | category | flops | bytes accessed | tf_op | source)
XLA Modules:
  0.0 112.6 jit_solution(1553656429130805749)
XLA Ops:
  0.0 2.6 %shard_map.73 = bf16[16,176,128]{2,1,0:T(8,128)(2,1)} custom-call(bf16[128,1152]{1,0:T(8,128)(2,1)} %bitcast.14, bf16[128,1152]{1,0:T(8,128)(2,1)} %bitcast.15, bf16[128,1152]{1,0:T(8,128)(2,1)} %bitcast.16, bf16[2,4,1152]{2,1,0:T(4,128)(2,1)} %k_in.1, bf16[2,4,1152]{2,1,0:T(4,128)(2,1)} %v_in.1), custom_call_target="tpu_custom_call" | custom-call | tf_op jit(solution)/shard_map/pallas_call | solution.py:295
  2.6 18.5 %all_to_all.10.got_ref.qg_ref = bf16[16,176,128]{2,1,0:T(8,128)(2,1)S(1)} all-to-all(bf16[16,176,128]{2,1,0:T(8,128)(2,1)} %shard_map.73), channel_id=1, replica_groups=mesh['yh'=2,'x'=4,'c'=2,'z'=8,'yl'=2] {'yh','x','yl'}, dimensions={0} | all-to-all | bytes 1441792 | tf_op jit(solution)/shard_map/all_to_all | solution.py:309
  21.2 0.1 shard_map.74
  21.3 6.4 %collective-permute-start.2 = (bf16[144,128]{1,0:T(8,128)(2,1)S(1)}, bf16[144,128]{1,0:T(8,128)(2,1)S(1)}, u32[]{:S(2)}, u32[]{:S(2)}) collective-permute-start(bf16[144,128]{1,0:T(8,128)(2,1)S(1)} %shard_map.74), channel_id=1, source_target_pairs={{0,12},{2,14},{4,8},{6,10},{8,4},{10,6},{12,0},{14,2},{1,13},{3,15... | collective-permute-start | bytes 110600 | tf_op jit(solution)/shard_map/ppermute | solution.py:269
  27.7 1.0 collective-permute-start.1
  28.6 1.5 %collective-permute-start = (bf16[144,128]{1,0:T(8,128)(2,1)S(1)}, bf16[144,128]{1,0:T(8,128)(2,1)S(1)}, u32[]{:S(2)}, u32[]{:S(2)}) collective-permute-start(bf16[144,128]{1,0:T(8,128)(2,1)S(1)} %shard_map.74), channel_id=1, source_target_pairs={{0,4},{2,6},{4,0},{6,2},{8,12},{10,14},{12,8},{14,10},{1,5},{3,7},... | collective-permute-start | bytes 110600 | tf_op jit(solution)/shard_map/ppermute | solution.py:269
  30.1 0.0 copy-start
  30.1 3.3 %copy-done = bf16[1152,3456]{1,0:T(8,128)(2,1)S(1)} copy-done((bf16[1152,3456]{1,0:T(8,128)(2,1)S(1)}, bf16[1152,3456]{1,0:T(8,128)(2,1)}, u32[]{:S(2)}) %copy-start) | copy-done | bytes 7962648
  33.4 0.0 copy-start.1
  33.4 1.1 copy-done.1
  34.4 1.3 %shard_map.75 = (bf16[256,1152]{1,0:T(8,128)(2,1)S(1)}, bf16[256,1152]{1,0:T(8,128)(2,1)S(1)}) custom-call(bf16[256,1152]{1,0:T(8,128)(2,1)S(1)} %copy-done.1, bf16[1152,3456]{1,0:T(8,128)(2,1)S(1)} %copy-done), custom_call_target="tpu_custom_call" | custom-call | flops 679477248 | bytes 5308416 | tf_op jit(solution)/shard_map/pallas_call | solution.py:280
  35.8 0.0 collective-permute-done.2
  35.8 0.0 collective-permute-done.1
  35.8 0.0 collective-permute-done
  35.8 0.1 collective-permute-start.4
  35.9 1.1 collective-permute-start.3
  37.0 1.3 %shard_map.77 = (bf16[256,1152]{1,0:T(8,128)(2,1)S(1)}, bf16[256,1152]{1,0:T(8,128)(2,1)S(1)}) custom-call(bf16[256,1152]{1,0:T(8,128)(2,1)S(1)} %copy-done.1, bf16[1152,3456]{1,0:T(8,128)(2,1)S(1)} %copy-done), custom_call_target="tpu_custom_call" | custom-call | flops 679477248 | bytes 5308416 | tf_op jit(solution)/shard_map/pallas_call | solution.py:280
  38.3 1.3 %shard_map.76 = (bf16[256,1152]{1,0:T(8,128)(2,1)S(1)}, bf16[256,1152]{1,0:T(8,128)(2,1)S(1)}) custom-call(bf16[256,1152]{1,0:T(8,128)(2,1)S(1)} %copy-done.1, bf16[1152,3456]{1,0:T(8,128)(2,1)S(1)} %copy-done), custom_call_target="tpu_custom_call" | custom-call | flops 679477248 | bytes 5308416 | tf_op jit(solution)/shard_map/pallas_call | solution.py:280
  39.7 0.0 collective-permute-done.4.kv_c
  39.7 2.5 %collective-permute-done.3.kv_b = bf16[4,144,128]{2,1,0:T(8,128)(2,1)S(1)} collective-permute-done((bf16[4,144,128]{2,1,0:T(8,128)(2,1)S(1)}, bf16[4,144,128]{2,1,0:T(8,128)(2,1)S(1)}, u32[]{:S(2)}, u32[]{:S(2)}) %collective-permute-start.3) | collective-permute-done | bytes 147488 | tf_op jit(solution)/shard_map/ppermute | solution.py:269
  42.2 0.0 collective-permute-start.5
  42.2 1.4 %collective-permute-done.5.kv_d = bf16[4,144,128]{2,1,0:T(8,128)(2,1)S(1)} collective-permute-done((bf16[4,144,128]{2,1,0:T(8,128)(2,1)S(1)}, bf16[4,144,128]{2,1,0:T(8,128)(2,1)S(1)}, u32[]{:S(2)}, u32[]{:S(2)}) %collective-permute-start.5) | collective-permute-done | bytes 147488 | tf_op jit(solution)/shard_map/ppermute | solution.py:269
  43.6 16.7 %shard_map.78 = (bf16[16,80,128]{2,1,0:T(8,128)(2,1)S(1)}, f32[8,144,128]{2,1,0:T(8,128)S(1)}, f32[8,144,128]{2,1,0:T(8,128)S(1)}) custom-call(bf16[16,176,128]{2,1,0:T(8,128)(2,1)S(1)} %all_to_all.10.got_ref.qg_ref, bf16[4,144,128]{2,1,0:T(8,128)(2,1)S(1)} %pad_maximum_fusion.kv_a, bf16[4,144,128]{2,1,0:T(8,128)(2,1)S(1)} %collective-permute-done.3.kv_b, ...), custom_call_target="tpu_custom_call" | custom-call | tf_op jit(solution)/shard_map/pallas_call | solution.py:328
  60.3 0.2 collective-permute-start.6
  60.5 1.9 %collective-permute-done.6 = f32[8,144,128]{2,1,0:T(8,128)S(1)} collective-permute-done((f32[8,144,128]{2,1,0:T(8,128)S(1)}, f32[8,144,128]{2,1,0:T(8,128)S(1)}, u32[]{:S(2)}, u32[]{:S(2)}) %collective-permute-start.6) | collective-permute-done | bytes 589856 | tf_op jit(solution)/shard_map/ppermute | solution.py:269
  62.4 0.1 add.6
  62.5 1.1 collective-permute-start.7
  63.6 4.9 %collective-permute-done.7 = bf16[4,144,128]{2,1,0:T(8,128)(2,1)S(1)} collective-permute-done((bf16[4,144,128]{2,1,0:T(8,128)(2,1)S(1)}, bf16[4,144,128]{2,1,0:T(8,128)(2,1)S(1)}, u32[]{:S(2)}, u32[]{:S(2)}) %collective-permute-start.7) | collective-permute-done | bytes 147488 | tf_op jit(solution)/shard_map/ppermute | solution.py:269
  68.5 4.1 %collective-permute-start.10 = (bf16[144,128]{1,0:T(8,128)(2,1)S(1)}, bf16[144,128]{1,0:T(8,128)(2,1)S(1)}, u32[]{:S(2)}, u32[]{:S(2)}) collective-permute-start(bf16[144,128]{1,0:T(8,128)(2,1)S(1)} %get-tuple-element.63), channel_id=1, source_target_pairs={{0,12},{2,14},{4,8},{6,10},{8,4},{10,6},{12,0},{14,2},{1,13},{3,15... | collective-permute-start | bytes 110600 | tf_op jit(solution)/shard_map/ppermute | solution.py:269
  72.6 1.2 %collective-permute-start.9 = (bf16[144,128]{1,0:T(8,128)(2,1)S(1)}, bf16[144,128]{1,0:T(8,128)(2,1)S(1)}, u32[]{:S(2)}, u32[]{:S(2)}) collective-permute-start(bf16[144,128]{1,0:T(8,128)(2,1)S(1)} %get-tuple-element.64), channel_id=1, source_target_pairs={{0,8},{2,10},{4,12},{6,14},{8,0},{10,2},{12,4},{14,6},{1,9},{3,11}... | collective-permute-start | bytes 110600 | tf_op jit(solution)/shard_map/ppermute | solution.py:269
  73.8 1.5 %collective-permute-start.8 = (bf16[144,128]{1,0:T(8,128)(2,1)S(1)}, bf16[144,128]{1,0:T(8,128)(2,1)S(1)}, u32[]{:S(2)}, u32[]{:S(2)}) collective-permute-start(bf16[144,128]{1,0:T(8,128)(2,1)S(1)} %get-tuple-element.65), channel_id=1, source_target_pairs={{0,4},{2,6},{4,0},{6,2},{8,12},{10,14},{12,8},{14,10},{1,5},{3,7},... | collective-permute-start | bytes 110600 | tf_op jit(solution)/shard_map/ppermute | solution.py:269
  75.3 0.0 collective-permute-done.10.came_c
  75.3 5.5 %collective-permute-done.9.came_b = bf16[144,128]{1,0:T(8,128)(2,1)S(1)} collective-permute-done((bf16[144,128]{1,0:T(8,128)(2,1)S(1)}, bf16[144,128]{1,0:T(8,128)(2,1)S(1)}, u32[]{:S(2)}, u32[]{:S(2)}) %collective-permute-start.9) | collective-permute-done | bytes 36896 | tf_op jit(solution)/shard_map/ppermute | solution.py:269
  80.9 0.0 collective-permute-done.8.came_a
  80.9 0.1 shard_map.79
  81.0 12.6 %all_to_all.11.back_ref = bf16[16,96,128]{2,1,0:T(8,128)(2,1)S(1)} all-to-all(bf16[16,96,128]{2,1,0:T(8,128)(2,1)S(1)} %shard_map.79), channel_id=1, replica_groups=mesh['yh'=2,'x'=4,'c'=2,'z'=8,'yl'=2] {'yh','x','yl'}, dimensions={0} | all-to-all | bytes 786432 | tf_op jit(solution)/shard_map/all_to_all | solution.py:347
  93.6 2.3 %shard_map.80 = (f32[72,256]{1,0:T(8,128)S(1)}, f32[4,256]{1,0:T(4,128)S(1)}, f32[4,256]{1,0:T(4,128)S(1)}) custom-call(bf16[16,96,128]{2,1,0:T(8,128)(2,1)S(1)} %all_to_all.11.back_ref, bf16[256,1152]{1,0:T(8,128)(2,1)S(1)} %get-tuple-element.49.refs_0_, bf16[256,1152]{1,0:T(8,128)(2,1)S(1)} %get-tuple-element.50.refs_1_, ...), custom_call_target="tpu_custom_call" | custom-call | tf_op jit(solution)/shard_map/pallas_call | solution.py:349
  95.9 0.1 collective-permute-start.11
  96.0 4.4 %collective-permute-start.12 = (f32[4,256]{1,0:T(4,128)S(1)}, f32[4,256]{1,0:T(4,128)S(1)}, u32[]{:S(2)}, u32[]{:S(2)}) collective-permute-start(f32[4,256]{1,0:T(4,128)S(1)} %get-tuple-element.57), channel_id=1, source_target_pairs={{16,32},{48,64},{80,96},{112,128},{144,160},{176,192},{208,224},{3... | collective-permute-start | bytes 12296 | tf_op jit(solution)/shard_map/ppermute | solution.py:275
  100.4 0.0 collective-permute-done.11.core_ref
  100.4 4.2 %collective-permute-done.12.chip_ref = f32[4,256]{1,0:T(4,128)S(1)} collective-permute-done((f32[4,256]{1,0:T(4,128)S(1)}, f32[4,256]{1,0:T(4,128)S(1)}, u32[]{:S(2)}, u32[]{:S(2)}) %collective-permute-start.12) | collective-permute-done | bytes 4128 | tf_op jit(solution)/shard_map/ppermute | solution.py:275
  104.6 0.1 shard_map.81
  104.6 0.9 collective-permute-start.13
  105.5 3.4 %collective-permute-start.14 = (f32[4,64]{1,0:T(4,128)S(1)}, f32[4,64]{1,0:T(4,128)S(1)}, u32[]{:S(2)}, u32[]{:S(2)}) collective-permute-start(f32[4,64]{1,0:T(4,128)S(1)} %get-tuple-element.60), channel_id=1, source_target_pairs={{1,2},{3,4},{5,6},{7,8},{9,10},{11,12},{13,14},{2,1},{4,3},{6,5},{... | collective-permute-start | bytes 3080 | tf_op jit(solution)/shard_map/ppermute | solution.py:275
  109.0 0.0 collective-permute-done.13.near_ref
  109.0 2.9 %collective-permute-done.14.far_ref = f32[4,64]{1,0:T(4,128)S(1)} collective-permute-done((f32[4,64]{1,0:T(4,128)S(1)}, f32[4,64]{1,0:T(4,128)S(1)}, u32[]{:S(2)}, u32[]{:S(2)}) %collective-permute-start.14) | collective-permute-done | bytes 1056 | tf_op jit(solution)/shard_map/ppermute | solution.py:275
  111.9 0.7 shard_map.82
  (5 shorter events, 0.1 us)
Async XLA Ops:
  21.3 14.5 %collective-permute-start.2 = (bf16[144,128]{1,0:T(8,128)(2,1)S(1)}, bf16[144,128]{1,0:T(8,128)(2,1)S(1)}, u32[]{:S(2)}, u32[]{:S(2)}) collective-permute-start(bf16[144,128]{1,0:T(8,128)(2,1)S(1)} %shard_map.74), channel_id=1, source_target_pairs={{0,12},{2,14},{4,8},{6,10},{8,4},{10,6},{12,0},{14,2},{1,13},{3,15... | collective-permute-start | bytes 110600 | tf_op jit(solution)/shard_map/ppermute | solution.py:269
  27.7 8.1 %collective-permute-start.1 = (bf16[144,128]{1,0:T(8,128)(2,1)S(1)}, bf16[144,128]{1,0:T(8,128)(2,1)S(1)}, u32[]{:S(2)}, u32[]{:S(2)}) collective-permute-start(bf16[144,128]{1,0:T(8,128)(2,1)S(1)} %shard_map.74), channel_id=1, source_target_pairs={{0,8},{2,10},{4,12},{6,14},{8,0},{10,2},{12,4},{14,6},{1,9},{3,11}... | collective-permute-start | bytes 110600 | tf_op jit(solution)/shard_map/ppermute | solution.py:269
  28.6 7.1 %collective-permute-start = (bf16[144,128]{1,0:T(8,128)(2,1)S(1)}, bf16[144,128]{1,0:T(8,128)(2,1)S(1)}, u32[]{:S(2)}, u32[]{:S(2)}) collective-permute-start(bf16[144,128]{1,0:T(8,128)(2,1)S(1)} %shard_map.74), channel_id=1, source_target_pairs={{0,4},{2,6},{4,0},{6,2},{8,12},{10,14},{12,8},{14,10},{1,5},{3,7},... | collective-permute-start | bytes 110600 | tf_op jit(solution)/shard_map/ppermute | solution.py:269
  30.1 3.3 %copy-start = (bf16[1152,3456]{1,0:T(8,128)(2,1)S(1)}, bf16[1152,3456]{1,0:T(8,128)(2,1)}, u32[]{:S(2)}) copy-start(bf16[1152,3456]{1,0:T(8,128)(2,1)} %qkv_ref.5) | copy-start | bytes 23887876
  33.4 1.1 copy-start.1
  35.8 3.8 %collective-permute-start.4 = (bf16[4,144,128]{2,1,0:T(8,128)(2,1)S(1)}, bf16[4,144,128]{2,1,0:T(8,128)(2,1)S(1)}, u32[]{:S(2)}, u32[]{:S(2)}) collective-permute-start(bf16[4,144,128]{2,1,0:T(8,128)(2,1)S(1)} %pad_maximum_fusion.kv_a), channel_id=1, source_target_pairs={{0,16},{16,0},{1,17},{17,1},{2,18},{18,2},{3,19},{19,3},{4,20},{20... | collective-permute-start | bytes 442376 | tf_op jit(solution)/shard_map/ppermute | solution.py:269
  35.9 6.3 %collective-permute-start.3 = (bf16[4,144,128]{2,1,0:T(8,128)(2,1)S(1)}, bf16[4,144,128]{2,1,0:T(8,128)(2,1)S(1)}, u32[]{:S(2)}, u32[]{:S(2)}) collective-permute-start(bf16[4,144,128]{2,1,0:T(8,128)(2,1)S(1)} %pad_maximum_fusion.kv_a), channel_id=1, source_target_pairs={{0,2},{2,0},{4,6},{6,4},{8,10},{10,8},{12,14},{14,12},{1,3},{3,1},... | collective-permute-start | bytes 442376 | tf_op jit(solution)/shard_map/ppermute | solution.py:269
  42.2 1.4 %collective-permute-start.5 = (bf16[4,144,128]{2,1,0:T(8,128)(2,1)S(1)}, bf16[4,144,128]{2,1,0:T(8,128)(2,1)S(1)}, u32[]{:S(2)}, u32[]{:S(2)}) collective-permute-start(bf16[4,144,128]{2,1,0:T(8,128)(2,1)S(1)} %collective-permute-done.3.kv_b), channel_id=1, source_target_pairs={{0,16},{16,0},{1,17},{17,1},{2,18},{18,2},{3,19},{19,3},{4,20},{20... | collective-permute-start | bytes 442376 | tf_op jit(solution)/shard_map/ppermute | solution.py:269
  60.3 2.1 %collective-permute-start.6 = (f32[8,144,128]{2,1,0:T(8,128)S(1)}, f32[8,144,128]{2,1,0:T(8,128)S(1)}, u32[]{:S(2)}, u32[]{:S(2)}) collective-permute-start(f32[8,144,128]{2,1,0:T(8,128)S(1)} %get-tuple-element.48), channel_id=1, source_target_pairs={{0,16},{16,0},{1,17},{17,1},{2,18},{18,2},{3,19},{19,3},{4,20},{20... | collective-permute-start | bytes 1769480 | tf_op jit(solution)/shard_map/ppermute | solution.py:269
  62.5 6.0 %collective-permute-start.7 = (bf16[4,144,128]{2,1,0:T(8,128)(2,1)S(1)}, bf16[4,144,128]{2,1,0:T(8,128)(2,1)S(1)}, u32[]{:S(2)}, u32[]{:S(2)}) collective-permute-start(bf16[4,144,128]{2,1,0:T(8,128)(2,1)S(1)} %slice.39), channel_id=1, source_target_pairs={{0,2},{2,0},{4,6},{6,4},{8,10},{10,8},{12,14},{14,12},{1,3},{3,1},... | collective-permute-start | bytes 442376 | tf_op jit(solution)/shard_map/ppermute | solution.py:269
  68.5 6.8 %collective-permute-start.10 = (bf16[144,128]{1,0:T(8,128)(2,1)S(1)}, bf16[144,128]{1,0:T(8,128)(2,1)S(1)}, u32[]{:S(2)}, u32[]{:S(2)}) collective-permute-start(bf16[144,128]{1,0:T(8,128)(2,1)S(1)} %get-tuple-element.63), channel_id=1, source_target_pairs={{0,12},{2,14},{4,8},{6,10},{8,4},{10,6},{12,0},{14,2},{1,13},{3,15... | collective-permute-start | bytes 110600 | tf_op jit(solution)/shard_map/ppermute | solution.py:269
  72.6 8.2 %collective-permute-start.9 = (bf16[144,128]{1,0:T(8,128)(2,1)S(1)}, bf16[144,128]{1,0:T(8,128)(2,1)S(1)}, u32[]{:S(2)}, u32[]{:S(2)}) collective-permute-start(bf16[144,128]{1,0:T(8,128)(2,1)S(1)} %get-tuple-element.64), channel_id=1, source_target_pairs={{0,8},{2,10},{4,12},{6,14},{8,0},{10,2},{12,4},{14,6},{1,9},{3,11}... | collective-permute-start | bytes 110600 | tf_op jit(solution)/shard_map/ppermute | solution.py:269
  73.8 7.1 %collective-permute-start.8 = (bf16[144,128]{1,0:T(8,128)(2,1)S(1)}, bf16[144,128]{1,0:T(8,128)(2,1)S(1)}, u32[]{:S(2)}, u32[]{:S(2)}) collective-permute-start(bf16[144,128]{1,0:T(8,128)(2,1)S(1)} %get-tuple-element.65), channel_id=1, source_target_pairs={{0,4},{2,6},{4,0},{6,2},{8,12},{10,14},{12,8},{14,10},{1,5},{3,7},... | collective-permute-start | bytes 110600 | tf_op jit(solution)/shard_map/ppermute | solution.py:269
  95.9 4.5 %collective-permute-start.11 = (f32[4,256]{1,0:T(4,128)S(1)}, f32[4,256]{1,0:T(4,128)S(1)}, u32[]{:S(2)}, u32[]{:S(2)}) collective-permute-start(f32[4,256]{1,0:T(4,128)S(1)} %get-tuple-element.56), channel_id=1, source_target_pairs={{0,16},{16,0},{1,17},{17,1},{2,18},{18,2},{3,19},{19,3},{4,20},{20... | collective-permute-start | bytes 12296 | tf_op jit(solution)/shard_map/ppermute | solution.py:269
  96.0 8.5 %collective-permute-start.12 = (f32[4,256]{1,0:T(4,128)S(1)}, f32[4,256]{1,0:T(4,128)S(1)}, u32[]{:S(2)}, u32[]{:S(2)}) collective-permute-start(f32[4,256]{1,0:T(4,128)S(1)} %get-tuple-element.57), channel_id=1, source_target_pairs={{16,32},{48,64},{80,96},{112,128},{144,160},{176,192},{208,224},{3... | collective-permute-start | bytes 12296 | tf_op jit(solution)/shard_map/ppermute | solution.py:275
  104.6 4.3 %collective-permute-start.13 = (f32[4,64]{1,0:T(4,128)S(1)}, f32[4,64]{1,0:T(4,128)S(1)}, u32[]{:S(2)}, u32[]{:S(2)}) collective-permute-start(f32[4,64]{1,0:T(4,128)S(1)} %get-tuple-element.59), channel_id=1, source_target_pairs={{0,1},{1,0},{2,3},{3,2},{4,5},{5,4},{6,7},{7,6},{8,9},{9,8},{10,11... | collective-permute-start | bytes 3080 | tf_op jit(solution)/shard_map/ppermute | solution.py:269
  105.5 6.4 %collective-permute-start.14 = (f32[4,64]{1,0:T(4,128)S(1)}, f32[4,64]{1,0:T(4,128)S(1)}, u32[]{:S(2)}, u32[]{:S(2)}) collective-permute-start(f32[4,64]{1,0:T(4,128)S(1)} %get-tuple-element.60), channel_id=1, source_target_pairs={{1,2},{3,4},{5,6},{7,8},{9,10},{11,12},{13,14},{2,1},{4,3},{6,5},{... | collective-permute-start | bytes 3080 | tf_op jit(solution)/shard_map/ppermute | solution.py:275

commit v4 on v3

--- a/solution.py
+++ b/solution.py
@@ -19,6 +19,10 @@
 CELLS = TOK // POOL**2
 FPAD = 80
 KEYS = 2048
+HALF = KEYS // 2
+TILE = 1024
+PER = TILE // TOK
+STEP = 256
 HEAD_AXES = ("yh", "x", "yl")
 BLK = ("yh", "x", "c")
 COL = ("z", "yl")
@@ -92,65 +96,143 @@
     out_ref[...] = jnp.concatenate([k_t[0:DH], v_t[0:DH]]).astype(bf16)
 
 
-def attention_kernel(
-    qg_ref, kv_a, kv_b, kv_c, kv_d, dq_ref, own_ref, other_ref, k_s, v_s, kt_s, e_s, dk_s, dv_s
-):
-    half = KEYS // 2
+def load_keys(kv_refs, k_s, kt_s=None, v_s=None):
     lane = lax.broadcasted_iota(jnp.int32, (128, 128), 1)
     pad = jnp.zeros((128 - DH, 128), f32)
-    for at, kv_ref in enumerate((kv_a, kv_b, kv_c, kv_d)):
+    norms = jnp.zeros((1, 128), f32)
+    for at, kv_ref in enumerate(kv_refs):
         for b in range(4):
             kv = kv_ref[b].astype(f32)
             keys = slice((4 * at + b) * 128, (4 * at + b + 1) * 128)
             k_t = jnp.concatenate([kv[0:DH], pad])
-            kt_s[:, keys] = k_t.astype(bf16)
+            norms = jnp.maximum(norms, jnp.sum(k_t * k_t, axis=0, keepdims=True))
             k_s[keys] = k_t.T.astype(bf16)
-            v = jnp.concatenate([kv[DH:], pad]).T
-            v_s[keys] = jnp.where((lane >= DH) & (lane < DH + 3), 1.0, v).astype(bf16)
+            if kt_s is not None:
+                kt_s[:, keys] = k_t.astype(bf16)
+                v = jnp.concatenate([kv[DH:], pad]).T
+                v_s[keys] = jnp.where((lane >= DH) & (lane < DH + 3), 1.0, v).astype(bf16)
+    return jnp.max(norms)
+
+
+def tile_of(qg_ref, t, row):
+    return jnp.concatenate([qg_ref[PER * t + n, row : row + FPAD] for n in range(PER)], axis=1)
+
+
+def log_sums(q_t, k_s, norm):
+    exact = q_t.astype(f32)
+    bound = jnp.sqrt(jnp.sum(exact * exact, axis=0, keepdims=True) * norm) * (SCALE2 * 1.001)
+
+    def scores(rows):
+        return jnp.dot(k_s[rows, 0:FPAD], q_t, preferred_element_type=f32) * SCALE2
+
+    total = jnp.zeros((1, TILE), f32)
+    for at in range(0, HALF, STEP):
+        exps = jnp.exp2(scores(slice(at, at + STEP)) - bound)
+        total = total + jnp.sum(exps, axis=0, keepdims=True)
+
+    def again():
+        def rows(n):
+            return pl.ds(pl.multiple_of(n * 128, 128), 128)
+
+        def largest(n, top):
+            return jnp.maximum(top, jnp.max(scores(rows(n)), axis=0, keepdims=True))
+
+        top = lax.fori_loop(0, HALF // 128, largest, jnp.full((1, TILE), -jnp.inf, f32))
+
+        def add(n, total):
+            return total + jnp.sum(jnp.exp2(scores(rows(n)) - top), axis=0, keepdims=True)
+
+        return top + jnp.log2(lax.fori_loop(0, HALF // 128, add, jnp.zeros((1, TILE), f32)))
+
+    return lax.cond(jnp.min(total) < 2.0**-90, again, lambda: bound + jnp.log2(total))
+
+
+def put_sums(out_ref, t, sums):
+    for n in range(PER):
+        out_ref[PER * t + n] = jnp.broadcast_to(sums[:, n * TOK : (n + 1) * TOK], (8, TOK))
+
+
+def get_sums(sums_ref, t):
+    return jnp.concatenate([sums_ref[PER * t + n, 0:1] for n in range(PER)], axis=1)
+
+
+def sums_kernel(qg_ref, kv_own, kv_other, out_ref, k_s):
+    norm = load_keys((kv_own, kv_other), k_s)
+
+    def tile(t, _):
+        put_sums(out_ref, t, log_sums(tile_of(qg_ref, t, 0), k_s, norm))
+        return 0
+
+    lax.fori_loop(0, KEYS // TILE, tile, 0)
+
+
+def gradients(qg_ref, sums_ref, k_s, kt_s, v_s, dk_s, dv_s, put_dq):
     dk_s[...] = jnp.zeros_like(dk_s)
     dv_s[...] = jnp.zeros_like(dv_s)
-    step = 512
-    blocks = [slice(at, at + step) for at in range(0, KEYS, step)]
 
     def tile(t, _):
-        q_t = jnp.concatenate([qg_ref[2 * t, 0:FPAD], qg_ref[2 * t + 1, 0:FPAD]], axis=1)
-        g_t = jnp.concatenate(
-            [qg_ref[2 * t, FPAD : 2 * FPAD], qg_ref[2 * t + 1, FPAD : 2 * FPAD]], axis=1
-        )
-        top = jnp.full((1, 2 * TOK), -jnp.inf, f32)
-        for b in blocks:
+        q_t = tile_of(qg_ref, t, 0)
+        g_t = tile_of(qg_ref, t, FPAD)
+        sums = get_sums(sums_ref, t)
+        dq = jnp.zeros((FPAD, TILE), f32)
+        for at in range(0, HALF, STEP):
+            b = slice(at, at + STEP)
             scores = jnp.dot(k_s[b, 0:FPAD], q_t, preferred_element_type=f32)
-            e_s[b] = scores
-            top = jnp.maximum(top, jnp.max(scores, axis=0, keepdims=True))
-        top = top * SCALE2
-        total = jnp.zeros((1, 2 * TOK), f32)
-        for b in blocks:
-            exps = jnp.exp2(e_s[b] * SCALE2 - top)
-            e_s[b] = exps
-            total = total + jnp.sum(exps, axis=0, keepdims=True)
-        inverse = 1.0 / total
-        dq = jnp.zeros((FPAD, 2 * TOK), f32)
-        for b in blocks:
-            probs = e_s[b] * inverse
+            probs = jnp.exp2(scores * SCALE2 - sums)
             half_probs = probs.astype(bf16)
             shifted = jnp.dot(v_s[b, 0:FPAD], g_t, preferred_element_type=f32)
             ds = (probs * shifted).astype(bf16)
             dk_s[b, 0:FPAD] += lax.dot_general(ds, q_t, NT, preferred_element_type=f32)
             dv_s[b, 0:FPAD] += lax.dot_general(half_probs, g_t, NT, preferred_element_type=f32)
             dq = dq + jnp.dot(kt_s[0:FPAD, b], ds, preferred_element_type=f32)
-        dq = (dq * SCALE).astype(bf16)
-        dq_ref[2 * t] = dq[:, 0:TOK]
-        dq_ref[2 * t + 1] = dq[:, TOK:]
+        for n in range(PER):
+            put_dq(PER * t + n, dq[:, n * TOK : (n + 1) * TOK])
         return 0
 
-    lax.fori_loop(0, HEADS // 2, tile, 0)
+    lax.fori_loop(0, KEYS // TILE, tile, 0)
+
+
+def put_keys(own_ref, other_ref, dk_s, dv_s):
     dk_t = dk_s[...].T
     dv_t = dv_s[...].T
-    for out, at in ((own_ref, 0), (other_ref, half)):
-        for b in range(8):
-            keys = slice(at + b * 128, at + (b + 1) * 128)
-            out[b, 0:DH] = dk_t[0:DH, keys] * SCALE
-            out[b, DH : 2 * DH] = dv_t[0:DH, keys]
+    for at, out in enumerate((own_ref, other_ref)):
+        for b in range(4):
+            keys = slice((4 * at + b) * 128, (4 * at + b + 1) * 128)
+            block = jnp.concatenate([dk_t[0:DH, keys] * SCALE, dv_t[0:DH, keys]])
+            out[b] = block.astype(out.dtype)
+
+
+def first_kernel(
+    qg_ref, kv_own, kv_other, sums_in, sums_ref, dq_ref, own_ref, other_ref, k_s, kt_s, v_s, dk_s, dv_s
+):
+    norm = load_keys((kv_own, kv_other), k_s, kt_s, v_s)
+
+    def tile(t, _):
+        mine = log_sums(tile_of(qg_ref, t, 0), k_s, norm)
+        other = get_sums(sums_in, t)
+        top = jnp.maximum(mine, other)
+        put_sums(sums_ref, t, top + jnp.log2(jnp.exp2(mine - top) + jnp.exp2(other - top)))
+        return 0
+
+    lax.fori_loop(0, KEYS // TILE, tile, 0)
+
+    def put_dq(n, dq):
+        dq_ref[n] = dq
+
+    gradients(qg_ref, sums_ref, k_s, kt_s, v_s, dk_s, dv_s, put_dq)
+    put_keys(own_ref, other_ref, dk_s, dv_s)
+
+
+def second_kernel(
+    qg_ref, kv_own, kv_other, sums_ref, dq_in, dq_ref, own_ref, other_ref, k_s, kt_s, v_s, dk_s, dv_s
+):
+    load_keys((kv_own, kv_other), k_s, kt_s, v_s)
+
+    def put_dq(n, dq):
+        dq_ref[n] = ((dq_in[n] + dq) * SCALE).astype(bf16)
+
+    gradients(qg_ref, sums_ref, k_s, kt_s, v_s, dk_s, dv_s, put_dq)
+    put_keys(own_ref, other_ref, dk_s, dv_s)
 
 
 def pack_back_kernel(dq_ref, mine_ref, came_a, came_b, came_c, send_ref):
@@ -242,7 +324,7 @@
     chip_out[...] = jnp.where(first, canvas[0:4], canvas[68:72])
 
 
-def rows_kernel(canvas_ref, core_ref, chip_ref, center_ref, near_out, far_out):
+def rows_kernel(canvas_ref, chip_ref, core_ref, center_ref, near_out, far_out):
     first = lax.axis_index("c") == 0
     above = jnp.where(first, chip_ref[...], core_ref[...])
     below = jnp.where(first, core_ref[...], chip_ref[...])
@@ -256,7 +338,7 @@
     far_out[...] = jnp.where(begins, left, right)
 
 
-def cols_kernel(center_ref, near_ref, far_ref, out_ref):
+def cols_kernel(center_ref, far_ref, near_ref, out_ref):
     begins = lax.axis_index("yl") == 0
     left = jnp.where(begins, far_ref[...], near_ref[...])
     right = jnp.where(begins, near_ref[...], far_ref[...])
@@ -273,6 +355,11 @@
     peers = lax.axis_size(axis)
     pairs = [(i, i + 1) for i in range(1, peers - 1, 2)]
     return lax.ppermute(x, axis, pairs + [(target, source) for source, target in pairs])
+
+
+def cost(products):
+    flops = products * 2 * KEYS * HALF * 256
+    return pl.CostEstimate(flops=flops, bytes_accessed=2**20, transcendentals=KEYS * HALF)
 
 
 def combined_weights(w_qkv, w_patch, part):
@@ -283,7 +370,7 @@
         12,
         [pltpu.VMEM((D, D), bf16), pltpu.SemaphoreType.DMA((D // 128,))],
         [WHOLE, ANYWHERE],
-        cost_estimate=pl.CostEstimate(flops=2 * 256 * D * D, bytes_accessed=4 * D * D, transcendentals=0),
+        cost_estimate=pl.CostEstimate(flops=2**20, bytes_accessed=2**16, transcendentals=0),
     )(w_patch, w_qkv)
 
 
@@ -315,32 +402,38 @@
         [ANYWHERE],
     )(got)
     came = [swapped(kv, "z", by) for by in (2, 4, 6)]
-    weights = list(combined_weights(w_qkv, w_patch, 0))
-    came, weights = lax.optimization_barrier((came, weights))
     kv_a = jnp.stack([kv] + came)
     kv_b = swapped(kv_a, "z", 1)
     kv_c = swapped(kv_a, "c", 1)
-    for part in (1, 2):
-        weights += combined_weights(w_qkv, w_patch, part)
-    kv_b, kv_c, weights = lax.optimization_barrier((kv_b, kv_c, weights))
+    keys = pltpu.VMEM((HALF, 128), bf16)
+    sums = jax.ShapeDtypeStruct((HEADS, 8, TOK), f32)
+    even_sums = call(sums_kernel, sums, 24, [keys], cost_estimate=cost(1))(got, kv_a, kv_c)
+    kv_b, even_sums = lax.optimization_barrier((kv_b, even_sums))
     kv_d = swapped(kv_b, "c", 1)
-    grads = jax.ShapeDtypeStruct((8, 2 * DH, 128), f32)
+    scratch = [keys, pltpu.VMEM((128, HALF), bf16), keys]
+    scratch += [pltpu.VMEM((HALF, 128), f32)] * 2
+    block = (4, 2 * DH, 128)
+    sums, dq, own, other = call(
+        first_kernel,
+        [sums, jax.ShapeDtypeStruct((HEADS, FPAD, TOK), f32)] + [jax.ShapeDtypeStruct(block, bf16)] * 2,
+        28,
+        scratch,
+        cost_estimate=cost(6),
+    )(got, kv_b, kv_d, even_sums)
+    came = [swapped(own, "z", 1), swapped(other, ("c", "z"), 9)]
     dq, own, other = call(
-        attention_kernel,
-        [jax.ShapeDtypeStruct((HEADS, FPAD, TOK), bf16), grads, grads],
-        32,
-        [
-            pltpu.VMEM((KEYS, 128), bf16),
-            pltpu.VMEM((KEYS, 128), bf16),
-            pltpu.VMEM((128, KEYS), bf16),
-            pltpu.VMEM((KEYS, 2 * TOK), f32),
-            pltpu.VMEM((KEYS, 128), f32),
-            pltpu.VMEM((KEYS, 128), f32),
-        ],
-    )(got, kv_a, kv_b, kv_c, kv_d)
-    mine = own + swapped(other, "c", 1)
-    mine = mine[:4] + swapped(mine[4:].astype(bf16), "z", 1).astype(f32)
+        second_kernel,
+        [jax.ShapeDtypeStruct((HEADS, FPAD, TOK), bf16)] + [jax.ShapeDtypeStruct(block, f32)] * 2,
+        28,
+        scratch,
+        cost_estimate=cost(5),
+    )(got, kv_a, kv_c, sums, dq)
+    own, other, came = lax.optimization_barrier((own, other, came))
+    mine = own + swapped(other, "c", 1) + came[0].astype(f32) + came[1].astype(f32)
+    mine, w_qkv, w_patch = lax.optimization_barrier((mine, w_qkv, w_patch))
     came = [swapped(mine[n].astype(bf16), "z", 2 * n) for n in (1, 2, 3)]
+    weights = [w for part in range(3) for w in combined_weights(w_qkv, w_patch, part)]
+    came, weights = lax.optimization_barrier((came, weights))
     send = call(pack_back_kernel, jax.ShapeDtypeStruct((HEADS, FPAD + 16, TOK), bf16), 8)(
         dq, mine[0:1], *came
     )
@@ -355,9 +448,9 @@
     strip = jax.ShapeDtypeStruct((4, 64), f32)
     center, to_near, to_far = call(
         rows_kernel, [jax.ShapeDtypeStruct((64, 128), f32), strip, strip], 4
-    )(canvas, swapped(to_core, "c", 1), neighbours(to_chip, BLK))
+    )(canvas, neighbours(to_chip, BLK), swapped(to_core, "c", 1))
     return call(cols_kernel, jax.ShapeDtypeStruct((64, 128), f32), 4)(
-        center, swapped(to_near, "yl", 1), neighbours(to_far, COL)
+        center, neighbours(to_far, COL), swapped(to_near, "yl", 1)
     )
 
 

time: 113 us -> 116 us (1.027)
  the two profiles are of different devices: /device:TPU:24 before, /device:TPU:48 now
where the time goes in v4:
time: 116 us
  Pallas kernels  39.9 us (34%)
  blocking collectives  31.4 us (27%)
  starting transfers between devices  25.5 us (22%)
  waiting for transfers between devices  18.8 us (16%)
    ppermute x14, starting transfers between devices, swapped(): return lax.ppermute(x, axis, [(i, i ^ by) for i in range(peers)])  18.8 us
    all_to_all x1, blocking collectives, on_device(): got = lax.all_to_all(send, HEAD_AXES, 0, 0, tiled=True)  18.8 us
    pallas_call x1, Pallas kernels, on_device(): call(first_kernel, [sums, jax.ShapeDtypeStruct((HEADS, FPAD, TOK), f32)]...  15 us
    all_to_all x1, blocking collectives, on_device(): back = lax.all_to_all(send, HEAD_AXES, 0, 0, tiled=True)  12.6 us
    ppermute x14, waiting for transfers between devices, swapped(): return lax.ppermute(x, axis, [(i, i ^ by) for i in range(peers)])  11.2 us
    pallas_call x1, Pallas kernels, on_device(): call(sums_kernel, sums, 24, [keys], cost_estimate=cost(1))(got, kv_a, kv_c)  9.29 us
    ppermute x2, waiting for transfers between devices, neighbours(): lax.ppermute(x, axis, pairs + [(target, source) for source, target in pai...  7.58 us
    ppermute x2, starting transfers between devices, neighbours(): lax.ppermute(x, axis, pairs + [(target, source) for source, target in pai...  6.66 us
  transfers between devices with their start and end apart: 16, of which 9 were waited for; matrix products, arithmetic and copies ran while one was open for 0% of the time, Pallas kernels for 16%

profile of v4, /device:TPU:48, one launch (start us, length us, event | category | flops | bytes accessed | tf_op | source)
XLA Modules:
  0.0 115.9 jit_solution(2752509946078786940)
XLA Ops:
  0.0 2.6 %shard_map.73 = bf16[16,176,128]{2,1,0:T(8,128)(2,1)} custom-call(bf16[128,1152]{1,0:T(8,128)(2,1)} %bitcast.16, bf16[128,1152]{1,0:T(8,128)(2,1)} %bitcast.17, bf16[128,1152]{1,0:T(8,128)(2,1)} %bitcast.18, bf16[2,4,1152]{2,1,0:T(4,128)(2,1)} %k_in.1, bf16[2,4,1152]{2,1,0:T(4,128)(2,1)} %v_in.1), custom_call_target="tpu_custom_call" | custom-call | tf_op jit(solution)/shard_map/pallas_call | solution.py:382
  2.6 18.8 %all_to_all.10.got_ref.qg_ref = bf16[16,176,128]{2,1,0:T(8,128)(2,1)S(1)} all-to-all(bf16[16,176,128]{2,1,0:T(8,128)(2,1)} %shard_map.73), channel_id=1, replica_groups=mesh['yh'=2,'x'=4,'c'=2,'z'=8,'yl'=2] {'yh','x','yl'}, dimensions={0} | all-to-all | bytes 1441792 | tf_op jit(solution)/shard_map/all_to_all | solution.py:396
  21.4 0.1 shard_map.74
  21.5 5.5 %collective-permute-start.2 = (bf16[144,128]{1,0:T(8,128)(2,1)S(1)}, bf16[144,128]{1,0:T(8,128)(2,1)S(1)}, u32[]{:S(2)}, u32[]{:S(2)}) collective-permute-start(bf16[144,128]{1,0:T(8,128)(2,1)S(1)} %shard_map.74), channel_id=1, source_target_pairs={{0,12},{2,14},{4,8},{6,10},{8,4},{10,6},{12,0},{14,2},{1,13},{3,15... | collective-permute-start | bytes 110600 | tf_op jit(solution)/shard_map/ppermute | solution.py:351
  27.0 1.4 %collective-permute-start.1 = (bf16[144,128]{1,0:T(8,128)(2,1)S(1)}, bf16[144,128]{1,0:T(8,128)(2,1)S(1)}, u32[]{:S(2)}, u32[]{:S(2)}) collective-permute-start(bf16[144,128]{1,0:T(8,128)(2,1)S(1)} %shard_map.74), channel_id=1, source_target_pairs={{0,8},{2,10},{4,12},{6,14},{8,0},{10,2},{12,4},{14,6},{1,9},{3,11}... | collective-permute-start | bytes 110600 | tf_op jit(solution)/shard_map/ppermute | solution.py:351
  28.4 1.0 collective-permute-start
  29.5 0.0 collective-permute-done.2
  29.5 5.4 %collective-permute-done.1 = bf16[144,128]{1,0:T(8,128)(2,1)S(1)} collective-permute-done((bf16[144,128]{1,0:T(8,128)(2,1)S(1)}, bf16[144,128]{1,0:T(8,128)(2,1)S(1)}, u32[]{:S(2)}, u32[]{:S(2)}) %collective-permute-start.1) | collective-permute-done | bytes 36896 | tf_op jit(solution)/shard_map/ppermute | solution.py:351
  34.9 0.0 collective-permute-done
  34.9 0.1 collective-permute-start.3
  35.0 1.1 collective-permute-start.4
  36.1 0.3 collective-permute-done.3.kv_other
  36.4 9.3 %shard_map.75.sums_in = f32[16,8,128]{2,1,0:T(8,128)S(1)} custom-call(bf16[16,176,128]{2,1,0:T(8,128)(2,1)S(1)} %all_to_all.10.got_ref.qg_ref, bf16[4,144,128]{2,1,0:T(8,128)(2,1)S(1)} %pad_maximum_fusion.kv_own, bf16[4,144,128]{2,1,0:T(8,128)(2,1)S(1)} %collective-permute-done.3.kv_other), custom_call_target="tpu_custom_call" | custom-call | flops 1073741824 | bytes 1048576 | tf_op jit(solution)/shard_map/pallas_call | solution.py:410
  45.7 0.0 slice-start.1
  45.7 0.0 collective-permute-done.4.kv_own
  45.7 0.2 collective-permute-start.5
  45.9 1.2 %collective-permute-done.5.kv_other = bf16[4,144,128]{2,1,0:T(8,128)(2,1)S(1)} collective-permute-done((bf16[4,144,128]{2,1,0:T(8,128)(2,1)S(1)}, bf16[4,144,128]{2,1,0:T(8,128)(2,1)S(1)}, u32[]{:S(2)}, u32[]{:S(2)}) %collective-permute-start.5) | collective-permute-done | bytes 147488 | tf_op jit(solution)/shard_map/ppermute | solution.py:351
  47.1 15.0 %shard_map.76 = (f32[16,8,128]{2,1,0:T(8,128)S(1)}, f32[16,80,128]{2,1,0:T(8,128)S(1)}, bf16[4,144,128]{2,1,0:T(8,128)(2,1)S(1)}, bf16[4,144,128]{2,1,0:T(8,128)(2,1)S(1)}) custom-call(bf16[16,176,128]{2,1,0:T(8,128)(2,1)S(1)} %all_to_all.10.got_ref.qg_ref, bf16[4,144,128]{2,1,0:T(8,128)(2,1)S(1)} %collective-permute-done.4.kv_own, ...), custom_call_target="tpu_custom_call" | custom-call | flops 6442450944 | bytes 1048576 | tf_op jit(solution)/shard_map/pallas_call | solution.py:416
  62.1 1.1 collective-permute-start.6
  63.2 0.5 collective-permute-start.7
  63.7 5.8 %shard_map.77 = (bf16[16,80,128]{2,1,0:T(8,128)(2,1)S(1)}, f32[4,144,128]{2,1,0:T(8,128)S(1)}, f32[4,144,128]{2,1,0:T(8,128)S(1)}) custom-call(bf16[16,176,128]{2,1,0:T(8,128)(2,1)S(1)} %all_to_all.10.got_ref.qg_ref, bf16[4,144,128]{2,1,0:T(8,128)(2,1)S(1)} %pad_maximum_fusion.kv_own, bf16[4,144,128]{2,1,0:T(8,128)(2,1)S(1)} %collective-permute-done.3.kv_other, ...), custom_call_target="tpu_custom_call" | custom-call | flops 5368709120 | bytes 1048576 | tf_op jit(solution)/shard_map/pallas_call | solution.py:424
  69.5 0.0 collective-permute-done.6
  69.5 0.9 collective-permute-done.7
  70.5 0.6 collective-permute-start.8
  71.1 1.2 %collective-permute-done.8 = f32[4,144,128]{2,1,0:T(8,128)S(1)} collective-permute-done((f32[4,144,128]{2,1,0:T(8,128)S(1)}, f32[4,144,128]{2,1,0:T(8,128)S(1)}, u32[]{:S(2)}, u32[]{:S(2)}) %collective-permute-start.8) | collective-permute-done | bytes 294944 | tf_op jit(solution)/shard_map/ppermute | solution.py:351
  72.3 0.1 convert_add_fusion
  72.4 2.1 %collective-permute-start.11 = (bf16[144,128]{1,0:T(8,128)(2,1)S(1)}, bf16[144,128]{1,0:T(8,128)(2,1)S(1)}, u32[]{:S(2)}, u32[]{:S(2)}) collective-permute-start(bf16[144,128]{1,0:T(8,128)(2,1)S(1)} %get-tuple-element.79), channel_id=1, source_target_pairs={{0,12},{2,14},{4,8},{6,10},{8,4},{10,6},{12,0},{14,2},{1,13},{3,15... | collective-permute-start | bytes 110600 | tf_op jit(solution)/shard_map/ppermute | solution.py:351
  74.5 3.4 %collective-permute-start.10 = (bf16[144,128]{1,0:T(8,128)(2,1)S(1)}, bf16[144,128]{1,0:T(8,128)(2,1)S(1)}, u32[]{:S(2)}, u32[]{:S(2)}) collective-permute-start(bf16[144,128]{1,0:T(8,128)(2,1)S(1)} %get-tuple-element.80), channel_id=1, source_target_pairs={{0,8},{2,10},{4,12},{6,14},{8,0},{10,2},{12,4},{14,6},{1,9},{3,11}... | collective-permute-start | bytes 110600 | tf_op jit(solution)/shard_map/ppermute | solution.py:351
  77.9 1.1 collective-permute-start.9
  79.1 1.3 %shard_map.80 = (bf16[256,1152]{1,0:T(8,128)(2,1)S(1)}, bf16[256,1152]{1,0:T(8,128)(2,1)S(1)}) custom-call(bf16[256,1152]{1,0:T(8,128)(2,1)S(1)} %copy-done, bf16[1152,3456]{1,0:T(8,128)(2,1)S(1)} %bitcast.14), custom_call_target="tpu_custom_call" | custom-call | flops 1048576 | bytes 65536 | tf_op jit(solution)/shard_map/pallas_call | solution.py:367
  80.4 1.3 %shard_map.79 = (bf16[256,1152]{1,0:T(8,128)(2,1)S(1)}, bf16[256,1152]{1,0:T(8,128)(2,1)S(1)}) custom-call(bf16[256,1152]{1,0:T(8,128)(2,1)S(1)} %copy-done, bf16[1152,3456]{1,0:T(8,128)(2,1)S(1)} %bitcast.14), custom_call_target="tpu_custom_call" | custom-call | flops 1048576 | bytes 65536 | tf_op jit(solution)/shard_map/pallas_call | solution.py:367
  81.7 1.3 %shard_map.78 = (bf16[256,1152]{1,0:T(8,128)(2,1)S(1)}, bf16[256,1152]{1,0:T(8,128)(2,1)S(1)}) custom-call(bf16[256,1152]{1,0:T(8,128)(2,1)S(1)} %copy-done, bf16[1152,3456]{1,0:T(8,128)(2,1)S(1)} %bitcast.14), custom_call_target="tpu_custom_call" | custom-call | flops 1048576 | bytes 65536 | tf_op jit(solution)/shard_map/pallas_call | solution.py:367
  83.0 0.0 collective-permute-done.11.came_c
  83.0 0.3 collective-permute-done.10.came_b
  83.3 0.0 collective-permute-done.9.came_a
  83.3 0.1 shard_map.81
  83.5 12.6 %all_to_all.11.back_ref = bf16[16,96,128]{2,1,0:T(8,128)(2,1)S(1)} all-to-all(bf16[16,96,128]{2,1,0:T(8,128)(2,1)S(1)} %shard_map.81), channel_id=1, replica_groups=mesh['yh'=2,'x'=4,'c'=2,'z'=8,'yl'=2] {'yh','x','yl'}, dimensions={0} | all-to-all | bytes 786432 | tf_op jit(solution)/shard_map/all_to_all | solution.py:440
  96.1 2.3 %shard_map.82 = (f32[72,256]{1,0:T(8,128)S(1)}, f32[4,256]{1,0:T(4,128)S(1)}, f32[4,256]{1,0:T(4,128)S(1)}) custom-call(bf16[16,96,128]{2,1,0:T(8,128)(2,1)S(1)} %all_to_all.11.back_ref, bf16[256,1152]{1,0:T(8,128)(2,1)S(1)} %get-tuple-element.67.refs_0_, bf16[256,1152]{1,0:T(8,128)(2,1)S(1)} %get-tuple-element.68.refs_1_, ...), custom_call_target="tpu_custom_call" | custom-call | tf_op jit(solution)/shard_map/pallas_call | solution.py:442
  98.4 2.1 %collective-permute-start.12 = (f32[4,256]{1,0:T(4,128)S(1)}, f32[4,256]{1,0:T(4,128)S(1)}, u32[]{:S(2)}, u32[]{:S(2)}) collective-permute-start(f32[4,256]{1,0:T(4,128)S(1)} %get-tuple-element.74), channel_id=1, source_target_pairs={{16,32},{48,64},{80,96},{112,128},{144,160},{176,192},{208,224},{3... | collective-permute-start | bytes 12296 | tf_op jit(solution)/shard_map/ppermute | solution.py:357
  100.5 0.6 collective-permute-start.13
  101.1 5.9 %collective-permute-done.12.chip_ref = f32[4,256]{1,0:T(4,128)S(1)} collective-permute-done((f32[4,256]{1,0:T(4,128)S(1)}, f32[4,256]{1,0:T(4,128)S(1)}, u32[]{:S(2)}, u32[]{:S(2)}) %collective-permute-start.12) | collective-permute-done | bytes 4128 | tf_op jit(solution)/shard_map/ppermute | solution.py:357
  106.9 0.0 collective-permute-done.13.core_ref
  106.9 0.1 shard_map.83
  107.0 4.5 %collective-permute-start.14 = (f32[4,64]{1,0:T(4,128)S(1)}, f32[4,64]{1,0:T(4,128)S(1)}, u32[]{:S(2)}, u32[]{:S(2)}) collective-permute-start(f32[4,64]{1,0:T(4,128)S(1)} %get-tuple-element.77), channel_id=1, source_target_pairs={{1,2},{3,4},{5,6},{7,8},{9,10},{11,12},{13,14},{2,1},{4,3},{6,5},{... | collective-permute-start | bytes 3080 | tf_op jit(solution)/shard_map/ppermute | solution.py:357
  111.6 0.1 collective-permute-start.15
  111.7 1.7 %collective-permute-done.14.far_ref = f32[4,64]{1,0:T(4,128)S(1)} collective-permute-done((f32[4,64]{1,0:T(4,128)S(1)}, f32[4,64]{1,0:T(4,128)S(1)}, u32[]{:S(2)}, u32[]{:S(2)}) %collective-permute-start.14) | collective-permute-done | bytes 1056 | tf_op jit(solution)/shard_map/ppermute | solution.py:357
  113.4 1.9 %collective-permute-done.15.near_ref = f32[4,64]{1,0:T(4,128)S(1)} collective-permute-done((f32[4,64]{1,0:T(4,128)S(1)}, f32[4,64]{1,0:T(4,128)S(1)}, u32[]{:S(2)}, u32[]{:S(2)}) %collective-permute-start.15) | collective-permute-done | bytes 1056 | tf_op jit(solution)/shard_map/ppermute | solution.py:351
  115.2 0.7 shard_map.84
  (10 shorter events, 0.1 us)
Async XLA Ops:
  21.5 8.0 %collective-permute-start.2 = (bf16[144,128]{1,0:T(8,128)(2,1)S(1)}, bf16[144,128]{1,0:T(8,128)(2,1)S(1)}, u32[]{:S(2)}, u32[]{:S(2)}) collective-permute-start(bf16[144,128]{1,0:T(8,128)(2,1)S(1)} %shard_map.74), channel_id=1, source_target_pairs={{0,12},{2,14},{4,8},{6,10},{8,4},{10,6},{12,0},{14,2},{1,13},{3,15... | collective-permute-start | bytes 110600 | tf_op jit(solution)/shard_map/ppermute | solution.py:351
  27.0 7.9 %collective-permute-start.1 = (bf16[144,128]{1,0:T(8,128)(2,1)S(1)}, bf16[144,128]{1,0:T(8,128)(2,1)S(1)}, u32[]{:S(2)}, u32[]{:S(2)}) collective-permute-start(bf16[144,128]{1,0:T(8,128)(2,1)S(1)} %shard_map.74), channel_id=1, source_target_pairs={{0,8},{2,10},{4,12},{6,14},{8,0},{10,2},{12,4},{14,6},{1,9},{3,11}... | collective-permute-start | bytes 110600 | tf_op jit(solution)/shard_map/ppermute | solution.py:351
  28.4 6.4 %collective-permute-start = (bf16[144,128]{1,0:T(8,128)(2,1)S(1)}, bf16[144,128]{1,0:T(8,128)(2,1)S(1)}, u32[]{:S(2)}, u32[]{:S(2)}) collective-permute-start(bf16[144,128]{1,0:T(8,128)(2,1)S(1)} %shard_map.74), channel_id=1, source_target_pairs={{0,4},{2,6},{4,0},{6,2},{8,12},{10,14},{12,8},{14,10},{1,5},{3,7},... | collective-permute-start | bytes 110600 | tf_op jit(solution)/shard_map/ppermute | solution.py:351
  34.9 1.5 %collective-permute-start.3 = (bf16[4,144,128]{2,1,0:T(8,128)(2,1)S(1)}, bf16[4,144,128]{2,1,0:T(8,128)(2,1)S(1)}, u32[]{:S(2)}, u32[]{:S(2)}) collective-permute-start(bf16[4,144,128]{2,1,0:T(8,128)(2,1)S(1)} %pad_maximum_fusion.kv_own), channel_id=1, source_target_pairs={{0,16},{16,0},{1,17},{17,1},{2,18},{18,2},{3,19},{19,3},{4,20},{20... | collective-permute-start | bytes 442376 | tf_op jit(solution)/shard_map/ppermute | solution.py:351
  35.0 10.7 %collective-permute-start.4 = (bf16[4,144,128]{2,1,0:T(8,128)(2,1)S(1)}, bf16[4,144,128]{2,1,0:T(8,128)(2,1)S(1)}, u32[]{:S(2)}, u32[]{:S(2)}) collective-permute-start(bf16[4,144,128]{2,1,0:T(8,128)(2,1)S(1)} %pad_maximum_fusion.kv_own), channel_id=1, source_target_pairs={{0,2},{2,0},{4,6},{6,4},{8,10},{10,8},{12,14},{14,12},{1,3},{3,1},... | collective-permute-start | bytes 442376 | tf_op jit(solution)/shard_map/ppermute | solution.py:351
  36.4 42.7 %slice-start = ((s8[7962624]{0:T(1024)(128)(4,1)}), s8[4194304]{0:T(1024)(128)(4,1)S(1)}, s32[]{:S(2)}) async-start(s8[7962624]{0:T(1024)(128)(4,1)} %bitcast.13), calls=%async_computation.2 | async-start | bytes 8388608
  45.7 33.4 %slice-start.1 = ((s8[7962624]{0:T(1024)(128)(4,1)}), s8[3768320]{0:T(1024)(128)(4,1)S(1)}, s32[]{:S(2)}) async-start(s8[7962624]{0:T(1024)(128)(4,1)} %bitcast.13), calls=%async_computation.3 | async-start | bytes 7536640
  45.7 1.5 %collective-permute-start.5 = (bf16[4,144,128]{2,1,0:T(8,128)(2,1)S(1)}, bf16[4,144,128]{2,1,0:T(8,128)(2,1)S(1)}, u32[]{:S(2)}, u32[]{:S(2)}) collective-permute-start(bf16[4,144,128]{2,1,0:T(8,128)(2,1)S(1)} %collective-permute-done.4.kv_own), channel_id=1, source_target_pairs={{0,16},{16,0},{1,17},{17,1},{2,18},{18,2},{3,19},{19,3},{4,20},{20... | collective-permute-start | bytes 442376 | tf_op jit(solution)/shard_map/ppermute | solution.py:351
  62.1 7.4 %collective-permute-start.6 = (bf16[4,144,128]{2,1,0:T(8,128)(2,1)S(1)}, bf16[4,144,128]{2,1,0:T(8,128)(2,1)S(1)}, u32[]{:S(2)}, u32[]{:S(2)}) collective-permute-start(bf16[4,144,128]{2,1,0:T(8,128)(2,1)S(1)} %get-tuple-element.49), channel_id=1, source_target_pairs={{0,2},{2,0},{4,6},{6,4},{8,10},{10,8},{12,14},{14,12},{1,3},{3,1},... | collective-permute-start | bytes 442376 | tf_op jit(solution)/shard_map/ppermute | solution.py:351
  63.2 7.3 %collective-permute-start.7 = (bf16[4,144,128]{2,1,0:T(8,128)(2,1)S(1)}, bf16[4,144,128]{2,1,0:T(8,128)(2,1)S(1)}, u32[]{:S(2)}, u32[]{:S(2)}) collective-permute-start(bf16[4,144,128]{2,1,0:T(8,128)(2,1)S(1)} %get-tuple-element.50), channel_id=1, source_target_pairs={{0,18},{2,16},{4,22},{6,20},{8,26},{10,24},{12,30},{14,28},{16,2},... | collective-permute-start | bytes 442376 | tf_op jit(solution)/shard_map/ppermute | solution.py:351
  63.7 15.3 %copy-start = (bf16[256,1152]{1,0:T(8,128)(2,1)S(1)}, bf16[256,1152]{1,0:T(8,128)(2,1)}, u32[]{:S(2)}) copy-start(bf16[256,1152]{1,0:T(8,128)(2,1)} %patch_ref.2) | copy-start | bytes 1769476
  70.5 1.8 %collective-permute-start.8 = (f32[4,144,128]{2,1,0:T(8,128)S(1)}, f32[4,144,128]{2,1,0:T(8,128)S(1)}, u32[]{:S(2)}, u32[]{:S(2)}) collective-permute-start(f32[4,144,128]{2,1,0:T(8,128)S(1)} %get-tuple-element.52), channel_id=1, source_target_pairs={{0,16},{16,0},{1,17},{17,1},{2,18},{18,2},{3,19},{19,3},{4,20},{20... | collective-permute-start | bytes 884744 | tf_op jit(solution)/shard_map/ppermute | solution.py:351
  72.4 10.6 %collective-permute-start.11 = (bf16[144,128]{1,0:T(8,128)(2,1)S(1)}, bf16[144,128]{1,0:T(8,128)(2,1)S(1)}, u32[]{:S(2)}, u32[]{:S(2)}) collective-permute-start(bf16[144,128]{1,0:T(8,128)(2,1)S(1)} %get-tuple-element.79), channel_id=1, source_target_pairs={{0,12},{2,14},{4,8},{6,10},{8,4},{10,6},{12,0},{14,2},{1,13},{3,15... | collective-permute-start | bytes 110600 | tf_op jit(solution)/shard_map/ppermute | solution.py:351
  74.5 8.8 %collective-permute-start.10 = (bf16[144,128]{1,0:T(8,128)(2,1)S(1)}, bf16[144,128]{1,0:T(8,128)(2,1)S(1)}, u32[]{:S(2)}, u32[]{:S(2)}) collective-permute-start(bf16[144,128]{1,0:T(8,128)(2,1)S(1)} %get-tuple-element.80), channel_id=1, source_target_pairs={{0,8},{2,10},{4,12},{6,14},{8,0},{10,2},{12,4},{14,6},{1,9},{3,11}... | collective-permute-start | bytes 110600 | tf_op jit(solution)/shard_map/ppermute | solution.py:351
  77.9 5.4 %collective-permute-start.9 = (bf16[144,128]{1,0:T(8,128)(2,1)S(1)}, bf16[144,128]{1,0:T(8,128)(2,1)S(1)}, u32[]{:S(2)}, u32[]{:S(2)}) collective-permute-start(bf16[144,128]{1,0:T(8,128)(2,1)S(1)} %get-tuple-element.81), channel_id=1, source_target_pairs={{0,4},{2,6},{4,0},{6,2},{8,12},{10,14},{12,8},{14,10},{1,5},{3,7},... | collective-permute-start | bytes 110600 | tf_op jit(solution)/shard_map/ppermute | solution.py:351
  98.4 8.5 %collective-permute-start.12 = (f32[4,256]{1,0:T(4,128)S(1)}, f32[4,256]{1,0:T(4,128)S(1)}, u32[]{:S(2)}, u32[]{:S(2)}) collective-permute-start(f32[4,256]{1,0:T(4,128)S(1)} %get-tuple-element.74), channel_id=1, source_target_pairs={{16,32},{48,64},{80,96},{112,128},{144,160},{176,192},{208,224},{3... | collective-permute-start | bytes 12296 | tf_op jit(solution)/shard_map/ppermute | solution.py:357
  100.5 6.4 %collective-permute-start.13 = (f32[4,256]{1,0:T(4,128)S(1)}, f32[4,256]{1,0:T(4,128)S(1)}, u32[]{:S(2)}, u32[]{:S(2)}) collective-permute-start(f32[4,256]{1,0:T(4,128)S(1)} %get-tuple-element.75), channel_id=1, source_target_pairs={{0,16},{16,0},{1,17},{17,1},{2,18},{18,2},{3,19},{19,3},{4,20},{20... | collective-permute-start | bytes 12296 | tf_op jit(solution)/shard_map/ppermute | solution.py:351
  107.0 6.4 %collective-permute-start.14 = (f32[4,64]{1,0:T(4,128)S(1)}, f32[4,64]{1,0:T(4,128)S(1)}, u32[]{:S(2)}, u32[]{:S(2)}) collective-permute-start(f32[4,64]{1,0:T(4,128)S(1)} %get-tuple-element.77), channel_id=1, source_target_pairs={{1,2},{3,4},{5,6},{7,8},{9,10},{11,12},{13,14},{2,1},{4,3},{6,5},{... | collective-permute-start | bytes 3080 | tf_op jit(solution)/shard_map/ppermute | solution.py:357
  111.6 3.7 %collective-permute-start.15 = (f32[4,64]{1,0:T(4,128)S(1)}, f32[4,64]{1,0:T(4,128)S(1)}, u32[]{:S(2)}, u32[]{:S(2)}) collective-permute-start(f32[4,64]{1,0:T(4,128)S(1)} %get-tuple-element.78), channel_id=1, source_target_pairs={{0,1},{1,0},{2,3},{3,2},{4,5},{5,4},{6,7},{7,6},{8,9},{9,8},{10,11... | collective-permute-start | bytes 3080 | tf_op jit(solution)/shard_map/ppermute | solution.py:351

commit v5 on v4

--- a/solution.py
+++ b/solution.py
@@ -18,9 +18,10 @@
 TOK = ROWS * COLS
 CELLS = TOK // POOL**2
 FPAD = 80
-KEYS = 2048
-HALF = KEYS // 2
+QUERIES = 2048
+HALF = 512
 TILE = 1024
+TILES = QUERIES // TILE
 PER = TILE // TOK
 STEP = 256
 HEAD_AXES = ("yh", "x", "yl")
@@ -44,27 +45,35 @@
     )
 
 
-def pack_kernel(q_in, g_in, o_in, k_in, v_in, out_ref, q_ref, g_ref, o_ref, k_ref, v_ref, send_ref, sems, out_sems):
-    copies = []
+def pack_kernel(
+    q_in, g_in, o_in, k_in, v_in, out_ref, q_ref, g_ref, o_ref, k_ref, v_ref, send_ref, sems, out_sems
+):
+    pairs = [(k_in, k_ref), (v_in, v_ref)]
     quarter = TOK // 4
-    for source, target in ((k_in, k_ref), (v_in, v_ref)):
-        copies.append((source, target))
     for source, target in ((q_in, q_ref), (g_in, g_ref), (o_in, o_ref)):
         for at in range(0, TOK, quarter):
-            copies.append((source.at[at : at + quarter], target.at[at : at + quarter]))
-    copies = [pltpu.make_async_copy(*pair, sems.at[n]) for n, pair in enumerate(copies)]
+            pairs.append((source.at[at : at + quarter], target.at[at : at + quarter]))
+    copies = [pltpu.make_async_copy(*pair, sems.at[n]) for n, pair in enumerate(pairs)]
     for copy in copies:
         copy.start()
-    for copy in copies:
+    for copy in copies[:6]:
         copy.wait()
-    outs = []
     q_t = q_ref[...].astype(f32).T
+    keys = jnp.concatenate([k_ref[0].astype(f32), k_ref[1].astype(f32)])
+    vals = jnp.concatenate([v_ref[0].astype(f32), v_ref[1].astype(f32)])
+    lanes = jnp.zeros((CELLS, 128 - DH), f32)
+    for h in range(HEADS):
+        part = slice(h * DH, (h + 1) * DH)
+        send_ref[h, 0:FPAD, :] = jnp.concatenate([q_t[part], jnp.zeros((8, TOK), f32)]).astype(bf16)
+        k_h = jnp.concatenate([keys[:, part], lanes], axis=1)
+        v_h = jnp.concatenate([vals[:, part], lanes], axis=1)
+        send_ref[h, 2 * FPAD : 2 * FPAD + 16, :] = jnp.concatenate([k_h, v_h]).astype(bf16)
+    for copy in copies[6:]:
+        copy.wait()
     g_t = g_ref[...].astype(f32).T
     prod = g_t * o_ref[...].astype(f32).T
-    keys = jnp.concatenate([k_ref[0].astype(f32), k_ref[1].astype(f32)])
-    vals = jnp.concatenate([v_ref[0].astype(f32), v_ref[1].astype(f32)])
     row = lax.broadcasted_iota(jnp.int32, (8, TOK), 0)
-    lanes = jnp.zeros((CELLS, 128 - DH), f32)
+    outs = []
     for h in range(HEADS):
         part = slice(h * DH, (h + 1) * DH)
         dot = -jnp.sum(prod[part], axis=0, keepdims=True)
@@ -72,11 +81,7 @@
         mid = (dot - high).astype(bf16).astype(f32)
         low = dot - high - mid
         dots = jnp.where(row == 0, high, jnp.where(row == 1, mid, jnp.where(row == 2, low, 0.0)))
-        send_ref[h, 0:FPAD, :] = jnp.concatenate([q_t[part], jnp.zeros((8, TOK), f32)]).astype(bf16)
         send_ref[h, FPAD : 2 * FPAD, :] = jnp.concatenate([g_t[part], dots]).astype(bf16)
-        k_h = jnp.concatenate([keys[:, part], lanes], axis=1)
-        v_h = jnp.concatenate([vals[:, part], lanes], axis=1)
-        send_ref[h, 2 * FPAD : 2 * FPAD + 16, :] = jnp.concatenate([k_h, v_h]).astype(bf16)
         if h % 4 == 3:
             heads = slice(h - 3, h + 1)
             copy = pltpu.make_async_copy(send_ref.at[heads], out_ref.at[heads], out_sems.at[h // 4])
@@ -96,21 +101,20 @@
     out_ref[...] = jnp.concatenate([k_t[0:DH], v_t[0:DH]]).astype(bf16)
 
 
-def load_keys(kv_refs, k_s, kt_s=None, v_s=None):
+def load_keys(kv_ref, k_s, kt_s=None, v_s=None):
     lane = lax.broadcasted_iota(jnp.int32, (128, 128), 1)
     pad = jnp.zeros((128 - DH, 128), f32)
     norms = jnp.zeros((1, 128), f32)
-    for at, kv_ref in enumerate(kv_refs):
-        for b in range(4):
-            kv = kv_ref[b].astype(f32)
-            keys = slice((4 * at + b) * 128, (4 * at + b + 1) * 128)
-            k_t = jnp.concatenate([kv[0:DH], pad])
-            norms = jnp.maximum(norms, jnp.sum(k_t * k_t, axis=0, keepdims=True))
-            k_s[keys] = k_t.T.astype(bf16)
-            if kt_s is not None:
-                kt_s[:, keys] = k_t.astype(bf16)
-                v = jnp.concatenate([kv[DH:], pad]).T
-                v_s[keys] = jnp.where((lane >= DH) & (lane < DH + 3), 1.0, v).astype(bf16)
+    for b in range(4):
+        kv = kv_ref[b].astype(f32)
+        keys = slice(b * 128, (b + 1) * 128)
+        k_t = jnp.concatenate([kv[0:DH], pad])
+        norms = jnp.maximum(norms, jnp.sum(k_t * k_t, axis=0, keepdims=True))
+        k_s[keys] = k_t.T.astype(bf16)
+        if kt_s is not None:
+            kt_s[:, keys] = k_t.astype(bf16)
+            v = jnp.concatenate([kv[DH:], pad]).T
+            v_s[keys] = jnp.where((lane >= DH) & (lane < DH + 3), 1.0, v).astype(bf16)
     return jnp.max(norms)
 
 
@@ -147,102 +151,121 @@
     return lax.cond(jnp.min(total) < 2.0**-90, again, lambda: bound + jnp.log2(total))
 
 
-def put_sums(out_ref, t, sums):
+def put_sums(out_ref, at, t, sums):
     for n in range(PER):
-        out_ref[PER * t + n] = jnp.broadcast_to(sums[:, n * TOK : (n + 1) * TOK], (8, TOK))
-
-
-def get_sums(sums_ref, t):
-    return jnp.concatenate([sums_ref[PER * t + n, 0:1] for n in range(PER)], axis=1)
-
-
-def sums_kernel(qg_ref, kv_own, kv_other, out_ref, k_s):
-    norm = load_keys((kv_own, kv_other), k_s)
-
-    def tile(t, _):
-        put_sums(out_ref, t, log_sums(tile_of(qg_ref, t, 0), k_s, norm))
-        return 0
-
-    lax.fori_loop(0, KEYS // TILE, tile, 0)
-
-
-def gradients(qg_ref, sums_ref, k_s, kt_s, v_s, dk_s, dv_s, put_dq):
+        out_ref[at, PER * t + n] = jnp.broadcast_to(sums[:, n * TOK : (n + 1) * TOK], (8, TOK))
+
+
+def get_sums(sums_ref, at, t):
+    return jnp.concatenate([sums_ref[at, PER * t + n, 0:1] for n in range(PER)], axis=1)
+
+
+def added(one, two):
+    top = jnp.maximum(one, two)
+    return top + jnp.log2(jnp.exp2(one - top) + jnp.exp2(two - top))
+
+
+def even_sums_kernel(qg_a, qg_b, kv_ref, out_ref, k_s):
+    norm = load_keys(kv_ref, k_s)
+    for at, qg_ref in enumerate((qg_a, qg_b)):
+
+        def tile(t, _):
+            put_sums(out_ref, at, t, log_sums(tile_of(qg_ref, t, 0), k_s, norm))
+            return 0
+
+        lax.fori_loop(0, TILES, tile, 0)
+
+
+def odd_sums_kernel(qg_a, qg_b, kv_ref, even_ref, out_ref, k_s):
+    norm = load_keys(kv_ref, k_s)
+    for at, qg_ref in enumerate((qg_a, qg_b)):
+
+        def tile(t, _):
+            mine = log_sums(tile_of(qg_ref, t, 0), k_s, norm)
+            put_sums(out_ref, at, t, added(mine, get_sums(even_ref, at, t)))
+            return 0
+
+        lax.fori_loop(0, TILES, tile, 0)
+
+
+def gradients(sums_ref, work, k_s, kt_s, v_s, dk_s, dv_s):
     dk_s[...] = jnp.zeros_like(dk_s)
     dv_s[...] = jnp.zeros_like(dv_s)
-
-    def tile(t, _):
-        q_t = tile_of(qg_ref, t, 0)
-        g_t = tile_of(qg_ref, t, FPAD)
-        sums = get_sums(sums_ref, t)
-        dq = jnp.zeros((FPAD, TILE), f32)
-        for at in range(0, HALF, STEP):
-            b = slice(at, at + STEP)
-            scores = jnp.dot(k_s[b, 0:FPAD], q_t, preferred_element_type=f32)
-            probs = jnp.exp2(scores * SCALE2 - sums)
-            half_probs = probs.astype(bf16)
-            shifted = jnp.dot(v_s[b, 0:FPAD], g_t, preferred_element_type=f32)
-            ds = (probs * shifted).astype(bf16)
-            dk_s[b, 0:FPAD] += lax.dot_general(ds, q_t, NT, preferred_element_type=f32)
-            dv_s[b, 0:FPAD] += lax.dot_general(half_probs, g_t, NT, preferred_element_type=f32)
-            dq = dq + jnp.dot(kt_s[0:FPAD, b], ds, preferred_element_type=f32)
-        for n in range(PER):
-            put_dq(PER * t + n, dq[:, n * TOK : (n + 1) * TOK])
-        return 0
-
-    lax.fori_loop(0, KEYS // TILE, tile, 0)
-
-
-def put_keys(own_ref, other_ref, dk_s, dv_s):
+    for at_core, (qg_ref, put_dq) in enumerate(work):
+
+        def tile(t, _):
+            q_t = tile_of(qg_ref, t, 0)
+            g_t = tile_of(qg_ref, t, FPAD)
+            sums = get_sums(sums_ref, at_core, t)
+            dq = jnp.zeros((FPAD, TILE), f32)
+            for at in range(0, HALF, STEP):
+                b = slice(at, at + STEP)
+                scores = jnp.dot(k_s[b, 0:FPAD], q_t, preferred_element_type=f32)
+                probs = jnp.exp2(scores * SCALE2 - sums)
+                half_probs = probs.astype(bf16)
+                shifted = jnp.dot(v_s[b, 0:FPAD], g_t, preferred_element_type=f32)
+                ds = (probs * shifted).astype(bf16)
+                dk_s[b, 0:FPAD] += lax.dot_general(ds, q_t, NT, preferred_element_type=f32)
+                dv_s[b, 0:FPAD] += lax.dot_general(half_probs, g_t, NT, preferred_element_type=f32)
+                dq = dq + jnp.dot(kt_s[0:FPAD, b], ds, preferred_element_type=f32)
+            for n in range(PER):
+                put_dq(PER * t + n, dq[:, n * TOK : (n + 1) * TOK])
+            return 0
+
+        lax.fori_loop(0, TILES, tile, 0)
+
+
+def put_keys(out_ref, dk_s, dv_s):
     dk_t = dk_s[...].T
     dv_t = dv_s[...].T
-    for at, out in enumerate((own_ref, other_ref)):
-        for b in range(4):
-            keys = slice((4 * at + b) * 128, (4 * at + b + 1) * 128)
-            block = jnp.concatenate([dk_t[0:DH, keys] * SCALE, dv_t[0:DH, keys]])
-            out[b] = block.astype(out.dtype)
+    for b in range(4):
+        keys = slice(b * 128, (b + 1) * 128)
+        block = jnp.concatenate([dk_t[0:DH, keys] * SCALE, dv_t[0:DH, keys]])
+        out_ref[b] = block.astype(out_ref.dtype)
 
 
 def first_kernel(
-    qg_ref, kv_own, kv_other, sums_in, sums_ref, dq_ref, own_ref, other_ref, k_s, kt_s, v_s, dk_s, dv_s
+    qg_a, qg_b, kv_ref, mine_ref, came_ref, sums_ref, dq_a, dq_b, out_ref,
+    k_s, kt_s, v_s, dk_s, dv_s,
 ):
-    norm = load_keys((kv_own, kv_other), k_s, kt_s, v_s)
-
-    def tile(t, _):
-        mine = log_sums(tile_of(qg_ref, t, 0), k_s, norm)
-        other = get_sums(sums_in, t)
-        top = jnp.maximum(mine, other)
-        put_sums(sums_ref, t, top + jnp.log2(jnp.exp2(mine - top) + jnp.exp2(other - top)))
-        return 0
-
-    lax.fori_loop(0, KEYS // TILE, tile, 0)
-
-    def put_dq(n, dq):
-        dq_ref[n] = dq
-
-    gradients(qg_ref, sums_ref, k_s, kt_s, v_s, dk_s, dv_s, put_dq)
-    put_keys(own_ref, other_ref, dk_s, dv_s)
+    load_keys(kv_ref, k_s, kt_s, v_s)
+    for at in (0, 1):
+        sums_ref[at] = added(mine_ref[at], came_ref[1 - at])
+
+    def put_a(n, dq):
+        dq_a[n] = dq
+
+    def put_b(n, dq):
+        dq_b[n] = dq
+
+    gradients(sums_ref, ((qg_a, put_a), (qg_b, put_b)), k_s, kt_s, v_s, dk_s, dv_s)
+    put_keys(out_ref, dk_s, dv_s)
 
 
 def second_kernel(
-    qg_ref, kv_own, kv_other, sums_ref, dq_in, dq_ref, own_ref, other_ref, k_s, kt_s, v_s, dk_s, dv_s
+    qg_a, qg_b, kv_ref, sums_ref, in_a, in_b, dq_a, dq_b, out_ref,
+    k_s, kt_s, v_s, dk_s, dv_s,
 ):
-    load_keys((kv_own, kv_other), k_s, kt_s, v_s)
-
-    def put_dq(n, dq):
-        dq_ref[n] = ((dq_in[n] + dq) * SCALE).astype(bf16)
-
-    gradients(qg_ref, sums_ref, k_s, kt_s, v_s, dk_s, dv_s, put_dq)
-    put_keys(own_ref, other_ref, dk_s, dv_s)
-
-
-def pack_back_kernel(dq_ref, mine_ref, came_a, came_b, came_c, send_ref):
+    load_keys(kv_ref, k_s, kt_s, v_s)
+
+    def put_a(n, dq):
+        dq_a[n] = in_a[n] + dq
+
+    def put_b(n, dq):
+        dq_b[n] = in_b[n] + dq
+
+    gradients(sums_ref, ((qg_a, put_a), (qg_b, put_b)), k_s, kt_s, v_s, dk_s, dv_s)
+    put_keys(out_ref, dk_s, dv_s)
+
+
+def pack_back_kernel(dq_ref, other_ref, mine_ref, came_a, came_b, came_c, send_ref):
     total = mine_ref[0]
     for came in (came_a, came_b, came_c):
         total = total + came[...].astype(f32)
     lanes = jnp.zeros((128, 128 - DH), f32)
     dk = jnp.concatenate([total[0:DH].T, lanes], axis=1)
     dv = jnp.concatenate([total[DH : 2 * DH].T, lanes], axis=1)
-    send_ref[:, 0:FPAD, :] = dq_ref[...]
+    send_ref[:, 0:FPAD, :] = ((dq_ref[...] + other_ref[...]) * SCALE).astype(bf16)
     for a in range(HEADS):
         cells = slice(a * CELLS, (a + 1) * CELLS)
         send_ref[a, FPAD : FPAD + 16, :] = jnp.concatenate([dk[cells], dv[cells]]).astype(bf16)
@@ -358,8 +381,8 @@
 
 
 def cost(products):
-    flops = products * 2 * KEYS * HALF * 256
-    return pl.CostEstimate(flops=flops, bytes_accessed=2**20, transcendentals=KEYS * HALF)
+    flops = products * 4 * QUERIES * HALF * 256
+    return pl.CostEstimate(flops=flops, bytes_accessed=2**20, transcendentals=2 * QUERIES * HALF)
 
 
 def combined_weights(w_qkv, w_patch, part):
@@ -402,40 +425,35 @@
         [ANYWHERE],
     )(got)
     came = [swapped(kv, "z", by) for by in (2, 4, 6)]
-    kv_a = jnp.stack([kv] + came)
-    kv_b = swapped(kv_a, "z", 1)
-    kv_c = swapped(kv_a, "c", 1)
+    even = jnp.stack([kv] + came)
+    odd = swapped(even, "z", 1)
+    there = swapped(got, "c", 1)
     keys = pltpu.VMEM((HALF, 128), bf16)
-    sums = jax.ShapeDtypeStruct((HEADS, 8, TOK), f32)
-    even_sums = call(sums_kernel, sums, 24, [keys], cost_estimate=cost(1))(got, kv_a, kv_c)
-    kv_b, even_sums = lax.optimization_barrier((kv_b, even_sums))
-    kv_d = swapped(kv_b, "c", 1)
+    sums = jax.ShapeDtypeStruct((2, HEADS, 8, TOK), f32)
+    even_sums = call(even_sums_kernel, sums, 24, [keys], cost_estimate=cost(1))(got, there, even)
+    odd, even_sums = lax.optimization_barrier((odd, even_sums))
+    mine = call(odd_sums_kernel, sums, 24, [keys], cost_estimate=cost(1))(got, there, odd, even_sums)
+    came = swapped(mine, "c", 1)
     scratch = [keys, pltpu.VMEM((128, HALF), bf16), keys]
     scratch += [pltpu.VMEM((HALF, 128), f32)] * 2
+    dq = [jax.ShapeDtypeStruct((HEADS, FPAD, TOK), f32)] * 2
     block = (4, 2 * DH, 128)
-    sums, dq, own, other = call(
-        first_kernel,
-        [sums, jax.ShapeDtypeStruct((HEADS, FPAD, TOK), f32)] + [jax.ShapeDtypeStruct(block, bf16)] * 2,
-        28,
-        scratch,
-        cost_estimate=cost(6),
-    )(got, kv_b, kv_d, even_sums)
-    came = [swapped(own, "z", 1), swapped(other, ("c", "z"), 9)]
-    dq, own, other = call(
-        second_kernel,
-        [jax.ShapeDtypeStruct((HEADS, FPAD, TOK), bf16)] + [jax.ShapeDtypeStruct(block, f32)] * 2,
-        28,
-        scratch,
-        cost_estimate=cost(5),
-    )(got, kv_a, kv_c, sums, dq)
-    own, other, came = lax.optimization_barrier((own, other, came))
-    mine = own + swapped(other, "c", 1) + came[0].astype(f32) + came[1].astype(f32)
+    sums, dq_here, dq_there, grads = call(
+        first_kernel, [sums] + dq + [jax.ShapeDtypeStruct(block, bf16)], 28, scratch, cost_estimate=cost(5)
+    )(got, there, odd, mine, came)
+    came = swapped(grads, "z", 1)
+    dq_here, dq_there, grads = call(
+        second_kernel, dq + [jax.ShapeDtypeStruct(block, f32)], 28, scratch, cost_estimate=cost(5)
+    )(got, there, even, sums, dq_here, dq_there)
+    dq_here, dq_there, grads, came = lax.optimization_barrier((dq_here, dq_there, grads, came))
+    dq_there = swapped(dq_there, "c", 1)
+    mine = grads + came.astype(f32)
     mine, w_qkv, w_patch = lax.optimization_barrier((mine, w_qkv, w_patch))
     came = [swapped(mine[n].astype(bf16), "z", 2 * n) for n in (1, 2, 3)]
     weights = [w for part in range(3) for w in combined_weights(w_qkv, w_patch, part)]
     came, weights = lax.optimization_barrier((came, weights))
     send = call(pack_back_kernel, jax.ShapeDtypeStruct((HEADS, FPAD + 16, TOK), bf16), 8)(
-        dq, mine[0:1], *came
+        dq_here, dq_there, mine[0:1], *came
     )
     back = lax.all_to_all(send, HEAD_AXES, 0, 0, tiled=True)
     strip = jax.ShapeDtypeStruct((4, 256), f32)

time: 116 us -> 115 us (level)
  the two profiles are of different devices: /device:TPU:48 before, /device:TPU:24 now
where the time goes in v5:
time: 115 us
  Pallas kernels  41.1 us (36%)
  blocking collectives  31.7 us (28%)
  starting transfers between devices  24.4 us (21%)
  waiting for transfers between devices  17 us (15%)
    all_to_all x1, blocking collectives, on_device(): got = lax.all_to_all(send, HEAD_AXES, 0, 0, tiled=True)  18.5 us
    ppermute x13, starting transfers between devices, swapped(): return lax.ppermute(x, axis, [(i, i ^ by) for i in range(peers)])  18.4 us
    all_to_all x1, blocking collectives, on_device(): back = lax.all_to_all(send, HEAD_AXES, 0, 0, tiled=True)  13.1 us
    pallas_call x1, Pallas kernels, on_device(): call(odd_sums_kernel, sums, 24, [keys], cost_estimate=cost(1))  9.89 us
    pallas_call x1, Pallas kernels, on_device(): call(even_sums_kernel, sums, 24, [keys], cost_estimate=cost(1))  9.72 us
    ppermute x2, waiting for transfers between devices, neighbours(): lax.ppermute(x, axis, pairs + [(target, source) for source, target in pai...  8.51 us
    ppermute x13, waiting for transfers between devices, swapped(): return lax.ppermute(x, axis, [(i, i ^ by) for i in range(peers)])  8.49 us
    ppermute x2, starting transfers between devices, neighbours(): lax.ppermute(x, axis, pairs + [(target, source) for source, target in pai...  5.99 us
  transfers between devices with their start and end apart: 15, of which 5 were waited for; matrix products, arithmetic and copies ran while one was open for 0% of the time, Pallas kernels for 17%

profile of v5, /device:TPU:24, one launch (start us, length us, event | category | flops | bytes accessed | tf_op | source)
XLA Modules:
  0.0 114.5 jit_solution(11038186574566878992)
XLA Ops:
  0.0 2.5 %shard_map.73 = bf16[16,176,128]{2,1,0:T(8,128)(2,1)} custom-call(bf16[128,1152]{1,0:T(8,128)(2,1)} %bitcast.16, bf16[128,1152]{1,0:T(8,128)(2,1)} %bitcast.17, bf16[128,1152]{1,0:T(8,128)(2,1)} %bitcast.18, bf16[2,4,1152]{2,1,0:T(4,128)(2,1)} %k_in.1, bf16[2,4,1152]{2,1,0:T(4,128)(2,1)} %v_in.1), custom_call_target="tpu_custom_call" | custom-call | tf_op jit(solution)/shard_map/pallas_call | solution.py:405
  2.5 18.5 %all_to_all.10.got_ref.qg_a = bf16[16,176,128]{2,1,0:T(8,128)(2,1)S(1)} all-to-all(bf16[16,176,128]{2,1,0:T(8,128)(2,1)} %shard_map.73), channel_id=1, replica_groups=mesh['yh'=2,'x'=4,'c'=2,'z'=8,'yl'=2] {'yh','x','yl'}, dimensions={0} | all-to-all | bytes 1441792 | tf_op jit(solution)/shard_map/all_to_all | solution.py:419
  21.0 0.0 collective-permute-start
  21.0 0.1 shard_map.74
  21.1 6.4 %collective-permute-start.3 = (bf16[144,128]{1,0:T(8,128)(2,1)S(1)}, bf16[144,128]{1,0:T(8,128)(2,1)S(1)}, u32[]{:S(2)}, u32[]{:S(2)}) collective-permute-start(bf16[144,128]{1,0:T(8,128)(2,1)S(1)} %shard_map.74), channel_id=1, source_target_pairs={{0,12},{2,14},{4,8},{6,10},{8,4},{10,6},{12,0},{14,2},{1,13},{3,15... | collective-permute-start | bytes 110600 | tf_op jit(solution)/shard_map/ppermute | solution.py:374
  27.5 1.0 collective-permute-start.2
  28.5 1.5 %collective-permute-start.1 = (bf16[144,128]{1,0:T(8,128)(2,1)S(1)}, bf16[144,128]{1,0:T(8,128)(2,1)S(1)}, u32[]{:S(2)}, u32[]{:S(2)}) collective-permute-start(bf16[144,128]{1,0:T(8,128)(2,1)S(1)} %shard_map.74), channel_id=1, source_target_pairs={{0,4},{2,6},{4,0},{6,2},{8,12},{10,14},{12,8},{14,10},{1,5},{3,7},... | collective-permute-start | bytes 110600 | tf_op jit(solution)/shard_map/ppermute | solution.py:374
  30.0 0.0 collective-permute-done.3
  30.0 5.9 %collective-permute-done.2 = bf16[144,128]{1,0:T(8,128)(2,1)S(1)} collective-permute-done((bf16[144,128]{1,0:T(8,128)(2,1)S(1)}, bf16[144,128]{1,0:T(8,128)(2,1)S(1)}, u32[]{:S(2)}, u32[]{:S(2)}) %collective-permute-start.2) | collective-permute-done | bytes 36896 | tf_op jit(solution)/shard_map/ppermute | solution.py:374
  35.9 0.0 collective-permute-done.1
  35.9 0.6 collective-permute-start.4
  36.5 0.0 collective-permute-done.qg_b
  36.5 9.7 %shard_map.75.even_ref = f32[2,16,8,128]{3,2,1,0:T(8,128)S(1)} custom-call(bf16[16,176,128]{2,1,0:T(8,128)(2,1)S(1)} %all_to_all.10.got_ref.qg_a, bf16[16,176,128]{2,1,0:T(8,128)(2,1)S(1)} %collective-permute-done.qg_b, bf16[4,144,128]{2,1,0:T(8,128)(2,1)S(1)} %pad_maximum_fusion.kv_ref), custom_call_target="tpu_custom_call" | custom-call | flops 1073741824 | bytes 1048576 | tf_op jit(solution)/shard_map/pallas_call | solution.py:433
  46.3 0.0 collective-permute-done.4.kv_ref
  46.3 9.9 %shard_map.76.mine_ref = f32[2,16,8,128]{3,2,1,0:T(8,128)S(1)} custom-call(bf16[16,176,128]{2,1,0:T(8,128)(2,1)S(1)} %all_to_all.10.got_ref.qg_a, bf16[16,176,128]{2,1,0:T(8,128)(2,1)S(1)} %collective-permute-done.qg_b, bf16[4,144,128]{2,1,0:T(8,128)(2,1)S(1)} %collective-permute-done.4.kv_ref, f32[2,16,8,128]{3,2,1,0:T(8,128)S(1)} %shard_map.75.even_ref), custom_call_target="tpu_custom_call" | custom-call | flops 1073741824 | bytes 1048576 | tf_op jit(solution)/shard_map/pallas_call | solution.py:435
  56.2 0.1 collective-permute-start.5
  56.3 1.3 %collective-permute-done.5.came_ref = f32[2,16,8,128]{3,2,1,0:T(8,128)S(1)} collective-permute-done((f32[2,16,8,128]{3,2,1,0:T(8,128)S(1)}, f32[2,16,8,128]{3,2,1,0:T(8,128)S(1)}, u32[]{:S(2)}, u32[]{:S(2)}) %collective-permute-start.5) | collective-permute-done | bytes 131104 | tf_op jit(solution)/shard_map/ppermute | solution.py:374
  57.6 5.8 %shard_map.77 = (f32[2,16,8,128]{3,2,1,0:T(8,128)S(1)}, f32[16,80,128]{2,1,0:T(8,128)S(1)}, f32[16,80,128]{2,1,0:T(8,128)S(1)}, bf16[4,144,128]{2,1,0:T(8,128)(2,1)S(1)}) custom-call(bf16[16,176,128]{2,1,0:T(8,128)(2,1)S(1)} %all_to_all.10.got_ref.qg_a, bf16[16,176,128]{2,1,0:T(8,128)(2,1)S(1)} %collective-permute-done.qg_b, ...), custom_call_target="tpu_custom_call" | custom-call | flops 5368709120 | bytes 1048576 | tf_op jit(solution)/shard_map/pallas_call | solution.py:441
  63.5 1.7 %collective-permute-start.6 = (bf16[4,144,128]{2,1,0:T(8,128)(2,1)S(1)}, bf16[4,144,128]{2,1,0:T(8,128)(2,1)S(1)}, u32[]{:S(2)}, u32[]{:S(2)}) collective-permute-start(bf16[4,144,128]{2,1,0:T(8,128)(2,1)S(1)} %get-tuple-element.50), channel_id=1, source_target_pairs={{0,2},{2,0},{4,6},{6,4},{8,10},{10,8},{12,14},{14,12},{1,3},{3,1},... | collective-permute-start | bytes 442376 | tf_op jit(solution)/shard_map/ppermute | solution.py:374
  65.2 5.9 %shard_map.78 = (f32[16,80,128]{2,1,0:T(8,128)S(1)}, f32[16,80,128]{2,1,0:T(8,128)S(1)}, f32[4,144,128]{2,1,0:T(8,128)S(1)}) custom-call(bf16[16,176,128]{2,1,0:T(8,128)(2,1)S(1)} %all_to_all.10.got_ref.qg_a, bf16[16,176,128]{2,1,0:T(8,128)(2,1)S(1)} %collective-permute-done.qg_b, bf16[4,144,128]{2,1,0:T(8,128)(2,1)S(1)} %pad_maximum_fusion.kv_ref, ...), custom_call_target="tpu_custom_call" | custom-call | flops 5368709120 | bytes 1048576 | tf_op jit(solution)/shard_map/pallas_call | solution.py:445
  71.1 0.0 collective-permute-done.6
  71.1 0.1 collective-permute-start.7
  71.3 1.6 %collective-permute-start.10 = (bf16[144,128]{1,0:T(8,128)(2,1)S(1)}, bf16[144,128]{1,0:T(8,128)(2,1)S(1)}, u32[]{:S(2)}, u32[]{:S(2)}) collective-permute-start(bf16[144,128]{1,0:T(8,128)(2,1)S(1)} %get-tuple-element.79), channel_id=1, source_target_pairs={{0,12},{2,14},{4,8},{6,10},{8,4},{10,6},{12,0},{14,2},{1,13},{3,15... | collective-permute-start | bytes 110600 | tf_op jit(solution)/shard_map/ppermute | solution.py:374
  73.0 3.0 %collective-permute-start.9 = (bf16[144,128]{1,0:T(8,128)(2,1)S(1)}, bf16[144,128]{1,0:T(8,128)(2,1)S(1)}, u32[]{:S(2)}, u32[]{:S(2)}) collective-permute-start(bf16[144,128]{1,0:T(8,128)(2,1)S(1)} %get-tuple-element.80), channel_id=1, source_target_pairs={{0,8},{2,10},{4,12},{6,14},{8,0},{10,2},{12,4},{14,6},{1,9},{3,11}... | collective-permute-start | bytes 110600 | tf_op jit(solution)/shard_map/ppermute | solution.py:374
  76.0 1.9 %collective-permute-start.8 = (bf16[144,128]{1,0:T(8,128)(2,1)S(1)}, bf16[144,128]{1,0:T(8,128)(2,1)S(1)}, u32[]{:S(2)}, u32[]{:S(2)}) collective-permute-start(bf16[144,128]{1,0:T(8,128)(2,1)S(1)} %get-tuple-element.81), channel_id=1, source_target_pairs={{0,4},{2,6},{4,0},{6,2},{8,12},{10,14},{12,8},{14,10},{1,5},{3,7},... | collective-permute-start | bytes 110600 | tf_op jit(solution)/shard_map/ppermute | solution.py:374
  77.9 0.0 slice-done
  77.9 0.0 slice-done.1
  77.9 0.0 copy-done
  77.9 1.3 %shard_map.81 = (bf16[256,1152]{1,0:T(8,128)(2,1)S(1)}, bf16[256,1152]{1,0:T(8,128)(2,1)S(1)}) custom-call(bf16[256,1152]{1,0:T(8,128)(2,1)S(1)} %copy-done, bf16[1152,3456]{1,0:T(8,128)(2,1)S(1)} %bitcast.14), custom_call_target="tpu_custom_call" | custom-call | flops 1048576 | bytes 65536 | tf_op jit(solution)/shard_map/pallas_call | solution.py:390
  79.3 1.3 %shard_map.80 = (bf16[256,1152]{1,0:T(8,128)(2,1)S(1)}, bf16[256,1152]{1,0:T(8,128)(2,1)S(1)}) custom-call(bf16[256,1152]{1,0:T(8,128)(2,1)S(1)} %copy-done, bf16[1152,3456]{1,0:T(8,128)(2,1)S(1)} %bitcast.14), custom_call_target="tpu_custom_call" | custom-call | flops 1048576 | bytes 65536 | tf_op jit(solution)/shard_map/pallas_call | solution.py:390
  80.6 1.3 %shard_map.79 = (bf16[256,1152]{1,0:T(8,128)(2,1)S(1)}, bf16[256,1152]{1,0:T(8,128)(2,1)S(1)}) custom-call(bf16[256,1152]{1,0:T(8,128)(2,1)S(1)} %copy-done, bf16[1152,3456]{1,0:T(8,128)(2,1)S(1)} %bitcast.14), custom_call_target="tpu_custom_call" | custom-call | flops 1048576 | bytes 65536 | tf_op jit(solution)/shard_map/pallas_call | solution.py:390
  81.9 0.0 collective-permute-done.10.came_c
  81.9 0.0 collective-permute-done.9.came_b
  81.9 0.0 collective-permute-done.8.came_a
  81.9 0.0 collective-permute-done.7.other_ref
  82.0 0.1 shard_map.82
  82.1 13.1 %all_to_all.11.back_ref = bf16[16,96,128]{2,1,0:T(8,128)(2,1)S(1)} all-to-all(bf16[16,96,128]{2,1,0:T(8,128)(2,1)S(1)} %shard_map.82), channel_id=1, replica_groups=mesh['yh'=2,'x'=4,'c'=2,'z'=8,'yl'=2] {'yh','x','yl'}, dimensions={0} | all-to-all | bytes 786432 | tf_op jit(solution)/shard_map/all_to_all | solution.py:458
  95.2 2.3 %shard_map.83 = (f32[72,256]{1,0:T(8,128)S(1)}, f32[4,256]{1,0:T(4,128)S(1)}, f32[4,256]{1,0:T(4,128)S(1)}) custom-call(bf16[16,96,128]{2,1,0:T(8,128)(2,1)S(1)} %all_to_all.11.back_ref, bf16[256,1152]{1,0:T(8,128)(2,1)S(1)} %get-tuple-element.67.refs_0_, bf16[256,1152]{1,0:T(8,128)(2,1)S(1)} %get-tuple-element.68.refs_1_, ...), custom_call_target="tpu_custom_call" | custom-call | tf_op jit(solution)/shard_map/pallas_call | solution.py:460
  97.6 2.1 %collective-permute-start.11 = (f32[4,256]{1,0:T(4,128)S(1)}, f32[4,256]{1,0:T(4,128)S(1)}, u32[]{:S(2)}, u32[]{:S(2)}) collective-permute-start(f32[4,256]{1,0:T(4,128)S(1)} %get-tuple-element.74), channel_id=1, source_target_pairs={{16,32},{48,64},{80,96},{112,128},{144,160},{176,192},{208,224},{3... | collective-permute-start | bytes 12296 | tf_op jit(solution)/shard_map/ppermute | solution.py:380
  99.6 0.3 collective-permute-start.12
  99.9 6.2 %collective-permute-done.11.chip_ref = f32[4,256]{1,0:T(4,128)S(1)} collective-permute-done((f32[4,256]{1,0:T(4,128)S(1)}, f32[4,256]{1,0:T(4,128)S(1)}, u32[]{:S(2)}, u32[]{:S(2)}) %collective-permute-start.11) | collective-permute-done | bytes 4128 | tf_op jit(solution)/shard_map/ppermute | solution.py:380
  106.1 0.0 collective-permute-done.12.core_ref
  106.1 0.1 shard_map.84
  106.2 3.9 %collective-permute-start.13 = (f32[4,64]{1,0:T(4,128)S(1)}, f32[4,64]{1,0:T(4,128)S(1)}, u32[]{:S(2)}, u32[]{:S(2)}) collective-permute-start(f32[4,64]{1,0:T(4,128)S(1)} %get-tuple-element.77), channel_id=1, source_target_pairs={{1,2},{3,4},{5,6},{7,8},{9,10},{11,12},{13,14},{2,1},{4,3},{6,5},{... | collective-permute-start | bytes 3080 | tf_op jit(solution)/shard_map/ppermute | solution.py:380
  110.1 0.1 collective-permute-start.14
  110.2 2.3 %collective-permute-done.13.far_ref = f32[4,64]{1,0:T(4,128)S(1)} collective-permute-done((f32[4,64]{1,0:T(4,128)S(1)}, f32[4,64]{1,0:T(4,128)S(1)}, u32[]{:S(2)}, u32[]{:S(2)}) %collective-permute-start.13) | collective-permute-done | bytes 1056 | tf_op jit(solution)/shard_map/ppermute | solution.py:380
  112.6 1.2 %collective-permute-done.14.near_ref = f32[4,64]{1,0:T(4,128)S(1)} collective-permute-done((f32[4,64]{1,0:T(4,128)S(1)}, f32[4,64]{1,0:T(4,128)S(1)}, u32[]{:S(2)}, u32[]{:S(2)}) %collective-permute-start.14) | collective-permute-done | bytes 1056 | tf_op jit(solution)/shard_map/ppermute | solution.py:374
  113.8 0.7 shard_map.85
  (9 shorter events, 0.1 us)
Async XLA Ops:
  21.0 15.5 %collective-permute-start = (bf16[16,176,128]{2,1,0:T(8,128)(2,1)S(1)}, bf16[16,176,128]{2,1,0:T(8,128)(2,1)S(1)}, u32[]{:S(2)}, u32[]{:S(2)}) collective-permute-start(bf16[16,176,128]{2,1,0:T(8,128)(2,1)S(1)} %all_to_all.10.got_ref.qg_a), channel_id=1, source_target_pairs={{0,16},{16,0},{1,17},{17,1},{2,18},{18,2},{3,19},{19,3},{4,20},{20... | collective-permute-start | bytes 2162696 | tf_op jit(solution)/shard_map/ppermute | solution.py:374
  21.1 8.9 %collective-permute-start.3 = (bf16[144,128]{1,0:T(8,128)(2,1)S(1)}, bf16[144,128]{1,0:T(8,128)(2,1)S(1)}, u32[]{:S(2)}, u32[]{:S(2)}) collective-permute-start(bf16[144,128]{1,0:T(8,128)(2,1)S(1)} %shard_map.74), channel_id=1, source_target_pairs={{0,12},{2,14},{4,8},{6,10},{8,4},{10,6},{12,0},{14,2},{1,13},{3,15... | collective-permute-start | bytes 110600 | tf_op jit(solution)/shard_map/ppermute | solution.py:374
  27.5 8.4 %collective-permute-start.2 = (bf16[144,128]{1,0:T(8,128)(2,1)S(1)}, bf16[144,128]{1,0:T(8,128)(2,1)S(1)}, u32[]{:S(2)}, u32[]{:S(2)}) collective-permute-start(bf16[144,128]{1,0:T(8,128)(2,1)S(1)} %shard_map.74), channel_id=1, source_target_pairs={{0,8},{2,10},{4,12},{6,14},{8,0},{10,2},{12,4},{14,6},{1,9},{3,11}... | collective-permute-start | bytes 110600 | tf_op jit(solution)/shard_map/ppermute | solution.py:374
  28.5 7.4 %collective-permute-start.1 = (bf16[144,128]{1,0:T(8,128)(2,1)S(1)}, bf16[144,128]{1,0:T(8,128)(2,1)S(1)}, u32[]{:S(2)}, u32[]{:S(2)}) collective-permute-start(bf16[144,128]{1,0:T(8,128)(2,1)S(1)} %shard_map.74), channel_id=1, source_target_pairs={{0,4},{2,6},{4,0},{6,2},{8,12},{10,14},{12,8},{14,10},{1,5},{3,7},... | collective-permute-start | bytes 110600 | tf_op jit(solution)/shard_map/ppermute | solution.py:374
  35.9 10.4 %collective-permute-start.4 = (bf16[4,144,128]{2,1,0:T(8,128)(2,1)S(1)}, bf16[4,144,128]{2,1,0:T(8,128)(2,1)S(1)}, u32[]{:S(2)}, u32[]{:S(2)}) collective-permute-start(bf16[4,144,128]{2,1,0:T(8,128)(2,1)S(1)} %pad_maximum_fusion.kv_ref), channel_id=1, source_target_pairs={{0,2},{2,0},{4,6},{6,4},{8,10},{10,8},{12,14},{14,12},{1,3},{3,1},... | collective-permute-start | bytes 442376 | tf_op jit(solution)/shard_map/ppermute | solution.py:374
  56.2 1.4 %collective-permute-start.5 = (f32[2,16,8,128]{3,2,1,0:T(8,128)S(1)}, f32[2,16,8,128]{3,2,1,0:T(8,128)S(1)}, u32[]{:S(2)}, u32[]{:S(2)}) collective-permute-start(f32[2,16,8,128]{3,2,1,0:T(8,128)S(1)} %shard_map.76.mine_ref), channel_id=1, source_target_pairs={{0,16},{16,0},{1,17},{17,1},{2,18},{18,2},{3,19},{19,3},{4,20},{20... | collective-permute-start | bytes 393224 | tf_op jit(solution)/shard_map/ppermute | solution.py:374
  57.6 20.3 %slice-start = ((s8[7962624]{0:T(1024)(128)(4,1)}), s8[4194304]{0:T(1024)(128)(4,1)S(1)}, s32[]{:S(2)}) async-start(s8[7962624]{0:T(1024)(128)(4,1)} %bitcast.13), calls=%async_computation.2 | async-start | bytes 8388608
  63.5 7.7 %collective-permute-start.6 = (bf16[4,144,128]{2,1,0:T(8,128)(2,1)S(1)}, bf16[4,144,128]{2,1,0:T(8,128)(2,1)S(1)}, u32[]{:S(2)}, u32[]{:S(2)}) collective-permute-start(bf16[4,144,128]{2,1,0:T(8,128)(2,1)S(1)} %get-tuple-element.50), channel_id=1, source_target_pairs={{0,2},{2,0},{4,6},{6,4},{8,10},{10,8},{12,14},{14,12},{1,3},{3,1},... | collective-permute-start | bytes 442376 | tf_op jit(solution)/shard_map/ppermute | solution.py:374
  65.2 12.7 %slice-start.1 = ((s8[7962624]{0:T(1024)(128)(4,1)}), s8[3768320]{0:T(1024)(128)(4,1)S(1)}, s32[]{:S(2)}) async-start(s8[7962624]{0:T(1024)(128)(4,1)} %bitcast.13), calls=%async_computation.3 | async-start | bytes 7536640
  65.2 12.7 %copy-start = (bf16[256,1152]{1,0:T(8,128)(2,1)S(1)}, bf16[256,1152]{1,0:T(8,128)(2,1)}, u32[]{:S(2)}) copy-start(bf16[256,1152]{1,0:T(8,128)(2,1)} %patch_ref.2) | copy-start | bytes 1769476
  71.1 10.8 %collective-permute-start.7 = (f32[16,80,128]{2,1,0:T(8,128)S(1)}, f32[16,80,128]{2,1,0:T(8,128)S(1)}, u32[]{:S(2)}, u32[]{:S(2)}) collective-permute-start(f32[16,80,128]{2,1,0:T(8,128)S(1)} %get-tuple-element.52), channel_id=1, source_target_pairs={{0,16},{16,0},{1,17},{17,1},{2,18},{18,2},{3,19},{19,3},{4,20},{20... | collective-permute-start | bytes 1966088 | tf_op jit(solution)/shard_map/ppermute | solution.py:374
  71.3 10.6 %collective-permute-start.10 = (bf16[144,128]{1,0:T(8,128)(2,1)S(1)}, bf16[144,128]{1,0:T(8,128)(2,1)S(1)}, u32[]{:S(2)}, u32[]{:S(2)}) collective-permute-start(bf16[144,128]{1,0:T(8,128)(2,1)S(1)} %get-tuple-element.79), channel_id=1, source_target_pairs={{0,12},{2,14},{4,8},{6,10},{8,4},{10,6},{12,0},{14,2},{1,13},{3,15... | collective-permute-start | bytes 110600 | tf_op jit(solution)/shard_map/ppermute | solution.py:374
  73.0 9.0 %collective-permute-start.9 = (bf16[144,128]{1,0:T(8,128)(2,1)S(1)}, bf16[144,128]{1,0:T(8,128)(2,1)S(1)}, u32[]{:S(2)}, u32[]{:S(2)}) collective-permute-start(bf16[144,128]{1,0:T(8,128)(2,1)S(1)} %get-tuple-element.80), channel_id=1, source_target_pairs={{0,8},{2,10},{4,12},{6,14},{8,0},{10,2},{12,4},{14,6},{1,9},{3,11}... | collective-permute-start | bytes 110600 | tf_op jit(solution)/shard_map/ppermute | solution.py:374
  76.0 6.0 %collective-permute-start.8 = (bf16[144,128]{1,0:T(8,128)(2,1)S(1)}, bf16[144,128]{1,0:T(8,128)(2,1)S(1)}, u32[]{:S(2)}, u32[]{:S(2)}) collective-permute-start(bf16[144,128]{1,0:T(8,128)(2,1)S(1)} %get-tuple-element.81), channel_id=1, source_target_pairs={{0,4},{2,6},{4,0},{6,2},{8,12},{10,14},{12,8},{14,10},{1,5},{3,7},... | collective-permute-start | bytes 110600 | tf_op jit(solution)/shard_map/ppermute | solution.py:374
  97.6 8.5 %collective-permute-start.11 = (f32[4,256]{1,0:T(4,128)S(1)}, f32[4,256]{1,0:T(4,128)S(1)}, u32[]{:S(2)}, u32[]{:S(2)}) collective-permute-start(f32[4,256]{1,0:T(4,128)S(1)} %get-tuple-element.74), channel_id=1, source_target_pairs={{16,32},{48,64},{80,96},{112,128},{144,160},{176,192},{208,224},{3... | collective-permute-start | bytes 12296 | tf_op jit(solution)/shard_map/ppermute | solution.py:380
  99.6 6.5 %collective-permute-start.12 = (f32[4,256]{1,0:T(4,128)S(1)}, f32[4,256]{1,0:T(4,128)S(1)}, u32[]{:S(2)}, u32[]{:S(2)}) collective-permute-start(f32[4,256]{1,0:T(4,128)S(1)} %get-tuple-element.75), channel_id=1, source_target_pairs={{0,16},{16,0},{1,17},{17,1},{2,18},{18,2},{3,19},{19,3},{4,20},{20... | collective-permute-start | bytes 12296 | tf_op jit(solution)/shard_map/ppermute | solution.py:374
  106.2 6.4 %collective-permute-start.13 = (f32[4,64]{1,0:T(4,128)S(1)}, f32[4,64]{1,0:T(4,128)S(1)}, u32[]{:S(2)}, u32[]{:S(2)}) collective-permute-start(f32[4,64]{1,0:T(4,128)S(1)} %get-tuple-element.77), channel_id=1, source_target_pairs={{1,2},{3,4},{5,6},{7,8},{9,10},{11,12},{13,14},{2,1},{4,3},{6,5},{... | collective-permute-start | bytes 3080 | tf_op jit(solution)/shard_map/ppermute | solution.py:380
  110.1 3.7 %collective-permute-start.14 = (f32[4,64]{1,0:T(4,128)S(1)}, f32[4,64]{1,0:T(4,128)S(1)}, u32[]{:S(2)}, u32[]{:S(2)}) collective-permute-start(f32[4,64]{1,0:T(4,128)S(1)} %get-tuple-element.78), channel_id=1, source_target_pairs={{0,1},{1,0},{2,3},{3,2},{4,5},{5,4},{6,7},{7,6},{8,9},{9,8},{10,11... | collective-permute-start | bytes 3080 | tf_op jit(solution)/shard_map/ppermute | solution.py:374

commit v6 on v5

--- a/solution.py
+++ b/solution.py
@@ -17,6 +17,7 @@
 ROWS, COLS = 8, 16
 TOK = ROWS * COLS
 CELLS = TOK // POOL**2
+EXTENDED = TOK + 2 * COLS
 FPAD = 80
 QUERIES = 2048
 HALF = 512
@@ -242,33 +243,66 @@
     put_keys(out_ref, dk_s, dv_s)
 
 
+def edge_rows(dq):
+    edges = jnp.concatenate([dq[0:DH, 0:COLS], dq[0:DH, TOK - COLS :]], axis=1)
+    pad = jnp.zeros((24, 32), f32)
+    return jnp.concatenate([edges[0:24], edges[24:48], edges[48:72], pad], axis=1)
+
+
 def second_kernel(
-    qg_a, qg_b, kv_ref, sums_ref, in_a, in_b, dq_a, dq_b, out_ref,
+    qg_a, qg_b, kv_ref, sums_ref, in_a, in_b, dq_a, dq_b, edge_a, edge_b, out_ref,
     k_s, kt_s, v_s, dk_s, dv_s,
 ):
     load_keys(kv_ref, k_s, kt_s, v_s)
 
     def put_a(n, dq):
-        dq_a[n] = in_a[n] + dq
+        dq = in_a[n] + dq
+        dq_a[n] = dq
+        edge_a[n] = edge_rows(dq)
 
     def put_b(n, dq):
-        dq_b[n] = in_b[n] + dq
+        dq = in_b[n] + dq
+        dq_b[n] = dq
+        edge_b[n] = edge_rows(dq)
 
     gradients(sums_ref, ((qg_a, put_a), (qg_b, put_b)), k_s, kt_s, v_s, dk_s, dv_s)
     put_keys(out_ref, dk_s, dv_s)
 
 
-def pack_back_kernel(dq_ref, other_ref, mine_ref, came_a, came_b, came_c, send_ref):
+def keys_sum_kernel(mine_ref, came_a, came_b, came_c, out_ref):
     total = mine_ref[0]
     for came in (came_a, came_b, came_c):
         total = total + came[...].astype(f32)
+    out_ref[...] = total.astype(bf16)
+
+
+def beside(x, first):
+    none = jnp.zeros_like(x[0:2])
+    above = jnp.where(first, jnp.concatenate([none, x[:-2]]), x)
+    below = jnp.where(first, x, jnp.concatenate([x[2:], none]))
+    return above, below
+
+
+def pack_back_kernel(dq_ref, came_ref, edge_ref, came_edge_ref, keys_ref, other_ref, send_ref):
+    first = lax.axis_index("c") == 0
+    dq = (dq_ref[...] + came_ref[...])[:, 0:DH] * SCALE
+    above, below = beside((edge_ref[...] + came_edge_ref[...]) * SCALE, first)
+    lane = lax.broadcasted_iota(jnp.int32, (HEADS, 24, 128), 2)
+    above = pltpu.roll(above, 128 - COLS, 2)
+    edges = jnp.where(lane % 32 < COLS, above, pltpu.roll(below, COLS, 2))
     lanes = jnp.zeros((128, 128 - DH), f32)
-    dk = jnp.concatenate([total[0:DH].T, lanes], axis=1)
-    dv = jnp.concatenate([total[DH : 2 * DH].T, lanes], axis=1)
-    send_ref[:, 0:FPAD, :] = ((dq_ref[...] + other_ref[...]) * SCALE).astype(bf16)
-    for a in range(HEADS):
-        cells = slice(a * CELLS, (a + 1) * CELLS)
-        send_ref[a, FPAD : FPAD + 16, :] = jnp.concatenate([dk[cells], dv[cells]]).astype(bf16)
+    row = lax.broadcasted_iota(jnp.int32, (HEADS, CELLS, 128), 1)
+
+    def cells(ref, part):
+        rows = ref[...].astype(f32)[part * DH : (part + 1) * DH].T
+        return jnp.concatenate([rows, lanes], axis=1).reshape(HEADS, CELLS, 128)
+
+    parts = [dq, edges, cells(keys_ref, 0), cells(keys_ref, 1)]
+    for part in (0, 1):
+        above, below = beside(cells(other_ref, part), first)
+        half = CELLS // 2
+        parts.append(jnp.where(row < half, pltpu.roll(above, half, 1), pltpu.roll(below, half, 1)))
+    send_ref[...] = jnp.concatenate(parts, axis=1).astype(bf16)
 
 
 def weights_kernel(part, patch_ref, qkv_ref, high_ref, low_ref, qkv_s, sems):
@@ -290,33 +324,42 @@
 
 
 def embed_kernel(back_ref, *refs):
-    weights, (canvas_ref, core_out, chip_out, joined, sheet) = refs[:6], refs[6:]
+    weights, (center_ref, near_out, far_out, joined, sheet) = refs[:6], refs[6:]
     cols = (((0,), (0,)), ((), ()))
-    cell = lax.broadcasted_iota(jnp.int32, (CELLS, TOK), 0)
-    token = lax.broadcasted_iota(jnp.int32, (CELLS, TOK), 1)
-    holds = (token // (POOL * COLS) == cell // 4) & (token % COLS // POOL == cell % 4)
+    cell = lax.broadcasted_iota(jnp.int32, (2 * CELLS, 2 * TOK), 0)
+    token = lax.broadcasted_iota(jnp.int32, (2 * CELLS, 2 * TOK), 1)
+    mine = token // (POOL * COLS) * 4 + token % COLS // POOL
+    beyond = CELLS + (token - TOK) // COLS * 4 + token % COLS // POOL
+    holds = (cell == jnp.where(token < TOK, mine, beyond)) & (token < EXTENDED)
     spread = jnp.where(holds, 1.0 / POOL**2, 0.0).astype(bf16)
     for h in range(HEADS):
-        mine = back_ref[h].astype(f32)
+        head = back_ref[h].astype(f32)
         rows = slice(h * DH, (h + 1) * DH)
-        joined[rows] = mine[0:DH]
+        joined[rows, 0:TOK] = head[0:DH]
+        edges = head[DH : DH + 24]
+        edges = [edges, pltpu.roll(edges, 96, 1), pltpu.roll(edges, 64, 1)]
+        joined[rows, TOK:] = jnp.concatenate(edges)
         for part in (0, 1):
-            at = FPAD + part * CELLS
-            pooled = mine[at : at + CELLS].astype(bf16)
+            at = DH + 24 + part * CELLS
+            pooled = jnp.concatenate([head[at : at + CELLS], head[at + 16 : at + 16 + CELLS]]).astype(bf16)
             wide = lax.dot_general(pooled, spread, cols, preferred_element_type=f32)
             joined[(part + 1) * D + h * DH : (part + 1) * D + (h + 1) * DH] = wide[0:DH]
     values = joined[...].astype(bf16)
-    patch = jnp.zeros((256, TOK), f32)
+    patch = jnp.zeros((256, 2 * TOK), f32)
     for n, weight in enumerate(weights):
         rows = slice(n // 2 * D, (n // 2 + 1) * D)
         patch = patch + jnp.dot(weight[...], values[rows], preferred_element_type=f32)
-    patch = jnp.concatenate([patch[0:128].T, patch[128:256].T])
+    sides = []
+    for side in (0, 1):
+        rows = slice(side * 128, (side + 1) * 128)
+        sides += [patch[rows, 0:TOK].T, patch[rows, TOK:].T[0 : EXTENDED - TOK]]
+    patch = jnp.concatenate(sides)
     high = patch.astype(bf16)
     rest = patch - high.astype(f32)
     mid = rest.astype(bf16)
     low = (rest - mid.astype(f32)).astype(bf16)
-    lane = lax.broadcasted_iota(jnp.int32, (2 * TOK, 256), 1)
-    row = lax.broadcasted_iota(jnp.int32, (2 * TOK, 256), 0)
+    lane = lax.broadcasted_iota(jnp.int32, (2 * EXTENDED, 256), 1)
+    row = lax.broadcasted_iota(jnp.int32, (2 * EXTENDED, 256), 0)
     here = lane % 128 // 8 == row % COLS
     sheet[...] = jnp.zeros_like(sheet)
     parts = jnp.concatenate([high, mid, low], axis=1)
@@ -328,34 +371,24 @@
         tile = jnp.concatenate([tile] * 3)
         wide = jnp.dot(parts, tile, preferred_element_type=f32)
         wide = jnp.where(here, wide, 0.0)
-        wide = jnp.sum(wide.reshape(2 * ROWS, COLS, 256), axis=1)
+        wide = jnp.sum(wide.reshape(2 * (ROWS + 2), COLS, 256), axis=1)
         for k in (0, 1):
             u = 2 * pair + k
             for side in (0, 1):
-                piece = wide[side * ROWS : (side + 1) * ROWS, k * 128 : (k + 1) * 128]
-                sheet[side, pl.ds(u, ROWS, stride=8), :] += piece
-    left = sheet[0]
-    right = sheet[1]
+                at_side = side * (ROWS + 2)
+                piece = wide[at_side : at_side + ROWS + 2, k * 128 : (k + 1) * 128]
+                sheet[side, pl.ds(u, ROWS, stride=8), :] += piece[0:ROWS]
+                if u >= 12:
+                    sheet[side, u - 8 : u - 7, :] += piece[ROWS : ROWS + 1]
+                if u < 4:
+                    sheet[side, 64 + u : 65 + u, :] += piece[ROWS + 1 :]
+    left = sheet[0, 4:68]
+    right = sheet[1, 4:68]
     lane = lax.broadcasted_iota(jnp.int32, left.shape, 1)
     center = jnp.where(lane < 124, pltpu.roll(left, 124, 1), 0.0)
-    center = center + jnp.where(lane >= 4, pltpu.roll(right, 4, 1), 0.0)
-    edges = jnp.where(lane < 4, left, pltpu.roll(right, 8, 1))
-    canvas = jnp.concatenate([center, jnp.where(lane < 8, edges, 0.0)], axis=1)
-    canvas_ref[...] = canvas
-    first = lax.axis_index("c") == 0
-    core_out[...] = jnp.where(first, canvas[68:72], canvas[0:4])
-    chip_out[...] = jnp.where(first, canvas[0:4], canvas[68:72])
-
-
-def rows_kernel(canvas_ref, chip_ref, core_ref, center_ref, near_out, far_out):
-    first = lax.axis_index("c") == 0
-    above = jnp.where(first, chip_ref[...], core_ref[...])
-    below = jnp.where(first, core_ref[...], chip_ref[...])
-    quiet = jnp.zeros((56, 256), f32)
-    canvas = canvas_ref[4:68] + jnp.concatenate([above, quiet, below])
-    center_ref[...] = canvas[:, 0:128]
-    edges = canvas[:, 128:256].T[0:8]
-    left, right = edges[0:4], edges[4:8]
+    center_ref[...] = center + jnp.where(lane >= 4, pltpu.roll(right, 4, 1), 0.0)
+    left = left.T[0:4]
+    right = right.T[124:128]
     begins = lax.axis_index("yl") == 0
     near_out[...] = jnp.where(begins, right, left)
     far_out[...] = jnp.where(begins, left, right)
@@ -442,31 +475,36 @@
         first_kernel, [sums] + dq + [jax.ShapeDtypeStruct(block, bf16)], 28, scratch, cost_estimate=cost(5)
     )(got, there, odd, mine, came)
     came = swapped(grads, "z", 1)
-    dq_here, dq_there, grads = call(
-        second_kernel, dq + [jax.ShapeDtypeStruct(block, f32)], 28, scratch, cost_estimate=cost(5)
+    edges = [jax.ShapeDtypeStruct((HEADS, 24, TOK), f32)] * 2
+    *dq, grads = call(
+        second_kernel,
+        dq + edges + [jax.ShapeDtypeStruct(block, f32)],
+        28,
+        scratch,
+        cost_estimate=cost(5),
     )(got, there, even, sums, dq_here, dq_there)
-    dq_here, dq_there, grads, came = lax.optimization_barrier((dq_here, dq_there, grads, came))
+    dq, grads, came = lax.optimization_barrier((dq, grads, came))
+    dq_here, dq_there, edge_here, edge_there = dq
     dq_there = swapped(dq_there, "c", 1)
+    edge_here = swapped(edge_here, "c", 1)
     mine = grads + came.astype(f32)
     mine, w_qkv, w_patch = lax.optimization_barrier((mine, w_qkv, w_patch))
     came = [swapped(mine[n].astype(bf16), "z", 2 * n) for n in (1, 2, 3)]
     weights = [w for part in range(3) for w in combined_weights(w_qkv, w_patch, part)]
     came, weights = lax.optimization_barrier((came, weights))
-    send = call(pack_back_kernel, jax.ShapeDtypeStruct((HEADS, FPAD + 16, TOK), bf16), 8)(
-        dq_here, dq_there, mine[0:1], *came
+    keys = call(keys_sum_kernel, jax.ShapeDtypeStruct((2 * DH, 128), bf16), 4)(mine[0:1], *came)
+    other = swapped(keys, "c", 1)
+    send = call(pack_back_kernel, jax.ShapeDtypeStruct((HEADS, 128, TOK), bf16), 16)(
+        dq_here, dq_there, edge_there, edge_here, keys, other
     )
     back = lax.all_to_all(send, HEAD_AXES, 0, 0, tiled=True)
-    strip = jax.ShapeDtypeStruct((4, 256), f32)
-    canvas, to_core, to_chip = call(
-        embed_kernel,
-        [jax.ShapeDtypeStruct((72, 256), f32), strip, strip],
-        24,
-        [pltpu.VMEM((3 * D, TOK), f32), pltpu.VMEM((2, 72, 128), f32)],
-    )(back, *weights)
     strip = jax.ShapeDtypeStruct((4, 64), f32)
     center, to_near, to_far = call(
-        rows_kernel, [jax.ShapeDtypeStruct((64, 128), f32), strip, strip], 4
-    )(canvas, neighbours(to_chip, BLK), swapped(to_core, "c", 1))
+        embed_kernel,
+        [jax.ShapeDtypeStruct((64, 128), f32), strip, strip],
+        28,
+        [pltpu.VMEM((3 * D, 2 * TOK), f32), pltpu.VMEM((2, 72, 128), f32)],
+    )(back, *weights)
     return call(cols_kernel, jax.ShapeDtypeStruct((64, 128), f32), 4)(
         center, neighbours(to_far, COL), swapped(to_near, "yl", 1)
     )

time: 115 us -> 113 us (0.983)
  the two profiles are of different devices: /device:TPU:24 before, /device:TPU:8 now
where the time goes in v6:
time: 113 us
  Pallas kernels  43.4 us (38%)
  blocking collectives  34.7 us (31%)
  starting transfers between devices  22.7 us (20%)
  waiting for transfers between devices  12 us (11%)
    all_to_all x1, blocking collectives, on_device(): got = lax.all_to_all(send, HEAD_AXES, 0, 0, tiled=True)  19.4 us
    ppermute x14, starting transfers between devices, swapped(): return lax.ppermute(x, axis, [(i, i ^ by) for i in range(peers)])  18.7 us
    all_to_all x1, blocking collectives, on_device(): back = lax.all_to_all(send, HEAD_AXES, 0, 0, tiled=True)  15.3 us
    pallas_call x1, Pallas kernels, on_device(): call(odd_sums_kernel, sums, 24, [keys], cost_estimate=cost(1))  9.89 us
    ppermute x14, waiting for transfers between devices, swapped(): return lax.ppermute(x, axis, [(i, i ^ by) for i in range(peers)])  9.74 us
    pallas_call x1, Pallas kernels, on_device(): call(even_sums_kernel, sums, 24, [keys], cost_estimate=cost(1))  9.71 us
    pallas_call x1, Pallas kernels, on_device(): call(second_kernel, dq + edges + [jax.ShapeDtypeStruct(block, f32)], 28,...  6.51 us
    pallas_call x1, Pallas kernels, on_device(): call(first_kernel, [sums] + dq + [jax.ShapeDtypeStruct(block, bf16)], 28,...  5.84 us
  transfers between devices with their start and end apart: 15, of which 5 were waited for; matrix products, arithmetic and copies ran while one was open for 0% of the time, Pallas kernels for 18%

profile of v6, /device:TPU:8, one launch (start us, length us, event | category | flops | bytes accessed | tf_op | source)
XLA Modules:
  0.0 113.2 jit_solution(14143270226026728797)
XLA Ops:
  0.0 2.5 %shard_map.73 = bf16[16,176,128]{2,1,0:T(8,128)(2,1)} custom-call(bf16[128,1152]{1,0:T(8,128)(2,1)} %bitcast.16, bf16[128,1152]{1,0:T(8,128)(2,1)} %bitcast.17, bf16[128,1152]{1,0:T(8,128)(2,1)} %bitcast.18, bf16[2,4,1152]{2,1,0:T(4,128)(2,1)} %k_in.1, bf16[2,4,1152]{2,1,0:T(4,128)(2,1)} %v_in.1), custom_call_target="tpu_custom_call" | custom-call | tf_op jit(solution)/shard_map/pallas_call | solution.py:438
  2.5 19.4 %all_to_all.10.got_ref.qg_a = bf16[16,176,128]{2,1,0:T(8,128)(2,1)S(1)} all-to-all(bf16[16,176,128]{2,1,0:T(8,128)(2,1)} %shard_map.73), channel_id=1, replica_groups=mesh['yh'=2,'x'=4,'c'=2,'z'=8,'yl'=2] {'yh','x','yl'}, dimensions={0} | all-to-all | bytes 1441792 | tf_op jit(solution)/shard_map/all_to_all | solution.py:452
  21.9 0.0 collective-permute-start
  21.9 0.1 shard_map.74
  22.0 6.4 %collective-permute-start.3 = (bf16[144,128]{1,0:T(8,128)(2,1)S(1)}, bf16[144,128]{1,0:T(8,128)(2,1)S(1)}, u32[]{:S(2)}, u32[]{:S(2)}) collective-permute-start(bf16[144,128]{1,0:T(8,128)(2,1)S(1)} %shard_map.74), channel_id=1, source_target_pairs={{0,12},{2,14},{4,8},{6,10},{8,4},{10,6},{12,0},{14,2},{1,13},{3,15... | collective-permute-start | bytes 110600 | tf_op jit(solution)/shard_map/ppermute | solution.py:407
  28.4 1.0 collective-permute-start.2
  29.4 1.5 %collective-permute-start.1 = (bf16[144,128]{1,0:T(8,128)(2,1)S(1)}, bf16[144,128]{1,0:T(8,128)(2,1)S(1)}, u32[]{:S(2)}, u32[]{:S(2)}) collective-permute-start(bf16[144,128]{1,0:T(8,128)(2,1)S(1)} %shard_map.74), channel_id=1, source_target_pairs={{0,4},{2,6},{4,0},{6,2},{8,12},{10,14},{12,8},{14,10},{1,5},{3,7},... | collective-permute-start | bytes 110600 | tf_op jit(solution)/shard_map/ppermute | solution.py:407
  30.8 0.0 collective-permute-done.3
  30.8 5.9 %collective-permute-done.2 = bf16[144,128]{1,0:T(8,128)(2,1)S(1)} collective-permute-done((bf16[144,128]{1,0:T(8,128)(2,1)S(1)}, bf16[144,128]{1,0:T(8,128)(2,1)S(1)}, u32[]{:S(2)}, u32[]{:S(2)}) %collective-permute-start.2) | collective-permute-done | bytes 36896 | tf_op jit(solution)/shard_map/ppermute | solution.py:407
  36.7 0.0 collective-permute-done.1
  36.8 0.6 collective-permute-start.4
  37.4 0.0 collective-permute-done.qg_b
  37.4 9.7 %shard_map.75.even_ref = f32[2,16,8,128]{3,2,1,0:T(8,128)S(1)} custom-call(bf16[16,176,128]{2,1,0:T(8,128)(2,1)S(1)} %all_to_all.10.got_ref.qg_a, bf16[16,176,128]{2,1,0:T(8,128)(2,1)S(1)} %collective-permute-done.qg_b, bf16[4,144,128]{2,1,0:T(8,128)(2,1)S(1)} %pad_maximum_fusion.kv_ref), custom_call_target="tpu_custom_call" | custom-call | flops 1073741824 | bytes 1048576 | tf_op jit(solution)/shard_map/pallas_call | solution.py:466
  47.1 0.0 collective-permute-done.4.kv_ref
  47.1 9.9 %shard_map.76.mine_ref = f32[2,16,8,128]{3,2,1,0:T(8,128)S(1)} custom-call(bf16[16,176,128]{2,1,0:T(8,128)(2,1)S(1)} %all_to_all.10.got_ref.qg_a, bf16[16,176,128]{2,1,0:T(8,128)(2,1)S(1)} %collective-permute-done.qg_b, bf16[4,144,128]{2,1,0:T(8,128)(2,1)S(1)} %collective-permute-done.4.kv_ref, f32[2,16,8,128]{3,2,1,0:T(8,128)S(1)} %shard_map.75.even_ref), custom_call_target="tpu_custom_call" | custom-call | flops 1073741824 | bytes 1048576 | tf_op jit(solution)/shard_map/pallas_call | solution.py:468
  57.0 0.1 collective-permute-start.5
  57.1 1.3 %collective-permute-done.5.came_ref = f32[2,16,8,128]{3,2,1,0:T(8,128)S(1)} collective-permute-done((f32[2,16,8,128]{3,2,1,0:T(8,128)S(1)}, f32[2,16,8,128]{3,2,1,0:T(8,128)S(1)}, u32[]{:S(2)}, u32[]{:S(2)}) %collective-permute-start.5) | collective-permute-done | bytes 131104 | tf_op jit(solution)/shard_map/ppermute | solution.py:407
  58.5 5.8 %shard_map.77 = (f32[2,16,8,128]{3,2,1,0:T(8,128)S(1)}, f32[16,80,128]{2,1,0:T(8,128)S(1)}, f32[16,80,128]{2,1,0:T(8,128)S(1)}, bf16[4,144,128]{2,1,0:T(8,128)(2,1)S(1)}) custom-call(bf16[16,176,128]{2,1,0:T(8,128)(2,1)S(1)} %all_to_all.10.got_ref.qg_a, bf16[16,176,128]{2,1,0:T(8,128)(2,1)S(1)} %collective-permute-done.qg_b, ...), custom_call_target="tpu_custom_call" | custom-call | flops 5368709120 | bytes 1048576 | tf_op jit(solution)/shard_map/pallas_call | solution.py:474
  64.3 1.8 %collective-permute-start.6 = (bf16[4,144,128]{2,1,0:T(8,128)(2,1)S(1)}, bf16[4,144,128]{2,1,0:T(8,128)(2,1)S(1)}, u32[]{:S(2)}, u32[]{:S(2)}) collective-permute-start(bf16[4,144,128]{2,1,0:T(8,128)(2,1)S(1)} %get-tuple-element.53), channel_id=1, source_target_pairs={{0,2},{2,0},{4,6},{6,4},{8,10},{10,8},{12,14},{14,12},{1,3},{3,1},... | collective-permute-start | bytes 442376 | tf_op jit(solution)/shard_map/ppermute | solution.py:407
  66.1 0.0 slice-start.1
  66.1 6.5 %shard_map.78 = (f32[16,80,128]{2,1,0:T(8,128)S(1)}, f32[16,80,128]{2,1,0:T(8,128)S(1)}, f32[16,24,128]{2,1,0:T(8,128)S(1)}, f32[16,24,128]{2,1,0:T(8,128)S(1)}, f32[4,144,128]{2,1,0:T(8,128)S(1)}) custom-call(bf16[16,176,128]{2,1,0:T(8,128)(2,1)S(1)} %all_to_all.10.got_ref.qg_a, bf16[16,176,128]{2,1,0:T(8,128)(2,1)S(1)} %collective-permute-done.qg_b, ...), custom_call_target="tpu_custom_call" | custom-call | flops 5368709120 | bytes 1048576 | tf_op jit(solution)/shard_map/pallas_call | solution.py:479
  72.6 0.0 collective-permute-done.6
  72.6 0.1 collective-permute-start.7
  72.7 0.5 collective-permute-start.8
  73.3 1.6 %collective-permute-start.11 = (bf16[144,128]{1,0:T(8,128)(2,1)S(1)}, bf16[144,128]{1,0:T(8,128)(2,1)S(1)}, u32[]{:S(2)}, u32[]{:S(2)}) collective-permute-start(bf16[144,128]{1,0:T(8,128)(2,1)S(1)} %get-tuple-element.81), channel_id=1, source_target_pairs={{0,12},{2,14},{4,8},{6,10},{8,4},{10,6},{12,0},{14,2},{1,13},{3,15... | collective-permute-start | bytes 110600 | tf_op jit(solution)/shard_map/ppermute | solution.py:407
  74.9 3.0 %collective-permute-start.10 = (bf16[144,128]{1,0:T(8,128)(2,1)S(1)}, bf16[144,128]{1,0:T(8,128)(2,1)S(1)}, u32[]{:S(2)}, u32[]{:S(2)}) collective-permute-start(bf16[144,128]{1,0:T(8,128)(2,1)S(1)} %get-tuple-element.82), channel_id=1, source_target_pairs={{0,8},{2,10},{4,12},{6,14},{8,0},{10,2},{12,4},{14,6},{1,9},{3,11}... | collective-permute-start | bytes 110600 | tf_op jit(solution)/shard_map/ppermute | solution.py:407
  77.9 2.0 %collective-permute-start.9 = (bf16[144,128]{1,0:T(8,128)(2,1)S(1)}, bf16[144,128]{1,0:T(8,128)(2,1)S(1)}, u32[]{:S(2)}, u32[]{:S(2)}) collective-permute-start(bf16[144,128]{1,0:T(8,128)(2,1)S(1)} %get-tuple-element.83), channel_id=1, source_target_pairs={{0,4},{2,6},{4,0},{6,2},{8,12},{10,14},{12,8},{14,10},{1,5},{3,7},... | collective-permute-start | bytes 110600 | tf_op jit(solution)/shard_map/ppermute | solution.py:407
  79.9 0.0 slice-done
  79.9 0.0 slice-done.1
  79.9 0.0 copy-done
  79.9 1.3 %shard_map.81 = (bf16[256,1152]{1,0:T(8,128)(2,1)S(1)}, bf16[256,1152]{1,0:T(8,128)(2,1)S(1)}) custom-call(bf16[256,1152]{1,0:T(8,128)(2,1)S(1)} %copy-done, bf16[1152,3456]{1,0:T(8,128)(2,1)S(1)} %bitcast.14), custom_call_target="tpu_custom_call" | custom-call | flops 1048576 | bytes 65536 | tf_op jit(solution)/shard_map/pallas_call | solution.py:423
  81.2 1.3 %shard_map.80 = (bf16[256,1152]{1,0:T(8,128)(2,1)S(1)}, bf16[256,1152]{1,0:T(8,128)(2,1)S(1)}) custom-call(bf16[256,1152]{1,0:T(8,128)(2,1)S(1)} %copy-done, bf16[1152,3456]{1,0:T(8,128)(2,1)S(1)} %bitcast.14), custom_call_target="tpu_custom_call" | custom-call | flops 1048576 | bytes 65536 | tf_op jit(solution)/shard_map/pallas_call | solution.py:423
  82.5 1.3 %shard_map.79 = (bf16[256,1152]{1,0:T(8,128)(2,1)S(1)}, bf16[256,1152]{1,0:T(8,128)(2,1)S(1)}) custom-call(bf16[256,1152]{1,0:T(8,128)(2,1)S(1)} %copy-done, bf16[1152,3456]{1,0:T(8,128)(2,1)S(1)} %bitcast.14), custom_call_target="tpu_custom_call" | custom-call | flops 1048576 | bytes 65536 | tf_op jit(solution)/shard_map/pallas_call | solution.py:423
  83.9 0.0 collective-permute-done.11.came_c
  83.9 0.0 collective-permute-done.10.came_b
  83.9 0.0 collective-permute-done.9.came_a
  83.9 0.1 collective-permute-start.12
  84.0 1.2 %collective-permute-done.12.other_ref = bf16[144,128]{1,0:T(8,128)(2,1)S(1)} collective-permute-done((bf16[144,128]{1,0:T(8,128)(2,1)S(1)}, bf16[144,128]{1,0:T(8,128)(2,1)S(1)}, u32[]{:S(2)}, u32[]{:S(2)}) %collective-permute-start.12) | collective-permute-done | bytes 36896 | tf_op jit(solution)/shard_map/ppermute | solution.py:407
  85.2 0.0 collective-permute-done.8.came_edge_ref
  85.2 0.0 collective-permute-done.7.came_ref
  85.2 0.2 shard_map.83
  85.5 15.3 %all_to_all.11.back_ref = bf16[16,128,128]{2,1,0:T(8,128)(2,1)S(1)} all-to-all(bf16[16,128,128]{2,1,0:T(8,128)(2,1)S(1)} %shard_map.83), channel_id=1, replica_groups=mesh['yh'=2,'x'=4,'c'=2,'z'=8,'yl'=2] {'yh','x','yl'}, dimensions={0} | all-to-all | bytes 1048576 | tf_op jit(solution)/shard_map/all_to_all | solution.py:500
  100.8 4.0 %shard_map.84 = (f32[64,128]{1,0:T(8,128)S(1)}, f32[4,64]{1,0:T(4,128)S(1)}, f32[4,64]{1,0:T(4,128)S(1)}) custom-call(bf16[16,128,128]{2,1,0:T(8,128)(2,1)S(1)} %all_to_all.11.back_ref, bf16[256,1152]{1,0:T(8,128)(2,1)S(1)} %get-tuple-element.72.refs_0_, bf16[256,1152]{1,0:T(8,128)(2,1)S(1)} %get-tuple-element.73.refs_1_, ...), custom_call_target="tpu_custom_call" | custom-call | tf_op jit(solution)/shard_map/pallas_call | solution.py:502
  104.8 4.0 %collective-permute-start.13 = (f32[4,64]{1,0:T(4,128)S(1)}, f32[4,64]{1,0:T(4,128)S(1)}, u32[]{:S(2)}, u32[]{:S(2)}) collective-permute-start(f32[4,64]{1,0:T(4,128)S(1)} %get-tuple-element.79), channel_id=1, source_target_pairs={{1,2},{3,4},{5,6},{7,8},{9,10},{11,12},{13,14},{2,1},{4,3},{6,5},{... | collective-permute-start | bytes 3080 | tf_op jit(solution)/shard_map/ppermute | solution.py:413
  108.8 0.1 collective-permute-start.14
  108.9 2.3 %collective-permute-done.13.far_ref = f32[4,64]{1,0:T(4,128)S(1)} collective-permute-done((f32[4,64]{1,0:T(4,128)S(1)}, f32[4,64]{1,0:T(4,128)S(1)}, u32[]{:S(2)}, u32[]{:S(2)}) %collective-permute-start.13) | collective-permute-done | bytes 1056 | tf_op jit(solution)/shard_map/ppermute | solution.py:413
  111.2 1.3 %collective-permute-done.14.near_ref = f32[4,64]{1,0:T(4,128)S(1)} collective-permute-done((f32[4,64]{1,0:T(4,128)S(1)}, f32[4,64]{1,0:T(4,128)S(1)}, u32[]{:S(2)}, u32[]{:S(2)}) %collective-permute-start.14) | collective-permute-done | bytes 1056 | tf_op jit(solution)/shard_map/ppermute | solution.py:407
  112.5 0.7 shard_map.85
  (9 shorter events, 0.1 us)
Async XLA Ops:
  21.9 15.5 %collective-permute-start = (bf16[16,176,128]{2,1,0:T(8,128)(2,1)S(1)}, bf16[16,176,128]{2,1,0:T(8,128)(2,1)S(1)}, u32[]{:S(2)}, u32[]{:S(2)}) collective-permute-start(bf16[16,176,128]{2,1,0:T(8,128)(2,1)S(1)} %all_to_all.10.got_ref.qg_a), channel_id=1, source_target_pairs={{0,16},{16,0},{1,17},{17,1},{2,18},{18,2},{3,19},{19,3},{4,20},{20... | collective-permute-start | bytes 2162696 | tf_op jit(solution)/shard_map/ppermute | solution.py:407
  22.0 8.9 %collective-permute-start.3 = (bf16[144,128]{1,0:T(8,128)(2,1)S(1)}, bf16[144,128]{1,0:T(8,128)(2,1)S(1)}, u32[]{:S(2)}, u32[]{:S(2)}) collective-permute-start(bf16[144,128]{1,0:T(8,128)(2,1)S(1)} %shard_map.74), channel_id=1, source_target_pairs={{0,12},{2,14},{4,8},{6,10},{8,4},{10,6},{12,0},{14,2},{1,13},{3,15... | collective-permute-start | bytes 110600 | tf_op jit(solution)/shard_map/ppermute | solution.py:407
  28.4 8.4 %collective-permute-start.2 = (bf16[144,128]{1,0:T(8,128)(2,1)S(1)}, bf16[144,128]{1,0:T(8,128)(2,1)S(1)}, u32[]{:S(2)}, u32[]{:S(2)}) collective-permute-start(bf16[144,128]{1,0:T(8,128)(2,1)S(1)} %shard_map.74), channel_id=1, source_target_pairs={{0,8},{2,10},{4,12},{6,14},{8,0},{10,2},{12,4},{14,6},{1,9},{3,11}... | collective-permute-start | bytes 110600 | tf_op jit(solution)/shard_map/ppermute | solution.py:407
  29.4 7.4 %collective-permute-start.1 = (bf16[144,128]{1,0:T(8,128)(2,1)S(1)}, bf16[144,128]{1,0:T(8,128)(2,1)S(1)}, u32[]{:S(2)}, u32[]{:S(2)}) collective-permute-start(bf16[144,128]{1,0:T(8,128)(2,1)S(1)} %shard_map.74), channel_id=1, source_target_pairs={{0,4},{2,6},{4,0},{6,2},{8,12},{10,14},{12,8},{14,10},{1,5},{3,7},... | collective-permute-start | bytes 110600 | tf_op jit(solution)/shard_map/ppermute | solution.py:407
  36.8 10.4 %collective-permute-start.4 = (bf16[4,144,128]{2,1,0:T(8,128)(2,1)S(1)}, bf16[4,144,128]{2,1,0:T(8,128)(2,1)S(1)}, u32[]{:S(2)}, u32[]{:S(2)}) collective-permute-start(bf16[4,144,128]{2,1,0:T(8,128)(2,1)S(1)} %pad_maximum_fusion.kv_ref), channel_id=1, source_target_pairs={{0,2},{2,0},{4,6},{6,4},{8,10},{10,8},{12,14},{14,12},{1,3},{3,1},... | collective-permute-start | bytes 442376 | tf_op jit(solution)/shard_map/ppermute | solution.py:407
  57.0 1.4 %collective-permute-start.5 = (f32[2,16,8,128]{3,2,1,0:T(8,128)S(1)}, f32[2,16,8,128]{3,2,1,0:T(8,128)S(1)}, u32[]{:S(2)}, u32[]{:S(2)}) collective-permute-start(f32[2,16,8,128]{3,2,1,0:T(8,128)S(1)} %shard_map.76.mine_ref), channel_id=1, source_target_pairs={{0,16},{16,0},{1,17},{17,1},{2,18},{18,2},{3,19},{19,3},{4,20},{20... | collective-permute-start | bytes 393224 | tf_op jit(solution)/shard_map/ppermute | solution.py:407
  58.5 21.4 %slice-start = ((s8[7962624]{0:T(1024)(128)(4,1)}), s8[4194304]{0:T(1024)(128)(4,1)S(1)}, s32[]{:S(2)}) async-start(s8[7962624]{0:T(1024)(128)(4,1)} %bitcast.13), calls=%async_computation.2 | async-start | bytes 8388608
  64.3 8.3 %collective-permute-start.6 = (bf16[4,144,128]{2,1,0:T(8,128)(2,1)S(1)}, bf16[4,144,128]{2,1,0:T(8,128)(2,1)S(1)}, u32[]{:S(2)}, u32[]{:S(2)}) collective-permute-start(bf16[4,144,128]{2,1,0:T(8,128)(2,1)S(1)} %get-tuple-element.53), channel_id=1, source_target_pairs={{0,2},{2,0},{4,6},{6,4},{8,10},{10,8},{12,14},{14,12},{1,3},{3,1},... | collective-permute-start | bytes 442376 | tf_op jit(solution)/shard_map/ppermute | solution.py:407
  66.1 13.8 %slice-start.1 = ((s8[7962624]{0:T(1024)(128)(4,1)}), s8[3768320]{0:T(1024)(128)(4,1)S(1)}, s32[]{:S(2)}) async-start(s8[7962624]{0:T(1024)(128)(4,1)} %bitcast.13), calls=%async_computation.3 | async-start | bytes 7536640
  66.1 13.8 %copy-start = (bf16[256,1152]{1,0:T(8,128)(2,1)S(1)}, bf16[256,1152]{1,0:T(8,128)(2,1)}, u32[]{:S(2)}) copy-start(bf16[256,1152]{1,0:T(8,128)(2,1)} %patch_ref.2) | copy-start | bytes 1769476
  72.6 12.6 %collective-permute-start.7 = (f32[16,80,128]{2,1,0:T(8,128)S(1)}, f32[16,80,128]{2,1,0:T(8,128)S(1)}, u32[]{:S(2)}, u32[]{:S(2)}) collective-permute-start(f32[16,80,128]{2,1,0:T(8,128)S(1)} %get-tuple-element.55), channel_id=1, source_target_pairs={{0,16},{16,0},{1,17},{17,1},{2,18},{18,2},{3,19},{19,3},{4,20},{20... | collective-permute-start | bytes 1966088 | tf_op jit(solution)/shard_map/ppermute | solution.py:407
  72.7 12.5 %collective-permute-start.8 = (f32[16,24,128]{2,1,0:T(8,128)S(1)}, f32[16,24,128]{2,1,0:T(8,128)S(1)}, u32[]{:S(2)}, u32[]{:S(2)}) collective-permute-start(f32[16,24,128]{2,1,0:T(8,128)S(1)} %get-tuple-element.57), channel_id=1, source_target_pairs={{0,16},{16,0},{1,17},{17,1},{2,18},{18,2},{3,19},{19,3},{4,20},{20... | collective-permute-start | bytes 589832 | tf_op jit(solution)/shard_map/ppermute | solution.py:407
  73.3 10.6 %collective-permute-start.11 = (bf16[144,128]{1,0:T(8,128)(2,1)S(1)}, bf16[144,128]{1,0:T(8,128)(2,1)S(1)}, u32[]{:S(2)}, u32[]{:S(2)}) collective-permute-start(bf16[144,128]{1,0:T(8,128)(2,1)S(1)} %get-tuple-element.81), channel_id=1, source_target_pairs={{0,12},{2,14},{4,8},{6,10},{8,4},{10,6},{12,0},{14,2},{1,13},{3,15... | collective-permute-start | bytes 110600 | tf_op jit(solution)/shard_map/ppermute | solution.py:407
  74.9 9.0 %collective-permute-start.10 = (bf16[144,128]{1,0:T(8,128)(2,1)S(1)}, bf16[144,128]{1,0:T(8,128)(2,1)S(1)}, u32[]{:S(2)}, u32[]{:S(2)}) collective-permute-start(bf16[144,128]{1,0:T(8,128)(2,1)S(1)} %get-tuple-element.82), channel_id=1, source_target_pairs={{0,8},{2,10},{4,12},{6,14},{8,0},{10,2},{12,4},{14,6},{1,9},{3,11}... | collective-permute-start | bytes 110600 | tf_op jit(solution)/shard_map/ppermute | solution.py:407
  77.9 6.0 %collective-permute-start.9 = (bf16[144,128]{1,0:T(8,128)(2,1)S(1)}, bf16[144,128]{1,0:T(8,128)(2,1)S(1)}, u32[]{:S(2)}, u32[]{:S(2)}) collective-permute-start(bf16[144,128]{1,0:T(8,128)(2,1)S(1)} %get-tuple-element.83), channel_id=1, source_target_pairs={{0,4},{2,6},{4,0},{6,2},{8,12},{10,14},{12,8},{14,10},{1,5},{3,7},... | collective-permute-start | bytes 110600 | tf_op jit(solution)/shard_map/ppermute | solution.py:407
  83.9 1.3 %collective-permute-start.12 = (bf16[144,128]{1,0:T(8,128)(2,1)S(1)}, bf16[144,128]{1,0:T(8,128)(2,1)S(1)}, u32[]{:S(2)}, u32[]{:S(2)}) collective-permute-start(bf16[144,128]{1,0:T(8,128)(2,1)S(1)} %shard_map.82.keys_ref), channel_id=1, source_target_pairs={{0,16},{16,0},{1,17},{17,1},{2,18},{18,2},{3,19},{19,3},{4,20},{20... | collective-permute-start | bytes 110600 | tf_op jit(solution)/shard_map/ppermute | solution.py:407
  104.8 6.4 %collective-permute-start.13 = (f32[4,64]{1,0:T(4,128)S(1)}, f32[4,64]{1,0:T(4,128)S(1)}, u32[]{:S(2)}, u32[]{:S(2)}) collective-permute-start(f32[4,64]{1,0:T(4,128)S(1)} %get-tuple-element.79), channel_id=1, source_target_pairs={{1,2},{3,4},{5,6},{7,8},{9,10},{11,12},{13,14},{2,1},{4,3},{6,5},{... | collective-permute-start | bytes 3080 | tf_op jit(solution)/shard_map/ppermute | solution.py:413
  108.8 3.7 %collective-permute-start.14 = (f32[4,64]{1,0:T(4,128)S(1)}, f32[4,64]{1,0:T(4,128)S(1)}, u32[]{:S(2)}, u32[]{:S(2)}) collective-permute-start(f32[4,64]{1,0:T(4,128)S(1)} %get-tuple-element.80), channel_id=1, source_target_pairs={{0,1},{1,0},{2,3},{3,2},{4,5},{5,4},{6,7},{7,6},{8,9},{9,8},{10,11... | collective-permute-start | bytes 3080 | tf_op jit(solution)/shard_map/ppermute | solution.py:407

commit v7 on v6

--- a/solution.py
+++ b/solution.py
@@ -244,9 +244,12 @@
 
 
 def edge_rows(dq):
-    edges = jnp.concatenate([dq[0:DH, 0:COLS], dq[0:DH, TOK - COLS :]], axis=1)
-    pad = jnp.zeros((24, 32), f32)
-    return jnp.concatenate([edges[0:24], edges[24:48], edges[48:72], pad], axis=1)
+    lane = lax.broadcasted_iota(jnp.int32, (24, TOK), 1)
+    edges = pltpu.roll(dq[0:24], COLS, 1)
+    for n in (1, 2):
+        rolled = pltpu.roll(dq[24 * n : 24 * (n + 1)], COLS + 32 * n, 1)
+        edges = jnp.where(lane < 32 * n, edges, rolled)
+    return edges
 
 
 def second_kernel(
@@ -288,8 +291,7 @@
     dq = (dq_ref[...] + came_ref[...])[:, 0:DH] * SCALE
     above, below = beside((edge_ref[...] + came_edge_ref[...]) * SCALE, first)
     lane = lax.broadcasted_iota(jnp.int32, (HEADS, 24, 128), 2)
-    above = pltpu.roll(above, 128 - COLS, 2)
-    edges = jnp.where(lane % 32 < COLS, above, pltpu.roll(below, COLS, 2))
+    edges = jnp.where(lane % 32 < COLS, above, below)
     lanes = jnp.zeros((128, 128 - DH), f32)
     row = lax.broadcasted_iota(jnp.int32, (HEADS, CELLS, 128), 1)
 
@@ -305,7 +307,7 @@
     send_ref[...] = jnp.concatenate(parts, axis=1).astype(bf16)
 
 
-def weights_kernel(part, patch_ref, qkv_ref, high_ref, low_ref, qkv_s, sems):
+def weights_kernel(part, patch_ref, qkv_ref, out_ref, qkv_s, sems):
     step = 128
     copies = []
     for n in range(D // step):
@@ -319,69 +321,87 @@
     both = both.reshape(16, 2, 8, D)
     both = jnp.concatenate([both[:, 0].reshape(128, D), both[:, 1].reshape(128, D)])
     high = both.astype(bf16)
-    high_ref[...] = high
-    low_ref[...] = (both - high.astype(f32)).astype(bf16)
+    out_ref[0:256] = high
+    out_ref[256:512] = (both - high.astype(f32)).astype(bf16)
+
+
+def split(x):
+    high = x.astype(bf16)
+    return high, (x - high.astype(f32)).astype(bf16)
+
+
+def iota(shape, dim):
+    return lax.broadcasted_iota(jnp.int32, shape, dim)
+
+
+def one_hot(where, value=1.0):
+    return jnp.where(where, value, 0.0).astype(bf16)
 
 
 def embed_kernel(back_ref, *refs):
-    weights, (center_ref, near_out, far_out, joined, sheet) = refs[:6], refs[6:]
-    cols = (((0,), (0,)), ((), ()))
-    cell = lax.broadcasted_iota(jnp.int32, (2 * CELLS, 2 * TOK), 0)
-    token = lax.broadcasted_iota(jnp.int32, (2 * CELLS, 2 * TOK), 1)
+    weights, (center_ref, near_out, far_out, joined, pooled, sheet) = refs[:3], refs[3:]
+    for h in range(0, HEADS, 2):
+        pair = []
+        wide = []
+        for n in (h, h + 1):
+            pair.append(back_ref[n, 0:TOK].astype(f32)[0:DH])
+            edges = back_ref[n, 64 : 64 + 32].astype(f32)[DH - 64 :]
+            wide += [edges, pltpu.roll(edges, 96, 1), pltpu.roll(edges, 64, 1)]
+        rows = slice(h * DH, (h + 2) * DH)
+        joined[rows, 0:TOK] = jnp.concatenate(pair).astype(bf16)
+        joined[rows, TOK:] = jnp.concatenate(wide).astype(bf16)
+    at = DH + 24
+    group = iota((DH, 128), 1) // 16
+    for h in range(0, HEADS, 4):
+        cells = []
+        for part in (0, 1):
+            for n in range(h, h + 4):
+                head = back_ref[n, at:].astype(f32)
+                cells += [head[part * CELLS : (part + 1) * CELLS], head[16 + part * CELLS : 16 + (part + 1) * CELLS]]
+        cells = jnp.concatenate(cells).T[0:DH]
+        for part in (0, 1):
+            for n in (0, 2):
+                two = [jnp.where(group == 4 * part + k, cells, 0.0) for k in (n, n + 1)]
+                rows = part * D + (h + n) * DH
+                pooled[rows : rows + 2 * DH] = jnp.concatenate(two).astype(bf16)
+    patch = jnp.dot(weights[0][...], joined[...], preferred_element_type=f32)
+    patch = patch[0:256] + patch[256:512]
+    cells = jnp.dot(weights[1][...], pooled[0:D], preferred_element_type=f32)
+    cells = cells + jnp.dot(weights[2][...], pooled[D:], preferred_element_type=f32)
+    cells = jnp.concatenate(split(cells[0:256] + cells[256:512]), axis=1)
+    cell, token = iota((256, 256), 0) % 16, iota((256, 256), 1)
     mine = token // (POOL * COLS) * 4 + token % COLS // POOL
     beyond = CELLS + (token - TOK) // COLS * 4 + token % COLS // POOL
     holds = (cell == jnp.where(token < TOK, mine, beyond)) & (token < EXTENDED)
-    spread = jnp.where(holds, 1.0 / POOL**2, 0.0).astype(bf16)
-    for h in range(HEADS):
-        head = back_ref[h].astype(f32)
-        rows = slice(h * DH, (h + 1) * DH)
-        joined[rows, 0:TOK] = head[0:DH]
-        edges = head[DH : DH + 24]
-        edges = [edges, pltpu.roll(edges, 96, 1), pltpu.roll(edges, 64, 1)]
-        joined[rows, TOK:] = jnp.concatenate(edges)
-        for part in (0, 1):
-            at = DH + 24 + part * CELLS
-            pooled = jnp.concatenate([head[at : at + CELLS], head[at + 16 : at + 16 + CELLS]]).astype(bf16)
-            wide = lax.dot_general(pooled, spread, cols, preferred_element_type=f32)
-            joined[(part + 1) * D + h * DH : (part + 1) * D + (h + 1) * DH] = wide[0:DH]
-    values = joined[...].astype(bf16)
-    patch = jnp.zeros((256, 2 * TOK), f32)
-    for n, weight in enumerate(weights):
-        rows = slice(n // 2 * D, (n // 2 + 1) * D)
-        patch = patch + jnp.dot(weight[...], values[rows], preferred_element_type=f32)
-    sides = []
-    for side in (0, 1):
-        rows = slice(side * 128, (side + 1) * 128)
-        sides += [patch[rows, 0:TOK].T, patch[rows, TOK:].T[0 : EXTENDED - TOK]]
-    patch = jnp.concatenate(sides)
-    high = patch.astype(bf16)
-    rest = patch - high.astype(f32)
-    mid = rest.astype(bf16)
-    low = (rest - mid.astype(f32)).astype(bf16)
-    lane = lax.broadcasted_iota(jnp.int32, (2 * EXTENDED, 256), 1)
-    row = lax.broadcasted_iota(jnp.int32, (2 * EXTENDED, 256), 0)
-    here = lane % 128 // 8 == row % COLS
+    patch = patch + jnp.dot(cells, one_hot(holds, 1.0 / POOL**2), preferred_element_type=f32)
+    to, token = iota((EXTENDED, 256), 0), iota((EXTENDED, 256), 1)
+    far = to - TOK
+    column = jnp.where(to < TOK, to // 8, far // 8 * 4 + far % 8 // 2)
+    source = jnp.where(to < TOK, to % 8 * COLS, TOK + far % 2 * COLS) + column
+    turned = lax.dot_general(
+        one_hot(token == source), jnp.concatenate(split(patch)), NT, preferred_element_type=f32
+    ).astype(bf16)
     sheet[...] = jnp.zeros_like(sheet)
-    parts = jnp.concatenate([high, mid, low], axis=1)
-    to = lax.broadcasted_iota(jnp.int32, (128, 256), 1)
-    at = lax.broadcasted_iota(jnp.int32, (128, 256), 0)
+    here = iota((EXTENDED, 256), 1) % 128 // 8 == column
+    to, at = iota((256, 256), 1), iota((256, 256), 0) % 128
     for pair in range(8):
-        tile = (to // 128 + 2 * pair == at // 8) & (to % 8 == at % 8)
-        tile = jnp.where(tile, 1.0, 0.0).astype(bf16)
-        tile = jnp.concatenate([tile] * 3)
-        wide = jnp.dot(parts, tile, preferred_element_type=f32)
-        wide = jnp.where(here, wide, 0.0)
-        wide = jnp.sum(wide.reshape(2 * (ROWS + 2), COLS, 256), axis=1)
-        for k in (0, 1):
-            u = 2 * pair + k
-            for side in (0, 1):
-                at_side = side * (ROWS + 2)
-                piece = wide[at_side : at_side + ROWS + 2, k * 128 : (k + 1) * 128]
-                sheet[side, pl.ds(u, ROWS, stride=8), :] += piece[0:ROWS]
+        tile = one_hot((to // 128 + 2 * pair == at // 8) & (to % 8 == at % 8))
+        for side in (0, 1):
+            parts = [turned[:, n * 256 + side * 128 : n * 256 + (side + 1) * 128] for n in (0, 1)]
+            wide = jnp.dot(jnp.concatenate(parts, axis=1), tile, preferred_element_type=f32)
+            wide = jnp.where(here, wide, 0.0)
+            own = jnp.sum(wide[0:TOK].reshape(COLS, ROWS, 256), axis=0)
+            edge = jnp.sum(wide[TOK:].reshape(4, 8, 256), axis=0)
+            edge = edge + pltpu.roll(edge, 4, 0)
+            edge = edge + pltpu.roll(edge, 2, 0)
+            for k in (0, 1):
+                u = 2 * pair + k
+                lanes = slice(k * 128, (k + 1) * 128)
+                sheet[side, pl.ds(u, ROWS, stride=8), :] += own[:, lanes]
                 if u >= 12:
-                    sheet[side, u - 8 : u - 7, :] += piece[ROWS : ROWS + 1]
+                    sheet[side, u - 8 : u - 7, :] += edge[0:1, lanes]
                 if u < 4:
-                    sheet[side, 64 + u : 65 + u, :] += piece[ROWS + 1 :]
+                    sheet[side, 64 + u : 65 + u, :] += edge[1:2, lanes]
     left = sheet[0, 4:68]
     right = sheet[1, 4:68]
     lane = lax.broadcasted_iota(jnp.int32, left.shape, 1)
@@ -419,10 +439,9 @@
 
 
 def combined_weights(w_qkv, w_patch, part):
-    shape = jax.ShapeDtypeStruct((256, D), bf16)
     return call(
         functools.partial(weights_kernel, part),
-        [shape, shape],
+        jax.ShapeDtypeStruct((512, D), bf16),
         12,
         [pltpu.VMEM((D, D), bf16), pltpu.SemaphoreType.DMA((D // 128,))],
         [WHOLE, ANYWHERE],
@@ -490,7 +509,7 @@
     mine = grads + came.astype(f32)
     mine, w_qkv, w_patch = lax.optimization_barrier((mine, w_qkv, w_patch))
     came = [swapped(mine[n].astype(bf16), "z", 2 * n) for n in (1, 2, 3)]
-    weights = [w for part in range(3) for w in combined_weights(w_qkv, w_patch, part)]
+    weights = [combined_weights(w_qkv, w_patch, part) for part in range(3)]
     came, weights = lax.optimization_barrier((came, weights))
     keys = call(keys_sum_kernel, jax.ShapeDtypeStruct((2 * DH, 128), bf16), 4)(mine[0:1], *came)
     other = swapped(keys, "c", 1)
@@ -503,7 +522,7 @@
         embed_kernel,
         [jax.ShapeDtypeStruct((64, 128), f32), strip, strip],
         28,
-        [pltpu.VMEM((3 * D, 2 * TOK), f32), pltpu.VMEM((2, 72, 128), f32)],
+        [pltpu.VMEM((D, 2 * TOK), bf16), pltpu.VMEM((2 * D, 128), bf16), pltpu.VMEM((2, 72, 128), f32)],
     )(back, *weights)
     return call(cols_kernel, jax.ShapeDtypeStruct((64, 128), f32), 4)(
         center, neighbours(to_far, COL), swapped(to_near, "yl", 1)

time: 113 us -> 112 us (level)
  Pallas kernels: 43.4 us -> 41.6 us
    pallas_call x1, Pallas kernels: 4.02 us -> 2.53 us  [on_device(): call(embed_kernel, [jax.ShapeDtypeStruct((64, 128), f32), strip, strip],...]
where the time goes in v7:
time: 112 us; the launch traced here: 111 us
  Pallas kernels  41.6 us (37%)
  blocking collectives  34.7 us (31%)
  starting transfers between devices  22.7 us (20%)
  waiting for transfers between devices  12 us (11%)
    all_to_all x1, blocking collectives, on_device(): got = lax.all_to_all(send, HEAD_AXES, 0, 0, tiled=True)  19.4 us
    ppermute x14, starting transfers between devices, swapped(): return lax.ppermute(x, axis, [(i, i ^ by) for i in range(peers)])  18.7 us
    all_to_all x1, blocking collectives, on_device(): back = lax.all_to_all(send, HEAD_AXES, 0, 0, tiled=True)  15.3 us
    pallas_call x1, Pallas kernels, on_device(): call(odd_sums_kernel, sums, 24, [keys], cost_estimate=cost(1))  9.89 us
    ppermute x14, waiting for transfers between devices, swapped(): return lax.ppermute(x, axis, [(i, i ^ by) for i in range(peers)])  9.79 us
    pallas_call x1, Pallas kernels, on_device(): call(even_sums_kernel, sums, 24, [keys], cost_estimate=cost(1))  9.69 us
    pallas_call x1, Pallas kernels, on_device(): call(second_kernel, dq + edges + [jax.ShapeDtypeStruct(block, f32)], 28,...  6.2 us
    pallas_call x1, Pallas kernels, on_device(): call(first_kernel, [sums] + dq + [jax.ShapeDtypeStruct(block, bf16)], 28,...  5.85 us
  transfers between devices with their start and end apart: 15, of which 5 were waited for; matrix products, arithmetic and copies ran while one was open for 0% of the time, Pallas kernels for 18%

profile of v7, /device:TPU:8, one launch (start us, length us, event | category | flops | bytes accessed | tf_op | source)
XLA Modules:
  0.0 111.4 jit_solution(6048540054154648198)
XLA Ops:
  0.0 2.5 %shard_map.73 = bf16[16,176,128]{2,1,0:T(8,128)(2,1)} custom-call(bf16[128,1152]{1,0:T(8,128)(2,1)} %bitcast.16, bf16[128,1152]{1,0:T(8,128)(2,1)} %bitcast.17, bf16[128,1152]{1,0:T(8,128)(2,1)} %bitcast.18, bf16[2,4,1152]{2,1,0:T(4,128)(2,1)} %k_in.1, bf16[2,4,1152]{2,1,0:T(4,128)(2,1)} %v_in.1), custom_call_target="tpu_custom_call" | custom-call | tf_op jit(solution)/shard_map/pallas_call | solution.py:457
  2.5 19.4 %all_to_all.10.got_ref.qg_a = bf16[16,176,128]{2,1,0:T(8,128)(2,1)S(1)} all-to-all(bf16[16,176,128]{2,1,0:T(8,128)(2,1)} %shard_map.73), channel_id=1, replica_groups=mesh['yh'=2,'x'=4,'c'=2,'z'=8,'yl'=2] {'yh','x','yl'}, dimensions={0} | all-to-all | bytes 1441792 | tf_op jit(solution)/shard_map/all_to_all | solution.py:471
  21.9 0.0 collective-permute-start
  21.9 0.1 shard_map.74
  22.0 6.4 %collective-permute-start.3 = (bf16[144,128]{1,0:T(8,128)(2,1)S(1)}, bf16[144,128]{1,0:T(8,128)(2,1)S(1)}, u32[]{:S(2)}, u32[]{:S(2)}) collective-permute-start(bf16[144,128]{1,0:T(8,128)(2,1)S(1)} %shard_map.74), channel_id=1, source_target_pairs={{0,12},{2,14},{4,8},{6,10},{8,4},{10,6},{12,0},{14,2},{1,13},{3,15... | collective-permute-start | bytes 110600 | tf_op jit(solution)/shard_map/ppermute | solution.py:427
  28.4 1.0 collective-permute-start.2
  29.4 1.5 %collective-permute-start.1 = (bf16[144,128]{1,0:T(8,128)(2,1)S(1)}, bf16[144,128]{1,0:T(8,128)(2,1)S(1)}, u32[]{:S(2)}, u32[]{:S(2)}) collective-permute-start(bf16[144,128]{1,0:T(8,128)(2,1)S(1)} %shard_map.74), channel_id=1, source_target_pairs={{0,4},{2,6},{4,0},{6,2},{8,12},{10,14},{12,8},{14,10},{1,5},{3,7},... | collective-permute-start | bytes 110600 | tf_op jit(solution)/shard_map/ppermute | solution.py:427
  30.8 0.0 collective-permute-done.3
  30.8 5.9 %collective-permute-done.2 = bf16[144,128]{1,0:T(8,128)(2,1)S(1)} collective-permute-done((bf16[144,128]{1,0:T(8,128)(2,1)S(1)}, bf16[144,128]{1,0:T(8,128)(2,1)S(1)}, u32[]{:S(2)}, u32[]{:S(2)}) %collective-permute-start.2) | collective-permute-done | bytes 36896 | tf_op jit(solution)/shard_map/ppermute | solution.py:427
  36.7 0.0 collective-permute-done.1
  36.8 0.6 collective-permute-start.4
  37.4 0.0 collective-permute-done.qg_b
  37.4 9.7 %shard_map.75.even_ref = f32[2,16,8,128]{3,2,1,0:T(8,128)S(1)} custom-call(bf16[16,176,128]{2,1,0:T(8,128)(2,1)S(1)} %all_to_all.10.got_ref.qg_a, bf16[16,176,128]{2,1,0:T(8,128)(2,1)S(1)} %collective-permute-done.qg_b, bf16[4,144,128]{2,1,0:T(8,128)(2,1)S(1)} %pad_maximum_fusion.kv_ref), custom_call_target="tpu_custom_call" | custom-call | flops 1073741824 | bytes 1048576 | tf_op jit(solution)/shard_map/pallas_call | solution.py:485
  47.1 0.0 collective-permute-done.4.kv_ref
  47.1 9.9 %shard_map.76.mine_ref = f32[2,16,8,128]{3,2,1,0:T(8,128)S(1)} custom-call(bf16[16,176,128]{2,1,0:T(8,128)(2,1)S(1)} %all_to_all.10.got_ref.qg_a, bf16[16,176,128]{2,1,0:T(8,128)(2,1)S(1)} %collective-permute-done.qg_b, bf16[4,144,128]{2,1,0:T(8,128)(2,1)S(1)} %collective-permute-done.4.kv_ref, f32[2,16,8,128]{3,2,1,0:T(8,128)S(1)} %shard_map.75.even_ref), custom_call_target="tpu_custom_call" | custom-call | flops 1073741824 | bytes 1048576 | tf_op jit(solution)/shard_map/pallas_call | solution.py:487
  57.0 0.1 collective-permute-start.5
  57.1 1.3 %collective-permute-done.5.came_ref = f32[2,16,8,128]{3,2,1,0:T(8,128)S(1)} collective-permute-done((f32[2,16,8,128]{3,2,1,0:T(8,128)S(1)}, f32[2,16,8,128]{3,2,1,0:T(8,128)S(1)}, u32[]{:S(2)}, u32[]{:S(2)}) %collective-permute-start.5) | collective-permute-done | bytes 131104 | tf_op jit(solution)/shard_map/ppermute | solution.py:427
  58.4 5.8 %shard_map.77 = (f32[2,16,8,128]{3,2,1,0:T(8,128)S(1)}, f32[16,80,128]{2,1,0:T(8,128)S(1)}, f32[16,80,128]{2,1,0:T(8,128)S(1)}, bf16[4,144,128]{2,1,0:T(8,128)(2,1)S(1)}) custom-call(bf16[16,176,128]{2,1,0:T(8,128)(2,1)S(1)} %all_to_all.10.got_ref.qg_a, bf16[16,176,128]{2,1,0:T(8,128)(2,1)S(1)} %collective-permute-done.qg_b, ...), custom_call_target="tpu_custom_call" | custom-call | flops 5368709120 | bytes 1048576 | tf_op jit(solution)/shard_map/pallas_call | solution.py:493
  64.3 1.8 %collective-permute-start.6 = (bf16[4,144,128]{2,1,0:T(8,128)(2,1)S(1)}, bf16[4,144,128]{2,1,0:T(8,128)(2,1)S(1)}, u32[]{:S(2)}, u32[]{:S(2)}) collective-permute-start(bf16[4,144,128]{2,1,0:T(8,128)(2,1)S(1)} %get-tuple-element.44), channel_id=1, source_target_pairs={{0,2},{2,0},{4,6},{6,4},{8,10},{10,8},{12,14},{14,12},{1,3},{3,1},... | collective-permute-start | bytes 442376 | tf_op jit(solution)/shard_map/ppermute | solution.py:427
  66.0 6.2 %shard_map.78 = (f32[16,80,128]{2,1,0:T(8,128)S(1)}, f32[16,80,128]{2,1,0:T(8,128)S(1)}, f32[16,24,128]{2,1,0:T(8,128)S(1)}, f32[16,24,128]{2,1,0:T(8,128)S(1)}, f32[4,144,128]{2,1,0:T(8,128)S(1)}) custom-call(bf16[16,176,128]{2,1,0:T(8,128)(2,1)S(1)} %all_to_all.10.got_ref.qg_a, bf16[16,176,128]{2,1,0:T(8,128)(2,1)S(1)} %collective-permute-done.qg_b, ...), custom_call_target="tpu_custom_call" | custom-call | flops 5368709120 | bytes 1048576 | tf_op jit(solution)/shard_map/pallas_call | solution.py:498
  72.2 0.0 copy-start
  72.3 0.0 collective-permute-done.6
  72.3 0.1 collective-permute-start.7
  72.4 0.5 collective-permute-start.8
  72.9 1.6 %collective-permute-start.11 = (bf16[144,128]{1,0:T(8,128)(2,1)S(1)}, bf16[144,128]{1,0:T(8,128)(2,1)S(1)}, u32[]{:S(2)}, u32[]{:S(2)}) collective-permute-start(bf16[144,128]{1,0:T(8,128)(2,1)S(1)} %get-tuple-element.63), channel_id=1, source_target_pairs={{0,12},{2,14},{4,8},{6,10},{8,4},{10,6},{12,0},{14,2},{1,13},{3,15... | collective-permute-start | bytes 110600 | tf_op jit(solution)/shard_map/ppermute | solution.py:427
  74.5 3.0 %collective-permute-start.10 = (bf16[144,128]{1,0:T(8,128)(2,1)S(1)}, bf16[144,128]{1,0:T(8,128)(2,1)S(1)}, u32[]{:S(2)}, u32[]{:S(2)}) collective-permute-start(bf16[144,128]{1,0:T(8,128)(2,1)S(1)} %get-tuple-element.64), channel_id=1, source_target_pairs={{0,8},{2,10},{4,12},{6,14},{8,0},{10,2},{12,4},{14,6},{1,9},{3,11}... | collective-permute-start | bytes 110600 | tf_op jit(solution)/shard_map/ppermute | solution.py:427
  77.6 1.9 %collective-permute-start.9 = (bf16[144,128]{1,0:T(8,128)(2,1)S(1)}, bf16[144,128]{1,0:T(8,128)(2,1)S(1)}, u32[]{:S(2)}, u32[]{:S(2)}) collective-permute-start(bf16[144,128]{1,0:T(8,128)(2,1)S(1)} %get-tuple-element.65), channel_id=1, source_target_pairs={{0,4},{2,6},{4,0},{6,2},{8,12},{10,14},{12,8},{14,10},{1,5},{3,7},... | collective-permute-start | bytes 110600 | tf_op jit(solution)/shard_map/ppermute | solution.py:427
  79.5 0.0 slice-done
  79.5 0.0 slice-done.1
  79.5 0.0 copy-done
  79.6 1.3 %shard_map.81.refs_2_ = bf16[512,1152]{1,0:T(8,128)(2,1)S(1)} custom-call(bf16[256,1152]{1,0:T(8,128)(2,1)S(1)} %copy-done, bf16[1152,3456]{1,0:T(8,128)(2,1)S(1)} %bitcast.14), custom_call_target="tpu_custom_call" | custom-call | flops 1048576 | bytes 65536 | tf_op jit(solution)/shard_map/pallas_call | solution.py:442
  80.9 1.3 %shard_map.80.refs_1_ = bf16[512,1152]{1,0:T(8,128)(2,1)S(1)} custom-call(bf16[256,1152]{1,0:T(8,128)(2,1)S(1)} %copy-done, bf16[1152,3456]{1,0:T(8,128)(2,1)S(1)} %bitcast.14), custom_call_target="tpu_custom_call" | custom-call | flops 1048576 | bytes 65536 | tf_op jit(solution)/shard_map/pallas_call | solution.py:442
  82.2 1.3 %shard_map.79.refs_0_ = bf16[512,1152]{1,0:T(8,128)(2,1)S(1)} custom-call(bf16[256,1152]{1,0:T(8,128)(2,1)S(1)} %copy-done, bf16[1152,3456]{1,0:T(8,128)(2,1)S(1)} %bitcast.14), custom_call_target="tpu_custom_call" | custom-call | flops 1048576 | bytes 65536 | tf_op jit(solution)/shard_map/pallas_call | solution.py:442
  83.5 0.0 collective-permute-done.11.came_c
  83.5 0.0 collective-permute-done.10.came_b
  83.6 0.0 collective-permute-done.9.came_a
  83.6 0.1 collective-permute-start.12
  83.7 1.2 %collective-permute-done.12.other_ref = bf16[144,128]{1,0:T(8,128)(2,1)S(1)} collective-permute-done((bf16[144,128]{1,0:T(8,128)(2,1)S(1)}, bf16[144,128]{1,0:T(8,128)(2,1)S(1)}, u32[]{:S(2)}, u32[]{:S(2)}) %collective-permute-start.12) | collective-permute-done | bytes 36896 | tf_op jit(solution)/shard_map/ppermute | solution.py:427
  84.9 0.0 collective-permute-done.8.came_edge_ref
  84.9 0.0 collective-permute-done.7.came_ref
  84.9 0.2 shard_map.83
  85.1 15.3 %all_to_all.11.back_ref = bf16[16,128,128]{2,1,0:T(8,128)(2,1)S(1)} all-to-all(bf16[16,128,128]{2,1,0:T(8,128)(2,1)S(1)} %shard_map.83), channel_id=1, replica_groups=mesh['yh'=2,'x'=4,'c'=2,'z'=8,'yl'=2] {'yh','x','yl'}, dimensions={0} | all-to-all | bytes 1048576 | tf_op jit(solution)/shard_map/all_to_all | solution.py:519
  100.4 2.5 %shard_map.84 = (f32[64,128]{1,0:T(8,128)S(1)}, f32[4,64]{1,0:T(4,128)S(1)}, f32[4,64]{1,0:T(4,128)S(1)}) custom-call(bf16[16,128,128]{2,1,0:T(8,128)(2,1)S(1)} %all_to_all.11.back_ref, bf16[512,1152]{1,0:T(8,128)(2,1)S(1)} %shard_map.79.refs_0_, bf16[512,1152]{1,0:T(8,128)(2,1)S(1)} %shard_map.80.refs_1_, bf16[512,1152]{1,0:T(8,128)(2,1)S(1)} %shard_map.81.refs_2_), custom_call_target="tpu_custom_call" | custom-call | tf_op jit(solution)/shard_map/pallas_call | solution.py:521
  103.0 4.0 %collective-permute-start.13 = (f32[4,64]{1,0:T(4,128)S(1)}, f32[4,64]{1,0:T(4,128)S(1)}, u32[]{:S(2)}, u32[]{:S(2)}) collective-permute-start(f32[4,64]{1,0:T(4,128)S(1)} %get-tuple-element.61), channel_id=1, source_target_pairs={{1,2},{3,4},{5,6},{7,8},{9,10},{11,12},{13,14},{2,1},{4,3},{6,5},{... | collective-permute-start | bytes 3080 | tf_op jit(solution)/shard_map/ppermute | solution.py:433
  107.0 0.1 collective-permute-start.14
  107.1 2.2 %collective-permute-done.13.far_ref = f32[4,64]{1,0:T(4,128)S(1)} collective-permute-done((f32[4,64]{1,0:T(4,128)S(1)}, f32[4,64]{1,0:T(4,128)S(1)}, u32[]{:S(2)}, u32[]{:S(2)}) %collective-permute-start.13) | collective-permute-done | bytes 1056 | tf_op jit(solution)/shard_map/ppermute | solution.py:433
  109.3 1.3 %collective-permute-done.14.near_ref = f32[4,64]{1,0:T(4,128)S(1)} collective-permute-done((f32[4,64]{1,0:T(4,128)S(1)}, f32[4,64]{1,0:T(4,128)S(1)}, u32[]{:S(2)}, u32[]{:S(2)}) %collective-permute-start.14) | collective-permute-done | bytes 1056 | tf_op jit(solution)/shard_map/ppermute | solution.py:427
  110.7 0.7 shard_map.85
  (9 shorter events, 0.1 us)
Async XLA Ops:
  21.9 15.5 %collective-permute-start = (bf16[16,176,128]{2,1,0:T(8,128)(2,1)S(1)}, bf16[16,176,128]{2,1,0:T(8,128)(2,1)S(1)}, u32[]{:S(2)}, u32[]{:S(2)}) collective-permute-start(bf16[16,176,128]{2,1,0:T(8,128)(2,1)S(1)} %all_to_all.10.got_ref.qg_a), channel_id=1, source_target_pairs={{0,16},{16,0},{1,17},{17,1},{2,18},{18,2},{3,19},{19,3},{4,20},{20... | collective-permute-start | bytes 2162696 | tf_op jit(solution)/shard_map/ppermute | solution.py:427
  22.0 8.9 %collective-permute-start.3 = (bf16[144,128]{1,0:T(8,128)(2,1)S(1)}, bf16[144,128]{1,0:T(8,128)(2,1)S(1)}, u32[]{:S(2)}, u32[]{:S(2)}) collective-permute-start(bf16[144,128]{1,0:T(8,128)(2,1)S(1)} %shard_map.74), channel_id=1, source_target_pairs={{0,12},{2,14},{4,8},{6,10},{8,4},{10,6},{12,0},{14,2},{1,13},{3,15... | collective-permute-start | bytes 110600 | tf_op jit(solution)/shard_map/ppermute | solution.py:427
  28.4 8.4 %collective-permute-start.2 = (bf16[144,128]{1,0:T(8,128)(2,1)S(1)}, bf16[144,128]{1,0:T(8,128)(2,1)S(1)}, u32[]{:S(2)}, u32[]{:S(2)}) collective-permute-start(bf16[144,128]{1,0:T(8,128)(2,1)S(1)} %shard_map.74), channel_id=1, source_target_pairs={{0,8},{2,10},{4,12},{6,14},{8,0},{10,2},{12,4},{14,6},{1,9},{3,11}... | collective-permute-start | bytes 110600 | tf_op jit(solution)/shard_map/ppermute | solution.py:427
  29.4 7.4 %collective-permute-start.1 = (bf16[144,128]{1,0:T(8,128)(2,1)S(1)}, bf16[144,128]{1,0:T(8,128)(2,1)S(1)}, u32[]{:S(2)}, u32[]{:S(2)}) collective-permute-start(bf16[144,128]{1,0:T(8,128)(2,1)S(1)} %shard_map.74), channel_id=1, source_target_pairs={{0,4},{2,6},{4,0},{6,2},{8,12},{10,14},{12,8},{14,10},{1,5},{3,7},... | collective-permute-start | bytes 110600 | tf_op jit(solution)/shard_map/ppermute | solution.py:427
  36.8 10.3 %collective-permute-start.4 = (bf16[4,144,128]{2,1,0:T(8,128)(2,1)S(1)}, bf16[4,144,128]{2,1,0:T(8,128)(2,1)S(1)}, u32[]{:S(2)}, u32[]{:S(2)}) collective-permute-start(bf16[4,144,128]{2,1,0:T(8,128)(2,1)S(1)} %pad_maximum_fusion.kv_ref), channel_id=1, source_target_pairs={{0,2},{2,0},{4,6},{6,4},{8,10},{10,8},{12,14},{14,12},{1,3},{3,1},... | collective-permute-start | bytes 442376 | tf_op jit(solution)/shard_map/ppermute | solution.py:427
  57.0 1.4 %collective-permute-start.5 = (f32[2,16,8,128]{3,2,1,0:T(8,128)S(1)}, f32[2,16,8,128]{3,2,1,0:T(8,128)S(1)}, u32[]{:S(2)}, u32[]{:S(2)}) collective-permute-start(f32[2,16,8,128]{3,2,1,0:T(8,128)S(1)} %shard_map.76.mine_ref), channel_id=1, source_target_pairs={{0,16},{16,0},{1,17},{17,1},{2,18},{18,2},{3,19},{19,3},{4,20},{20... | collective-permute-start | bytes 393224 | tf_op jit(solution)/shard_map/ppermute | solution.py:427
  64.3 8.0 %collective-permute-start.6 = (bf16[4,144,128]{2,1,0:T(8,128)(2,1)S(1)}, bf16[4,144,128]{2,1,0:T(8,128)(2,1)S(1)}, u32[]{:S(2)}, u32[]{:S(2)}) collective-permute-start(bf16[4,144,128]{2,1,0:T(8,128)(2,1)S(1)} %get-tuple-element.44), channel_id=1, source_target_pairs={{0,2},{2,0},{4,6},{6,4},{8,10},{10,8},{12,14},{14,12},{1,3},{3,1},... | collective-permute-start | bytes 442376 | tf_op jit(solution)/shard_map/ppermute | solution.py:427
  66.0 13.5 %slice-start = ((s8[7962624]{0:T(1024)(128)(4,1)}), s8[4194304]{0:T(1024)(128)(4,1)S(1)}, s32[]{:S(2)}) async-start(s8[7962624]{0:T(1024)(128)(4,1)} %bitcast.13), calls=%async_computation.2 | async-start | bytes 8388608
  66.0 13.5 %slice-start.1 = ((s8[7962624]{0:T(1024)(128)(4,1)}), s8[3768320]{0:T(1024)(128)(4,1)S(1)}, s32[]{:S(2)}) async-start(s8[7962624]{0:T(1024)(128)(4,1)} %bitcast.13), calls=%async_computation.3 | async-start | bytes 7536640
  72.2 7.3 %copy-start = (bf16[256,1152]{1,0:T(8,128)(2,1)S(1)}, bf16[256,1152]{1,0:T(8,128)(2,1)}, u32[]{:S(2)}) copy-start(bf16[256,1152]{1,0:T(8,128)(2,1)} %patch_ref.2) | copy-start | bytes 1769476
  72.3 12.6 %collective-permute-start.7 = (f32[16,80,128]{2,1,0:T(8,128)S(1)}, f32[16,80,128]{2,1,0:T(8,128)S(1)}, u32[]{:S(2)}, u32[]{:S(2)}) collective-permute-start(f32[16,80,128]{2,1,0:T(8,128)S(1)} %get-tuple-element.46), channel_id=1, source_target_pairs={{0,16},{16,0},{1,17},{17,1},{2,18},{18,2},{3,19},{19,3},{4,20},{20... | collective-permute-start | bytes 1966088 | tf_op jit(solution)/shard_map/ppermute | solution.py:427
  72.4 12.5 %collective-permute-start.8 = (f32[16,24,128]{2,1,0:T(8,128)S(1)}, f32[16,24,128]{2,1,0:T(8,128)S(1)}, u32[]{:S(2)}, u32[]{:S(2)}) collective-permute-start(f32[16,24,128]{2,1,0:T(8,128)S(1)} %get-tuple-element.48), channel_id=1, source_target_pairs={{0,16},{16,0},{1,17},{17,1},{2,18},{18,2},{3,19},{19,3},{4,20},{20... | collective-permute-start | bytes 589832 | tf_op jit(solution)/shard_map/ppermute | solution.py:427
  72.9 10.6 %collective-permute-start.11 = (bf16[144,128]{1,0:T(8,128)(2,1)S(1)}, bf16[144,128]{1,0:T(8,128)(2,1)S(1)}, u32[]{:S(2)}, u32[]{:S(2)}) collective-permute-start(bf16[144,128]{1,0:T(8,128)(2,1)S(1)} %get-tuple-element.63), channel_id=1, source_target_pairs={{0,12},{2,14},{4,8},{6,10},{8,4},{10,6},{12,0},{14,2},{1,13},{3,15... | collective-permute-start | bytes 110600 | tf_op jit(solution)/shard_map/ppermute | solution.py:427
  74.5 9.0 %collective-permute-start.10 = (bf16[144,128]{1,0:T(8,128)(2,1)S(1)}, bf16[144,128]{1,0:T(8,128)(2,1)S(1)}, u32[]{:S(2)}, u32[]{:S(2)}) collective-permute-start(bf16[144,128]{1,0:T(8,128)(2,1)S(1)} %get-tuple-element.64), channel_id=1, source_target_pairs={{0,8},{2,10},{4,12},{6,14},{8,0},{10,2},{12,4},{14,6},{1,9},{3,11}... | collective-permute-start | bytes 110600 | tf_op jit(solution)/shard_map/ppermute | solution.py:427
  77.6 6.0 %collective-permute-start.9 = (bf16[144,128]{1,0:T(8,128)(2,1)S(1)}, bf16[144,128]{1,0:T(8,128)(2,1)S(1)}, u32[]{:S(2)}, u32[]{:S(2)}) collective-permute-start(bf16[144,128]{1,0:T(8,128)(2,1)S(1)} %get-tuple-element.65), channel_id=1, source_target_pairs={{0,4},{2,6},{4,0},{6,2},{8,12},{10,14},{12,8},{14,10},{1,5},{3,7},... | collective-permute-start | bytes 110600 | tf_op jit(solution)/shard_map/ppermute | solution.py:427
  83.6 1.3 %collective-permute-start.12 = (bf16[144,128]{1,0:T(8,128)(2,1)S(1)}, bf16[144,128]{1,0:T(8,128)(2,1)S(1)}, u32[]{:S(2)}, u32[]{:S(2)}) collective-permute-start(bf16[144,128]{1,0:T(8,128)(2,1)S(1)} %shard_map.82.keys_ref), channel_id=1, source_target_pairs={{0,16},{16,0},{1,17},{17,1},{2,18},{18,2},{3,19},{19,3},{4,20},{20... | collective-permute-start | bytes 110600 | tf_op jit(solution)/shard_map/ppermute | solution.py:427
  103.0 6.4 %collective-permute-start.13 = (f32[4,64]{1,0:T(4,128)S(1)}, f32[4,64]{1,0:T(4,128)S(1)}, u32[]{:S(2)}, u32[]{:S(2)}) collective-permute-start(f32[4,64]{1,0:T(4,128)S(1)} %get-tuple-element.61), channel_id=1, source_target_pairs={{1,2},{3,4},{5,6},{7,8},{9,10},{11,12},{13,14},{2,1},{4,3},{6,5},{... | collective-permute-start | bytes 3080 | tf_op jit(solution)/shard_map/ppermute | solution.py:433
  107.0 3.7 %collective-permute-start.14 = (f32[4,64]{1,0:T(4,128)S(1)}, f32[4,64]{1,0:T(4,128)S(1)}, u32[]{:S(2)}, u32[]{:S(2)}) collective-permute-start(f32[4,64]{1,0:T(4,128)S(1)} %get-tuple-element.62), channel_id=1, source_target_pairs={{0,1},{1,0},{2,3},{3,2},{4,5},{5,4},{6,7},{7,6},{8,9},{9,8},{10,11... | collective-permute-start | bytes 3080 | tf_op jit(solution)/shard_map/ppermute | solution.py:427

commit v8 on v7

--- a/solution.py
+++ b/solution.py
@@ -21,12 +21,13 @@
 FPAD = 80
 QUERIES = 2048
 HALF = 512
-TILE = 1024
+TILE = 2048
 TILES = QUERIES // TILE
 PER = TILE // TOK
 STEP = 256
 HEAD_AXES = ("yh", "x", "yl")
 BLK = ("yh", "x", "c")
+EVEN = (2, 6, 4)
 COL = ("z", "yl")
 NT = (((1,), (1,)), ((), ()))
 WHOLE = pl.BlockSpec(memory_space=pltpu.VMEM)
@@ -153,12 +154,13 @@
 
 
 def put_sums(out_ref, at, t, sums):
-    for n in range(PER):
-        out_ref[at, PER * t + n] = jnp.broadcast_to(sums[:, n * TOK : (n + 1) * TOK], (8, TOK))
+    rows = [sums[:, n * TOK : (n + 1) * TOK] for n in range(PER)]
+    out_ref[at, pl.ds(PER * t, PER)] = jnp.concatenate(rows)
 
 
 def get_sums(sums_ref, at, t):
-    return jnp.concatenate([sums_ref[at, PER * t + n, 0:1] for n in range(PER)], axis=1)
+    rows = sums_ref[at, pl.ds(PER * t, PER)]
+    return jnp.concatenate([rows[n : n + 1] for n in range(PER)], axis=1)
 
 
 def added(one, two):
@@ -476,12 +478,12 @@
         [pltpu.VMEM((HEADS, 16, 128), bf16), dma(())],
         [ANYWHERE],
     )(got)
-    came = [swapped(kv, "z", by) for by in (2, 4, 6)]
+    came = [swapped(kv, "z", by) for by in EVEN]
     even = jnp.stack([kv] + came)
     odd = swapped(even, "z", 1)
     there = swapped(got, "c", 1)
     keys = pltpu.VMEM((HALF, 128), bf16)
-    sums = jax.ShapeDtypeStruct((2, HEADS, 8, TOK), f32)
+    sums = jax.ShapeDtypeStruct((2, HEADS, TOK), f32)
     even_sums = call(even_sums_kernel, sums, 24, [keys], cost_estimate=cost(1))(got, there, even)
     odd, even_sums = lax.optimization_barrier((odd, even_sums))
     mine = call(odd_sums_kernel, sums, 24, [keys], cost_estimate=cost(1))(got, there, odd, even_sums)
@@ -508,7 +510,7 @@
     edge_here = swapped(edge_here, "c", 1)
     mine = grads + came.astype(f32)
     mine, w_qkv, w_patch = lax.optimization_barrier((mine, w_qkv, w_patch))
-    came = [swapped(mine[n].astype(bf16), "z", 2 * n) for n in (1, 2, 3)]
+    came = [swapped(mine[n + 1].astype(bf16), "z", by) for n, by in enumerate(EVEN)]
     weights = [combined_weights(w_qkv, w_patch, part) for part in range(3)]
     came, weights = lax.optimization_barrier((came, weights))
     keys = call(keys_sum_kernel, jax.ShapeDtypeStruct((2 * DH, 128), bf16), 4)(mine[0:1], *came)

time: 112 us -> 104 us (0.929)
  Pallas kernels: 41.6 us -> 34.8 us
  waiting for transfers between devices: 12 us -> 10.8 us
    pallas_call x1, Pallas kernels: 9.89 us -> 6.95 us  [on_device(): call(odd_sums_kernel, sums, 24, [keys], cost_estimate=cost(1))]
    pallas_call x1, Pallas kernels: 9.69 us -> 6.89 us  [on_device(): call(even_sums_kernel, sums, 24, [keys], cost_estimate=cost(1))]
    ppermute x14, waiting for transfers between devices: 9.79 us -> 8.6 us  [swapped(): return lax.ppermute(x, axis, [(i, i ^ by) for i in range(peers)])]
  transfers between devices with their start and end apart: 15 -> 15, of which waited for: 5 -> 7; matrix products, arithmetic and copies ran while one was open for 0% -> 0% of each run, Pallas kernels for 18% -> 16%
where the time goes in v8:
time: 104 us
  Pallas kernels  34.8 us (33%)
  blocking collectives  34.7 us (33%)
  starting transfers between devices  22.9 us (22%)
  waiting for transfers between devices  10.8 us (10%)
    all_to_all x1, blocking collectives, on_device(): got = lax.all_to_all(send, HEAD_AXES, 0, 0, tiled=True)  19.4 us
    ppermute x14, starting transfers between devices, swapped(): return lax.ppermute(x, axis, [(i, i ^ by) for i in range(peers)])  18.8 us
    all_to_all x1, blocking collectives, on_device(): back = lax.all_to_all(send, HEAD_AXES, 0, 0, tiled=True)  15.3 us
    ppermute x14, waiting for transfers between devices, swapped(): return lax.ppermute(x, axis, [(i, i ^ by) for i in range(peers)])  8.6 us
    pallas_call x1, Pallas kernels, on_device(): call(odd_sums_kernel, sums, 24, [keys], cost_estimate=cost(1))  6.95 us
    pallas_call x1, Pallas kernels, on_device(): call(even_sums_kernel, sums, 24, [keys], cost_estimate=cost(1))  6.89 us
    pallas_call x1, Pallas kernels, on_device(): call(second_kernel, dq + edges + [jax.ShapeDtypeStruct(block, f32)], 28,...  5.59 us
    pallas_call x1, Pallas kernels, on_device(): call(first_kernel, [sums] + dq + [jax.ShapeDtypeStruct(block, bf16)], 28,...  5.44 us
  transfers between devices with their start and end apart: 15, of which 7 were waited for; matrix products, arithmetic and copies ran while one was open for 0% of the time, Pallas kernels for 16%

profile of v8, /device:TPU:8, one launch (start us, length us, event | category | flops | bytes accessed | tf_op | source)
XLA Modules:
  0.0 103.6 jit_solution(14590473434654850531)
XLA Ops:
  0.0 2.5 %shard_map.73 = bf16[16,176,128]{2,1,0:T(8,128)(2,1)} custom-call(bf16[128,1152]{1,0:T(8,128)(2,1)} %bitcast.16, bf16[128,1152]{1,0:T(8,128)(2,1)} %bitcast.17, bf16[128,1152]{1,0:T(8,128)(2,1)} %bitcast.18, bf16[2,4,1152]{2,1,0:T(4,128)(2,1)} %k_in.1, bf16[2,4,1152]{2,1,0:T(4,128)(2,1)} %v_in.1), custom_call_target="tpu_custom_call" | custom-call | tf_op jit(solution)/shard_map/pallas_call | solution.py:459
  2.5 19.4 %all_to_all.10.got_ref.qg_a = bf16[16,176,128]{2,1,0:T(8,128)(2,1)S(1)} all-to-all(bf16[16,176,128]{2,1,0:T(8,128)(2,1)} %shard_map.73), channel_id=1, replica_groups=mesh['yh'=2,'x'=4,'c'=2,'z'=8,'yl'=2] {'yh','x','yl'}, dimensions={0} | all-to-all | bytes 1441792 | tf_op jit(solution)/shard_map/all_to_all | solution.py:473
  21.9 0.0 collective-permute-start
  21.9 0.1 shard_map.74
  22.0 7.3 %collective-permute-start.3 = (bf16[144,128]{1,0:T(8,128)(2,1)S(1)}, bf16[144,128]{1,0:T(8,128)(2,1)S(1)}, u32[]{:S(2)}, u32[]{:S(2)}) collective-permute-start(bf16[144,128]{1,0:T(8,128)(2,1)S(1)} %shard_map.74), channel_id=1, source_target_pairs={{0,8},{2,10},{4,12},{6,14},{8,0},{10,2},{12,4},{14,6},{1,9},{3,11}... | collective-permute-start | bytes 110600 | tf_op jit(solution)/shard_map/ppermute | solution.py:429
  29.2 0.0 collective-permute-start.2
  29.3 1.5 %collective-permute-start.1 = (bf16[144,128]{1,0:T(8,128)(2,1)S(1)}, bf16[144,128]{1,0:T(8,128)(2,1)S(1)}, u32[]{:S(2)}, u32[]{:S(2)}) collective-permute-start(bf16[144,128]{1,0:T(8,128)(2,1)S(1)} %shard_map.74), channel_id=1, source_target_pairs={{0,4},{2,6},{4,0},{6,2},{8,12},{10,14},{12,8},{14,10},{1,5},{3,7},... | collective-permute-start | bytes 110600 | tf_op jit(solution)/shard_map/ppermute | solution.py:429
  30.7 0.8 collective-permute-done.3
  31.5 3.8 %collective-permute-done.2 = bf16[144,128]{1,0:T(8,128)(2,1)S(1)} collective-permute-done((bf16[144,128]{1,0:T(8,128)(2,1)S(1)}, bf16[144,128]{1,0:T(8,128)(2,1)S(1)}, u32[]{:S(2)}, u32[]{:S(2)}) %collective-permute-start.2) | collective-permute-done | bytes 36896 | tf_op jit(solution)/shard_map/ppermute | solution.py:429
  35.3 0.0 collective-permute-done.1
  35.3 1.6 %collective-permute-start.4 = (bf16[4,144,128]{2,1,0:T(8,128)(2,1)S(1)}, bf16[4,144,128]{2,1,0:T(8,128)(2,1)S(1)}, u32[]{:S(2)}, u32[]{:S(2)}) collective-permute-start(bf16[4,144,128]{2,1,0:T(8,128)(2,1)S(1)} %pad_maximum_fusion.kv_ref), channel_id=1, source_target_pairs={{0,2},{2,0},{4,6},{6,4},{8,10},{10,8},{12,14},{14,12},{1,3},{3,1},... | collective-permute-start | bytes 442376 | tf_op jit(solution)/shard_map/ppermute | solution.py:429
  36.9 0.0 collective-permute-done.qg_b
  36.9 6.9 %shard_map.75.even_ref = f32[2,16,128]{2,1,0:T(8,128)S(1)} custom-call(bf16[16,176,128]{2,1,0:T(8,128)(2,1)S(1)} %all_to_all.10.got_ref.qg_a, bf16[16,176,128]{2,1,0:T(8,128)(2,1)S(1)} %collective-permute-done.qg_b, bf16[4,144,128]{2,1,0:T(8,128)(2,1)S(1)} %pad_maximum_fusion.kv_ref), custom_call_target="tpu_custom_call" | custom-call | flops 1073741824 | bytes 1048576 | tf_op jit(solution)/shard_map/pallas_call | solution.py:487
  43.8 0.0 collective-permute-done.4.kv_ref
  43.9 7.0 %shard_map.76.mine_ref = f32[2,16,128]{2,1,0:T(8,128)S(1)} custom-call(bf16[16,176,128]{2,1,0:T(8,128)(2,1)S(1)} %all_to_all.10.got_ref.qg_a, bf16[16,176,128]{2,1,0:T(8,128)(2,1)S(1)} %collective-permute-done.qg_b, bf16[4,144,128]{2,1,0:T(8,128)(2,1)S(1)} %collective-permute-done.4.kv_ref, f32[2,16,128]{2,1,0:T(8,128)S(1)} %shard_map.75.even_ref), custom_call_target="tpu_custom_call" | custom-call | flops 1073741824 | bytes 1048576 | tf_op jit(solution)/shard_map/pallas_call | solution.py:489
  50.8 0.3 collective-permute-start.5
  51.1 1.2 %collective-permute-done.5.came_ref = f32[2,16,128]{2,1,0:T(8,128)S(1)} collective-permute-done((f32[2,16,128]{2,1,0:T(8,128)S(1)}, f32[2,16,128]{2,1,0:T(8,128)S(1)}, u32[]{:S(2)}, u32[]{:S(2)}) %collective-permute-start.5) | collective-permute-done | bytes 16416 | tf_op jit(solution)/shard_map/ppermute | solution.py:429
  52.3 5.4 %shard_map.77 = (f32[2,16,128]{2,1,0:T(8,128)S(1)}, f32[16,80,128]{2,1,0:T(8,128)S(1)}, f32[16,80,128]{2,1,0:T(8,128)S(1)}, bf16[4,144,128]{2,1,0:T(8,128)(2,1)S(1)}) custom-call(bf16[16,176,128]{2,1,0:T(8,128)(2,1)S(1)} %all_to_all.10.got_ref.qg_a, bf16[16,176,128]{2,1,0:T(8,128)(2,1)S(1)} %collective-permute-done.qg_b, ...), custom_call_target="tpu_custom_call" | custom-call | flops 5368709120 | bytes 1048576 | tf_op jit(solution)/shard_map/pallas_call | solution.py:495
  57.7 0.6 collective-permute-start.6
  58.3 5.6 %shard_map.78 = (f32[16,80,128]{2,1,0:T(8,128)S(1)}, f32[16,80,128]{2,1,0:T(8,128)S(1)}, f32[16,24,128]{2,1,0:T(8,128)S(1)}, f32[16,24,128]{2,1,0:T(8,128)S(1)}, f32[4,144,128]{2,1,0:T(8,128)S(1)}) custom-call(bf16[16,176,128]{2,1,0:T(8,128)(2,1)S(1)} %all_to_all.10.got_ref.qg_a, bf16[16,176,128]{2,1,0:T(8,128)(2,1)S(1)} %collective-permute-done.qg_b, ...), custom_call_target="tpu_custom_call" | custom-call | flops 5368709120 | bytes 1048576 | tf_op jit(solution)/shard_map/pallas_call | solution.py:500
  63.9 0.0 copy-start
  63.9 0.0 collective-permute-done.6
  64.0 0.1 collective-permute-start.7
  64.1 0.5 collective-permute-start.8
  64.6 4.2 %collective-permute-start.11 = (bf16[144,128]{1,0:T(8,128)(2,1)S(1)}, bf16[144,128]{1,0:T(8,128)(2,1)S(1)}, u32[]{:S(2)}, u32[]{:S(2)}) collective-permute-start(bf16[144,128]{1,0:T(8,128)(2,1)S(1)} %get-tuple-element.63), channel_id=1, source_target_pairs={{0,8},{2,10},{4,12},{6,14},{8,0},{10,2},{12,4},{14,6},{1,9},{3,11}... | collective-permute-start | bytes 110600 | tf_op jit(solution)/shard_map/ppermute | solution.py:429
  68.8 1.6 %collective-permute-start.10 = (bf16[144,128]{1,0:T(8,128)(2,1)S(1)}, bf16[144,128]{1,0:T(8,128)(2,1)S(1)}, u32[]{:S(2)}, u32[]{:S(2)}) collective-permute-start(bf16[144,128]{1,0:T(8,128)(2,1)S(1)} %get-tuple-element.64), channel_id=1, source_target_pairs={{0,12},{2,14},{4,8},{6,10},{8,4},{10,6},{12,0},{14,2},{1,13},{3,15... | collective-permute-start | bytes 110600 | tf_op jit(solution)/shard_map/ppermute | solution.py:429
  70.4 1.0 collective-permute-start.9
  71.4 0.0 slice-done
  71.5 0.0 slice-done.1
  71.5 0.0 copy-done
  71.5 1.3 %shard_map.81.refs_2_ = bf16[512,1152]{1,0:T(8,128)(2,1)S(1)} custom-call(bf16[256,1152]{1,0:T(8,128)(2,1)S(1)} %copy-done, bf16[1152,3456]{1,0:T(8,128)(2,1)S(1)} %bitcast.14), custom_call_target="tpu_custom_call" | custom-call | flops 1048576 | bytes 65536 | tf_op jit(solution)/shard_map/pallas_call | solution.py:444
  72.8 1.3 %shard_map.80.refs_1_ = bf16[512,1152]{1,0:T(8,128)(2,1)S(1)} custom-call(bf16[256,1152]{1,0:T(8,128)(2,1)S(1)} %copy-done, bf16[1152,3456]{1,0:T(8,128)(2,1)S(1)} %bitcast.14), custom_call_target="tpu_custom_call" | custom-call | flops 1048576 | bytes 65536 | tf_op jit(solution)/shard_map/pallas_call | solution.py:444
  74.1 1.3 %shard_map.79.refs_0_ = bf16[512,1152]{1,0:T(8,128)(2,1)S(1)} custom-call(bf16[256,1152]{1,0:T(8,128)(2,1)S(1)} %copy-done, bf16[1152,3456]{1,0:T(8,128)(2,1)S(1)} %bitcast.14), custom_call_target="tpu_custom_call" | custom-call | flops 1048576 | bytes 65536 | tf_op jit(solution)/shard_map/pallas_call | solution.py:444
  75.4 0.0 collective-permute-done.11.came_c
  75.5 0.0 collective-permute-done.10.came_b
  75.5 0.2 collective-permute-done.9.came_a
  75.7 0.1 collective-permute-start.12
  75.8 1.2 %collective-permute-done.12.other_ref = bf16[144,128]{1,0:T(8,128)(2,1)S(1)} collective-permute-done((bf16[144,128]{1,0:T(8,128)(2,1)S(1)}, bf16[144,128]{1,0:T(8,128)(2,1)S(1)}, u32[]{:S(2)}, u32[]{:S(2)}) %collective-permute-start.12) | collective-permute-done | bytes 36896 | tf_op jit(solution)/shard_map/ppermute | solution.py:429
  77.0 0.0 collective-permute-done.8.came_edge_ref
  77.0 0.0 collective-permute-done.7.came_ref
  77.0 0.2 shard_map.83
  77.2 15.3 %all_to_all.11.back_ref = bf16[16,128,128]{2,1,0:T(8,128)(2,1)S(1)} all-to-all(bf16[16,128,128]{2,1,0:T(8,128)(2,1)S(1)} %shard_map.83), channel_id=1, replica_groups=mesh['yh'=2,'x'=4,'c'=2,'z'=8,'yl'=2] {'yh','x','yl'}, dimensions={0} | all-to-all | bytes 1048576 | tf_op jit(solution)/shard_map/all_to_all | solution.py:521
  92.5 2.5 %shard_map.84 = (f32[64,128]{1,0:T(8,128)S(1)}, f32[4,64]{1,0:T(4,128)S(1)}, f32[4,64]{1,0:T(4,128)S(1)}) custom-call(bf16[16,128,128]{2,1,0:T(8,128)(2,1)S(1)} %all_to_all.11.back_ref, bf16[512,1152]{1,0:T(8,128)(2,1)S(1)} %shard_map.79.refs_0_, bf16[512,1152]{1,0:T(8,128)(2,1)S(1)} %shard_map.80.refs_1_, bf16[512,1152]{1,0:T(8,128)(2,1)S(1)} %shard_map.81.refs_2_), custom_call_target="tpu_custom_call" | custom-call | tf_op jit(solution)/shard_map/pallas_call | solution.py:523
  95.1 4.1 %collective-permute-start.13 = (f32[4,64]{1,0:T(4,128)S(1)}, f32[4,64]{1,0:T(4,128)S(1)}, u32[]{:S(2)}, u32[]{:S(2)}) collective-permute-start(f32[4,64]{1,0:T(4,128)S(1)} %get-tuple-element.61), channel_id=1, source_target_pairs={{1,2},{3,4},{5,6},{7,8},{9,10},{11,12},{13,14},{2,1},{4,3},{6,5},{... | collective-permute-start | bytes 3080 | tf_op jit(solution)/shard_map/ppermute | solution.py:435
  99.2 0.1 collective-permute-start.14
  99.3 2.2 %collective-permute-done.13.far_ref = f32[4,64]{1,0:T(4,128)S(1)} collective-permute-done((f32[4,64]{1,0:T(4,128)S(1)}, f32[4,64]{1,0:T(4,128)S(1)}, u32[]{:S(2)}, u32[]{:S(2)}) %collective-permute-start.13) | collective-permute-done | bytes 1056 | tf_op jit(solution)/shard_map/ppermute | solution.py:435
  101.5 1.4 %collective-permute-done.14.near_ref = f32[4,64]{1,0:T(4,128)S(1)} collective-permute-done((f32[4,64]{1,0:T(4,128)S(1)}, f32[4,64]{1,0:T(4,128)S(1)}, u32[]{:S(2)}, u32[]{:S(2)}) %collective-permute-start.14) | collective-permute-done | bytes 1056 | tf_op jit(solution)/shard_map/ppermute | solution.py:429
  102.9 0.7 shard_map.85
  (9 shorter events, 0.1 us)
Async XLA Ops:
  21.9 15.1 %collective-permute-start = (bf16[16,176,128]{2,1,0:T(8,128)(2,1)S(1)}, bf16[16,176,128]{2,1,0:T(8,128)(2,1)S(1)}, u32[]{:S(2)}, u32[]{:S(2)}) collective-permute-start(bf16[16,176,128]{2,1,0:T(8,128)(2,1)S(1)} %all_to_all.10.got_ref.qg_a), channel_id=1, source_target_pairs={{0,16},{16,0},{1,17},{17,1},{2,18},{18,2},{3,19},{19,3},{4,20},{20... | collective-permute-start | bytes 2162696 | tf_op jit(solution)/shard_map/ppermute | solution.py:429
  22.0 9.5 %collective-permute-start.3 = (bf16[144,128]{1,0:T(8,128)(2,1)S(1)}, bf16[144,128]{1,0:T(8,128)(2,1)S(1)}, u32[]{:S(2)}, u32[]{:S(2)}) collective-permute-start(bf16[144,128]{1,0:T(8,128)(2,1)S(1)} %shard_map.74), channel_id=1, source_target_pairs={{0,8},{2,10},{4,12},{6,14},{8,0},{10,2},{12,4},{14,6},{1,9},{3,11}... | collective-permute-start | bytes 110600 | tf_op jit(solution)/shard_map/ppermute | solution.py:429
  29.2 6.1 %collective-permute-start.2 = (bf16[144,128]{1,0:T(8,128)(2,1)S(1)}, bf16[144,128]{1,0:T(8,128)(2,1)S(1)}, u32[]{:S(2)}, u32[]{:S(2)}) collective-permute-start(bf16[144,128]{1,0:T(8,128)(2,1)S(1)} %shard_map.74), channel_id=1, source_target_pairs={{0,12},{2,14},{4,8},{6,10},{8,4},{10,6},{12,0},{14,2},{1,13},{3,15... | collective-permute-start | bytes 110600 | tf_op jit(solution)/shard_map/ppermute | solution.py:429
  29.3 6.1 %collective-permute-start.1 = (bf16[144,128]{1,0:T(8,128)(2,1)S(1)}, bf16[144,128]{1,0:T(8,128)(2,1)S(1)}, u32[]{:S(2)}, u32[]{:S(2)}) collective-permute-start(bf16[144,128]{1,0:T(8,128)(2,1)S(1)} %shard_map.74), channel_id=1, source_target_pairs={{0,4},{2,6},{4,0},{6,2},{8,12},{10,14},{12,8},{14,10},{1,5},{3,7},... | collective-permute-start | bytes 110600 | tf_op jit(solution)/shard_map/ppermute | solution.py:429
  35.3 8.5 %collective-permute-start.4 = (bf16[4,144,128]{2,1,0:T(8,128)(2,1)S(1)}, bf16[4,144,128]{2,1,0:T(8,128)(2,1)S(1)}, u32[]{:S(2)}, u32[]{:S(2)}) collective-permute-start(bf16[4,144,128]{2,1,0:T(8,128)(2,1)S(1)} %pad_maximum_fusion.kv_ref), channel_id=1, source_target_pairs={{0,2},{2,0},{4,6},{6,4},{8,10},{10,8},{12,14},{14,12},{1,3},{3,1},... | collective-permute-start | bytes 442376 | tf_op jit(solution)/shard_map/ppermute | solution.py:429
  50.8 1.5 %collective-permute-start.5 = (f32[2,16,128]{2,1,0:T(8,128)S(1)}, f32[2,16,128]{2,1,0:T(8,128)S(1)}, u32[]{:S(2)}, u32[]{:S(2)}) collective-permute-start(f32[2,16,128]{2,1,0:T(8,128)S(1)} %shard_map.76.mine_ref), channel_id=1, source_target_pairs={{0,16},{16,0},{1,17},{17,1},{2,18},{18,2},{3,19},{19,3},{4,20},{20... | collective-permute-start | bytes 49160 | tf_op jit(solution)/shard_map/ppermute | solution.py:429
  57.7 6.2 %collective-permute-start.6 = (bf16[4,144,128]{2,1,0:T(8,128)(2,1)S(1)}, bf16[4,144,128]{2,1,0:T(8,128)(2,1)S(1)}, u32[]{:S(2)}, u32[]{:S(2)}) collective-permute-start(bf16[4,144,128]{2,1,0:T(8,128)(2,1)S(1)} %get-tuple-element.44), channel_id=1, source_target_pairs={{0,2},{2,0},{4,6},{6,4},{8,10},{10,8},{12,14},{14,12},{1,3},{3,1},... | collective-permute-start | bytes 442376 | tf_op jit(solution)/shard_map/ppermute | solution.py:429
  58.3 13.1 %slice-start = ((s8[7962624]{0:T(1024)(128)(4,1)}), s8[4194304]{0:T(1024)(128)(4,1)S(1)}, s32[]{:S(2)}) async-start(s8[7962624]{0:T(1024)(128)(4,1)} %bitcast.13), calls=%async_computation.2 | async-start | bytes 8388608
  58.3 13.1 %slice-start.1 = ((s8[7962624]{0:T(1024)(128)(4,1)}), s8[3768320]{0:T(1024)(128)(4,1)S(1)}, s32[]{:S(2)}) async-start(s8[7962624]{0:T(1024)(128)(4,1)} %bitcast.13), calls=%async_computation.3 | async-start | bytes 7536640
  63.9 7.5 %copy-start = (bf16[256,1152]{1,0:T(8,128)(2,1)S(1)}, bf16[256,1152]{1,0:T(8,128)(2,1)}, u32[]{:S(2)}) copy-start(bf16[256,1152]{1,0:T(8,128)(2,1)} %patch_ref.2) | copy-start | bytes 1769476
  64.0 13.1 %collective-permute-start.7 = (f32[16,80,128]{2,1,0:T(8,128)S(1)}, f32[16,80,128]{2,1,0:T(8,128)S(1)}, u32[]{:S(2)}, u32[]{:S(2)}) collective-permute-start(f32[16,80,128]{2,1,0:T(8,128)S(1)} %get-tuple-element.46), channel_id=1, source_target_pairs={{0,16},{16,0},{1,17},{17,1},{2,18},{18,2},{3,19},{19,3},{4,20},{20... | collective-permute-start | bytes 1966088 | tf_op jit(solution)/shard_map/ppermute | solution.py:429
  64.1 13.0 %collective-permute-start.8 = (f32[16,24,128]{2,1,0:T(8,128)S(1)}, f32[16,24,128]{2,1,0:T(8,128)S(1)}, u32[]{:S(2)}, u32[]{:S(2)}) collective-permute-start(f32[16,24,128]{2,1,0:T(8,128)S(1)} %get-tuple-element.48), channel_id=1, source_target_pairs={{0,16},{16,0},{1,17},{17,1},{2,18},{18,2},{3,19},{19,3},{4,20},{20... | collective-permute-start | bytes 589832 | tf_op jit(solution)/shard_map/ppermute | solution.py:429
  64.6 10.8 %collective-permute-start.11 = (bf16[144,128]{1,0:T(8,128)(2,1)S(1)}, bf16[144,128]{1,0:T(8,128)(2,1)S(1)}, u32[]{:S(2)}, u32[]{:S(2)}) collective-permute-start(bf16[144,128]{1,0:T(8,128)(2,1)S(1)} %get-tuple-element.63), channel_id=1, source_target_pairs={{0,8},{2,10},{4,12},{6,14},{8,0},{10,2},{12,4},{14,6},{1,9},{3,11}... | collective-permute-start | bytes 110600 | tf_op jit(solution)/shard_map/ppermute | solution.py:429
  68.8 6.6 %collective-permute-start.10 = (bf16[144,128]{1,0:T(8,128)(2,1)S(1)}, bf16[144,128]{1,0:T(8,128)(2,1)S(1)}, u32[]{:S(2)}, u32[]{:S(2)}) collective-permute-start(bf16[144,128]{1,0:T(8,128)(2,1)S(1)} %get-tuple-element.64), channel_id=1, source_target_pairs={{0,12},{2,14},{4,8},{6,10},{8,4},{10,6},{12,0},{14,2},{1,13},{3,15... | collective-permute-start | bytes 110600 | tf_op jit(solution)/shard_map/ppermute | solution.py:429
  70.4 5.2 %collective-permute-start.9 = (bf16[144,128]{1,0:T(8,128)(2,1)S(1)}, bf16[144,128]{1,0:T(8,128)(2,1)S(1)}, u32[]{:S(2)}, u32[]{:S(2)}) collective-permute-start(bf16[144,128]{1,0:T(8,128)(2,1)S(1)} %get-tuple-element.65), channel_id=1, source_target_pairs={{0,4},{2,6},{4,0},{6,2},{8,12},{10,14},{12,8},{14,10},{1,5},{3,7},... | collective-permute-start | bytes 110600 | tf_op jit(solution)/shard_map/ppermute | solution.py:429
  75.7 1.3 %collective-permute-start.12 = (bf16[144,128]{1,0:T(8,128)(2,1)S(1)}, bf16[144,128]{1,0:T(8,128)(2,1)S(1)}, u32[]{:S(2)}, u32[]{:S(2)}) collective-permute-start(bf16[144,128]{1,0:T(8,128)(2,1)S(1)} %shard_map.82.keys_ref), channel_id=1, source_target_pairs={{0,16},{16,0},{1,17},{17,1},{2,18},{18,2},{3,19},{19,3},{4,20},{20... | collective-permute-start | bytes 110600 | tf_op jit(solution)/shard_map/ppermute | solution.py:429
  95.1 6.4 %collective-permute-start.13 = (f32[4,64]{1,0:T(4,128)S(1)}, f32[4,64]{1,0:T(4,128)S(1)}, u32[]{:S(2)}, u32[]{:S(2)}) collective-permute-start(f32[4,64]{1,0:T(4,128)S(1)} %get-tuple-element.61), channel_id=1, source_target_pairs={{1,2},{3,4},{5,6},{7,8},{9,10},{11,12},{13,14},{2,1},{4,3},{6,5},{... | collective-permute-start | bytes 3080 | tf_op jit(solution)/shard_map/ppermute | solution.py:435
  99.2 3.7 %collective-permute-start.14 = (f32[4,64]{1,0:T(4,128)S(1)}, f32[4,64]{1,0:T(4,128)S(1)}, u32[]{:S(2)}, u32[]{:S(2)}) collective-permute-start(f32[4,64]{1,0:T(4,128)S(1)} %get-tuple-element.62), channel_id=1, source_target_pairs={{0,1},{1,0},{2,3},{3,2},{4,5},{5,4},{6,7},{7,6},{8,9},{9,8},{10,11... | collective-permute-start | bytes 3080 | tf_op jit(solution)/shard_map/ppermute | solution.py:429

commit v9 on v8

--- a/solution.py
+++ b/solution.py
@@ -21,15 +21,14 @@
 FPAD = 80
 QUERIES = 2048
 HALF = 512
-TILE = 2048
-TILES = QUERIES // TILE
-PER = TILE // TOK
+TILE = 2 * QUERIES
 STEP = 256
 HEAD_AXES = ("yh", "x", "yl")
 BLK = ("yh", "x", "c")
 EVEN = (2, 6, 4)
 COL = ("z", "yl")
 NT = (((1,), (1,)), ((), ()))
+SMALL = pl.CostEstimate(flops=2**20, bytes_accessed=2**16, transcendentals=0)
 WHOLE = pl.BlockSpec(memory_space=pltpu.VMEM)
 ANYWHERE = pl.BlockSpec(memory_space=pl.ANY)
 bf16, f32 = jnp.bfloat16, jnp.float32
@@ -120,8 +119,9 @@
     return jnp.max(norms)
 
 
-def tile_of(qg_ref, t, row):
-    return jnp.concatenate([qg_ref[PER * t + n, row : row + FPAD] for n in range(PER)], axis=1)
+def tile_of(qg_refs, row):
+    blocks = [qg_ref[n, row : row + FPAD] for qg_ref in qg_refs for n in range(HEADS)]
+    return jnp.concatenate(blocks, axis=1)
 
 
 def log_sums(q_t, k_s, norm):
@@ -153,14 +153,14 @@
     return lax.cond(jnp.min(total) < 2.0**-90, again, lambda: bound + jnp.log2(total))
 
 
-def put_sums(out_ref, at, t, sums):
-    rows = [sums[:, n * TOK : (n + 1) * TOK] for n in range(PER)]
-    out_ref[at, pl.ds(PER * t, PER)] = jnp.concatenate(rows)
-
-
-def get_sums(sums_ref, at, t):
-    rows = sums_ref[at, pl.ds(PER * t, PER)]
-    return jnp.concatenate([rows[n : n + 1] for n in range(PER)], axis=1)
+def put_sums(out_ref, sums):
+    rows = [sums[:, n * TOK : (n + 1) * TOK] for n in range(2 * HEADS)]
+    out_ref[...] = jnp.concatenate(rows).reshape(2, HEADS, TOK)
+
+
+def get_sums(sums_ref):
+    rows = sums_ref[...].reshape(2 * HEADS, TOK)
+    return jnp.concatenate([rows[n : n + 1] for n in range(2 * HEADS)], axis=1)
 
 
 def added(one, two):
@@ -170,52 +170,32 @@
 
 def even_sums_kernel(qg_a, qg_b, kv_ref, out_ref, k_s):
     norm = load_keys(kv_ref, k_s)
-    for at, qg_ref in enumerate((qg_a, qg_b)):
-
-        def tile(t, _):
-            put_sums(out_ref, at, t, log_sums(tile_of(qg_ref, t, 0), k_s, norm))
-            return 0
-
-        lax.fori_loop(0, TILES, tile, 0)
+    put_sums(out_ref, log_sums(tile_of((qg_a, qg_b), 0), k_s, norm))
 
 
 def odd_sums_kernel(qg_a, qg_b, kv_ref, even_ref, out_ref, k_s):
     norm = load_keys(kv_ref, k_s)
-    for at, qg_ref in enumerate((qg_a, qg_b)):
-
-        def tile(t, _):
-            mine = log_sums(tile_of(qg_ref, t, 0), k_s, norm)
-            put_sums(out_ref, at, t, added(mine, get_sums(even_ref, at, t)))
-            return 0
-
-        lax.fori_loop(0, TILES, tile, 0)
-
-
-def gradients(sums_ref, work, k_s, kt_s, v_s, dk_s, dv_s):
-    dk_s[...] = jnp.zeros_like(dk_s)
-    dv_s[...] = jnp.zeros_like(dv_s)
-    for at_core, (qg_ref, put_dq) in enumerate(work):
-
-        def tile(t, _):
-            q_t = tile_of(qg_ref, t, 0)
-            g_t = tile_of(qg_ref, t, FPAD)
-            sums = get_sums(sums_ref, at_core, t)
-            dq = jnp.zeros((FPAD, TILE), f32)
-            for at in range(0, HALF, STEP):
-                b = slice(at, at + STEP)
-                scores = jnp.dot(k_s[b, 0:FPAD], q_t, preferred_element_type=f32)
-                probs = jnp.exp2(scores * SCALE2 - sums)
-                half_probs = probs.astype(bf16)
-                shifted = jnp.dot(v_s[b, 0:FPAD], g_t, preferred_element_type=f32)
-                ds = (probs * shifted).astype(bf16)
-                dk_s[b, 0:FPAD] += lax.dot_general(ds, q_t, NT, preferred_element_type=f32)
-                dv_s[b, 0:FPAD] += lax.dot_general(half_probs, g_t, NT, preferred_element_type=f32)
-                dq = dq + jnp.dot(kt_s[0:FPAD, b], ds, preferred_element_type=f32)
-            for n in range(PER):
-                put_dq(PER * t + n, dq[:, n * TOK : (n + 1) * TOK])
-            return 0
-
-        lax.fori_loop(0, TILES, tile, 0)
+    mine = log_sums(tile_of((qg_a, qg_b), 0), k_s, norm)
+    put_sums(out_ref, added(mine, get_sums(even_ref)))
+
+
+def gradients(sums_ref, qg_refs, put_dq, k_s, kt_s, v_s, dk_s, dv_s):
+    q_t = tile_of(qg_refs, 0)
+    g_t = tile_of(qg_refs, FPAD)
+    sums = get_sums(sums_ref)
+    dq = jnp.zeros((FPAD, TILE), f32)
+    for at in range(0, HALF, STEP):
+        b = slice(at, at + STEP)
+        scores = jnp.dot(k_s[b, 0:FPAD], q_t, preferred_element_type=f32)
+        probs = jnp.exp2(scores * SCALE2 - sums)
+        half_probs = probs.astype(bf16)
+        shifted = jnp.dot(v_s[b, 0:FPAD], g_t, preferred_element_type=f32)
+        ds = (probs * shifted).astype(bf16)
+        dk_s[b, 0:FPAD] = lax.dot_general(ds, q_t, NT, preferred_element_type=f32)
+        dv_s[b, 0:FPAD] = lax.dot_general(half_probs, g_t, NT, preferred_element_type=f32)
+        dq = dq + jnp.dot(kt_s[0:FPAD, b], ds, preferred_element_type=f32)
+    for n in range(2 * HEADS):
+        put_dq(n // HEADS, n % HEADS, dq[:, n * TOK : (n + 1) * TOK])
 
 
 def put_keys(out_ref, dk_s, dv_s):
@@ -235,13 +215,10 @@
     for at in (0, 1):
         sums_ref[at] = added(mine_ref[at], came_ref[1 - at])
 
-    def put_a(n, dq):
-        dq_a[n] = dq
-
-    def put_b(n, dq):
-        dq_b[n] = dq
-
-    gradients(sums_ref, ((qg_a, put_a), (qg_b, put_b)), k_s, kt_s, v_s, dk_s, dv_s)
+    def put_dq(at, n, dq):
+        (dq_a, dq_b)[at][n] = dq
+
+    gradients(sums_ref, (qg_a, qg_b), put_dq, k_s, kt_s, v_s, dk_s, dv_s)
     put_keys(out_ref, dk_s, dv_s)
 
 
@@ -260,17 +237,12 @@
 ):
     load_keys(kv_ref, k_s, kt_s, v_s)
 
-    def put_a(n, dq):
-        dq = in_a[n] + dq
-        dq_a[n] = dq
-        edge_a[n] = edge_rows(dq)
-
-    def put_b(n, dq):
-        dq = in_b[n] + dq
-        dq_b[n] = dq
-        edge_b[n] = edge_rows(dq)
-
-    gradients(sums_ref, ((qg_a, put_a), (qg_b, put_b)), k_s, kt_s, v_s, dk_s, dv_s)
+    def put_dq(at, n, dq):
+        dq = (in_a, in_b)[at][n] + dq
+        (dq_a, dq_b)[at][n] = dq
+        (edge_a, edge_b)[at][n] = edge_rows(dq)
+
+    gradients(sums_ref, (qg_a, qg_b), put_dq, k_s, kt_s, v_s, dk_s, dv_s)
     put_keys(out_ref, dk_s, dv_s)
 
 
@@ -341,7 +313,7 @@
 
 
 def embed_kernel(back_ref, *refs):
-    weights, (center_ref, near_out, far_out, joined, pooled, sheet) = refs[:3], refs[3:]
+    weights, (turned_ref, near_out, far_out, joined, pooled, sheet) = refs[:3], refs[3:]
     for h in range(0, HEADS, 2):
         pair = []
         wide = []
@@ -377,14 +349,38 @@
     holds = (cell == jnp.where(token < TOK, mine, beyond)) & (token < EXTENDED)
     patch = patch + jnp.dot(cells, one_hot(holds, 1.0 / POOL**2), preferred_element_type=f32)
     to, token = iota((EXTENDED, 256), 0), iota((EXTENDED, 256), 1)
-    far = to - TOK
-    column = jnp.where(to < TOK, to // 8, far // 8 * 4 + far % 8 // 2)
-    source = jnp.where(to < TOK, to % 8 * COLS, TOK + far % 2 * COLS) + column
+    source = jnp.where(to < TOK, to % 8 * COLS, TOK + to % 2 * COLS) + column_of(to)
     turned = lax.dot_general(
         one_hot(token == source), jnp.concatenate(split(patch)), NT, preferred_element_type=f32
-    ).astype(bf16)
+    )
+    turned_ref[...] = turned.astype(bf16)
+    whole = turned[:, 0:256] + turned[:, 256:512]
+    left, right = whole[:, 0:128], whole[:, 128:256]
+    lane = iota((8, 128), 1)
+    own = jnp.where(lane % 8 < 4, left[0:ROWS], right[TOK - ROWS : TOK])
+    beyond = jnp.where(lane % 8 < 4, left[TOK : TOK + 8], pltpu.roll(right[EXTENDED - 8 :], 2, 0))
     sheet[...] = jnp.zeros_like(sheet)
-    here = iota((EXTENDED, 256), 1) % 128 // 8 == column
+    for u in range(16):
+        sheet[pl.ds(u, ROWS, stride=8), :] += pltpu.roll(own, (128 - 8 * u) % 128, 1)
+        if u >= 12:
+            sheet[u - 8 : u - 7, :] += pltpu.roll(beyond, 128 - 8 * u, 1)[0:1]
+        if u < 4:
+            sheet[64 + u : 65 + u, :] += pltpu.roll(beyond, (128 - 8 * u) % 128, 1)[1:2]
+    edges = sheet[4:68].T
+    begins = lax.axis_index("yl") == 0
+    near_out[...] = jnp.where(begins, edges[4:8], edges[0:4])
+    far_out[...] = jnp.where(begins, edges[0:4], edges[4:8])
+
+
+def column_of(row):
+    far = row - TOK
+    return jnp.where(row < TOK, row // 8, far // 8 * 4 + far % 8 // 2)
+
+
+def fold_kernel(turned_ref, center_ref, sheet):
+    turned = turned_ref[...]
+    sheet[...] = jnp.zeros_like(sheet)
+    here = iota((EXTENDED, 256), 1) % 128 // 8 == column_of(iota((EXTENDED, 256), 0))
     to, at = iota((256, 256), 1), iota((256, 256), 0) % 128
     for pair in range(8):
         tile = one_hot((to // 128 + 2 * pair == at // 8) & (to % 8 == at % 8))
@@ -409,11 +405,6 @@
     lane = lax.broadcasted_iota(jnp.int32, left.shape, 1)
     center = jnp.where(lane < 124, pltpu.roll(left, 124, 1), 0.0)
     center_ref[...] = center + jnp.where(lane >= 4, pltpu.roll(right, 4, 1), 0.0)
-    left = left.T[0:4]
-    right = right.T[124:128]
-    begins = lax.axis_index("yl") == 0
-    near_out[...] = jnp.where(begins, right, left)
-    far_out[...] = jnp.where(begins, left, right)
 
 
 def cols_kernel(center_ref, far_ref, near_ref, out_ref):
@@ -447,7 +438,7 @@
         12,
         [pltpu.VMEM((D, D), bf16), pltpu.SemaphoreType.DMA((D // 128,))],
         [WHOLE, ANYWHERE],
-        cost_estimate=pl.CostEstimate(flops=2**20, bytes_accessed=2**16, transcendentals=0),
+        cost_estimate=SMALL,
     )(w_patch, w_qkv)
 
 
@@ -493,14 +484,14 @@
     dq = [jax.ShapeDtypeStruct((HEADS, FPAD, TOK), f32)] * 2
     block = (4, 2 * DH, 128)
     sums, dq_here, dq_there, grads = call(
-        first_kernel, [sums] + dq + [jax.ShapeDtypeStruct(block, bf16)], 28, scratch, cost_estimate=cost(5)
+        first_kernel, [sums] + dq + [jax.ShapeDtypeStruct(block, bf16)], 32, scratch, cost_estimate=cost(5)
     )(got, there, odd, mine, came)
     came = swapped(grads, "z", 1)
     edges = [jax.ShapeDtypeStruct((HEADS, 24, TOK), f32)] * 2
     *dq, grads = call(
         second_kernel,
         dq + edges + [jax.ShapeDtypeStruct(block, f32)],
-        28,
+        32,
         scratch,
         cost_estimate=cost(5),
     )(got, there, even, sums, dq_here, dq_there)
@@ -520,15 +511,22 @@
     )
     back = lax.all_to_all(send, HEAD_AXES, 0, 0, tiled=True)
     strip = jax.ShapeDtypeStruct((4, 64), f32)
-    center, to_near, to_far = call(
+    turned, to_near, to_far = call(
         embed_kernel,
-        [jax.ShapeDtypeStruct((64, 128), f32), strip, strip],
+        [jax.ShapeDtypeStruct((EXTENDED, 512), bf16), strip, strip],
         28,
-        [pltpu.VMEM((D, 2 * TOK), bf16), pltpu.VMEM((2 * D, 128), bf16), pltpu.VMEM((2, 72, 128), f32)],
+        [pltpu.VMEM((D, 2 * TOK), bf16), pltpu.VMEM((2 * D, 128), bf16), pltpu.VMEM((72, 128), f32)],
     )(back, *weights)
-    return call(cols_kernel, jax.ShapeDtypeStruct((64, 128), f32), 4)(
-        center, neighbours(to_far, COL), swapped(to_near, "yl", 1)
-    )
+    far, near = neighbours(to_far, COL), swapped(to_near, "yl", 1)
+    center = call(
+        fold_kernel,
+        jax.ShapeDtypeStruct((64, 128), f32),
+        8,
+        [pltpu.VMEM((2, 72, 128), f32)],
+        cost_estimate=SMALL,
+    )(turned)
+    far, near, center = lax.optimization_barrier((far, near, center))
+    return call(cols_kernel, jax.ShapeDtypeStruct((64, 128), f32), 4)(center, far, near)
 
 
 def solution(mesh):

time: 104 us -> 100 us (0.962)
  Pallas kernels: 34.8 us -> 32 us
    pallas_call x1, Pallas kernels: 6.89 us -> 5.61 us  [on_device(): call(even_sums_kernel, sums, 24, [keys], cost_estimate=cost(1))]
    pallas_call x1, Pallas kernels: 6.95 us -> 5.68 us  [on_device(): call(odd_sums_kernel, sums, 24, [keys], cost_estimate=cost(1))]
    pallas_call x3 -> x4, Pallas kernels: 13.6 us -> 13.3 us  [the longest x1 5.45 us: on_device(): call(second_kernel, dq + edges + [jax.ShapeDtypeStruct(block, f32)], 32,...]
where the time goes in v9:
time: 100 us; the launch traced here: 99.9 us
  blocking collectives  34.7 us (35%)
  Pallas kernels  32 us (32%)
  starting transfers between devices  22.7 us (23%)
  waiting for transfers between devices  10.2 us (10%)
    all_to_all x1, blocking collectives, on_device(): got = lax.all_to_all(send, HEAD_AXES, 0, 0, tiled=True)  19.4 us
    ppermute x14, starting transfers between devices, swapped(): return lax.ppermute(x, axis, [(i, i ^ by) for i in range(peers)])  18.5 us
    all_to_all x1, blocking collectives, on_device(): back = lax.all_to_all(send, HEAD_AXES, 0, 0, tiled=True)  15.3 us
    ppermute x14, waiting for transfers between devices, swapped(): return lax.ppermute(x, axis, [(i, i ^ by) for i in range(peers)])  8.65 us
    pallas_call x1, Pallas kernels, on_device(): call(odd_sums_kernel, sums, 24, [keys], cost_estimate=cost(1))  5.68 us
    pallas_call x1, Pallas kernels, on_device(): call(even_sums_kernel, sums, 24, [keys], cost_estimate=cost(1))  5.61 us
    pallas_call x1, Pallas kernels, on_device(): call(second_kernel, dq + edges + [jax.ShapeDtypeStruct(block, f32)], 32,...  5.45 us
    pallas_call x1, Pallas kernels, on_device(): call(first_kernel, [sums] + dq + [jax.ShapeDtypeStruct(block, bf16)], 32,...  5.39 us
  transfers between devices with their start and end apart: 15, of which 7 were waited for; matrix products, arithmetic and copies ran while one was open for 0% of the time, Pallas kernels for 16%

profile of v9, /device:TPU:8, one launch (start us, length us, event | category | flops | bytes accessed | tf_op | source)
XLA Modules:
  0.0 99.9 jit_solution(12661824155704415205)
XLA Ops:
  0.0 2.5 %shard_map.73 = bf16[16,176,128]{2,1,0:T(8,128)(2,1)} custom-call(bf16[128,1152]{1,0:T(8,128)(2,1)} %bitcast.16, bf16[128,1152]{1,0:T(8,128)(2,1)} %bitcast.17, bf16[128,1152]{1,0:T(8,128)(2,1)} %bitcast.18, bf16[2,4,1152]{2,1,0:T(4,128)(2,1)} %k_in.1, bf16[2,4,1152]{2,1,0:T(4,128)(2,1)} %v_in.1), custom_call_target="tpu_custom_call" | custom-call | tf_op jit(solution)/shard_map/pallas_call | solution.py:450
  2.5 19.4 %all_to_all.10.got_ref.qg_a = bf16[16,176,128]{2,1,0:T(8,128)(2,1)S(1)} all-to-all(bf16[16,176,128]{2,1,0:T(8,128)(2,1)} %shard_map.73), channel_id=1, replica_groups=mesh['yh'=2,'x'=4,'c'=2,'z'=8,'yl'=2] {'yh','x','yl'}, dimensions={0} | all-to-all | bytes 1441792 | tf_op jit(solution)/shard_map/all_to_all | solution.py:464
  21.9 0.0 collective-permute-start
  21.9 0.1 shard_map.74
  22.0 7.3 %collective-permute-start.3 = (bf16[144,128]{1,0:T(8,128)(2,1)S(1)}, bf16[144,128]{1,0:T(8,128)(2,1)S(1)}, u32[]{:S(2)}, u32[]{:S(2)}) collective-permute-start(bf16[144,128]{1,0:T(8,128)(2,1)S(1)} %shard_map.74), channel_id=1, source_target_pairs={{0,8},{2,10},{4,12},{6,14},{8,0},{10,2},{12,4},{14,6},{1,9},{3,11}... | collective-permute-start | bytes 110600 | tf_op jit(solution)/shard_map/ppermute | solution.py:420
  29.2 0.0 collective-permute-start.2
  29.3 1.5 %collective-permute-start.1 = (bf16[144,128]{1,0:T(8,128)(2,1)S(1)}, bf16[144,128]{1,0:T(8,128)(2,1)S(1)}, u32[]{:S(2)}, u32[]{:S(2)}) collective-permute-start(bf16[144,128]{1,0:T(8,128)(2,1)S(1)} %shard_map.74), channel_id=1, source_target_pairs={{0,4},{2,6},{4,0},{6,2},{8,12},{10,14},{12,8},{14,10},{1,5},{3,7},... | collective-permute-start | bytes 110600 | tf_op jit(solution)/shard_map/ppermute | solution.py:420
  30.7 0.8 collective-permute-done.3
  31.5 3.8 %collective-permute-done.2 = bf16[144,128]{1,0:T(8,128)(2,1)S(1)} collective-permute-done((bf16[144,128]{1,0:T(8,128)(2,1)S(1)}, bf16[144,128]{1,0:T(8,128)(2,1)S(1)}, u32[]{:S(2)}, u32[]{:S(2)}) %collective-permute-start.2) | collective-permute-done | bytes 36896 | tf_op jit(solution)/shard_map/ppermute | solution.py:420
  35.3 0.0 collective-permute-done.1
  35.3 1.6 %collective-permute-start.4 = (bf16[4,144,128]{2,1,0:T(8,128)(2,1)S(1)}, bf16[4,144,128]{2,1,0:T(8,128)(2,1)S(1)}, u32[]{:S(2)}, u32[]{:S(2)}) collective-permute-start(bf16[4,144,128]{2,1,0:T(8,128)(2,1)S(1)} %pad_maximum_fusion.kv_ref), channel_id=1, source_target_pairs={{0,2},{2,0},{4,6},{6,4},{8,10},{10,8},{12,14},{14,12},{1,3},{3,1},... | collective-permute-start | bytes 442376 | tf_op jit(solution)/shard_map/ppermute | solution.py:420
  36.9 0.0 collective-permute-done.qg_b
  36.9 5.6 %shard_map.75.even_ref = f32[2,16,128]{2,1,0:T(8,128)S(1)} custom-call(bf16[16,176,128]{2,1,0:T(8,128)(2,1)S(1)} %all_to_all.10.got_ref.qg_a, bf16[16,176,128]{2,1,0:T(8,128)(2,1)S(1)} %collective-permute-done.qg_b, bf16[4,144,128]{2,1,0:T(8,128)(2,1)S(1)} %pad_maximum_fusion.kv_ref), custom_call_target="tpu_custom_call" | custom-call | flops 1073741824 | bytes 1048576 | tf_op jit(solution)/shard_map/pallas_call | solution.py:478
  42.6 0.0 collective-permute-done.4.kv_ref
  42.6 5.7 %shard_map.76.mine_ref = f32[2,16,128]{2,1,0:T(8,128)S(1)} custom-call(bf16[16,176,128]{2,1,0:T(8,128)(2,1)S(1)} %all_to_all.10.got_ref.qg_a, bf16[16,176,128]{2,1,0:T(8,128)(2,1)S(1)} %collective-permute-done.qg_b, bf16[4,144,128]{2,1,0:T(8,128)(2,1)S(1)} %collective-permute-done.4.kv_ref, f32[2,16,128]{2,1,0:T(8,128)S(1)} %shard_map.75.even_ref), custom_call_target="tpu_custom_call" | custom-call | flops 1073741824 | bytes 1048576 | tf_op jit(solution)/shard_map/pallas_call | solution.py:480
  48.3 0.3 collective-permute-start.5
  48.5 1.2 %collective-permute-done.5.came_ref = f32[2,16,128]{2,1,0:T(8,128)S(1)} collective-permute-done((f32[2,16,128]{2,1,0:T(8,128)S(1)}, f32[2,16,128]{2,1,0:T(8,128)S(1)}, u32[]{:S(2)}, u32[]{:S(2)}) %collective-permute-start.5) | collective-permute-done | bytes 16416 | tf_op jit(solution)/shard_map/ppermute | solution.py:420
  49.7 5.4 %shard_map.77 = (f32[2,16,128]{2,1,0:T(8,128)S(1)}, f32[16,80,128]{2,1,0:T(8,128)S(1)}, f32[16,80,128]{2,1,0:T(8,128)S(1)}, bf16[4,144,128]{2,1,0:T(8,128)(2,1)S(1)}) custom-call(bf16[16,176,128]{2,1,0:T(8,128)(2,1)S(1)} %all_to_all.10.got_ref.qg_a, bf16[16,176,128]{2,1,0:T(8,128)(2,1)S(1)} %collective-permute-done.qg_b, ...), custom_call_target="tpu_custom_call" | custom-call | flops 5368709120 | bytes 1048576 | tf_op jit(solution)/shard_map/pallas_call | solution.py:486
  55.1 0.6 collective-permute-start.6
  55.7 5.5 %shard_map.78 = (f32[16,80,128]{2,1,0:T(8,128)S(1)}, f32[16,80,128]{2,1,0:T(8,128)S(1)}, f32[16,24,128]{2,1,0:T(8,128)S(1)}, f32[16,24,128]{2,1,0:T(8,128)S(1)}, f32[4,144,128]{2,1,0:T(8,128)S(1)}) custom-call(bf16[16,176,128]{2,1,0:T(8,128)(2,1)S(1)} %all_to_all.10.got_ref.qg_a, bf16[16,176,128]{2,1,0:T(8,128)(2,1)S(1)} %collective-permute-done.qg_b, ...), custom_call_target="tpu_custom_call" | custom-call | flops 5368709120 | bytes 1048576 | tf_op jit(solution)/shard_map/pallas_call | solution.py:491
  61.1 0.0 copy-start
  61.1 0.0 collective-permute-done.6
  61.1 0.1 collective-permute-start.7
  61.2 0.5 collective-permute-start.8
  61.8 4.0 %collective-permute-start.11 = (bf16[144,128]{1,0:T(8,128)(2,1)S(1)}, bf16[144,128]{1,0:T(8,128)(2,1)S(1)}, u32[]{:S(2)}, u32[]{:S(2)}) collective-permute-start(bf16[144,128]{1,0:T(8,128)(2,1)S(1)} %get-tuple-element.69), channel_id=1, source_target_pairs={{0,8},{2,10},{4,12},{6,14},{8,0},{10,2},{12,4},{14,6},{1,9},{3,11}... | collective-permute-start | bytes 110600 | tf_op jit(solution)/shard_map/ppermute | solution.py:420
  65.9 1.6 %collective-permute-start.10 = (bf16[144,128]{1,0:T(8,128)(2,1)S(1)}, bf16[144,128]{1,0:T(8,128)(2,1)S(1)}, u32[]{:S(2)}, u32[]{:S(2)}) collective-permute-start(bf16[144,128]{1,0:T(8,128)(2,1)S(1)} %get-tuple-element.70), channel_id=1, source_target_pairs={{0,12},{2,14},{4,8},{6,10},{8,4},{10,6},{12,0},{14,2},{1,13},{3,15... | collective-permute-start | bytes 110600 | tf_op jit(solution)/shard_map/ppermute | solution.py:420
  67.5 0.9 collective-permute-start.9
  68.4 0.0 slice-done
  68.4 0.0 slice-done.1
  68.4 1.3 %shard_map.81.refs_2_ = bf16[512,1152]{1,0:T(8,128)(2,1)S(1)} custom-call(bf16[256,1152]{1,0:T(8,128)(2,1)S(1)} %copy-done, bf16[1152,3456]{1,0:T(8,128)(2,1)S(1)} %bitcast.14), custom_call_target="tpu_custom_call" | custom-call | flops 1048576 | bytes 65536 | tf_op jit(solution)/shard_map/pallas_call | solution.py:435
  69.8 1.3 %shard_map.80.refs_1_ = bf16[512,1152]{1,0:T(8,128)(2,1)S(1)} custom-call(bf16[256,1152]{1,0:T(8,128)(2,1)S(1)} %copy-done, bf16[1152,3456]{1,0:T(8,128)(2,1)S(1)} %bitcast.14), custom_call_target="tpu_custom_call" | custom-call | flops 1048576 | bytes 65536 | tf_op jit(solution)/shard_map/pallas_call | solution.py:435
  71.1 1.3 %shard_map.79.refs_0_ = bf16[512,1152]{1,0:T(8,128)(2,1)S(1)} custom-call(bf16[256,1152]{1,0:T(8,128)(2,1)S(1)} %copy-done, bf16[1152,3456]{1,0:T(8,128)(2,1)S(1)} %bitcast.14), custom_call_target="tpu_custom_call" | custom-call | flops 1048576 | bytes 65536 | tf_op jit(solution)/shard_map/pallas_call | solution.py:435
  72.4 0.0 collective-permute-done.11.came_c
  72.4 0.0 collective-permute-done.10.came_b
  72.4 0.2 collective-permute-done.9.came_a
  72.7 0.1 collective-permute-start.12
  72.8 1.2 %collective-permute-done.12.other_ref = bf16[144,128]{1,0:T(8,128)(2,1)S(1)} collective-permute-done((bf16[144,128]{1,0:T(8,128)(2,1)S(1)}, bf16[144,128]{1,0:T(8,128)(2,1)S(1)}, u32[]{:S(2)}, u32[]{:S(2)}) %collective-permute-start.12) | collective-permute-done | bytes 36896 | tf_op jit(solution)/shard_map/ppermute | solution.py:420
  74.0 0.0 collective-permute-done.8.came_edge_ref
  74.0 0.0 collective-permute-done.7.came_ref
  74.0 0.2 shard_map.83
  74.2 15.3 %all_to_all.11.back_ref = bf16[16,128,128]{2,1,0:T(8,128)(2,1)S(1)} all-to-all(bf16[16,128,128]{2,1,0:T(8,128)(2,1)S(1)} %shard_map.83), channel_id=1, replica_groups=mesh['yh'=2,'x'=4,'c'=2,'z'=8,'yl'=2] {'yh','x','yl'}, dimensions={0} | all-to-all | bytes 1048576 | tf_op jit(solution)/shard_map/all_to_all | solution.py:512
  89.5 1.8 %shard_map.84 = (bf16[160,512]{1,0:T(8,128)(2,1)S(1)}, f32[4,64]{1,0:T(4,128)S(1)}, f32[4,64]{1,0:T(4,128)S(1)}) custom-call(bf16[16,128,128]{2,1,0:T(8,128)(2,1)S(1)} %all_to_all.11.back_ref, bf16[512,1152]{1,0:T(8,128)(2,1)S(1)} %shard_map.79.refs_0_, bf16[512,1152]{1,0:T(8,128)(2,1)S(1)} %shard_map.80.refs_1_, bf16[512,1152]{1,0:T(8,128)(2,1)S(1)} %shard_map.81.refs_2_), custom_call_target="tpu_custom_call" | custom-call | tf_op jit(solution)/shard_map/pallas_call | solution.py:514
  91.4 4.1 %collective-permute-start.13 = (f32[4,64]{1,0:T(4,128)S(1)}, f32[4,64]{1,0:T(4,128)S(1)}, u32[]{:S(2)}, u32[]{:S(2)}) collective-permute-start(f32[4,64]{1,0:T(4,128)S(1)} %get-tuple-element.63), channel_id=1, source_target_pairs={{1,2},{3,4},{5,6},{7,8},{9,10},{11,12},{13,14},{2,1},{4,3},{6,5},{... | collective-permute-start | bytes 3080 | tf_op jit(solution)/shard_map/ppermute | solution.py:426
  95.5 0.1 collective-permute-start.14
  95.6 0.6 shard_map.85.center_ref
  96.2 1.5 %collective-permute-done.13.far_ref = f32[4,64]{1,0:T(4,128)S(1)} collective-permute-done((f32[4,64]{1,0:T(4,128)S(1)}, f32[4,64]{1,0:T(4,128)S(1)}, u32[]{:S(2)}, u32[]{:S(2)}) %collective-permute-start.13) | collective-permute-done | bytes 1056 | tf_op jit(solution)/shard_map/ppermute | solution.py:426
  97.8 1.4 %collective-permute-done.14.near_ref = f32[4,64]{1,0:T(4,128)S(1)} collective-permute-done((f32[4,64]{1,0:T(4,128)S(1)}, f32[4,64]{1,0:T(4,128)S(1)}, u32[]{:S(2)}, u32[]{:S(2)}) %collective-permute-start.14) | collective-permute-done | bytes 1056 | tf_op jit(solution)/shard_map/ppermute | solution.py:420
  99.2 0.7 shard_map.86
  (10 shorter events, 0.1 us)
Async XLA Ops:
  21.9 15.1 %collective-permute-start = (bf16[16,176,128]{2,1,0:T(8,128)(2,1)S(1)}, bf16[16,176,128]{2,1,0:T(8,128)(2,1)S(1)}, u32[]{:S(2)}, u32[]{:S(2)}) collective-permute-start(bf16[16,176,128]{2,1,0:T(8,128)(2,1)S(1)} %all_to_all.10.got_ref.qg_a), channel_id=1, source_target_pairs={{0,16},{16,0},{1,17},{17,1},{2,18},{18,2},{3,19},{19,3},{4,20},{20... | collective-permute-start | bytes 2162696 | tf_op jit(solution)/shard_map/ppermute | solution.py:420
  22.0 9.5 %collective-permute-start.3 = (bf16[144,128]{1,0:T(8,128)(2,1)S(1)}, bf16[144,128]{1,0:T(8,128)(2,1)S(1)}, u32[]{:S(2)}, u32[]{:S(2)}) collective-permute-start(bf16[144,128]{1,0:T(8,128)(2,1)S(1)} %shard_map.74), channel_id=1, source_target_pairs={{0,8},{2,10},{4,12},{6,14},{8,0},{10,2},{12,4},{14,6},{1,9},{3,11}... | collective-permute-start | bytes 110600 | tf_op jit(solution)/shard_map/ppermute | solution.py:420
  29.2 6.1 %collective-permute-start.2 = (bf16[144,128]{1,0:T(8,128)(2,1)S(1)}, bf16[144,128]{1,0:T(8,128)(2,1)S(1)}, u32[]{:S(2)}, u32[]{:S(2)}) collective-permute-start(bf16[144,128]{1,0:T(8,128)(2,1)S(1)} %shard_map.74), channel_id=1, source_target_pairs={{0,12},{2,14},{4,8},{6,10},{8,4},{10,6},{12,0},{14,2},{1,13},{3,15... | collective-permute-start | bytes 110600 | tf_op jit(solution)/shard_map/ppermute | solution.py:420
  29.3 6.1 %collective-permute-start.1 = (bf16[144,128]{1,0:T(8,128)(2,1)S(1)}, bf16[144,128]{1,0:T(8,128)(2,1)S(1)}, u32[]{:S(2)}, u32[]{:S(2)}) collective-permute-start(bf16[144,128]{1,0:T(8,128)(2,1)S(1)} %shard_map.74), channel_id=1, source_target_pairs={{0,4},{2,6},{4,0},{6,2},{8,12},{10,14},{12,8},{14,10},{1,5},{3,7},... | collective-permute-start | bytes 110600 | tf_op jit(solution)/shard_map/ppermute | solution.py:420
  35.3 7.2 %collective-permute-start.4 = (bf16[4,144,128]{2,1,0:T(8,128)(2,1)S(1)}, bf16[4,144,128]{2,1,0:T(8,128)(2,1)S(1)}, u32[]{:S(2)}, u32[]{:S(2)}) collective-permute-start(bf16[4,144,128]{2,1,0:T(8,128)(2,1)S(1)} %pad_maximum_fusion.kv_ref), channel_id=1, source_target_pairs={{0,2},{2,0},{4,6},{6,4},{8,10},{10,8},{12,14},{14,12},{1,3},{3,1},... | collective-permute-start | bytes 442376 | tf_op jit(solution)/shard_map/ppermute | solution.py:420
  48.3 1.5 %collective-permute-start.5 = (f32[2,16,128]{2,1,0:T(8,128)S(1)}, f32[2,16,128]{2,1,0:T(8,128)S(1)}, u32[]{:S(2)}, u32[]{:S(2)}) collective-permute-start(f32[2,16,128]{2,1,0:T(8,128)S(1)} %shard_map.76.mine_ref), channel_id=1, source_target_pairs={{0,16},{16,0},{1,17},{17,1},{2,18},{18,2},{3,19},{19,3},{4,20},{20... | collective-permute-start | bytes 49160 | tf_op jit(solution)/shard_map/ppermute | solution.py:420
  55.1 6.0 %collective-permute-start.6 = (bf16[4,144,128]{2,1,0:T(8,128)(2,1)S(1)}, bf16[4,144,128]{2,1,0:T(8,128)(2,1)S(1)}, u32[]{:S(2)}, u32[]{:S(2)}) collective-permute-start(bf16[4,144,128]{2,1,0:T(8,128)(2,1)S(1)} %get-tuple-element.47), channel_id=1, source_target_pairs={{0,2},{2,0},{4,6},{6,4},{8,10},{10,8},{12,14},{14,12},{1,3},{3,1},... | collective-permute-start | bytes 442376 | tf_op jit(solution)/shard_map/ppermute | solution.py:420
  55.7 12.7 %slice-start = ((s8[7962624]{0:T(1024)(128)(4,1)}), s8[4194304]{0:T(1024)(128)(4,1)S(1)}, s32[]{:S(2)}) async-start(s8[7962624]{0:T(1024)(128)(4,1)} %bitcast.13), calls=%async_computation.2 | async-start | bytes 8388608
  55.7 12.8 %slice-start.1 = ((s8[7962624]{0:T(1024)(128)(4,1)}), s8[3768320]{0:T(1024)(128)(4,1)S(1)}, s32[]{:S(2)}) async-start(s8[7962624]{0:T(1024)(128)(4,1)} %bitcast.13), calls=%async_computation.3 | async-start | bytes 7536640
  61.1 7.3 %copy-start = (bf16[256,1152]{1,0:T(8,128)(2,1)S(1)}, bf16[256,1152]{1,0:T(8,128)(2,1)}, u32[]{:S(2)}) copy-start(bf16[256,1152]{1,0:T(8,128)(2,1)} %patch_ref.2) | copy-start | bytes 1769476
  61.1 12.9 %collective-permute-start.7 = (f32[16,80,128]{2,1,0:T(8,128)S(1)}, f32[16,80,128]{2,1,0:T(8,128)S(1)}, u32[]{:S(2)}, u32[]{:S(2)}) collective-permute-start(f32[16,80,128]{2,1,0:T(8,128)S(1)} %get-tuple-element.49), channel_id=1, source_target_pairs={{0,16},{16,0},{1,17},{17,1},{2,18},{18,2},{3,19},{19,3},{4,20},{20... | collective-permute-start | bytes 1966088 | tf_op jit(solution)/shard_map/ppermute | solution.py:420
  61.2 12.8 %collective-permute-start.8 = (f32[16,24,128]{2,1,0:T(8,128)S(1)}, f32[16,24,128]{2,1,0:T(8,128)S(1)}, u32[]{:S(2)}, u32[]{:S(2)}) collective-permute-start(f32[16,24,128]{2,1,0:T(8,128)S(1)} %get-tuple-element.51), channel_id=1, source_target_pairs={{0,16},{16,0},{1,17},{17,1},{2,18},{18,2},{3,19},{19,3},{4,20},{20... | collective-permute-start | bytes 589832 | tf_op jit(solution)/shard_map/ppermute | solution.py:420
  61.8 10.6 %collective-permute-start.11 = (bf16[144,128]{1,0:T(8,128)(2,1)S(1)}, bf16[144,128]{1,0:T(8,128)(2,1)S(1)}, u32[]{:S(2)}, u32[]{:S(2)}) collective-permute-start(bf16[144,128]{1,0:T(8,128)(2,1)S(1)} %get-tuple-element.69), channel_id=1, source_target_pairs={{0,8},{2,10},{4,12},{6,14},{8,0},{10,2},{12,4},{14,6},{1,9},{3,11}... | collective-permute-start | bytes 110600 | tf_op jit(solution)/shard_map/ppermute | solution.py:420
  65.9 6.6 %collective-permute-start.10 = (bf16[144,128]{1,0:T(8,128)(2,1)S(1)}, bf16[144,128]{1,0:T(8,128)(2,1)S(1)}, u32[]{:S(2)}, u32[]{:S(2)}) collective-permute-start(bf16[144,128]{1,0:T(8,128)(2,1)S(1)} %get-tuple-element.70), channel_id=1, source_target_pairs={{0,12},{2,14},{4,8},{6,10},{8,4},{10,6},{12,0},{14,2},{1,13},{3,15... | collective-permute-start | bytes 110600 | tf_op jit(solution)/shard_map/ppermute | solution.py:420
  67.5 5.2 %collective-permute-start.9 = (bf16[144,128]{1,0:T(8,128)(2,1)S(1)}, bf16[144,128]{1,0:T(8,128)(2,1)S(1)}, u32[]{:S(2)}, u32[]{:S(2)}) collective-permute-start(bf16[144,128]{1,0:T(8,128)(2,1)S(1)} %get-tuple-element.71), channel_id=1, source_target_pairs={{0,4},{2,6},{4,0},{6,2},{8,12},{10,14},{12,8},{14,10},{1,5},{3,7},... | collective-permute-start | bytes 110600 | tf_op jit(solution)/shard_map/ppermute | solution.py:420
  72.7 1.3 %collective-permute-start.12 = (bf16[144,128]{1,0:T(8,128)(2,1)S(1)}, bf16[144,128]{1,0:T(8,128)(2,1)S(1)}, u32[]{:S(2)}, u32[]{:S(2)}) collective-permute-start(bf16[144,128]{1,0:T(8,128)(2,1)S(1)} %shard_map.82.keys_ref), channel_id=1, source_target_pairs={{0,16},{16,0},{1,17},{17,1},{2,18},{18,2},{3,19},{19,3},{4,20},{20... | collective-permute-start | bytes 110600 | tf_op jit(solution)/shard_map/ppermute | solution.py:420
  91.4 6.4 %collective-permute-start.13 = (f32[4,64]{1,0:T(4,128)S(1)}, f32[4,64]{1,0:T(4,128)S(1)}, u32[]{:S(2)}, u32[]{:S(2)}) collective-permute-start(f32[4,64]{1,0:T(4,128)S(1)} %get-tuple-element.63), channel_id=1, source_target_pairs={{1,2},{3,4},{5,6},{7,8},{9,10},{11,12},{13,14},{2,1},{4,3},{6,5},{... | collective-permute-start | bytes 3080 | tf_op jit(solution)/shard_map/ppermute | solution.py:426
  95.5 3.7 %collective-permute-start.14 = (f32[4,64]{1,0:T(4,128)S(1)}, f32[4,64]{1,0:T(4,128)S(1)}, u32[]{:S(2)}, u32[]{:S(2)}) collective-permute-start(f32[4,64]{1,0:T(4,128)S(1)} %get-tuple-element.64), channel_id=1, source_target_pairs={{0,1},{1,0},{2,3},{3,2},{4,5},{5,4},{6,7},{7,6},{8,9},{9,8},{10,11... | collective-permute-start | bytes 3080 | tf_op jit(solution)/shard_map/ppermute | solution.py:420

commit v10 on v9

--- a/solution.py
+++ b/solution.py
@@ -1,4 +1,3 @@
-import functools
 import math
 
 import jax
@@ -102,12 +101,12 @@
     out_ref[...] = jnp.concatenate([k_t[0:DH], v_t[0:DH]]).astype(bf16)
 
 
-def load_keys(kv_ref, k_s, kt_s=None, v_s=None):
+def load_keys(blocks, k_s, kt_s=None, v_s=None):
     lane = lax.broadcasted_iota(jnp.int32, (128, 128), 1)
     pad = jnp.zeros((128 - DH, 128), f32)
     norms = jnp.zeros((1, 128), f32)
-    for b in range(4):
-        kv = kv_ref[b].astype(f32)
+    for b, block in enumerate(blocks):
+        kv = block.astype(f32)
         keys = slice(b * 128, (b + 1) * 128)
         k_t = jnp.concatenate([kv[0:DH], pad])
         norms = jnp.maximum(norms, jnp.sum(k_t * k_t, axis=0, keepdims=True))
@@ -168,15 +167,15 @@
     return top + jnp.log2(jnp.exp2(one - top) + jnp.exp2(two - top))
 
 
-def even_sums_kernel(qg_a, qg_b, kv_ref, out_ref, k_s):
-    norm = load_keys(kv_ref, k_s)
+def first_sums_kernel(qg_a, qg_b, kv_0, kv_1, kv_2, kv_6, out_ref, k_s):
+    norm = load_keys((kv_0[...], kv_1[...], kv_2[...], kv_6[...]), k_s)
     put_sums(out_ref, log_sums(tile_of((qg_a, qg_b), 0), k_s, norm))
 
 
-def odd_sums_kernel(qg_a, qg_b, kv_ref, even_ref, out_ref, k_s):
-    norm = load_keys(kv_ref, k_s)
+def second_sums_kernel(qg_a, qg_b, kv_37, kv_45, first_ref, out_ref, k_s):
+    norm = load_keys((kv_37[0], kv_37[1], kv_45[0], kv_45[1]), k_s)
     mine = log_sums(tile_of((qg_a, qg_b), 0), k_s, norm)
-    put_sums(out_ref, added(mine, get_sums(even_ref)))
+    put_sums(out_ref, added(mine, get_sums(first_ref)))
 
 
 def gradients(sums_ref, qg_refs, put_dq, k_s, kt_s, v_s, dk_s, dv_s):
@@ -208,10 +207,10 @@
 
 
 def first_kernel(
-    qg_a, qg_b, kv_ref, mine_ref, came_ref, sums_ref, dq_a, dq_b, out_ref,
+    qg_a, qg_b, kv_1, kv_37, kv_45, mine_ref, came_ref, sums_ref, dq_a, dq_b, out_ref,
     k_s, kt_s, v_s, dk_s, dv_s,
 ):
-    load_keys(kv_ref, k_s, kt_s, v_s)
+    load_keys((kv_1[...], kv_37[0], kv_37[1], kv_45[1]), k_s, kt_s, v_s)
     for at in (0, 1):
         sums_ref[at] = added(mine_ref[at], came_ref[1 - at])
 
@@ -232,10 +231,10 @@
 
 
 def second_kernel(
-    qg_a, qg_b, kv_ref, sums_ref, in_a, in_b, dq_a, dq_b, edge_a, edge_b, out_ref,
+    qg_a, qg_b, kv_0, kv_2, kv_6, kv_45, sums_ref, in_a, in_b, dq_a, dq_b, edge_a, edge_b, out_ref,
     k_s, kt_s, v_s, dk_s, dv_s,
 ):
-    load_keys(kv_ref, k_s, kt_s, v_s)
+    load_keys((kv_0[...], kv_2[...], kv_6[...], kv_45[0]), k_s, kt_s, v_s)
 
     def put_dq(at, n, dq):
         dq = (in_a, in_b)[at][n] + dq
@@ -281,22 +280,15 @@
     send_ref[...] = jnp.concatenate(parts, axis=1).astype(bf16)
 
 
-def weights_kernel(part, patch_ref, qkv_ref, out_ref, qkv_s, sems):
-    step = 128
-    copies = []
-    for n in range(D // step):
-        rows = slice(n * step, (n + 1) * step)
-        source = qkv_ref.at[rows, part * D : (part + 1) * D]
-        copies.append(pltpu.make_async_copy(source, qkv_s.at[rows], sems.at[n]))
-        copies[-1].start()
-    for copy in copies:
-        copy.wait()
-    both = jnp.dot(patch_ref[...], qkv_s[...], preferred_element_type=f32)
-    both = both.reshape(16, 2, 8, D)
-    both = jnp.concatenate([both[:, 0].reshape(128, D), both[:, 1].reshape(128, D)])
-    high = both.astype(bf16)
-    out_ref[0:256] = high
-    out_ref[256:512] = (both - high.astype(f32)).astype(bf16)
+def weights_kernel(patch_ref, qkv_ref, out_ref):
+    for part in range(3):
+        cols = slice(part * D, (part + 1) * D)
+        both = jnp.dot(patch_ref[...], qkv_ref[:, cols], preferred_element_type=f32)
+        both = both.reshape(16, 2, 8, D)
+        both = jnp.concatenate([both[:, 0].reshape(128, D), both[:, 1].reshape(128, D)])
+        high, low = split(both)
+        out_ref[0:256, cols] = high
+        out_ref[256:512, cols] = low
 
 
 def split(x):
@@ -312,8 +304,7 @@
     return jnp.where(where, value, 0.0).astype(bf16)
 
 
-def embed_kernel(back_ref, *refs):
-    weights, (turned_ref, near_out, far_out, joined, pooled, sheet) = refs[:3], refs[3:]
+def embed_kernel(back_ref, weights, turned_ref, near_out, far_out, joined, pooled, sheet):
     for h in range(0, HEADS, 2):
         pair = []
         wide = []
@@ -338,10 +329,9 @@
                 two = [jnp.where(group == 4 * part + k, cells, 0.0) for k in (n, n + 1)]
                 rows = part * D + (h + n) * DH
                 pooled[rows : rows + 2 * DH] = jnp.concatenate(two).astype(bf16)
-    patch = jnp.dot(weights[0][...], joined[...], preferred_element_type=f32)
+    patch = jnp.dot(weights[:, 0:D], joined[...], preferred_element_type=f32)
     patch = patch[0:256] + patch[256:512]
-    cells = jnp.dot(weights[1][...], pooled[0:D], preferred_element_type=f32)
-    cells = cells + jnp.dot(weights[2][...], pooled[D:], preferred_element_type=f32)
+    cells = jnp.dot(weights[:, D:], pooled[...], preferred_element_type=f32)
     cells = jnp.concatenate(split(cells[0:256] + cells[256:512]), axis=1)
     cell, token = iota((256, 256), 0) % 16, iota((256, 256), 1)
     mine = token // (POOL * COLS) * 4 + token % COLS // POOL
@@ -431,17 +421,6 @@
     return pl.CostEstimate(flops=flops, bytes_accessed=2**20, transcendentals=2 * QUERIES * HALF)
 
 
-def combined_weights(w_qkv, w_patch, part):
-    return call(
-        functools.partial(weights_kernel, part),
-        jax.ShapeDtypeStruct((512, D), bf16),
-        12,
-        [pltpu.VMEM((D, D), bf16), pltpu.SemaphoreType.DMA((D // 128,))],
-        [WHOLE, ANYWHERE],
-        cost_estimate=SMALL,
-    )(w_patch, w_qkv)
-
-
 def on_device(queries, key_states, values, saved_out, grad_out, w_qkv, w_patch):
     tokens = pltpu.VMEM((TOK, D), bf16)
     cells = pltpu.VMEM((2, 4, D), bf16)
@@ -469,15 +448,15 @@
         [pltpu.VMEM((HEADS, 16, 128), bf16), dma(())],
         [ANYWHERE],
     )(got)
-    came = [swapped(kv, "z", by) for by in EVEN]
-    even = jnp.stack([kv] + came)
-    odd = swapped(even, "z", 1)
+    kv_1, kv_2, kv_6 = [swapped(kv, "z", by) for by in (1, 2, 6)]
+    kv_37 = swapped(jnp.stack([kv_2, kv_6]), "z", 1)
+    kv_45 = swapped(jnp.stack([kv, kv_1]), "z", 4)
     there = swapped(got, "c", 1)
     keys = pltpu.VMEM((HALF, 128), bf16)
     sums = jax.ShapeDtypeStruct((2, HEADS, TOK), f32)
-    even_sums = call(even_sums_kernel, sums, 24, [keys], cost_estimate=cost(1))(got, there, even)
-    odd, even_sums = lax.optimization_barrier((odd, even_sums))
-    mine = call(odd_sums_kernel, sums, 24, [keys], cost_estimate=cost(1))(got, there, odd, even_sums)
+    mine = call(first_sums_kernel, sums, 24, [keys], cost_estimate=cost(1))(got, there, kv, kv_1, kv_2, kv_6)
+    kv_37, kv_45, mine = lax.optimization_barrier((kv_37, kv_45, mine))
+    mine = call(second_sums_kernel, sums, 24, [keys], cost_estimate=cost(1))(got, there, kv_37, kv_45, mine)
     came = swapped(mine, "c", 1)
     scratch = [keys, pltpu.VMEM((128, HALF), bf16), keys]
     scratch += [pltpu.VMEM((HALF, 128), f32)] * 2
@@ -485,7 +464,7 @@
     block = (4, 2 * DH, 128)
     sums, dq_here, dq_there, grads = call(
         first_kernel, [sums] + dq + [jax.ShapeDtypeStruct(block, bf16)], 32, scratch, cost_estimate=cost(5)
-    )(got, there, odd, mine, came)
+    )(got, there, kv_1, kv_37, kv_45, mine, came)
     came = swapped(grads, "z", 1)
     edges = [jax.ShapeDtypeStruct((HEADS, 24, TOK), f32)] * 2
     *dq, grads = call(
@@ -494,7 +473,7 @@
         32,
         scratch,
         cost_estimate=cost(5),
-    )(got, there, even, sums, dq_here, dq_there)
+    )(got, there, kv, kv_2, kv_6, kv_45, sums, dq_here, dq_there)
     dq, grads, came = lax.optimization_barrier((dq, grads, came))
     dq_here, dq_there, edge_here, edge_there = dq
     dq_there = swapped(dq_there, "c", 1)
@@ -502,7 +481,9 @@
     mine = grads + came.astype(f32)
     mine, w_qkv, w_patch = lax.optimization_barrier((mine, w_qkv, w_patch))
     came = [swapped(mine[n + 1].astype(bf16), "z", by) for n, by in enumerate(EVEN)]
-    weights = [combined_weights(w_qkv, w_patch, part) for part in range(3)]
+    weights = call(
+        weights_kernel, jax.ShapeDtypeStruct((512, 3 * D), bf16), 24, cost_estimate=SMALL
+    )(w_patch, w_qkv)
     came, weights = lax.optimization_barrier((came, weights))
     keys = call(keys_sum_kernel, jax.ShapeDtypeStruct((2 * DH, 128), bf16), 4)(mine[0:1], *came)
     other = swapped(keys, "c", 1)
@@ -516,7 +497,7 @@
         [jax.ShapeDtypeStruct((EXTENDED, 512), bf16), strip, strip],
         28,
         [pltpu.VMEM((D, 2 * TOK), bf16), pltpu.VMEM((2 * D, 128), bf16), pltpu.VMEM((72, 128), f32)],
-    )(back, *weights)
+    )(back, weights)
     far, near = neighbours(to_far, COL), swapped(to_near, "yl", 1)
     center = call(
         fold_kernel,

time: 100 us -> 98.5 us (0.985)
  waiting for transfers between devices: 10.2 us -> 6.51 us
  starting transfers between devices: 22.7 us -> 25.9 us
  Pallas kernels: 32 us -> 30.8 us
    ppermute x14 -> x15, waiting for transfers between devices: 8.65 us -> 5.33 us  [swapped(): return lax.ppermute(x, axis, [(i, i ^ by) for i in range(peers)])]
    ppermute x14 -> x15, starting transfers between devices: 18.5 us -> 21.5 us  [swapped(): return lax.ppermute(x, axis, [(i, i ^ by) for i in range(peers)])]
    pallas_call x5 -> x3, Pallas kernels: 15.2 us -> 14 us  [the longest x1 5.66 us: on_device(): call(second_sums_kernel, sums, 24, [keys], cost_estimate=cost(1))]
  transfers between devices with their start and end apart: 15 -> 16, of which waited for: 7 -> 6; matrix products, arithmetic and copies ran while one was open for 0% -> 0% of each run, Pallas kernels for 16% -> 15%
where the time goes in v10:
time: 98.5 us; the launch traced here: 98.2 us
  blocking collectives  34.7 us (35%)
  Pallas kernels  30.8 us (31%)
  starting transfers between devices  25.9 us (26%)
  waiting for transfers between devices  6.51 us (7%)
    ppermute x15, starting transfers between devices, swapped(): return lax.ppermute(x, axis, [(i, i ^ by) for i in range(peers)])  21.5 us
    all_to_all x1, blocking collectives, on_device(): got = lax.all_to_all(send, HEAD_AXES, 0, 0, tiled=True)  19.4 us
    all_to_all x1, blocking collectives, on_device(): back = lax.all_to_all(send, HEAD_AXES, 0, 0, tiled=True)  15.3 us
    pallas_call x1, Pallas kernels, on_device(): call(second_sums_kernel, sums, 24, [keys], cost_estimate=cost(1))  5.66 us
    pallas_call x1, Pallas kernels, on_device(): call(first_sums_kernel, sums, 24, [keys], cost_estimate=cost(1))  5.59 us
    pallas_call x1, Pallas kernels, on_device(): call(second_kernel, dq + edges + [jax.ShapeDtypeStruct(block, f32)], 32,...  5.47 us
    pallas_call x1, Pallas kernels, on_device(): call(first_kernel, [sums] + dq + [jax.ShapeDtypeStruct(block, bf16)], 32,...  5.39 us
    ppermute x15, waiting for transfers between devices, swapped(): return lax.ppermute(x, axis, [(i, i ^ by) for i in range(peers)])  5.33 us
  transfers between devices with their start and end apart: 16, of which 6 were waited for; matrix products, arithmetic and copies ran while one was open for 0% of the time, Pallas kernels for 15%

profile of v10, /device:TPU:8, one launch (start us, length us, event | category | flops | bytes accessed | tf_op | source)
XLA Modules:
  0.0 98.2 jit_solution(6082302529902242001)
XLA Ops:
  0.0 2.5 %shard_map.73 = bf16[16,176,128]{2,1,0:T(8,128)(2,1)} custom-call(bf16[128,1152]{1,0:T(8,128)(2,1)} %bitcast.19, bf16[128,1152]{1,0:T(8,128)(2,1)} %bitcast.20, bf16[128,1152]{1,0:T(8,128)(2,1)} %bitcast.21, bf16[2,4,1152]{2,1,0:T(4,128)(2,1)} %k_in.1, bf16[2,4,1152]{2,1,0:T(4,128)(2,1)} %v_in.1), custom_call_target="tpu_custom_call" | custom-call | tf_op jit(solution)/shard_map/pallas_call | solution.py:429
  2.5 19.4 %all_to_all.10.got_ref.qg_a = bf16[16,176,128]{2,1,0:T(8,128)(2,1)S(1)} all-to-all(bf16[16,176,128]{2,1,0:T(8,128)(2,1)} %shard_map.73), channel_id=1, replica_groups=mesh['yh'=2,'x'=4,'c'=2,'z'=8,'yl'=2] {'yh','x','yl'}, dimensions={0} | all-to-all | bytes 1441792 | tf_op jit(solution)/shard_map/all_to_all | solution.py:443
  21.8 0.0 collective-permute-start
  21.9 0.1 shard_map.74.kv_0
  22.0 2.0 %collective-permute-start.4 = (bf16[144,128]{1,0:T(8,128)(2,1)S(1)}, bf16[144,128]{1,0:T(8,128)(2,1)S(1)}, u32[]{:S(2)}, u32[]{:S(2)}) collective-permute-start(bf16[144,128]{1,0:T(8,128)(2,1)S(1)} %shard_map.74.kv_0), channel_id=1, source_target_pairs={{0,2},{2,0},{4,6},{6,4},{8,10},{10,8},{12,14},{14,12},{1,3},{3,1},... | collective-permute-start | bytes 110600 | tf_op jit(solution)/shard_map/ppermute | solution.py:410
  24.0 5.4 %collective-permute-start.2 = (bf16[144,128]{1,0:T(8,128)(2,1)S(1)}, bf16[144,128]{1,0:T(8,128)(2,1)S(1)}, u32[]{:S(2)}, u32[]{:S(2)}) collective-permute-start(bf16[144,128]{1,0:T(8,128)(2,1)S(1)} %shard_map.74.kv_0), channel_id=1, source_target_pairs={{0,12},{2,14},{4,8},{6,10},{8,4},{10,6},{12,0},{14,2},{1,13},{3,15... | collective-permute-start | bytes 110600 | tf_op jit(solution)/shard_map/ppermute | solution.py:410
  29.4 1.5 %collective-permute-start.1 = (bf16[144,128]{1,0:T(8,128)(2,1)S(1)}, bf16[144,128]{1,0:T(8,128)(2,1)S(1)}, u32[]{:S(2)}, u32[]{:S(2)}) collective-permute-start(bf16[144,128]{1,0:T(8,128)(2,1)S(1)} %shard_map.74.kv_0), channel_id=1, source_target_pairs={{0,4},{2,6},{4,0},{6,2},{8,12},{10,14},{12,8},{14,10},{1,5},{3,7},... | collective-permute-start | bytes 110600 | tf_op jit(solution)/shard_map/ppermute | solution.py:410
  30.8 0.0 collective-permute-done.4.kv_1
  30.8 2.8 %collective-permute-start.5 = (bf16[2,144,128]{2,1,0:T(8,128)(2,1)S(1)}, bf16[2,144,128]{2,1,0:T(8,128)(2,1)S(1)}, u32[]{:S(2)}, u32[]{:S(2)}) collective-permute-start(bf16[2,144,128]{2,1,0:T(8,128)(2,1)S(1)} %pad_maximum_fusion.1), channel_id=1, source_target_pairs={{0,8},{2,10},{4,12},{6,14},{8,0},{10,2},{12,4},{14,6},{1,9},{3,11}... | collective-permute-start | bytes 221192 | tf_op jit(solution)/shard_map/ppermute | solution.py:410
  33.6 0.0 collective-permute-done.2.kv_6
  33.6 0.6 collective-permute-done.1.kv_2
  34.2 1.1 %collective-permute-start.3 = (bf16[2,144,128]{2,1,0:T(8,128)(2,1)S(1)}, bf16[2,144,128]{2,1,0:T(8,128)(2,1)S(1)}, u32[]{:S(2)}, u32[]{:S(2)}) collective-permute-start(bf16[2,144,128]{2,1,0:T(8,128)(2,1)S(1)} %pad_maximum_fusion), channel_id=1, source_target_pairs={{0,2},{2,0},{4,6},{6,4},{8,10},{10,8},{12,14},{14,12},{1,3},{3,1},... | collective-permute-start | bytes 221192 | tf_op jit(solution)/shard_map/ppermute | solution.py:410
  35.3 0.0 collective-permute-done.qg_b
  35.3 5.6 %shard_map.75.first_ref = f32[2,16,128]{2,1,0:T(8,128)S(1)} custom-call(bf16[16,176,128]{2,1,0:T(8,128)(2,1)S(1)} %all_to_all.10.got_ref.qg_a, bf16[16,176,128]{2,1,0:T(8,128)(2,1)S(1)} %collective-permute-done.qg_b, bf16[144,128]{1,0:T(8,128)(2,1)S(1)} %shard_map.74.kv_0, bf16[144,128]{1,0:T(8,128)(2,1)S(1)} %collective-permute-done.4.kv_1, ...), custom_call_target="tpu_custom_call" | custom-call | flops 1073741824 | bytes 1048576 | tf_op jit(solution)/shard_map/pallas_call | solution.py:457
  40.9 0.0 collective-permute-done.5.kv_45
  41.0 0.0 collective-permute-done.3.kv_37
  41.0 5.7 %shard_map.76.mine_ref = f32[2,16,128]{2,1,0:T(8,128)S(1)} custom-call(bf16[16,176,128]{2,1,0:T(8,128)(2,1)S(1)} %all_to_all.10.got_ref.qg_a, bf16[16,176,128]{2,1,0:T(8,128)(2,1)S(1)} %collective-permute-done.qg_b, bf16[2,144,128]{2,1,0:T(8,128)(2,1)S(1)} %collective-permute-done.3.kv_37, bf16[2,144,128]{2,1,0:T(8,128)(2,1)S(1)} %collective-permute-done.5.kv_45, ...), custom_call_target="tpu_custom_call" | custom-call | flops 1073741824 | bytes 1048576 | tf_op jit(solution)/shard_map/pallas_call | solution.py:459
  46.6 0.3 collective-permute-start.6
  46.9 1.2 %collective-permute-done.6.came_ref = f32[2,16,128]{2,1,0:T(8,128)S(1)} collective-permute-done((f32[2,16,128]{2,1,0:T(8,128)S(1)}, f32[2,16,128]{2,1,0:T(8,128)S(1)}, u32[]{:S(2)}, u32[]{:S(2)}) %collective-permute-start.6) | collective-permute-done | bytes 16416 | tf_op jit(solution)/shard_map/ppermute | solution.py:410
  48.1 5.4 %shard_map.77 = (f32[2,16,128]{2,1,0:T(8,128)S(1)}, f32[16,80,128]{2,1,0:T(8,128)S(1)}, f32[16,80,128]{2,1,0:T(8,128)S(1)}, bf16[4,144,128]{2,1,0:T(8,128)(2,1)S(1)}) custom-call(bf16[16,176,128]{2,1,0:T(8,128)(2,1)S(1)} %all_to_all.10.got_ref.qg_a, bf16[16,176,128]{2,1,0:T(8,128)(2,1)S(1)} %collective-permute-done.qg_b, ...), custom_call_target="tpu_custom_call" | custom-call | flops 5368709120 | bytes 1048576 | tf_op jit(solution)/shard_map/pallas_call | solution.py:465
  53.5 1.1 %collective-permute-start.7 = (bf16[4,144,128]{2,1,0:T(8,128)(2,1)S(1)}, bf16[4,144,128]{2,1,0:T(8,128)(2,1)S(1)}, u32[]{:S(2)}, u32[]{:S(2)}) collective-permute-start(bf16[4,144,128]{2,1,0:T(8,128)(2,1)S(1)} %get-tuple-element.47), channel_id=1, source_target_pairs={{0,2},{2,0},{4,6},{6,4},{8,10},{10,8},{12,14},{14,12},{1,3},{3,1},... | collective-permute-start | bytes 442376 | tf_op jit(solution)/shard_map/ppermute | solution.py:410
  54.6 5.5 %shard_map.78 = (f32[16,80,128]{2,1,0:T(8,128)S(1)}, f32[16,80,128]{2,1,0:T(8,128)S(1)}, f32[16,24,128]{2,1,0:T(8,128)S(1)}, f32[16,24,128]{2,1,0:T(8,128)S(1)}, f32[4,144,128]{2,1,0:T(8,128)S(1)}) custom-call(bf16[16,176,128]{2,1,0:T(8,128)(2,1)S(1)} %all_to_all.10.got_ref.qg_a, bf16[16,176,128]{2,1,0:T(8,128)(2,1)S(1)} %collective-permute-done.qg_b, ...), custom_call_target="tpu_custom_call" | custom-call | flops 5368709120 | bytes 1048576 | tf_op jit(solution)/shard_map/pallas_call | solution.py:470
  60.1 0.0 collective-permute-done.7
  60.1 0.1 collective-permute-start.8
  60.2 0.5 collective-permute-start.9
  60.8 2.7 %collective-permute-start.12 = (bf16[144,128]{1,0:T(8,128)(2,1)S(1)}, bf16[144,128]{1,0:T(8,128)(2,1)S(1)}, u32[]{:S(2)}, u32[]{:S(2)}) collective-permute-start(bf16[144,128]{1,0:T(8,128)(2,1)S(1)} %get-tuple-element.67), channel_id=1, source_target_pairs={{0,8},{2,10},{4,12},{6,14},{8,0},{10,2},{12,4},{14,6},{1,9},{3,11}... | collective-permute-start | bytes 110600 | tf_op jit(solution)/shard_map/ppermute | solution.py:410
  63.5 2.4 %collective-permute-start.11 = (bf16[144,128]{1,0:T(8,128)(2,1)S(1)}, bf16[144,128]{1,0:T(8,128)(2,1)S(1)}, u32[]{:S(2)}, u32[]{:S(2)}) collective-permute-start(bf16[144,128]{1,0:T(8,128)(2,1)S(1)} %get-tuple-element.68), channel_id=1, source_target_pairs={{0,12},{2,14},{4,8},{6,10},{8,4},{10,6},{12,0},{14,2},{1,13},{3,15... | collective-permute-start | bytes 110600 | tf_op jit(solution)/shard_map/ppermute | solution.py:410
  65.9 1.5 %collective-permute-start.10 = (bf16[144,128]{1,0:T(8,128)(2,1)S(1)}, bf16[144,128]{1,0:T(8,128)(2,1)S(1)}, u32[]{:S(2)}, u32[]{:S(2)}) collective-permute-start(bf16[144,128]{1,0:T(8,128)(2,1)S(1)} %get-tuple-element.69), channel_id=1, source_target_pairs={{0,4},{2,6},{4,0},{6,2},{8,12},{10,14},{12,8},{14,10},{1,5},{3,7},... | collective-permute-start | bytes 110600 | tf_op jit(solution)/shard_map/ppermute | solution.py:410
  67.3 0.0 slice-done
  67.4 0.0 slice-done.1
  67.4 0.0 copy-done
  67.4 2.8 %shard_map.79.weights = bf16[512,3456]{1,0:T(8,128)(2,1)S(1)} custom-call(bf16[256,1152]{1,0:T(8,128)(2,1)S(1)} %copy-done, bf16[1152,3456]{1,0:T(8,128)(2,1)S(1)} %bitcast.14), custom_call_target="tpu_custom_call" | custom-call | flops 1048576 | bytes 65536 | tf_op jit(solution)/shard_map/pallas_call | solution.py:484
  70.1 0.0 collective-permute-done.12.came_c
  70.1 0.0 collective-permute-done.11.came_b
  70.2 0.6 collective-permute-done.10.came_a
  70.7 0.1 collective-permute-start.13
  70.8 1.2 %collective-permute-done.13.other_ref = bf16[144,128]{1,0:T(8,128)(2,1)S(1)} collective-permute-done((bf16[144,128]{1,0:T(8,128)(2,1)S(1)}, bf16[144,128]{1,0:T(8,128)(2,1)S(1)}, u32[]{:S(2)}, u32[]{:S(2)}) %collective-permute-start.13) | collective-permute-done | bytes 36896 | tf_op jit(solution)/shard_map/ppermute | solution.py:410
  72.1 0.0 collective-permute-done.9.came_edge_ref
  72.1 0.0 collective-permute-done.8.came_ref
  72.1 0.2 shard_map.81
  72.2 15.3 %all_to_all.11.back_ref = bf16[16,128,128]{2,1,0:T(8,128)(2,1)S(1)} all-to-all(bf16[16,128,128]{2,1,0:T(8,128)(2,1)S(1)} %shard_map.81), channel_id=1, replica_groups=mesh['yh'=2,'x'=4,'c'=2,'z'=8,'yl'=2] {'yh','x','yl'}, dimensions={0} | all-to-all | bytes 1048576 | tf_op jit(solution)/shard_map/all_to_all | solution.py:493
  87.5 1.9 %shard_map.82 = (bf16[160,512]{1,0:T(8,128)(2,1)S(1)}, f32[4,64]{1,0:T(4,128)S(1)}, f32[4,64]{1,0:T(4,128)S(1)}) custom-call(bf16[16,128,128]{2,1,0:T(8,128)(2,1)S(1)} %all_to_all.11.back_ref, bf16[512,3456]{1,0:T(8,128)(2,1)S(1)} %shard_map.79.weights), custom_call_target="tpu_custom_call" | custom-call | tf_op jit(solution)/shard_map/pallas_call | solution.py:495
  89.4 4.5 %collective-permute-start.14 = (f32[4,64]{1,0:T(4,128)S(1)}, f32[4,64]{1,0:T(4,128)S(1)}, u32[]{:S(2)}, u32[]{:S(2)}) collective-permute-start(f32[4,64]{1,0:T(4,128)S(1)} %get-tuple-element.61), channel_id=1, source_target_pairs={{1,2},{3,4},{5,6},{7,8},{9,10},{11,12},{13,14},{2,1},{4,3},{6,5},{... | collective-permute-start | bytes 3080 | tf_op jit(solution)/shard_map/ppermute | solution.py:416
  93.9 0.1 collective-permute-start.15
  94.0 0.6 shard_map.83.center_ref
  94.6 1.2 %collective-permute-done.14.far_ref = f32[4,64]{1,0:T(4,128)S(1)} collective-permute-done((f32[4,64]{1,0:T(4,128)S(1)}, f32[4,64]{1,0:T(4,128)S(1)}, u32[]{:S(2)}, u32[]{:S(2)}) %collective-permute-start.14) | collective-permute-done | bytes 1056 | tf_op jit(solution)/shard_map/ppermute | solution.py:416
  95.8 1.8 %collective-permute-done.15.near_ref = f32[4,64]{1,0:T(4,128)S(1)} collective-permute-done((f32[4,64]{1,0:T(4,128)S(1)}, f32[4,64]{1,0:T(4,128)S(1)}, u32[]{:S(2)}, u32[]{:S(2)}) %collective-permute-start.15) | collective-permute-done | bytes 1056 | tf_op jit(solution)/shard_map/ppermute | solution.py:410
  97.5 0.7 shard_map.84
  (11 shorter events, 0.1 us)
Async XLA Ops:
  21.8 13.5 %collective-permute-start = (bf16[16,176,128]{2,1,0:T(8,128)(2,1)S(1)}, bf16[16,176,128]{2,1,0:T(8,128)(2,1)S(1)}, u32[]{:S(2)}, u32[]{:S(2)}) collective-permute-start(bf16[16,176,128]{2,1,0:T(8,128)(2,1)S(1)} %all_to_all.10.got_ref.qg_a), channel_id=1, source_target_pairs={{0,16},{16,0},{1,17},{17,1},{2,18},{18,2},{3,19},{19,3},{4,20},{20... | collective-permute-start | bytes 2162696 | tf_op jit(solution)/shard_map/ppermute | solution.py:410
  22.0 8.9 %collective-permute-start.4 = (bf16[144,128]{1,0:T(8,128)(2,1)S(1)}, bf16[144,128]{1,0:T(8,128)(2,1)S(1)}, u32[]{:S(2)}, u32[]{:S(2)}) collective-permute-start(bf16[144,128]{1,0:T(8,128)(2,1)S(1)} %shard_map.74.kv_0), channel_id=1, source_target_pairs={{0,2},{2,0},{4,6},{6,4},{8,10},{10,8},{12,14},{14,12},{1,3},{3,1},... | collective-permute-start | bytes 110600 | tf_op jit(solution)/shard_map/ppermute | solution.py:410
  24.0 9.6 %collective-permute-start.2 = (bf16[144,128]{1,0:T(8,128)(2,1)S(1)}, bf16[144,128]{1,0:T(8,128)(2,1)S(1)}, u32[]{:S(2)}, u32[]{:S(2)}) collective-permute-start(bf16[144,128]{1,0:T(8,128)(2,1)S(1)} %shard_map.74.kv_0), channel_id=1, source_target_pairs={{0,12},{2,14},{4,8},{6,10},{8,4},{10,6},{12,0},{14,2},{1,13},{3,15... | collective-permute-start | bytes 110600 | tf_op jit(solution)/shard_map/ppermute | solution.py:410
  29.4 4.9 %collective-permute-start.1 = (bf16[144,128]{1,0:T(8,128)(2,1)S(1)}, bf16[144,128]{1,0:T(8,128)(2,1)S(1)}, u32[]{:S(2)}, u32[]{:S(2)}) collective-permute-start(bf16[144,128]{1,0:T(8,128)(2,1)S(1)} %shard_map.74.kv_0), channel_id=1, source_target_pairs={{0,4},{2,6},{4,0},{6,2},{8,12},{10,14},{12,8},{14,10},{1,5},{3,7},... | collective-permute-start | bytes 110600 | tf_op jit(solution)/shard_map/ppermute | solution.py:410
  30.8 10.1 %collective-permute-start.5 = (bf16[2,144,128]{2,1,0:T(8,128)(2,1)S(1)}, bf16[2,144,128]{2,1,0:T(8,128)(2,1)S(1)}, u32[]{:S(2)}, u32[]{:S(2)}) collective-permute-start(bf16[2,144,128]{2,1,0:T(8,128)(2,1)S(1)} %pad_maximum_fusion.1), channel_id=1, source_target_pairs={{0,8},{2,10},{4,12},{6,14},{8,0},{10,2},{12,4},{14,6},{1,9},{3,11}... | collective-permute-start | bytes 221192 | tf_op jit(solution)/shard_map/ppermute | solution.py:410
  34.2 6.7 %collective-permute-start.3 = (bf16[2,144,128]{2,1,0:T(8,128)(2,1)S(1)}, bf16[2,144,128]{2,1,0:T(8,128)(2,1)S(1)}, u32[]{:S(2)}, u32[]{:S(2)}) collective-permute-start(bf16[2,144,128]{2,1,0:T(8,128)(2,1)S(1)} %pad_maximum_fusion), channel_id=1, source_target_pairs={{0,2},{2,0},{4,6},{6,4},{8,10},{10,8},{12,14},{14,12},{1,3},{3,1},... | collective-permute-start | bytes 221192 | tf_op jit(solution)/shard_map/ppermute | solution.py:410
  46.6 1.5 %collective-permute-start.6 = (f32[2,16,128]{2,1,0:T(8,128)S(1)}, f32[2,16,128]{2,1,0:T(8,128)S(1)}, u32[]{:S(2)}, u32[]{:S(2)}) collective-permute-start(f32[2,16,128]{2,1,0:T(8,128)S(1)} %shard_map.76.mine_ref), channel_id=1, source_target_pairs={{0,16},{16,0},{1,17},{17,1},{2,18},{18,2},{3,19},{19,3},{4,20},{20... | collective-permute-start | bytes 49160 | tf_op jit(solution)/shard_map/ppermute | solution.py:410
  48.1 19.3 %slice-start = ((s8[7962624]{0:T(1024)(128)(4,1)}), s8[4194304]{0:T(1024)(128)(4,1)S(1)}, s32[]{:S(2)}) async-start(s8[7962624]{0:T(1024)(128)(4,1)} %bitcast.13), calls=%async_computation.2 | async-start | bytes 8388608
  53.5 6.6 %collective-permute-start.7 = (bf16[4,144,128]{2,1,0:T(8,128)(2,1)S(1)}, bf16[4,144,128]{2,1,0:T(8,128)(2,1)S(1)}, u32[]{:S(2)}, u32[]{:S(2)}) collective-permute-start(bf16[4,144,128]{2,1,0:T(8,128)(2,1)S(1)} %get-tuple-element.47), channel_id=1, source_target_pairs={{0,2},{2,0},{4,6},{6,4},{8,10},{10,8},{12,14},{14,12},{1,3},{3,1},... | collective-permute-start | bytes 442376 | tf_op jit(solution)/shard_map/ppermute | solution.py:410
  54.6 12.8 %slice-start.1 = ((s8[7962624]{0:T(1024)(128)(4,1)}), s8[3768320]{0:T(1024)(128)(4,1)S(1)}, s32[]{:S(2)}) async-start(s8[7962624]{0:T(1024)(128)(4,1)} %bitcast.13), calls=%async_computation.3 | async-start | bytes 7536640
  54.6 12.8 %copy-start = (bf16[256,1152]{1,0:T(8,128)(2,1)S(1)}, bf16[256,1152]{1,0:T(8,128)(2,1)}, u32[]{:S(2)}) copy-start(bf16[256,1152]{1,0:T(8,128)(2,1)} %patch_ref) | copy-start | bytes 1769476
  60.1 12.0 %collective-permute-start.8 = (f32[16,80,128]{2,1,0:T(8,128)S(1)}, f32[16,80,128]{2,1,0:T(8,128)S(1)}, u32[]{:S(2)}, u32[]{:S(2)}) collective-permute-start(f32[16,80,128]{2,1,0:T(8,128)S(1)} %get-tuple-element.49), channel_id=1, source_target_pairs={{0,16},{16,0},{1,17},{17,1},{2,18},{18,2},{3,19},{19,3},{4,20},{20... | collective-permute-start | bytes 1966088 | tf_op jit(solution)/shard_map/ppermute | solution.py:410
  60.2 11.9 %collective-permute-start.9 = (f32[16,24,128]{2,1,0:T(8,128)S(1)}, f32[16,24,128]{2,1,0:T(8,128)S(1)}, u32[]{:S(2)}, u32[]{:S(2)}) collective-permute-start(f32[16,24,128]{2,1,0:T(8,128)S(1)} %get-tuple-element.51), channel_id=1, source_target_pairs={{0,16},{16,0},{1,17},{17,1},{2,18},{18,2},{3,19},{19,3},{4,20},{20... | collective-permute-start | bytes 589832 | tf_op jit(solution)/shard_map/ppermute | solution.py:410
  60.8 9.4 %collective-permute-start.12 = (bf16[144,128]{1,0:T(8,128)(2,1)S(1)}, bf16[144,128]{1,0:T(8,128)(2,1)S(1)}, u32[]{:S(2)}, u32[]{:S(2)}) collective-permute-start(bf16[144,128]{1,0:T(8,128)(2,1)S(1)} %get-tuple-element.67), channel_id=1, source_target_pairs={{0,8},{2,10},{4,12},{6,14},{8,0},{10,2},{12,4},{14,6},{1,9},{3,11}... | collective-permute-start | bytes 110600 | tf_op jit(solution)/shard_map/ppermute | solution.py:410
  63.5 6.7 %collective-permute-start.11 = (bf16[144,128]{1,0:T(8,128)(2,1)S(1)}, bf16[144,128]{1,0:T(8,128)(2,1)S(1)}, u32[]{:S(2)}, u32[]{:S(2)}) collective-permute-start(bf16[144,128]{1,0:T(8,128)(2,1)S(1)} %get-tuple-element.68), channel_id=1, source_target_pairs={{0,12},{2,14},{4,8},{6,10},{8,4},{10,6},{12,0},{14,2},{1,13},{3,15... | collective-permute-start | bytes 110600 | tf_op jit(solution)/shard_map/ppermute | solution.py:410
  65.9 4.9 %collective-permute-start.10 = (bf16[144,128]{1,0:T(8,128)(2,1)S(1)}, bf16[144,128]{1,0:T(8,128)(2,1)S(1)}, u32[]{:S(2)}, u32[]{:S(2)}) collective-permute-start(bf16[144,128]{1,0:T(8,128)(2,1)S(1)} %get-tuple-element.69), channel_id=1, source_target_pairs={{0,4},{2,6},{4,0},{6,2},{8,12},{10,14},{12,8},{14,10},{1,5},{3,7},... | collective-permute-start | bytes 110600 | tf_op jit(solution)/shard_map/ppermute | solution.py:410
  70.7 1.3 %collective-permute-start.13 = (bf16[144,128]{1,0:T(8,128)(2,1)S(1)}, bf16[144,128]{1,0:T(8,128)(2,1)S(1)}, u32[]{:S(2)}, u32[]{:S(2)}) collective-permute-start(bf16[144,128]{1,0:T(8,128)(2,1)S(1)} %shard_map.80.keys_ref), channel_id=1, source_target_pairs={{0,16},{16,0},{1,17},{17,1},{2,18},{18,2},{3,19},{19,3},{4,20},{20... | collective-permute-start | bytes 110600 | tf_op jit(solution)/shard_map/ppermute | solution.py:410
  89.4 6.4 %collective-permute-start.14 = (f32[4,64]{1,0:T(4,128)S(1)}, f32[4,64]{1,0:T(4,128)S(1)}, u32[]{:S(2)}, u32[]{:S(2)}) collective-permute-start(f32[4,64]{1,0:T(4,128)S(1)} %get-tuple-element.61), channel_id=1, source_target_pairs={{1,2},{3,4},{5,6},{7,8},{9,10},{11,12},{13,14},{2,1},{4,3},{6,5},{... | collective-permute-start | bytes 3080 | tf_op jit(solution)/shard_map/ppermute | solution.py:416
  93.9 3.7 %collective-permute-start.15 = (f32[4,64]{1,0:T(4,128)S(1)}, f32[4,64]{1,0:T(4,128)S(1)}, u32[]{:S(2)}, u32[]{:S(2)}) collective-permute-start(f32[4,64]{1,0:T(4,128)S(1)} %get-tuple-element.62), channel_id=1, source_target_pairs={{0,1},{1,0},{2,3},{3,2},{4,5},{5,4},{6,7},{7,6},{8,9},{9,8},{10,11... | collective-permute-start | bytes 3080 | tf_op jit(solution)/shard_map/ppermute | solution.py:410

commit v11 on v10

--- a/solution.py
+++ b/solution.py
@@ -26,6 +26,7 @@
 BLK = ("yh", "x", "c")
 EVEN = (2, 6, 4)
 COL = ("z", "yl")
+REST = 96
 NT = (((1,), (1,)), ((), ()))
 SMALL = pl.CostEstimate(flops=2**20, bytes_accessed=2**16, transcendentals=0)
 WHOLE = pl.BlockSpec(memory_space=pltpu.VMEM)
@@ -272,12 +273,20 @@
         rows = ref[...].astype(f32)[part * DH : (part + 1) * DH].T
         return jnp.concatenate([rows, lanes], axis=1).reshape(HEADS, CELLS, 128)
 
-    parts = [dq, edges, cells(keys_ref, 0), cells(keys_ref, 1)]
+    both = []
     for part in (0, 1):
         above, below = beside(cells(other_ref, part), first)
         half = CELLS // 2
-        parts.append(jnp.where(row < half, pltpu.roll(above, half, 1), pltpu.roll(below, half, 1)))
-    send_ref[...] = jnp.concatenate(parts, axis=1).astype(bf16)
+        near = jnp.where(row < half, pltpu.roll(above, half, 1), pltpu.roll(below, half, 1))
+        both.append(jnp.concatenate([cells(keys_ref, part), near], axis=1))
+    dk, dv = both
+    lane = lax.broadcasted_iota(jnp.int32, dk.shape, 2)
+    mixed = jnp.where(lane < DH, dk, pltpu.roll(dv, DH, 2))
+    rest = pltpu.roll(dv, REST - (128 - DH), 2)
+    rest = jnp.concatenate([rest, jnp.zeros((HEADS, 8, 128), f32)], axis=1)
+    lane = lax.broadcasted_iota(jnp.int32, edges.shape, 2)
+    edges = jnp.where(lane < REST, edges, rest)
+    send_ref[...] = jnp.concatenate([dq, edges, mixed], axis=1).astype(bf16)
 
 
 def weights_kernel(patch_ref, qkv_ref, out_ref):
@@ -315,14 +324,17 @@
         rows = slice(h * DH, (h + 2) * DH)
         joined[rows, 0:TOK] = jnp.concatenate(pair).astype(bf16)
         joined[rows, TOK:] = jnp.concatenate(wide).astype(bf16)
-    at = DH + 24
     group = iota((DH, 128), 1) // 16
+    fits = 128 - DH
+    lane = iota((16, 128), 1)
     for h in range(0, HEADS, 4):
-        cells = []
-        for part in (0, 1):
-            for n in range(h, h + 4):
-                head = back_ref[n, at:].astype(f32)
-                cells += [head[part * CELLS : (part + 1) * CELLS], head[16 + part * CELLS : 16 + (part + 1) * CELLS]]
+        keys, vals = [], []
+        for n in range(h, h + 4):
+            rest = back_ref[n, 64 : 64 + 32].astype(f32)[8 : 8 + 16]
+            mixed = back_ref[n, 96:112].astype(f32)
+            keys.append(mixed)
+            vals.append(jnp.where(lane < fits, pltpu.roll(mixed, fits, 1), pltpu.roll(rest, 128 - (REST - fits), 1)))
+        cells = keys + vals
         cells = jnp.concatenate(cells).T[0:DH]
         for part in (0, 1):
             for n in (0, 2):
@@ -487,7 +499,7 @@
     came, weights = lax.optimization_barrier((came, weights))
     keys = call(keys_sum_kernel, jax.ShapeDtypeStruct((2 * DH, 128), bf16), 4)(mine[0:1], *came)
     other = swapped(keys, "c", 1)
-    send = call(pack_back_kernel, jax.ShapeDtypeStruct((HEADS, 128, TOK), bf16), 16)(
+    send = call(pack_back_kernel, jax.ShapeDtypeStruct((HEADS, 112, TOK), bf16), 16)(
         dq_here, dq_there, edge_there, edge_here, keys, other
     )
     back = lax.all_to_all(send, HEAD_AXES, 0, 0, tiled=True)

time: 98.5 us -> 97.9 us (level)
  no operation moved by 1% of the time
where the time goes in v11:
time: 97.9 us; the launch traced here: 97.7 us
  blocking collectives  34 us (35%)
  Pallas kernels  30.9 us (32%)
  starting transfers between devices  25.9 us (26%)
  waiting for transfers between devices  6.51 us (7%)
    ppermute x15, starting transfers between devices, swapped(): return lax.ppermute(x, axis, [(i, i ^ by) for i in range(peers)])  21.5 us
    all_to_all x1, blocking collectives, on_device(): got = lax.all_to_all(send, HEAD_AXES, 0, 0, tiled=True)  19.4 us
    all_to_all x1, blocking collectives, on_device(): back = lax.all_to_all(send, HEAD_AXES, 0, 0, tiled=True)  14.6 us
    pallas_call x1, Pallas kernels, on_device(): call(second_sums_kernel, sums, 24, [keys], cost_estimate=cost(1))  5.66 us
    pallas_call x1, Pallas kernels, on_device(): call(first_sums_kernel, sums, 24, [keys], cost_estimate=cost(1))  5.59 us
    pallas_call x1, Pallas kernels, on_device(): call(second_kernel, dq + edges + [jax.ShapeDtypeStruct(block, f32)], 32,...  5.47 us
    pallas_call x1, Pallas kernels, on_device(): call(first_kernel, [sums] + dq + [jax.ShapeDtypeStruct(block, bf16)], 32,...  5.39 us
    ppermute x15, waiting for transfers between devices, swapped(): return lax.ppermute(x, axis, [(i, i ^ by) for i in range(peers)])  5.33 us
  transfers between devices with their start and end apart: 16, of which 6 were waited for; matrix products, arithmetic and copies ran while one was open for 0% of the time, Pallas kernels for 15%

profile of v11, /device:TPU:8, one launch (start us, length us, event | category | flops | bytes accessed | tf_op | source)
XLA Modules:
  0.0 97.7 jit_solution(8351744097102847809)
XLA Ops:
  0.0 2.5 %shard_map.73 = bf16[16,176,128]{2,1,0:T(8,128)(2,1)} custom-call(bf16[128,1152]{1,0:T(8,128)(2,1)} %bitcast.19, bf16[128,1152]{1,0:T(8,128)(2,1)} %bitcast.20, bf16[128,1152]{1,0:T(8,128)(2,1)} %bitcast.21, bf16[2,4,1152]{2,1,0:T(4,128)(2,1)} %k_in.1, bf16[2,4,1152]{2,1,0:T(4,128)(2,1)} %v_in.1), custom_call_target="tpu_custom_call" | custom-call | tf_op jit(solution)/shard_map/pallas_call | solution.py:441
  2.5 19.4 %all_to_all.10.got_ref.qg_a = bf16[16,176,128]{2,1,0:T(8,128)(2,1)S(1)} all-to-all(bf16[16,176,128]{2,1,0:T(8,128)(2,1)} %shard_map.73), channel_id=1, replica_groups=mesh['yh'=2,'x'=4,'c'=2,'z'=8,'yl'=2] {'yh','x','yl'}, dimensions={0} | all-to-all | bytes 1441792 | tf_op jit(solution)/shard_map/all_to_all | solution.py:455
  21.8 0.0 collective-permute-start
  21.9 0.1 shard_map.74.kv_0
  22.0 2.0 %collective-permute-start.4 = (bf16[144,128]{1,0:T(8,128)(2,1)S(1)}, bf16[144,128]{1,0:T(8,128)(2,1)S(1)}, u32[]{:S(2)}, u32[]{:S(2)}) collective-permute-start(bf16[144,128]{1,0:T(8,128)(2,1)S(1)} %shard_map.74.kv_0), channel_id=1, source_target_pairs={{0,2},{2,0},{4,6},{6,4},{8,10},{10,8},{12,14},{14,12},{1,3},{3,1},... | collective-permute-start | bytes 110600 | tf_op jit(solution)/shard_map/ppermute | solution.py:422
  24.0 5.4 %collective-permute-start.2 = (bf16[144,128]{1,0:T(8,128)(2,1)S(1)}, bf16[144,128]{1,0:T(8,128)(2,1)S(1)}, u32[]{:S(2)}, u32[]{:S(2)}) collective-permute-start(bf16[144,128]{1,0:T(8,128)(2,1)S(1)} %shard_map.74.kv_0), channel_id=1, source_target_pairs={{0,12},{2,14},{4,8},{6,10},{8,4},{10,6},{12,0},{14,2},{1,13},{3,15... | collective-permute-start | bytes 110600 | tf_op jit(solution)/shard_map/ppermute | solution.py:422
  29.4 1.5 %collective-permute-start.1 = (bf16[144,128]{1,0:T(8,128)(2,1)S(1)}, bf16[144,128]{1,0:T(8,128)(2,1)S(1)}, u32[]{:S(2)}, u32[]{:S(2)}) collective-permute-start(bf16[144,128]{1,0:T(8,128)(2,1)S(1)} %shard_map.74.kv_0), channel_id=1, source_target_pairs={{0,4},{2,6},{4,0},{6,2},{8,12},{10,14},{12,8},{14,10},{1,5},{3,7},... | collective-permute-start | bytes 110600 | tf_op jit(solution)/shard_map/ppermute | solution.py:422
  30.8 0.0 collective-permute-done.4.kv_1
  30.8 2.8 %collective-permute-start.5 = (bf16[2,144,128]{2,1,0:T(8,128)(2,1)S(1)}, bf16[2,144,128]{2,1,0:T(8,128)(2,1)S(1)}, u32[]{:S(2)}, u32[]{:S(2)}) collective-permute-start(bf16[2,144,128]{2,1,0:T(8,128)(2,1)S(1)} %pad_maximum_fusion.1), channel_id=1, source_target_pairs={{0,8},{2,10},{4,12},{6,14},{8,0},{10,2},{12,4},{14,6},{1,9},{3,11}... | collective-permute-start | bytes 221192 | tf_op jit(solution)/shard_map/ppermute | solution.py:422
  33.6 0.0 collective-permute-done.2.kv_6
  33.6 0.6 collective-permute-done.1.kv_2
  34.2 1.1 %collective-permute-start.3 = (bf16[2,144,128]{2,1,0:T(8,128)(2,1)S(1)}, bf16[2,144,128]{2,1,0:T(8,128)(2,1)S(1)}, u32[]{:S(2)}, u32[]{:S(2)}) collective-permute-start(bf16[2,144,128]{2,1,0:T(8,128)(2,1)S(1)} %pad_maximum_fusion), channel_id=1, source_target_pairs={{0,2},{2,0},{4,6},{6,4},{8,10},{10,8},{12,14},{14,12},{1,3},{3,1},... | collective-permute-start | bytes 221192 | tf_op jit(solution)/shard_map/ppermute | solution.py:422
  35.3 0.0 collective-permute-done.qg_b
  35.3 5.6 %shard_map.75.first_ref = f32[2,16,128]{2,1,0:T(8,128)S(1)} custom-call(bf16[16,176,128]{2,1,0:T(8,128)(2,1)S(1)} %all_to_all.10.got_ref.qg_a, bf16[16,176,128]{2,1,0:T(8,128)(2,1)S(1)} %collective-permute-done.qg_b, bf16[144,128]{1,0:T(8,128)(2,1)S(1)} %shard_map.74.kv_0, bf16[144,128]{1,0:T(8,128)(2,1)S(1)} %collective-permute-done.4.kv_1, ...), custom_call_target="tpu_custom_call" | custom-call | flops 1073741824 | bytes 1048576 | tf_op jit(solution)/shard_map/pallas_call | solution.py:469
  40.9 0.0 collective-permute-done.5.kv_45
  41.0 0.0 collective-permute-done.3.kv_37
  41.0 5.7 %shard_map.76.mine_ref = f32[2,16,128]{2,1,0:T(8,128)S(1)} custom-call(bf16[16,176,128]{2,1,0:T(8,128)(2,1)S(1)} %all_to_all.10.got_ref.qg_a, bf16[16,176,128]{2,1,0:T(8,128)(2,1)S(1)} %collective-permute-done.qg_b, bf16[2,144,128]{2,1,0:T(8,128)(2,1)S(1)} %collective-permute-done.3.kv_37, bf16[2,144,128]{2,1,0:T(8,128)(2,1)S(1)} %collective-permute-done.5.kv_45, ...), custom_call_target="tpu_custom_call" | custom-call | flops 1073741824 | bytes 1048576 | tf_op jit(solution)/shard_map/pallas_call | solution.py:471
  46.6 0.3 collective-permute-start.6
  46.9 1.2 %collective-permute-done.6.came_ref = f32[2,16,128]{2,1,0:T(8,128)S(1)} collective-permute-done((f32[2,16,128]{2,1,0:T(8,128)S(1)}, f32[2,16,128]{2,1,0:T(8,128)S(1)}, u32[]{:S(2)}, u32[]{:S(2)}) %collective-permute-start.6) | collective-permute-done | bytes 16416 | tf_op jit(solution)/shard_map/ppermute | solution.py:422
  48.1 5.4 %shard_map.77 = (f32[2,16,128]{2,1,0:T(8,128)S(1)}, f32[16,80,128]{2,1,0:T(8,128)S(1)}, f32[16,80,128]{2,1,0:T(8,128)S(1)}, bf16[4,144,128]{2,1,0:T(8,128)(2,1)S(1)}) custom-call(bf16[16,176,128]{2,1,0:T(8,128)(2,1)S(1)} %all_to_all.10.got_ref.qg_a, bf16[16,176,128]{2,1,0:T(8,128)(2,1)S(1)} %collective-permute-done.qg_b, ...), custom_call_target="tpu_custom_call" | custom-call | flops 5368709120 | bytes 1048576 | tf_op jit(solution)/shard_map/pallas_call | solution.py:477
  53.5 1.1 %collective-permute-start.7 = (bf16[4,144,128]{2,1,0:T(8,128)(2,1)S(1)}, bf16[4,144,128]{2,1,0:T(8,128)(2,1)S(1)}, u32[]{:S(2)}, u32[]{:S(2)}) collective-permute-start(bf16[4,144,128]{2,1,0:T(8,128)(2,1)S(1)} %get-tuple-element.47), channel_id=1, source_target_pairs={{0,2},{2,0},{4,6},{6,4},{8,10},{10,8},{12,14},{14,12},{1,3},{3,1},... | collective-permute-start | bytes 442376 | tf_op jit(solution)/shard_map/ppermute | solution.py:422
  54.6 5.5 %shard_map.78 = (f32[16,80,128]{2,1,0:T(8,128)S(1)}, f32[16,80,128]{2,1,0:T(8,128)S(1)}, f32[16,24,128]{2,1,0:T(8,128)S(1)}, f32[16,24,128]{2,1,0:T(8,128)S(1)}, f32[4,144,128]{2,1,0:T(8,128)S(1)}) custom-call(bf16[16,176,128]{2,1,0:T(8,128)(2,1)S(1)} %all_to_all.10.got_ref.qg_a, bf16[16,176,128]{2,1,0:T(8,128)(2,1)S(1)} %collective-permute-done.qg_b, ...), custom_call_target="tpu_custom_call" | custom-call | flops 5368709120 | bytes 1048576 | tf_op jit(solution)/shard_map/pallas_call | solution.py:482
  60.1 0.0 collective-permute-done.7
  60.1 0.1 collective-permute-start.8
  60.2 0.5 collective-permute-start.9
  60.8 2.7 %collective-permute-start.12 = (bf16[144,128]{1,0:T(8,128)(2,1)S(1)}, bf16[144,128]{1,0:T(8,128)(2,1)S(1)}, u32[]{:S(2)}, u32[]{:S(2)}) collective-permute-start(bf16[144,128]{1,0:T(8,128)(2,1)S(1)} %get-tuple-element.67), channel_id=1, source_target_pairs={{0,8},{2,10},{4,12},{6,14},{8,0},{10,2},{12,4},{14,6},{1,9},{3,11}... | collective-permute-start | bytes 110600 | tf_op jit(solution)/shard_map/ppermute | solution.py:422
  63.5 2.4 %collective-permute-start.11 = (bf16[144,128]{1,0:T(8,128)(2,1)S(1)}, bf16[144,128]{1,0:T(8,128)(2,1)S(1)}, u32[]{:S(2)}, u32[]{:S(2)}) collective-permute-start(bf16[144,128]{1,0:T(8,128)(2,1)S(1)} %get-tuple-element.68), channel_id=1, source_target_pairs={{0,12},{2,14},{4,8},{6,10},{8,4},{10,6},{12,0},{14,2},{1,13},{3,15... | collective-permute-start | bytes 110600 | tf_op jit(solution)/shard_map/ppermute | solution.py:422
  65.9 1.5 %collective-permute-start.10 = (bf16[144,128]{1,0:T(8,128)(2,1)S(1)}, bf16[144,128]{1,0:T(8,128)(2,1)S(1)}, u32[]{:S(2)}, u32[]{:S(2)}) collective-permute-start(bf16[144,128]{1,0:T(8,128)(2,1)S(1)} %get-tuple-element.69), channel_id=1, source_target_pairs={{0,4},{2,6},{4,0},{6,2},{8,12},{10,14},{12,8},{14,10},{1,5},{3,7},... | collective-permute-start | bytes 110600 | tf_op jit(solution)/shard_map/ppermute | solution.py:422
  67.3 0.0 slice-done
  67.4 0.0 slice-done.1
  67.4 0.0 copy-done
  67.4 2.8 %shard_map.79.weights = bf16[512,3456]{1,0:T(8,128)(2,1)S(1)} custom-call(bf16[256,1152]{1,0:T(8,128)(2,1)S(1)} %copy-done, bf16[1152,3456]{1,0:T(8,128)(2,1)S(1)} %bitcast.14), custom_call_target="tpu_custom_call" | custom-call | flops 1048576 | bytes 65536 | tf_op jit(solution)/shard_map/pallas_call | solution.py:496
  70.1 0.0 collective-permute-done.12.came_c
  70.1 0.0 collective-permute-done.11.came_b
  70.2 0.6 collective-permute-done.10.came_a
  70.7 0.1 collective-permute-start.13
  70.8 1.2 %collective-permute-done.13.other_ref = bf16[144,128]{1,0:T(8,128)(2,1)S(1)} collective-permute-done((bf16[144,128]{1,0:T(8,128)(2,1)S(1)}, bf16[144,128]{1,0:T(8,128)(2,1)S(1)}, u32[]{:S(2)}, u32[]{:S(2)}) %collective-permute-start.13) | collective-permute-done | bytes 36896 | tf_op jit(solution)/shard_map/ppermute | solution.py:422
  72.1 0.0 collective-permute-done.9.came_edge_ref
  72.1 0.0 collective-permute-done.8.came_ref
  72.1 0.3 shard_map.81
  72.3 14.6 %all_to_all.11.back_ref = bf16[16,112,128]{2,1,0:T(8,128)(2,1)S(1)} all-to-all(bf16[16,112,128]{2,1,0:T(8,128)(2,1)S(1)} %shard_map.81), channel_id=1, replica_groups=mesh['yh'=2,'x'=4,'c'=2,'z'=8,'yl'=2] {'yh','x','yl'}, dimensions={0} | all-to-all | bytes 917504 | tf_op jit(solution)/shard_map/all_to_all | solution.py:505
  86.9 1.9 %shard_map.82 = (bf16[160,512]{1,0:T(8,128)(2,1)S(1)}, f32[4,64]{1,0:T(4,128)S(1)}, f32[4,64]{1,0:T(4,128)S(1)}) custom-call(bf16[16,112,128]{2,1,0:T(8,128)(2,1)S(1)} %all_to_all.11.back_ref, bf16[512,3456]{1,0:T(8,128)(2,1)S(1)} %shard_map.79.weights), custom_call_target="tpu_custom_call" | custom-call | tf_op jit(solution)/shard_map/pallas_call | solution.py:507
  88.8 4.5 %collective-permute-start.14 = (f32[4,64]{1,0:T(4,128)S(1)}, f32[4,64]{1,0:T(4,128)S(1)}, u32[]{:S(2)}, u32[]{:S(2)}) collective-permute-start(f32[4,64]{1,0:T(4,128)S(1)} %get-tuple-element.61), channel_id=1, source_target_pairs={{1,2},{3,4},{5,6},{7,8},{9,10},{11,12},{13,14},{2,1},{4,3},{6,5},{... | collective-permute-start | bytes 3080 | tf_op jit(solution)/shard_map/ppermute | solution.py:428
  93.3 0.1 collective-permute-start.15
  93.4 0.6 shard_map.83.center_ref
  94.0 1.2 %collective-permute-done.14.far_ref = f32[4,64]{1,0:T(4,128)S(1)} collective-permute-done((f32[4,64]{1,0:T(4,128)S(1)}, f32[4,64]{1,0:T(4,128)S(1)}, u32[]{:S(2)}, u32[]{:S(2)}) %collective-permute-start.14) | collective-permute-done | bytes 1056 | tf_op jit(solution)/shard_map/ppermute | solution.py:428
  95.2 1.8 %collective-permute-done.15.near_ref = f32[4,64]{1,0:T(4,128)S(1)} collective-permute-done((f32[4,64]{1,0:T(4,128)S(1)}, f32[4,64]{1,0:T(4,128)S(1)}, u32[]{:S(2)}, u32[]{:S(2)}) %collective-permute-start.15) | collective-permute-done | bytes 1056 | tf_op jit(solution)/shard_map/ppermute | solution.py:422
  97.0 0.7 shard_map.84
  (11 shorter events, 0.1 us)
Async XLA Ops:
  21.8 13.5 %collective-permute-start = (bf16[16,176,128]{2,1,0:T(8,128)(2,1)S(1)}, bf16[16,176,128]{2,1,0:T(8,128)(2,1)S(1)}, u32[]{:S(2)}, u32[]{:S(2)}) collective-permute-start(bf16[16,176,128]{2,1,0:T(8,128)(2,1)S(1)} %all_to_all.10.got_ref.qg_a), channel_id=1, source_target_pairs={{0,16},{16,0},{1,17},{17,1},{2,18},{18,2},{3,19},{19,3},{4,20},{20... | collective-permute-start | bytes 2162696 | tf_op jit(solution)/shard_map/ppermute | solution.py:422
  22.0 8.9 %collective-permute-start.4 = (bf16[144,128]{1,0:T(8,128)(2,1)S(1)}, bf16[144,128]{1,0:T(8,128)(2,1)S(1)}, u32[]{:S(2)}, u32[]{:S(2)}) collective-permute-start(bf16[144,128]{1,0:T(8,128)(2,1)S(1)} %shard_map.74.kv_0), channel_id=1, source_target_pairs={{0,2},{2,0},{4,6},{6,4},{8,10},{10,8},{12,14},{14,12},{1,3},{3,1},... | collective-permute-start | bytes 110600 | tf_op jit(solution)/shard_map/ppermute | solution.py:422
  24.0 9.6 %collective-permute-start.2 = (bf16[144,128]{1,0:T(8,128)(2,1)S(1)}, bf16[144,128]{1,0:T(8,128)(2,1)S(1)}, u32[]{:S(2)}, u32[]{:S(2)}) collective-permute-start(bf16[144,128]{1,0:T(8,128)(2,1)S(1)} %shard_map.74.kv_0), channel_id=1, source_target_pairs={{0,12},{2,14},{4,8},{6,10},{8,4},{10,6},{12,0},{14,2},{1,13},{3,15... | collective-permute-start | bytes 110600 | tf_op jit(solution)/shard_map/ppermute | solution.py:422
  29.4 4.9 %collective-permute-start.1 = (bf16[144,128]{1,0:T(8,128)(2,1)S(1)}, bf16[144,128]{1,0:T(8,128)(2,1)S(1)}, u32[]{:S(2)}, u32[]{:S(2)}) collective-permute-start(bf16[144,128]{1,0:T(8,128)(2,1)S(1)} %shard_map.74.kv_0), channel_id=1, source_target_pairs={{0,4},{2,6},{4,0},{6,2},{8,12},{10,14},{12,8},{14,10},{1,5},{3,7},... | collective-permute-start | bytes 110600 | tf_op jit(solution)/shard_map/ppermute | solution.py:422
  30.8 10.1 %collective-permute-start.5 = (bf16[2,144,128]{2,1,0:T(8,128)(2,1)S(1)}, bf16[2,144,128]{2,1,0:T(8,128)(2,1)S(1)}, u32[]{:S(2)}, u32[]{:S(2)}) collective-permute-start(bf16[2,144,128]{2,1,0:T(8,128)(2,1)S(1)} %pad_maximum_fusion.1), channel_id=1, source_target_pairs={{0,8},{2,10},{4,12},{6,14},{8,0},{10,2},{12,4},{14,6},{1,9},{3,11}... | collective-permute-start | bytes 221192 | tf_op jit(solution)/shard_map/ppermute | solution.py:422
  34.2 6.7 %collective-permute-start.3 = (bf16[2,144,128]{2,1,0:T(8,128)(2,1)S(1)}, bf16[2,144,128]{2,1,0:T(8,128)(2,1)S(1)}, u32[]{:S(2)}, u32[]{:S(2)}) collective-permute-start(bf16[2,144,128]{2,1,0:T(8,128)(2,1)S(1)} %pad_maximum_fusion), channel_id=1, source_target_pairs={{0,2},{2,0},{4,6},{6,4},{8,10},{10,8},{12,14},{14,12},{1,3},{3,1},... | collective-permute-start | bytes 221192 | tf_op jit(solution)/shard_map/ppermute | solution.py:422
  46.6 1.5 %collective-permute-start.6 = (f32[2,16,128]{2,1,0:T(8,128)S(1)}, f32[2,16,128]{2,1,0:T(8,128)S(1)}, u32[]{:S(2)}, u32[]{:S(2)}) collective-permute-start(f32[2,16,128]{2,1,0:T(8,128)S(1)} %shard_map.76.mine_ref), channel_id=1, source_target_pairs={{0,16},{16,0},{1,17},{17,1},{2,18},{18,2},{3,19},{19,3},{4,20},{20... | collective-permute-start | bytes 49160 | tf_op jit(solution)/shard_map/ppermute | solution.py:422
  48.1 19.3 %slice-start = ((s8[7962624]{0:T(1024)(128)(4,1)}), s8[4194304]{0:T(1024)(128)(4,1)S(1)}, s32[]{:S(2)}) async-start(s8[7962624]{0:T(1024)(128)(4,1)} %bitcast.13), calls=%async_computation.2 | async-start | bytes 8388608
  53.5 6.6 %collective-permute-start.7 = (bf16[4,144,128]{2,1,0:T(8,128)(2,1)S(1)}, bf16[4,144,128]{2,1,0:T(8,128)(2,1)S(1)}, u32[]{:S(2)}, u32[]{:S(2)}) collective-permute-start(bf16[4,144,128]{2,1,0:T(8,128)(2,1)S(1)} %get-tuple-element.47), channel_id=1, source_target_pairs={{0,2},{2,0},{4,6},{6,4},{8,10},{10,8},{12,14},{14,12},{1,3},{3,1},... | collective-permute-start | bytes 442376 | tf_op jit(solution)/shard_map/ppermute | solution.py:422
  54.6 12.8 %slice-start.1 = ((s8[7962624]{0:T(1024)(128)(4,1)}), s8[3768320]{0:T(1024)(128)(4,1)S(1)}, s32[]{:S(2)}) async-start(s8[7962624]{0:T(1024)(128)(4,1)} %bitcast.13), calls=%async_computation.3 | async-start | bytes 7536640
  54.6 12.8 %copy-start = (bf16[256,1152]{1,0:T(8,128)(2,1)S(1)}, bf16[256,1152]{1,0:T(8,128)(2,1)}, u32[]{:S(2)}) copy-start(bf16[256,1152]{1,0:T(8,128)(2,1)} %patch_ref) | copy-start | bytes 1769476
  60.1 12.0 %collective-permute-start.8 = (f32[16,80,128]{2,1,0:T(8,128)S(1)}, f32[16,80,128]{2,1,0:T(8,128)S(1)}, u32[]{:S(2)}, u32[]{:S(2)}) collective-permute-start(f32[16,80,128]{2,1,0:T(8,128)S(1)} %get-tuple-element.49), channel_id=1, source_target_pairs={{0,16},{16,0},{1,17},{17,1},{2,18},{18,2},{3,19},{19,3},{4,20},{20... | collective-permute-start | bytes 1966088 | tf_op jit(solution)/shard_map/ppermute | solution.py:422
  60.2 11.9 %collective-permute-start.9 = (f32[16,24,128]{2,1,0:T(8,128)S(1)}, f32[16,24,128]{2,1,0:T(8,128)S(1)}, u32[]{:S(2)}, u32[]{:S(2)}) collective-permute-start(f32[16,24,128]{2,1,0:T(8,128)S(1)} %get-tuple-element.51), channel_id=1, source_target_pairs={{0,16},{16,0},{1,17},{17,1},{2,18},{18,2},{3,19},{19,3},{4,20},{20... | collective-permute-start | bytes 589832 | tf_op jit(solution)/shard_map/ppermute | solution.py:422
  60.8 9.4 %collective-permute-start.12 = (bf16[144,128]{1,0:T(8,128)(2,1)S(1)}, bf16[144,128]{1,0:T(8,128)(2,1)S(1)}, u32[]{:S(2)}, u32[]{:S(2)}) collective-permute-start(bf16[144,128]{1,0:T(8,128)(2,1)S(1)} %get-tuple-element.67), channel_id=1, source_target_pairs={{0,8},{2,10},{4,12},{6,14},{8,0},{10,2},{12,4},{14,6},{1,9},{3,11}... | collective-permute-start | bytes 110600 | tf_op jit(solution)/shard_map/ppermute | solution.py:422
  63.5 6.7 %collective-permute-start.11 = (bf16[144,128]{1,0:T(8,128)(2,1)S(1)}, bf16[144,128]{1,0:T(8,128)(2,1)S(1)}, u32[]{:S(2)}, u32[]{:S(2)}) collective-permute-start(bf16[144,128]{1,0:T(8,128)(2,1)S(1)} %get-tuple-element.68), channel_id=1, source_target_pairs={{0,12},{2,14},{4,8},{6,10},{8,4},{10,6},{12,0},{14,2},{1,13},{3,15... | collective-permute-start | bytes 110600 | tf_op jit(solution)/shard_map/ppermute | solution.py:422
  65.9 4.9 %collective-permute-start.10 = (bf16[144,128]{1,0:T(8,128)(2,1)S(1)}, bf16[144,128]{1,0:T(8,128)(2,1)S(1)}, u32[]{:S(2)}, u32[]{:S(2)}) collective-permute-start(bf16[144,128]{1,0:T(8,128)(2,1)S(1)} %get-tuple-element.69), channel_id=1, source_target_pairs={{0,4},{2,6},{4,0},{6,2},{8,12},{10,14},{12,8},{14,10},{1,5},{3,7},... | collective-permute-start | bytes 110600 | tf_op jit(solution)/shard_map/ppermute | solution.py:422
  70.7 1.3 %collective-permute-start.13 = (bf16[144,128]{1,0:T(8,128)(2,1)S(1)}, bf16[144,128]{1,0:T(8,128)(2,1)S(1)}, u32[]{:S(2)}, u32[]{:S(2)}) collective-permute-start(bf16[144,128]{1,0:T(8,128)(2,1)S(1)} %shard_map.80.keys_ref), channel_id=1, source_target_pairs={{0,16},{16,0},{1,17},{17,1},{2,18},{18,2},{3,19},{19,3},{4,20},{20... | collective-permute-start | bytes 110600 | tf_op jit(solution)/shard_map/ppermute | solution.py:422
  88.8 6.4 %collective-permute-start.14 = (f32[4,64]{1,0:T(4,128)S(1)}, f32[4,64]{1,0:T(4,128)S(1)}, u32[]{:S(2)}, u32[]{:S(2)}) collective-permute-start(f32[4,64]{1,0:T(4,128)S(1)} %get-tuple-element.61), channel_id=1, source_target_pairs={{1,2},{3,4},{5,6},{7,8},{9,10},{11,12},{13,14},{2,1},{4,3},{6,5},{... | collective-permute-start | bytes 3080 | tf_op jit(solution)/shard_map/ppermute | solution.py:428
  93.3 3.7 %collective-permute-start.15 = (f32[4,64]{1,0:T(4,128)S(1)}, f32[4,64]{1,0:T(4,128)S(1)}, u32[]{:S(2)}, u32[]{:S(2)}) collective-permute-start(f32[4,64]{1,0:T(4,128)S(1)} %get-tuple-element.62), channel_id=1, source_target_pairs={{0,1},{1,0},{2,3},{3,2},{4,5},{5,4},{6,7},{7,6},{8,9},{9,8},{10,11... | collective-permute-start | bytes 3080 | tf_op jit(solution)/shard_map/ppermute | solution.py:422

commit v12 on v11

--- a/solution.py
+++ b/solution.py
@@ -102,21 +102,32 @@
     out_ref[...] = jnp.concatenate([k_t[0:DH], v_t[0:DH]]).astype(bf16)
 
 
-def load_keys(blocks, k_s, kt_s=None, v_s=None):
+def key_rows(kv):
+    return jnp.concatenate([kv.astype(f32)[0:DH], jnp.zeros((128 - DH, 128), f32)])
+
+
+def load_keys(blocks, k_s):
+    norms = jnp.zeros((1, 128), f32)
+    for b, block in enumerate(blocks):
+        k_t = key_rows(block)
+        norms = jnp.maximum(norms, jnp.sum(k_t * k_t, axis=0, keepdims=True))
+        k_s[b * 128 : (b + 1) * 128] = k_t.T.astype(bf16)
+    return jnp.max(norms)
+
+
+def layouts_kernel(kv_0, kv_1, kv_2, kv_6, kv_37, kv_45, k_odd, kt_odd, v_odd, k_even, kt_even, v_even):
+    odd = (kv_1[...], kv_37[0], kv_37[1], kv_45[1]), k_odd, kt_odd, v_odd
+    even = (kv_0[...], kv_2[...], kv_6[...], kv_45[0]), k_even, kt_even, v_even
     lane = lax.broadcasted_iota(jnp.int32, (128, 128), 1)
     pad = jnp.zeros((128 - DH, 128), f32)
-    norms = jnp.zeros((1, 128), f32)
-    for b, block in enumerate(blocks):
-        kv = block.astype(f32)
-        keys = slice(b * 128, (b + 1) * 128)
-        k_t = jnp.concatenate([kv[0:DH], pad])
-        norms = jnp.maximum(norms, jnp.sum(k_t * k_t, axis=0, keepdims=True))
-        k_s[keys] = k_t.T.astype(bf16)
-        if kt_s is not None:
-            kt_s[:, keys] = k_t.astype(bf16)
-            v = jnp.concatenate([kv[DH:], pad]).T
-            v_s[keys] = jnp.where((lane >= DH) & (lane < DH + 3), 1.0, v).astype(bf16)
-    return jnp.max(norms)
+    for blocks, k_ref, kt_ref, v_ref in (odd, even):
+        for b, block in enumerate(blocks):
+            keys = slice(b * 128, (b + 1) * 128)
+            k_t = key_rows(block)
+            k_ref[keys] = k_t.T.astype(bf16)
+            kt_ref[:, keys] = k_t[0:FPAD].astype(bf16)
+            v = jnp.concatenate([block.astype(f32)[DH:], pad]).T
+            v_ref[keys] = jnp.where((lane >= DH) & (lane < DH + 3), 1.0, v).astype(bf16)
 
 
 def tile_of(qg_refs, row):
@@ -132,7 +143,8 @@
         return jnp.dot(k_s[rows, 0:FPAD], q_t, preferred_element_type=f32) * SCALE2
 
     total = jnp.zeros((1, TILE), f32)
-    for at in range(0, HALF, STEP):
+    count = k_s.shape[0]
+    for at in range(0, count, STEP):
         exps = jnp.exp2(scores(slice(at, at + STEP)) - bound)
         total = total + jnp.sum(exps, axis=0, keepdims=True)
 
@@ -143,12 +155,12 @@
         def largest(n, top):
             return jnp.maximum(top, jnp.max(scores(rows(n)), axis=0, keepdims=True))
 
-        top = lax.fori_loop(0, HALF // 128, largest, jnp.full((1, TILE), -jnp.inf, f32))
+        top = lax.fori_loop(0, count // 128, largest, jnp.full((1, TILE), -jnp.inf, f32))
 
         def add(n, total):
             return total + jnp.sum(jnp.exp2(scores(rows(n)) - top), axis=0, keepdims=True)
 
-        return top + jnp.log2(lax.fori_loop(0, HALF // 128, add, jnp.zeros((1, TILE), f32)))
+        return top + jnp.log2(lax.fori_loop(0, count // 128, add, jnp.zeros((1, TILE), f32)))
 
     return lax.cond(jnp.min(total) < 2.0**-90, again, lambda: bound + jnp.log2(total))
 
@@ -193,7 +205,7 @@
         ds = (probs * shifted).astype(bf16)
         dk_s[b, 0:FPAD] = lax.dot_general(ds, q_t, NT, preferred_element_type=f32)
         dv_s[b, 0:FPAD] = lax.dot_general(half_probs, g_t, NT, preferred_element_type=f32)
-        dq = dq + jnp.dot(kt_s[0:FPAD, b], ds, preferred_element_type=f32)
+        dq = dq + jnp.dot(kt_s[:, b], ds, preferred_element_type=f32)
     for n in range(2 * HEADS):
         put_dq(n // HEADS, n % HEADS, dq[:, n * TOK : (n + 1) * TOK])
 
@@ -208,10 +220,8 @@
 
 
 def first_kernel(
-    qg_a, qg_b, kv_1, kv_37, kv_45, mine_ref, came_ref, sums_ref, dq_a, dq_b, out_ref,
-    k_s, kt_s, v_s, dk_s, dv_s,
+    qg_a, qg_b, k_s, kt_s, v_s, mine_ref, came_ref, sums_ref, dq_a, dq_b, out_ref, dk_s, dv_s
 ):
-    load_keys((kv_1[...], kv_37[0], kv_37[1], kv_45[1]), k_s, kt_s, v_s)
     for at in (0, 1):
         sums_ref[at] = added(mine_ref[at], came_ref[1 - at])
 
@@ -232,15 +242,17 @@
 
 
 def second_kernel(
-    qg_a, qg_b, kv_0, kv_2, kv_6, kv_45, sums_ref, in_a, in_b, dq_a, dq_b, edge_a, edge_b, out_ref,
-    k_s, kt_s, v_s, dk_s, dv_s,
+    qg_a, qg_b, k_s, kt_s, v_s, sums_ref, in_a, in_b, here_ref, edge_ref, away_ref, out_ref, dk_s, dv_s
 ):
-    load_keys((kv_0[...], kv_2[...], kv_6[...], kv_45[0]), k_s, kt_s, v_s)
-
     def put_dq(at, n, dq):
         dq = (in_a, in_b)[at][n] + dq
-        (dq_a, dq_b)[at][n] = dq
-        (edge_a, edge_b)[at][n] = edge_rows(dq)
+        edges = edge_rows(dq)
+        if at == 0:
+            here_ref[n] = dq[0:DH]
+            away_ref[n, DH:] = edges
+        else:
+            away_ref[n, 0:DH] = dq[0:DH]
+            edge_ref[n] = edges
 
     gradients(sums_ref, (qg_a, qg_b), put_dq, k_s, kt_s, v_s, dk_s, dv_s)
     put_keys(out_ref, dk_s, dv_s)
@@ -260,10 +272,10 @@
     return above, below
 
 
-def pack_back_kernel(dq_ref, came_ref, edge_ref, came_edge_ref, keys_ref, other_ref, send_ref):
+def pack_back_kernel(dq_ref, edge_ref, came_ref, keys_ref, other_ref, send_ref):
     first = lax.axis_index("c") == 0
-    dq = (dq_ref[...] + came_ref[...])[:, 0:DH] * SCALE
-    above, below = beside((edge_ref[...] + came_edge_ref[...]) * SCALE, first)
+    dq = (dq_ref[...] + came_ref[:, 0:DH]) * SCALE
+    above, below = beside((edge_ref[...] + came_ref[:, DH:]) * SCALE, first)
     lane = lax.broadcasted_iota(jnp.int32, (HEADS, 24, 128), 2)
     edges = jnp.where(lane % 32 < COLS, above, below)
     lanes = jnp.zeros((128, 128 - DH), f32)
@@ -409,7 +421,7 @@
     center_ref[...] = center + jnp.where(lane >= 4, pltpu.roll(right, 4, 1), 0.0)
 
 
-def cols_kernel(center_ref, far_ref, near_ref, out_ref):
+def cols_kernel(center_ref, near_ref, far_ref, out_ref):
     begins = lax.axis_index("yl") == 0
     left = jnp.where(begins, far_ref[...], near_ref[...])
     right = jnp.where(begins, near_ref[...], far_ref[...])
@@ -464,32 +476,34 @@
     kv_37 = swapped(jnp.stack([kv_2, kv_6]), "z", 1)
     kv_45 = swapped(jnp.stack([kv, kv_1]), "z", 4)
     there = swapped(got, "c", 1)
+    sums = jax.ShapeDtypeStruct((2, HEADS, TOK), f32)
     keys = pltpu.VMEM((HALF, 128), bf16)
-    sums = jax.ShapeDtypeStruct((2, HEADS, TOK), f32)
     mine = call(first_sums_kernel, sums, 24, [keys], cost_estimate=cost(1))(got, there, kv, kv_1, kv_2, kv_6)
     kv_37, kv_45, mine = lax.optimization_barrier((kv_37, kv_45, mine))
     mine = call(second_sums_kernel, sums, 24, [keys], cost_estimate=cost(1))(got, there, kv_37, kv_45, mine)
+    mine, kv_45 = lax.optimization_barrier((mine, kv_45))
     came = swapped(mine, "c", 1)
-    scratch = [keys, pltpu.VMEM((128, HALF), bf16), keys]
-    scratch += [pltpu.VMEM((HALF, 128), f32)] * 2
+    layout = [jax.ShapeDtypeStruct(shape, bf16) for shape in ((HALF, 128), (FPAD, HALF), (HALF, 128))]
+    layouts = call(layouts_kernel, layout * 2, 8, cost_estimate=SMALL)(kv, kv_1, kv_2, kv_6, kv_37, kv_45)
+    came, layouts = lax.optimization_barrier((came, layouts))
+    scratch = [pltpu.VMEM((HALF, 128), f32)] * 2
     dq = [jax.ShapeDtypeStruct((HEADS, FPAD, TOK), f32)] * 2
     block = (4, 2 * DH, 128)
     sums, dq_here, dq_there, grads = call(
         first_kernel, [sums] + dq + [jax.ShapeDtypeStruct(block, bf16)], 32, scratch, cost_estimate=cost(5)
-    )(got, there, kv_1, kv_37, kv_45, mine, came)
+    )(got, there, *layouts[:3], mine, came)
     came = swapped(grads, "z", 1)
-    edges = [jax.ShapeDtypeStruct((HEADS, 24, TOK), f32)] * 2
+    shapes = [jax.ShapeDtypeStruct((HEADS, rows, TOK), f32) for rows in (DH, 24, DH + 24)]
     *dq, grads = call(
         second_kernel,
-        dq + edges + [jax.ShapeDtypeStruct(block, f32)],
+        shapes + [jax.ShapeDtypeStruct(block, f32)],
         32,
         scratch,
         cost_estimate=cost(5),
-    )(got, there, kv, kv_2, kv_6, kv_45, sums, dq_here, dq_there)
+    )(got, there, *layouts[3:], sums, dq_here, dq_there)
     dq, grads, came = lax.optimization_barrier((dq, grads, came))
-    dq_here, dq_there, edge_here, edge_there = dq
-    dq_there = swapped(dq_there, "c", 1)
-    edge_here = swapped(edge_here, "c", 1)
+    dq_here, edges, away = dq
+    away = swapped(away, "c", 1)
     mine = grads + came.astype(f32)
     mine, w_qkv, w_patch = lax.optimization_barrier((mine, w_qkv, w_patch))
     came = [swapped(mine[n + 1].astype(bf16), "z", by) for n, by in enumerate(EVEN)]
@@ -500,7 +514,7 @@
     keys = call(keys_sum_kernel, jax.ShapeDtypeStruct((2 * DH, 128), bf16), 4)(mine[0:1], *came)
     other = swapped(keys, "c", 1)
     send = call(pack_back_kernel, jax.ShapeDtypeStruct((HEADS, 112, TOK), bf16), 16)(
-        dq_here, dq_there, edge_there, edge_here, keys, other
+        dq_here, edges, away, keys, other
     )
     back = lax.all_to_all(send, HEAD_AXES, 0, 0, tiled=True)
     strip = jax.ShapeDtypeStruct((4, 64), f32)
@@ -510,7 +524,7 @@
         28,
         [pltpu.VMEM((D, 2 * TOK), bf16), pltpu.VMEM((2 * D, 128), bf16), pltpu.VMEM((72, 128), f32)],
     )(back, weights)
-    far, near = neighbours(to_far, COL), swapped(to_near, "yl", 1)
+    near, far = swapped(to_near, "yl", 1), neighbours(to_far, COL)
     center = call(
         fold_kernel,
         jax.ShapeDtypeStruct((64, 128), f32),
@@ -518,8 +532,8 @@
         [pltpu.VMEM((2, 72, 128), f32)],
         cost_estimate=SMALL,
     )(turned)
-    far, near, center = lax.optimization_barrier((far, near, center))
-    return call(cols_kernel, jax.ShapeDtypeStruct((64, 128), f32), 4)(center, far, near)
+    near, far, center = lax.optimization_barrier((near, far, center))
+    return call(cols_kernel, jax.ShapeDtypeStruct((64, 128), f32), 4)(center, near, far)
 
 
 def solution(mesh):

time: 97.9 us -> 97 us (level)
    ppermute x15 -> x14, waiting for transfers between devices: 5.33 us -> 3.47 us  [swapped(): return lax.ppermute(x, axis, [(i, i ^ by) for i in range(peers)])]
    ppermute x1, waiting for transfers between devices: 1.18 us -> 2.2 us  [neighbours(): lax.ppermute(x, axis, pairs + [(target, source) for source, target in pai...]
    ppermute x15 -> x14, starting transfers between devices: 21.5 us -> 22.4 us  [swapped(): return lax.ppermute(x, axis, [(i, i ^ by) for i in range(peers)])]
    pallas_call x1 -> x2, Pallas kernels: 5.47 us -> 5.59 us  [the longest x1 5.37 us: on_device(): call(second_kernel, shapes + [jax.ShapeDtypeStruct(block, f32)], 32, scra...]
  transfers between devices with their start and end apart: 16 -> 15, of which waited for: 6 -> 5; matrix products, arithmetic and copies ran while one was open for 0% -> 0% of each run, Pallas kernels for 15% -> 15%
where the time goes in v12:
time: 97 us; the launch traced here: 96.7 us
  blocking collectives  34 us (35%)
  Pallas kernels  30.8 us (32%)
  starting transfers between devices  25.9 us (27%)
  waiting for transfers between devices  5.67 us (6%)
    ppermute x14, starting transfers between devices, swapped(): return lax.ppermute(x, axis, [(i, i ^ by) for i in range(peers)])  22.4 us
    all_to_all x1, blocking collectives, on_device(): got = lax.all_to_all(send, HEAD_AXES, 0, 0, tiled=True)  19.4 us
    all_to_all x1, blocking collectives, on_device(): back = lax.all_to_all(send, HEAD_AXES, 0, 0, tiled=True)  14.6 us
    pallas_call x1, Pallas kernels, on_device(): call(second_sums_kernel, sums, 24, [keys], cost_estimate=cost(1))  5.66 us
    pallas_call x1, Pallas kernels, on_device(): call(first_sums_kernel, sums, 24, [keys], cost_estimate=cost(1))  5.58 us
    pallas_call x1, Pallas kernels, on_device(): call(second_kernel, shapes + [jax.ShapeDtypeStruct(block, f32)], 32, scra...  5.37 us
    pallas_call x1, Pallas kernels, on_device(): call(first_kernel, [sums] + dq + [jax.ShapeDtypeStruct(block, bf16)], 32,...  5.26 us
    ppermute x1, starting transfers between devices, neighbours(): lax.ppermute(x, axis, pairs + [(target, source) for source, target in pai...  3.52 us
  transfers between devices with their start and end apart: 15, of which 5 were waited for; matrix products, arithmetic and copies ran while one was open for 0% of the time, Pallas kernels for 15%

profile of v12, /device:TPU:8, one launch (start us, length us, event | category | flops | bytes accessed | tf_op | source)
XLA Modules:
  0.0 96.7 jit_solution(6301083851878121521)
XLA Ops:
  0.0 2.5 %shard_map.73 = bf16[16,176,128]{2,1,0:T(8,128)(2,1)} custom-call(bf16[128,1152]{1,0:T(8,128)(2,1)} %bitcast.19, bf16[128,1152]{1,0:T(8,128)(2,1)} %bitcast.20, bf16[128,1152]{1,0:T(8,128)(2,1)} %bitcast.21, bf16[2,4,1152]{2,1,0:T(4,128)(2,1)} %k_in.1, bf16[2,4,1152]{2,1,0:T(4,128)(2,1)} %v_in.1), custom_call_target="tpu_custom_call" | custom-call | tf_op jit(solution)/shard_map/pallas_call | solution.py:453
  2.5 19.4 %all_to_all.10.got_ref.qg_a = bf16[16,176,128]{2,1,0:T(8,128)(2,1)S(1)} all-to-all(bf16[16,176,128]{2,1,0:T(8,128)(2,1)} %shard_map.73), channel_id=1, replica_groups=mesh['yh'=2,'x'=4,'c'=2,'z'=8,'yl'=2] {'yh','x','yl'}, dimensions={0} | all-to-all | bytes 1441792 | tf_op jit(solution)/shard_map/all_to_all | solution.py:467
  21.8 0.0 collective-permute-start
  21.9 0.1 shard_map.74.kv_0
  22.0 2.0 %collective-permute-start.4 = (bf16[144,128]{1,0:T(8,128)(2,1)S(1)}, bf16[144,128]{1,0:T(8,128)(2,1)S(1)}, u32[]{:S(2)}, u32[]{:S(2)}) collective-permute-start(bf16[144,128]{1,0:T(8,128)(2,1)S(1)} %shard_map.74.kv_0), channel_id=1, source_target_pairs={{0,2},{2,0},{4,6},{6,4},{8,10},{10,8},{12,14},{14,12},{1,3},{3,1},... | collective-permute-start | bytes 110600 | tf_op jit(solution)/shard_map/ppermute | solution.py:434
  24.0 5.4 %collective-permute-start.2 = (bf16[144,128]{1,0:T(8,128)(2,1)S(1)}, bf16[144,128]{1,0:T(8,128)(2,1)S(1)}, u32[]{:S(2)}, u32[]{:S(2)}) collective-permute-start(bf16[144,128]{1,0:T(8,128)(2,1)S(1)} %shard_map.74.kv_0), channel_id=1, source_target_pairs={{0,12},{2,14},{4,8},{6,10},{8,4},{10,6},{12,0},{14,2},{1,13},{3,15... | collective-permute-start | bytes 110600 | tf_op jit(solution)/shard_map/ppermute | solution.py:434
  29.4 1.5 %collective-permute-start.1 = (bf16[144,128]{1,0:T(8,128)(2,1)S(1)}, bf16[144,128]{1,0:T(8,128)(2,1)S(1)}, u32[]{:S(2)}, u32[]{:S(2)}) collective-permute-start(bf16[144,128]{1,0:T(8,128)(2,1)S(1)} %shard_map.74.kv_0), channel_id=1, source_target_pairs={{0,4},{2,6},{4,0},{6,2},{8,12},{10,14},{12,8},{14,10},{1,5},{3,7},... | collective-permute-start | bytes 110600 | tf_op jit(solution)/shard_map/ppermute | solution.py:434
  30.8 0.0 collective-permute-done.4.kv_1
  30.8 2.8 %collective-permute-start.5 = (bf16[2,144,128]{2,1,0:T(8,128)(2,1)S(1)}, bf16[2,144,128]{2,1,0:T(8,128)(2,1)S(1)}, u32[]{:S(2)}, u32[]{:S(2)}) collective-permute-start(bf16[2,144,128]{2,1,0:T(8,128)(2,1)S(1)} %pad_maximum_fusion.1), channel_id=1, source_target_pairs={{0,8},{2,10},{4,12},{6,14},{8,0},{10,2},{12,4},{14,6},{1,9},{3,11}... | collective-permute-start | bytes 221192 | tf_op jit(solution)/shard_map/ppermute | solution.py:434
  33.6 0.0 collective-permute-done.2.kv_6
  33.6 0.6 collective-permute-done.1.kv_2
  34.2 1.1 %collective-permute-start.3 = (bf16[2,144,128]{2,1,0:T(8,128)(2,1)S(1)}, bf16[2,144,128]{2,1,0:T(8,128)(2,1)S(1)}, u32[]{:S(2)}, u32[]{:S(2)}) collective-permute-start(bf16[2,144,128]{2,1,0:T(8,128)(2,1)S(1)} %pad_maximum_fusion), channel_id=1, source_target_pairs={{0,2},{2,0},{4,6},{6,4},{8,10},{10,8},{12,14},{14,12},{1,3},{3,1},... | collective-permute-start | bytes 221192 | tf_op jit(solution)/shard_map/ppermute | solution.py:434
  35.3 0.0 collective-permute-done.qg_b
  35.3 5.6 %shard_map.75.first_ref = f32[2,16,128]{2,1,0:T(8,128)S(1)} custom-call(bf16[16,176,128]{2,1,0:T(8,128)(2,1)S(1)} %all_to_all.10.got_ref.qg_a, bf16[16,176,128]{2,1,0:T(8,128)(2,1)S(1)} %collective-permute-done.qg_b, bf16[144,128]{1,0:T(8,128)(2,1)S(1)} %shard_map.74.kv_0, bf16[144,128]{1,0:T(8,128)(2,1)S(1)} %collective-permute-done.4.kv_1, ...), custom_call_target="tpu_custom_call" | custom-call | flops 1073741824 | bytes 1048576 | tf_op jit(solution)/shard_map/pallas_call | solution.py:481
  40.9 0.0 collective-permute-done.5.kv_45
  40.9 0.0 collective-permute-done.3.kv_37
  41.0 5.7 %shard_map.76.mine_ref = f32[2,16,128]{2,1,0:T(8,128)S(1)} custom-call(bf16[16,176,128]{2,1,0:T(8,128)(2,1)S(1)} %all_to_all.10.got_ref.qg_a, bf16[16,176,128]{2,1,0:T(8,128)(2,1)S(1)} %collective-permute-done.qg_b, bf16[2,144,128]{2,1,0:T(8,128)(2,1)S(1)} %collective-permute-done.3.kv_37, bf16[2,144,128]{2,1,0:T(8,128)(2,1)S(1)} %collective-permute-done.5.kv_45, ...), custom_call_target="tpu_custom_call" | custom-call | flops 1073741824 | bytes 1048576 | tf_op jit(solution)/shard_map/pallas_call | solution.py:483
  46.6 0.3 collective-permute-start.6
  46.9 0.2 shard_map.77
  47.1 0.9 collective-permute-done.6.came_ref
  48.1 0.0 slice-start
  48.1 5.3 %shard_map.78 = (f32[2,16,128]{2,1,0:T(8,128)S(1)}, f32[16,80,128]{2,1,0:T(8,128)S(1)}, f32[16,80,128]{2,1,0:T(8,128)S(1)}, bf16[4,144,128]{2,1,0:T(8,128)(2,1)S(1)}) custom-call(bf16[16,176,128]{2,1,0:T(8,128)(2,1)S(1)} %all_to_all.10.got_ref.qg_a, bf16[16,176,128]{2,1,0:T(8,128)(2,1)S(1)} %collective-permute-done.qg_b, ...), custom_call_target="tpu_custom_call" | custom-call | flops 5368709120 | bytes 1048576 | tf_op jit(solution)/shard_map/pallas_call | solution.py:492
  53.3 1.1 %collective-permute-start.7 = (bf16[4,144,128]{2,1,0:T(8,128)(2,1)S(1)}, bf16[4,144,128]{2,1,0:T(8,128)(2,1)S(1)}, u32[]{:S(2)}, u32[]{:S(2)}) collective-permute-start(bf16[4,144,128]{2,1,0:T(8,128)(2,1)S(1)} %get-tuple-element.74), channel_id=1, source_target_pairs={{0,2},{2,0},{4,6},{6,4},{8,10},{10,8},{12,14},{14,12},{1,3},{3,1},... | collective-permute-start | bytes 442376 | tf_op jit(solution)/shard_map/ppermute | solution.py:434
  54.4 5.4 %shard_map.79 = (f32[16,72,128]{2,1,0:T(8,128)S(1)}, f32[16,24,128]{2,1,0:T(8,128)S(1)}, f32[16,96,128]{2,1,0:T(8,128)S(1)}, f32[4,144,128]{2,1,0:T(8,128)S(1)}) custom-call(bf16[16,176,128]{2,1,0:T(8,128)(2,1)S(1)} %all_to_all.10.got_ref.qg_a, bf16[16,176,128]{2,1,0:T(8,128)(2,1)S(1)} %collective-permute-done.qg_b, ...), custom_call_target="tpu_custom_call" | custom-call | flops 5368709120 | bytes 1048576 | tf_op jit(solution)/shard_map/pallas_call | solution.py:497
  59.8 0.0 collective-permute-done.7
  59.8 0.1 collective-permute-start.8
  60.0 2.8 %collective-permute-start.11 = (bf16[144,128]{1,0:T(8,128)(2,1)S(1)}, bf16[144,128]{1,0:T(8,128)(2,1)S(1)}, u32[]{:S(2)}, u32[]{:S(2)}) collective-permute-start(bf16[144,128]{1,0:T(8,128)(2,1)S(1)} %get-tuple-element.93), channel_id=1, source_target_pairs={{0,8},{2,10},{4,12},{6,14},{8,0},{10,2},{12,4},{14,6},{1,9},{3,11}... | collective-permute-start | bytes 110600 | tf_op jit(solution)/shard_map/ppermute | solution.py:434
  62.8 2.4 %collective-permute-start.10 = (bf16[144,128]{1,0:T(8,128)(2,1)S(1)}, bf16[144,128]{1,0:T(8,128)(2,1)S(1)}, u32[]{:S(2)}, u32[]{:S(2)}) collective-permute-start(bf16[144,128]{1,0:T(8,128)(2,1)S(1)} %get-tuple-element.94), channel_id=1, source_target_pairs={{0,12},{2,14},{4,8},{6,10},{8,4},{10,6},{12,0},{14,2},{1,13},{3,15... | collective-permute-start | bytes 110600 | tf_op jit(solution)/shard_map/ppermute | solution.py:434
  65.2 1.4 %collective-permute-start.9 = (bf16[144,128]{1,0:T(8,128)(2,1)S(1)}, bf16[144,128]{1,0:T(8,128)(2,1)S(1)}, u32[]{:S(2)}, u32[]{:S(2)}) collective-permute-start(bf16[144,128]{1,0:T(8,128)(2,1)S(1)} %get-tuple-element.95), channel_id=1, source_target_pairs={{0,4},{2,6},{4,0},{6,2},{8,12},{10,14},{12,8},{14,10},{1,5},{3,7},... | collective-permute-start | bytes 110600 | tf_op jit(solution)/shard_map/ppermute | solution.py:434
  66.6 0.0 slice-done
  66.6 0.0 slice-done.1
  66.6 0.0 copy-done
  66.6 2.7 %shard_map.80.weights = bf16[512,3456]{1,0:T(8,128)(2,1)S(1)} custom-call(bf16[256,1152]{1,0:T(8,128)(2,1)S(1)} %copy-done, bf16[1152,3456]{1,0:T(8,128)(2,1)S(1)} %bitcast.14), custom_call_target="tpu_custom_call" | custom-call | flops 1048576 | bytes 65536 | tf_op jit(solution)/shard_map/pallas_call | solution.py:510
  69.3 0.0 collective-permute-done.11.came_c
  69.3 0.0 collective-permute-done.10.came_b
  69.3 0.7 collective-permute-done.9.came_a
  70.0 0.1 collective-permute-start.12
  70.1 1.2 %collective-permute-done.12.other_ref = bf16[144,128]{1,0:T(8,128)(2,1)S(1)} collective-permute-done((bf16[144,128]{1,0:T(8,128)(2,1)S(1)}, bf16[144,128]{1,0:T(8,128)(2,1)S(1)}, u32[]{:S(2)}, u32[]{:S(2)}) %collective-permute-start.12) | collective-permute-done | bytes 36896 | tf_op jit(solution)/shard_map/ppermute | solution.py:434
  71.3 0.0 collective-permute-done.8.came_ref
  71.3 0.3 shard_map.82
  71.6 14.6 %all_to_all.11.back_ref = bf16[16,112,128]{2,1,0:T(8,128)(2,1)S(1)} all-to-all(bf16[16,112,128]{2,1,0:T(8,128)(2,1)S(1)} %shard_map.82), channel_id=1, replica_groups=mesh['yh'=2,'x'=4,'c'=2,'z'=8,'yl'=2] {'yh','x','yl'}, dimensions={0} | all-to-all | bytes 917504 | tf_op jit(solution)/shard_map/all_to_all | solution.py:519
  86.2 1.9 %shard_map.83 = (bf16[160,512]{1,0:T(8,128)(2,1)S(1)}, f32[4,64]{1,0:T(4,128)S(1)}, f32[4,64]{1,0:T(4,128)S(1)}) custom-call(bf16[16,112,128]{2,1,0:T(8,128)(2,1)S(1)} %all_to_all.11.back_ref, bf16[512,3456]{1,0:T(8,128)(2,1)S(1)} %shard_map.80.weights), custom_call_target="tpu_custom_call" | custom-call | tf_op jit(solution)/shard_map/pallas_call | solution.py:521
  88.1 1.5 %collective-permute-start.13 = (f32[4,64]{1,0:T(4,128)S(1)}, f32[4,64]{1,0:T(4,128)S(1)}, u32[]{:S(2)}, u32[]{:S(2)}) collective-permute-start(f32[4,64]{1,0:T(4,128)S(1)} %get-tuple-element.87), channel_id=1, source_target_pairs={{0,1},{1,0},{2,3},{3,2},{4,5},{5,4},{6,7},{7,6},{8,9},{9,8},{10,11... | collective-permute-start | bytes 3080 | tf_op jit(solution)/shard_map/ppermute | solution.py:434
  89.6 3.5 %collective-permute-start.14 = (f32[4,64]{1,0:T(4,128)S(1)}, f32[4,64]{1,0:T(4,128)S(1)}, u32[]{:S(2)}, u32[]{:S(2)}) collective-permute-start(f32[4,64]{1,0:T(4,128)S(1)} %get-tuple-element.88), channel_id=1, source_target_pairs={{1,2},{3,4},{5,6},{7,8},{9,10},{11,12},{13,14},{2,1},{4,3},{6,5},{... | collective-permute-start | bytes 3080 | tf_op jit(solution)/shard_map/ppermute | solution.py:440
  93.1 0.6 shard_map.84.center_ref
  93.8 0.0 collective-permute-done.13.near_ref
  93.8 2.2 %collective-permute-done.14.far_ref = f32[4,64]{1,0:T(4,128)S(1)} collective-permute-done((f32[4,64]{1,0:T(4,128)S(1)}, f32[4,64]{1,0:T(4,128)S(1)}, u32[]{:S(2)}, u32[]{:S(2)}) %collective-permute-start.14) | collective-permute-done | bytes 1056 | tf_op jit(solution)/shard_map/ppermute | solution.py:440
  96.0 0.7 shard_map.85
  (10 shorter events, 0.1 us)
Async XLA Ops:
  21.8 13.5 %collective-permute-start = (bf16[16,176,128]{2,1,0:T(8,128)(2,1)S(1)}, bf16[16,176,128]{2,1,0:T(8,128)(2,1)S(1)}, u32[]{:S(2)}, u32[]{:S(2)}) collective-permute-start(bf16[16,176,128]{2,1,0:T(8,128)(2,1)S(1)} %all_to_all.10.got_ref.qg_a), channel_id=1, source_target_pairs={{0,16},{16,0},{1,17},{17,1},{2,18},{18,2},{3,19},{19,3},{4,20},{20... | collective-permute-start | bytes 2162696 | tf_op jit(solution)/shard_map/ppermute | solution.py:434
  22.0 8.9 %collective-permute-start.4 = (bf16[144,128]{1,0:T(8,128)(2,1)S(1)}, bf16[144,128]{1,0:T(8,128)(2,1)S(1)}, u32[]{:S(2)}, u32[]{:S(2)}) collective-permute-start(bf16[144,128]{1,0:T(8,128)(2,1)S(1)} %shard_map.74.kv_0), channel_id=1, source_target_pairs={{0,2},{2,0},{4,6},{6,4},{8,10},{10,8},{12,14},{14,12},{1,3},{3,1},... | collective-permute-start | bytes 110600 | tf_op jit(solution)/shard_map/ppermute | solution.py:434
  24.0 9.6 %collective-permute-start.2 = (bf16[144,128]{1,0:T(8,128)(2,1)S(1)}, bf16[144,128]{1,0:T(8,128)(2,1)S(1)}, u32[]{:S(2)}, u32[]{:S(2)}) collective-permute-start(bf16[144,128]{1,0:T(8,128)(2,1)S(1)} %shard_map.74.kv_0), channel_id=1, source_target_pairs={{0,12},{2,14},{4,8},{6,10},{8,4},{10,6},{12,0},{14,2},{1,13},{3,15... | collective-permute-start | bytes 110600 | tf_op jit(solution)/shard_map/ppermute | solution.py:434
  29.4 4.9 %collective-permute-start.1 = (bf16[144,128]{1,0:T(8,128)(2,1)S(1)}, bf16[144,128]{1,0:T(8,128)(2,1)S(1)}, u32[]{:S(2)}, u32[]{:S(2)}) collective-permute-start(bf16[144,128]{1,0:T(8,128)(2,1)S(1)} %shard_map.74.kv_0), channel_id=1, source_target_pairs={{0,4},{2,6},{4,0},{6,2},{8,12},{10,14},{12,8},{14,10},{1,5},{3,7},... | collective-permute-start | bytes 110600 | tf_op jit(solution)/shard_map/ppermute | solution.py:434
  30.8 10.1 %collective-permute-start.5 = (bf16[2,144,128]{2,1,0:T(8,128)(2,1)S(1)}, bf16[2,144,128]{2,1,0:T(8,128)(2,1)S(1)}, u32[]{:S(2)}, u32[]{:S(2)}) collective-permute-start(bf16[2,144,128]{2,1,0:T(8,128)(2,1)S(1)} %pad_maximum_fusion.1), channel_id=1, source_target_pairs={{0,8},{2,10},{4,12},{6,14},{8,0},{10,2},{12,4},{14,6},{1,9},{3,11}... | collective-permute-start | bytes 221192 | tf_op jit(solution)/shard_map/ppermute | solution.py:434
  34.2 6.7 %collective-permute-start.3 = (bf16[2,144,128]{2,1,0:T(8,128)(2,1)S(1)}, bf16[2,144,128]{2,1,0:T(8,128)(2,1)S(1)}, u32[]{:S(2)}, u32[]{:S(2)}) collective-permute-start(bf16[2,144,128]{2,1,0:T(8,128)(2,1)S(1)} %pad_maximum_fusion), channel_id=1, source_target_pairs={{0,2},{2,0},{4,6},{6,4},{8,10},{10,8},{12,14},{14,12},{1,3},{3,1},... | collective-permute-start | bytes 221192 | tf_op jit(solution)/shard_map/ppermute | solution.py:434
  46.6 1.5 %collective-permute-start.6 = (f32[2,16,128]{2,1,0:T(8,128)S(1)}, f32[2,16,128]{2,1,0:T(8,128)S(1)}, u32[]{:S(2)}, u32[]{:S(2)}) collective-permute-start(f32[2,16,128]{2,1,0:T(8,128)S(1)} %shard_map.76.mine_ref), channel_id=1, source_target_pairs={{0,16},{16,0},{1,17},{17,1},{2,18},{18,2},{3,19},{19,3},{4,20},{20... | collective-permute-start | bytes 49160 | tf_op jit(solution)/shard_map/ppermute | solution.py:434
  48.1 18.5 %slice-start = ((s8[7962624]{0:T(1024)(128)(4,1)}), s8[4194304]{0:T(1024)(128)(4,1)S(1)}, s32[]{:S(2)}) async-start(s8[7962624]{0:T(1024)(128)(4,1)} %bitcast.13), calls=%async_computation.2 | async-start | bytes 8388608
  53.3 6.5 %collective-permute-start.7 = (bf16[4,144,128]{2,1,0:T(8,128)(2,1)S(1)}, bf16[4,144,128]{2,1,0:T(8,128)(2,1)S(1)}, u32[]{:S(2)}, u32[]{:S(2)}) collective-permute-start(bf16[4,144,128]{2,1,0:T(8,128)(2,1)S(1)} %get-tuple-element.74), channel_id=1, source_target_pairs={{0,2},{2,0},{4,6},{6,4},{8,10},{10,8},{12,14},{14,12},{1,3},{3,1},... | collective-permute-start | bytes 442376 | tf_op jit(solution)/shard_map/ppermute | solution.py:434
  54.4 12.2 %slice-start.1 = ((s8[7962624]{0:T(1024)(128)(4,1)}), s8[3768320]{0:T(1024)(128)(4,1)S(1)}, s32[]{:S(2)}) async-start(s8[7962624]{0:T(1024)(128)(4,1)} %bitcast.13), calls=%async_computation.3 | async-start | bytes 7536640
  54.4 12.2 %copy-start = (bf16[256,1152]{1,0:T(8,128)(2,1)S(1)}, bf16[256,1152]{1,0:T(8,128)(2,1)}, u32[]{:S(2)}) copy-start(bf16[256,1152]{1,0:T(8,128)(2,1)} %patch_ref) | copy-start | bytes 1769476
  59.8 11.5 %collective-permute-start.8 = (f32[16,96,128]{2,1,0:T(8,128)S(1)}, f32[16,96,128]{2,1,0:T(8,128)S(1)}, u32[]{:S(2)}, u32[]{:S(2)}) collective-permute-start(f32[16,96,128]{2,1,0:T(8,128)S(1)} %get-tuple-element.77), channel_id=1, source_target_pairs={{0,16},{16,0},{1,17},{17,1},{2,18},{18,2},{3,19},{19,3},{4,20},{20... | collective-permute-start | bytes 2359304 | tf_op jit(solution)/shard_map/ppermute | solution.py:434
  60.0 9.3 %collective-permute-start.11 = (bf16[144,128]{1,0:T(8,128)(2,1)S(1)}, bf16[144,128]{1,0:T(8,128)(2,1)S(1)}, u32[]{:S(2)}, u32[]{:S(2)}) collective-permute-start(bf16[144,128]{1,0:T(8,128)(2,1)S(1)} %get-tuple-element.93), channel_id=1, source_target_pairs={{0,8},{2,10},{4,12},{6,14},{8,0},{10,2},{12,4},{14,6},{1,9},{3,11}... | collective-permute-start | bytes 110600 | tf_op jit(solution)/shard_map/ppermute | solution.py:434
  62.8 6.6 %collective-permute-start.10 = (bf16[144,128]{1,0:T(8,128)(2,1)S(1)}, bf16[144,128]{1,0:T(8,128)(2,1)S(1)}, u32[]{:S(2)}, u32[]{:S(2)}) collective-permute-start(bf16[144,128]{1,0:T(8,128)(2,1)S(1)} %get-tuple-element.94), channel_id=1, source_target_pairs={{0,12},{2,14},{4,8},{6,10},{8,4},{10,6},{12,0},{14,2},{1,13},{3,15... | collective-permute-start | bytes 110600 | tf_op jit(solution)/shard_map/ppermute | solution.py:434
  65.2 4.9 %collective-permute-start.9 = (bf16[144,128]{1,0:T(8,128)(2,1)S(1)}, bf16[144,128]{1,0:T(8,128)(2,1)S(1)}, u32[]{:S(2)}, u32[]{:S(2)}) collective-permute-start(bf16[144,128]{1,0:T(8,128)(2,1)S(1)} %get-tuple-element.95), channel_id=1, source_target_pairs={{0,4},{2,6},{4,0},{6,2},{8,12},{10,14},{12,8},{14,10},{1,5},{3,7},... | collective-permute-start | bytes 110600 | tf_op jit(solution)/shard_map/ppermute | solution.py:434
  70.0 1.3 %collective-permute-start.12 = (bf16[144,128]{1,0:T(8,128)(2,1)S(1)}, bf16[144,128]{1,0:T(8,128)(2,1)S(1)}, u32[]{:S(2)}, u32[]{:S(2)}) collective-permute-start(bf16[144,128]{1,0:T(8,128)(2,1)S(1)} %shard_map.81.keys_ref), channel_id=1, source_target_pairs={{0,16},{16,0},{1,17},{17,1},{2,18},{18,2},{3,19},{19,3},{4,20},{20... | collective-permute-start | bytes 110600 | tf_op jit(solution)/shard_map/ppermute | solution.py:434
  88.1 5.7 %collective-permute-start.13 = (f32[4,64]{1,0:T(4,128)S(1)}, f32[4,64]{1,0:T(4,128)S(1)}, u32[]{:S(2)}, u32[]{:S(2)}) collective-permute-start(f32[4,64]{1,0:T(4,128)S(1)} %get-tuple-element.87), channel_id=1, source_target_pairs={{0,1},{1,0},{2,3},{3,2},{4,5},{5,4},{6,7},{7,6},{8,9},{9,8},{10,11... | collective-permute-start | bytes 3080 | tf_op jit(solution)/shard_map/ppermute | solution.py:434
  89.6 6.4 %collective-permute-start.14 = (f32[4,64]{1,0:T(4,128)S(1)}, f32[4,64]{1,0:T(4,128)S(1)}, u32[]{:S(2)}, u32[]{:S(2)}) collective-permute-start(f32[4,64]{1,0:T(4,128)S(1)} %get-tuple-element.88), channel_id=1, source_target_pairs={{1,2},{3,4},{5,6},{7,8},{9,10},{11,12},{13,14},{2,1},{4,3},{6,5},{... | collective-permute-start | bytes 3080 | tf_op jit(solution)/shard_map/ppermute | solution.py:440

commit v13 on v12

--- a/solution.py
+++ b/solution.py
@@ -306,10 +306,12 @@
         cols = slice(part * D, (part + 1) * D)
         both = jnp.dot(patch_ref[...], qkv_ref[:, cols], preferred_element_type=f32)
         both = both.reshape(16, 2, 8, D)
-        both = jnp.concatenate([both[:, 0].reshape(128, D), both[:, 1].reshape(128, D)])
-        high, low = split(both)
-        out_ref[0:256, cols] = high
-        out_ref[256:512, cols] = low
+        left, right = both[:, 0].reshape(128, D), both[:, 1].reshape(128, D)
+        outer = lax.broadcasted_iota(jnp.int32, (128, D), 0) % 8 < 4
+        for at, rows in ((0, jnp.where(outer, left, right)), (256, jnp.where(outer, right, left))):
+            high, low = split(rows)
+            out_ref[at : at + 128, cols] = high
+            out_ref[at + 128 : at + 256, cols] = low
 
 
 def split(x):
@@ -325,7 +327,26 @@
     return jnp.where(where, value, 0.0).astype(bf16)
 
 
-def embed_kernel(back_ref, weights, turned_ref, near_out, far_out, joined, pooled, sheet):
+def turn(weights, joined, pooled):
+    def product(rows, values):
+        out = jnp.dot(rows, values, preferred_element_type=f32)
+        return out[0:128] + out[128:256]
+
+    patch = product(weights[:, 0:D], joined)
+    cells = jnp.concatenate(split(product(weights[:, D:], pooled)), axis=1)
+    cell, token = iota((256, 256), 0) % 16, iota((256, 256), 1)
+    mine = token // (POOL * COLS) * 4 + token % COLS // POOL
+    beyond = CELLS + (token - TOK) // COLS * 4 + token % COLS // POOL
+    holds = (cell == jnp.where(token < TOK, mine, beyond)) & (token < EXTENDED)
+    patch = patch + jnp.dot(cells, one_hot(holds, 1.0 / POOL**2), preferred_element_type=f32)
+    to, token = iota((EXTENDED, 256), 0), iota((EXTENDED, 256), 1)
+    source = jnp.where(to < TOK, to % 8 * COLS, TOK + to % 2 * COLS) + column_of(to)
+    return lax.dot_general(
+        one_hot(token == source), jnp.concatenate(split(patch)), NT, preferred_element_type=f32
+    )
+
+
+def embed_kernel(back_ref, weights, turned_ref, joined, pooled, near_out, far_out, sheet):
     for h in range(0, HEADS, 2):
         pair = []
         wide = []
@@ -353,23 +374,9 @@
                 two = [jnp.where(group == 4 * part + k, cells, 0.0) for k in (n, n + 1)]
                 rows = part * D + (h + n) * DH
                 pooled[rows : rows + 2 * DH] = jnp.concatenate(two).astype(bf16)
-    patch = jnp.dot(weights[:, 0:D], joined[...], preferred_element_type=f32)
-    patch = patch[0:256] + patch[256:512]
-    cells = jnp.dot(weights[:, D:], pooled[...], preferred_element_type=f32)
-    cells = jnp.concatenate(split(cells[0:256] + cells[256:512]), axis=1)
-    cell, token = iota((256, 256), 0) % 16, iota((256, 256), 1)
-    mine = token // (POOL * COLS) * 4 + token % COLS // POOL
-    beyond = CELLS + (token - TOK) // COLS * 4 + token % COLS // POOL
-    holds = (cell == jnp.where(token < TOK, mine, beyond)) & (token < EXTENDED)
-    patch = patch + jnp.dot(cells, one_hot(holds, 1.0 / POOL**2), preferred_element_type=f32)
-    to, token = iota((EXTENDED, 256), 0), iota((EXTENDED, 256), 1)
-    source = jnp.where(to < TOK, to % 8 * COLS, TOK + to % 2 * COLS) + column_of(to)
-    turned = lax.dot_general(
-        one_hot(token == source), jnp.concatenate(split(patch)), NT, preferred_element_type=f32
-    )
+    turned = turn(weights[0:256], joined[...], pooled[...])
     turned_ref[...] = turned.astype(bf16)
-    whole = turned[:, 0:256] + turned[:, 256:512]
-    left, right = whole[:, 0:128], whole[:, 128:256]
+    left = right = turned[:, 0:128] + turned[:, 128:256]
     lane = iota((8, 128), 1)
     own = jnp.where(lane % 8 < 4, left[0:ROWS], right[TOK - ROWS : TOK])
     beyond = jnp.where(lane % 8 < 4, left[TOK : TOK + 8], pltpu.roll(right[EXTENDED - 8 :], 2, 0))
@@ -391,16 +398,19 @@
     return jnp.where(row < TOK, row // 8, far // 8 * 4 + far % 8 // 2)
 
 
-def fold_kernel(turned_ref, center_ref, sheet):
-    turned = turned_ref[...]
+def fold_kernel(outer_ref, weights, joined, pooled, center_ref, sheet):
+    outer = outer_ref[...].astype(f32)
+    inner = turn(weights[256:512], joined[...], pooled[...])
+    low_half = iota(outer.shape, 1) % 8 < 4
+    halves = [jnp.where(low_half, outer, inner), jnp.where(low_half, inner, outer)]
+    halves = [half.astype(bf16) for half in halves]
     sheet[...] = jnp.zeros_like(sheet)
     here = iota((EXTENDED, 256), 1) % 128 // 8 == column_of(iota((EXTENDED, 256), 0))
     to, at = iota((256, 256), 1), iota((256, 256), 0) % 128
     for pair in range(8):
         tile = one_hot((to // 128 + 2 * pair == at // 8) & (to % 8 == at % 8))
         for side in (0, 1):
-            parts = [turned[:, n * 256 + side * 128 : n * 256 + (side + 1) * 128] for n in (0, 1)]
-            wide = jnp.dot(jnp.concatenate(parts, axis=1), tile, preferred_element_type=f32)
+            wide = jnp.dot(halves[side], tile, preferred_element_type=f32)
             wide = jnp.where(here, wide, 0.0)
             own = jnp.sum(wide[0:TOK].reshape(COLS, ROWS, 256), axis=0)
             edge = jnp.sum(wide[TOK:].reshape(4, 8, 256), axis=0)
@@ -518,20 +528,21 @@
     )
     back = lax.all_to_all(send, HEAD_AXES, 0, 0, tiled=True)
     strip = jax.ShapeDtypeStruct((4, 64), f32)
-    turned, to_near, to_far = call(
+    shapes = [(EXTENDED, 256), (D, 2 * TOK), (2 * D, 128)]
+    *parts, to_near, to_far = call(
         embed_kernel,
-        [jax.ShapeDtypeStruct((EXTENDED, 512), bf16), strip, strip],
+        [jax.ShapeDtypeStruct(shape, bf16) for shape in shapes] + [strip, strip],
         28,
-        [pltpu.VMEM((D, 2 * TOK), bf16), pltpu.VMEM((2 * D, 128), bf16), pltpu.VMEM((72, 128), f32)],
+        [pltpu.VMEM((72, 128), f32)],
     )(back, weights)
     near, far = swapped(to_near, "yl", 1), neighbours(to_far, COL)
     center = call(
         fold_kernel,
         jax.ShapeDtypeStruct((64, 128), f32),
-        8,
+        20,
         [pltpu.VMEM((2, 72, 128), f32)],
         cost_estimate=SMALL,
-    )(turned)
+    )(parts[0], weights, *parts[1:])
     near, far, center = lax.optimization_barrier((near, far, center))
     return call(cols_kernel, jax.ShapeDtypeStruct((64, 128), f32), 4)(center, near, far)
 

time: 97 us -> 96.4 us (level)
  transfers between devices with their start and end apart: 15 -> 15, of which waited for: 5 -> 5; matrix products, arithmetic and copies ran while one was open for 0% -> 0% of each run, Pallas kernels for 15% -> 16%
where the time goes in v13:
time: 96.4 us; the launch traced here: 96.1 us
  blocking collectives  34 us (35%)
  Pallas kernels  31.1 us (32%)
  starting transfers between devices  25.9 us (27%)
  waiting for transfers between devices  4.77 us (5%)
    ppermute x14, starting transfers between devices, swapped(): return lax.ppermute(x, axis, [(i, i ^ by) for i in range(peers)])  22.4 us
    all_to_all x1, blocking collectives, on_device(): got = lax.all_to_all(send, HEAD_AXES, 0, 0, tiled=True)  19.4 us
    all_to_all x1, blocking collectives, on_device(): back = lax.all_to_all(send, HEAD_AXES, 0, 0, tiled=True)  14.6 us
    pallas_call x1, Pallas kernels, on_device(): call(second_sums_kernel, sums, 24, [keys], cost_estimate=cost(1))  5.66 us
    pallas_call x1, Pallas kernels, on_device(): call(first_sums_kernel, sums, 24, [keys], cost_estimate=cost(1))  5.58 us
    pallas_call x1, Pallas kernels, on_device(): call(second_kernel, shapes + [jax.ShapeDtypeStruct(block, f32)], 32, scra...  5.37 us
    pallas_call x1, Pallas kernels, on_device(): call(first_kernel, [sums] + dq + [jax.ShapeDtypeStruct(block, bf16)], 32,...  5.26 us
    ppermute x1, starting transfers between devices, neighbours(): lax.ppermute(x, axis, pairs + [(target, source) for source, target in pai...  3.52 us
  transfers between devices with their start and end apart: 15, of which 5 were waited for; matrix products, arithmetic and copies ran while one was open for 0% of the time, Pallas kernels for 16%

profile of v13, /device:TPU:8, one launch (start us, length us, event | category | flops | bytes accessed | tf_op | source)
XLA Modules:
  0.0 96.1 jit_solution(4839263621273446747)
XLA Ops:
  0.0 2.5 %shard_map.73 = bf16[16,176,128]{2,1,0:T(8,128)(2,1)} custom-call(bf16[128,1152]{1,0:T(8,128)(2,1)} %bitcast.19, bf16[128,1152]{1,0:T(8,128)(2,1)} %bitcast.20, bf16[128,1152]{1,0:T(8,128)(2,1)} %bitcast.21, bf16[2,4,1152]{2,1,0:T(4,128)(2,1)} %k_in.1, bf16[2,4,1152]{2,1,0:T(4,128)(2,1)} %v_in.1), custom_call_target="tpu_custom_call" | custom-call | tf_op jit(solution)/shard_map/pallas_call | solution.py:463
  2.5 19.4 %all_to_all.10.got_ref.qg_a = bf16[16,176,128]{2,1,0:T(8,128)(2,1)S(1)} all-to-all(bf16[16,176,128]{2,1,0:T(8,128)(2,1)} %shard_map.73), channel_id=1, replica_groups=mesh['yh'=2,'x'=4,'c'=2,'z'=8,'yl'=2] {'yh','x','yl'}, dimensions={0} | all-to-all | bytes 1441792 | tf_op jit(solution)/shard_map/all_to_all | solution.py:477
  21.8 0.0 collective-permute-start
  21.9 0.1 shard_map.74.kv_0
  22.0 2.0 %collective-permute-start.4 = (bf16[144,128]{1,0:T(8,128)(2,1)S(1)}, bf16[144,128]{1,0:T(8,128)(2,1)S(1)}, u32[]{:S(2)}, u32[]{:S(2)}) collective-permute-start(bf16[144,128]{1,0:T(8,128)(2,1)S(1)} %shard_map.74.kv_0), channel_id=1, source_target_pairs={{0,2},{2,0},{4,6},{6,4},{8,10},{10,8},{12,14},{14,12},{1,3},{3,1},... | collective-permute-start | bytes 110600 | tf_op jit(solution)/shard_map/ppermute | solution.py:444
  24.0 5.4 %collective-permute-start.2 = (bf16[144,128]{1,0:T(8,128)(2,1)S(1)}, bf16[144,128]{1,0:T(8,128)(2,1)S(1)}, u32[]{:S(2)}, u32[]{:S(2)}) collective-permute-start(bf16[144,128]{1,0:T(8,128)(2,1)S(1)} %shard_map.74.kv_0), channel_id=1, source_target_pairs={{0,12},{2,14},{4,8},{6,10},{8,4},{10,6},{12,0},{14,2},{1,13},{3,15... | collective-permute-start | bytes 110600 | tf_op jit(solution)/shard_map/ppermute | solution.py:444
  29.4 1.5 %collective-permute-start.1 = (bf16[144,128]{1,0:T(8,128)(2,1)S(1)}, bf16[144,128]{1,0:T(8,128)(2,1)S(1)}, u32[]{:S(2)}, u32[]{:S(2)}) collective-permute-start(bf16[144,128]{1,0:T(8,128)(2,1)S(1)} %shard_map.74.kv_0), channel_id=1, source_target_pairs={{0,4},{2,6},{4,0},{6,2},{8,12},{10,14},{12,8},{14,10},{1,5},{3,7},... | collective-permute-start | bytes 110600 | tf_op jit(solution)/shard_map/ppermute | solution.py:444
  30.8 0.0 collective-permute-done.4.kv_1
  30.8 2.8 %collective-permute-start.5 = (bf16[2,144,128]{2,1,0:T(8,128)(2,1)S(1)}, bf16[2,144,128]{2,1,0:T(8,128)(2,1)S(1)}, u32[]{:S(2)}, u32[]{:S(2)}) collective-permute-start(bf16[2,144,128]{2,1,0:T(8,128)(2,1)S(1)} %pad_maximum_fusion.1), channel_id=1, source_target_pairs={{0,8},{2,10},{4,12},{6,14},{8,0},{10,2},{12,4},{14,6},{1,9},{3,11}... | collective-permute-start | bytes 221192 | tf_op jit(solution)/shard_map/ppermute | solution.py:444
  33.6 0.0 collective-permute-done.2.kv_6
  33.6 0.6 collective-permute-done.1.kv_2
  34.2 1.1 %collective-permute-start.3 = (bf16[2,144,128]{2,1,0:T(8,128)(2,1)S(1)}, bf16[2,144,128]{2,1,0:T(8,128)(2,1)S(1)}, u32[]{:S(2)}, u32[]{:S(2)}) collective-permute-start(bf16[2,144,128]{2,1,0:T(8,128)(2,1)S(1)} %pad_maximum_fusion), channel_id=1, source_target_pairs={{0,2},{2,0},{4,6},{6,4},{8,10},{10,8},{12,14},{14,12},{1,3},{3,1},... | collective-permute-start | bytes 221192 | tf_op jit(solution)/shard_map/ppermute | solution.py:444
  35.3 0.0 collective-permute-done.qg_b
  35.3 5.6 %shard_map.75.first_ref = f32[2,16,128]{2,1,0:T(8,128)S(1)} custom-call(bf16[16,176,128]{2,1,0:T(8,128)(2,1)S(1)} %all_to_all.10.got_ref.qg_a, bf16[16,176,128]{2,1,0:T(8,128)(2,1)S(1)} %collective-permute-done.qg_b, bf16[144,128]{1,0:T(8,128)(2,1)S(1)} %shard_map.74.kv_0, bf16[144,128]{1,0:T(8,128)(2,1)S(1)} %collective-permute-done.4.kv_1, ...), custom_call_target="tpu_custom_call" | custom-call | flops 1073741824 | bytes 1048576 | tf_op jit(solution)/shard_map/pallas_call | solution.py:491
  40.9 0.0 collective-permute-done.5.kv_45
  40.9 0.0 collective-permute-done.3.kv_37
  41.0 5.7 %shard_map.76.mine_ref = f32[2,16,128]{2,1,0:T(8,128)S(1)} custom-call(bf16[16,176,128]{2,1,0:T(8,128)(2,1)S(1)} %all_to_all.10.got_ref.qg_a, bf16[16,176,128]{2,1,0:T(8,128)(2,1)S(1)} %collective-permute-done.qg_b, bf16[2,144,128]{2,1,0:T(8,128)(2,1)S(1)} %collective-permute-done.3.kv_37, bf16[2,144,128]{2,1,0:T(8,128)(2,1)S(1)} %collective-permute-done.5.kv_45, ...), custom_call_target="tpu_custom_call" | custom-call | flops 1073741824 | bytes 1048576 | tf_op jit(solution)/shard_map/pallas_call | solution.py:493
  46.6 0.3 collective-permute-start.6
  46.9 0.2 shard_map.77
  47.1 0.9 collective-permute-done.6.came_ref
  48.1 0.0 slice-start
  48.1 5.3 %shard_map.78 = (f32[2,16,128]{2,1,0:T(8,128)S(1)}, f32[16,80,128]{2,1,0:T(8,128)S(1)}, f32[16,80,128]{2,1,0:T(8,128)S(1)}, bf16[4,144,128]{2,1,0:T(8,128)(2,1)S(1)}) custom-call(bf16[16,176,128]{2,1,0:T(8,128)(2,1)S(1)} %all_to_all.10.got_ref.qg_a, bf16[16,176,128]{2,1,0:T(8,128)(2,1)S(1)} %collective-permute-done.qg_b, ...), custom_call_target="tpu_custom_call" | custom-call | flops 5368709120 | bytes 1048576 | tf_op jit(solution)/shard_map/pallas_call | solution.py:502
  53.3 1.1 %collective-permute-start.7 = (bf16[4,144,128]{2,1,0:T(8,128)(2,1)S(1)}, bf16[4,144,128]{2,1,0:T(8,128)(2,1)S(1)}, u32[]{:S(2)}, u32[]{:S(2)}) collective-permute-start(bf16[4,144,128]{2,1,0:T(8,128)(2,1)S(1)} %get-tuple-element.76), channel_id=1, source_target_pairs={{0,2},{2,0},{4,6},{6,4},{8,10},{10,8},{12,14},{14,12},{1,3},{3,1},... | collective-permute-start | bytes 442376 | tf_op jit(solution)/shard_map/ppermute | solution.py:444
  54.4 5.4 %shard_map.79 = (f32[16,72,128]{2,1,0:T(8,128)S(1)}, f32[16,24,128]{2,1,0:T(8,128)S(1)}, f32[16,96,128]{2,1,0:T(8,128)S(1)}, f32[4,144,128]{2,1,0:T(8,128)S(1)}) custom-call(bf16[16,176,128]{2,1,0:T(8,128)(2,1)S(1)} %all_to_all.10.got_ref.qg_a, bf16[16,176,128]{2,1,0:T(8,128)(2,1)S(1)} %collective-permute-done.qg_b, ...), custom_call_target="tpu_custom_call" | custom-call | flops 5368709120 | bytes 1048576 | tf_op jit(solution)/shard_map/pallas_call | solution.py:507
  59.8 0.0 collective-permute-done.7
  59.8 0.1 collective-permute-start.8
  60.0 2.8 %collective-permute-start.11 = (bf16[144,128]{1,0:T(8,128)(2,1)S(1)}, bf16[144,128]{1,0:T(8,128)(2,1)S(1)}, u32[]{:S(2)}, u32[]{:S(2)}) collective-permute-start(bf16[144,128]{1,0:T(8,128)(2,1)S(1)} %get-tuple-element.97), channel_id=1, source_target_pairs={{0,8},{2,10},{4,12},{6,14},{8,0},{10,2},{12,4},{14,6},{1,9},{3,11}... | collective-permute-start | bytes 110600 | tf_op jit(solution)/shard_map/ppermute | solution.py:444
  62.8 2.4 %collective-permute-start.10 = (bf16[144,128]{1,0:T(8,128)(2,1)S(1)}, bf16[144,128]{1,0:T(8,128)(2,1)S(1)}, u32[]{:S(2)}, u32[]{:S(2)}) collective-permute-start(bf16[144,128]{1,0:T(8,128)(2,1)S(1)} %get-tuple-element.98), channel_id=1, source_target_pairs={{0,12},{2,14},{4,8},{6,10},{8,4},{10,6},{12,0},{14,2},{1,13},{3,15... | collective-permute-start | bytes 110600 | tf_op jit(solution)/shard_map/ppermute | solution.py:444
  65.2 1.4 %collective-permute-start.9 = (bf16[144,128]{1,0:T(8,128)(2,1)S(1)}, bf16[144,128]{1,0:T(8,128)(2,1)S(1)}, u32[]{:S(2)}, u32[]{:S(2)}) collective-permute-start(bf16[144,128]{1,0:T(8,128)(2,1)S(1)} %get-tuple-element.99), channel_id=1, source_target_pairs={{0,4},{2,6},{4,0},{6,2},{8,12},{10,14},{12,8},{14,10},{1,5},{3,7},... | collective-permute-start | bytes 110600 | tf_op jit(solution)/shard_map/ppermute | solution.py:444
  66.6 0.0 slice-done
  66.6 0.0 slice-done.1
  66.6 0.0 copy-done
  66.6 2.7 %shard_map.80.weights = bf16[512,3456]{1,0:T(8,128)(2,1)S(1)} custom-call(bf16[256,1152]{1,0:T(8,128)(2,1)S(1)} %copy-done, bf16[1152,3456]{1,0:T(8,128)(2,1)S(1)} %bitcast.14), custom_call_target="tpu_custom_call" | custom-call | flops 1048576 | bytes 65536 | tf_op jit(solution)/shard_map/pallas_call | solution.py:520
  69.3 0.0 collective-permute-done.11.came_c
  69.3 0.0 collective-permute-done.10.came_b
  69.3 0.7 collective-permute-done.9.came_a
  70.0 0.1 collective-permute-start.12
  70.1 1.2 %collective-permute-done.12.other_ref = bf16[144,128]{1,0:T(8,128)(2,1)S(1)} collective-permute-done((bf16[144,128]{1,0:T(8,128)(2,1)S(1)}, bf16[144,128]{1,0:T(8,128)(2,1)S(1)}, u32[]{:S(2)}, u32[]{:S(2)}) %collective-permute-start.12) | collective-permute-done | bytes 36896 | tf_op jit(solution)/shard_map/ppermute | solution.py:444
  71.3 0.0 collective-permute-done.8.came_ref
  71.3 0.3 shard_map.82
  71.6 14.6 %all_to_all.11.back_ref = bf16[16,112,128]{2,1,0:T(8,128)(2,1)S(1)} all-to-all(bf16[16,112,128]{2,1,0:T(8,128)(2,1)S(1)} %shard_map.82), channel_id=1, replica_groups=mesh['yh'=2,'x'=4,'c'=2,'z'=8,'yl'=2] {'yh','x','yl'}, dimensions={0} | all-to-all | bytes 917504 | tf_op jit(solution)/shard_map/all_to_all | solution.py:529
  86.2 1.3 %shard_map.83 = (bf16[160,256]{1,0:T(8,128)(2,1)S(1)}, bf16[1152,256]{1,0:T(8,128)(2,1)S(1)}, bf16[2304,128]{1,0:T(8,128)(2,1)S(1)}, f32[4,64]{1,0:T(4,128)S(1)}, f32[4,64]{1,0:T(4,128)S(1)}) custom-call(bf16[16,112,128]{2,1,0:T(8,128)(2,1)S(1)} %all_to_all.11.back_ref, bf16[512,3456]{1,0:T(8,128)(2,1)S(1)} %shard_map.80.weights), custom_call_target="tpu_custom_call" | custom-call | tf_op jit(solution)/shard_map/pallas_call | solution.py:532
  87.5 1.5 %collective-permute-start.13 = (f32[4,64]{1,0:T(4,128)S(1)}, f32[4,64]{1,0:T(4,128)S(1)}, u32[]{:S(2)}, u32[]{:S(2)}) collective-permute-start(f32[4,64]{1,0:T(4,128)S(1)} %get-tuple-element.89), channel_id=1, source_target_pairs={{0,1},{1,0},{2,3},{3,2},{4,5},{5,4},{6,7},{7,6},{8,9},{9,8},{10,11... | collective-permute-start | bytes 3080 | tf_op jit(solution)/shard_map/ppermute | solution.py:444
  89.0 3.5 %collective-permute-start.14 = (f32[4,64]{1,0:T(4,128)S(1)}, f32[4,64]{1,0:T(4,128)S(1)}, u32[]{:S(2)}, u32[]{:S(2)}) collective-permute-start(f32[4,64]{1,0:T(4,128)S(1)} %get-tuple-element.90), channel_id=1, source_target_pairs={{1,2},{3,4},{5,6},{7,8},{9,10},{11,12},{13,14},{2,1},{4,3},{6,5},{... | collective-permute-start | bytes 3080 | tf_op jit(solution)/shard_map/ppermute | solution.py:450
  92.5 1.5 %shard_map.84.center_ref = f32[64,128]{1,0:T(8,128)S(1)} custom-call(bf16[160,256]{1,0:T(8,128)(2,1)S(1)} %get-tuple-element.91.outer_ref, bf16[512,3456]{1,0:T(8,128)(2,1)S(1)} %shard_map.80.weights, bf16[1152,256]{1,0:T(8,128)(2,1)S(1)} %get-tuple-element.92.joined, bf16[2304,128]{1,0:T(8,128)(2,1)S(1)} %get-tuple-element.93.pooled), custom_call_target="tpu_custom_call" | custom-call | flops 1048576 | bytes 65536 | tf_op jit(solution)/shard_map/pallas_call | solution.py:539
  94.1 0.0 collective-permute-done.13.near_ref
  94.1 1.3 %collective-permute-done.14.far_ref = f32[4,64]{1,0:T(4,128)S(1)} collective-permute-done((f32[4,64]{1,0:T(4,128)S(1)}, f32[4,64]{1,0:T(4,128)S(1)}, u32[]{:S(2)}, u32[]{:S(2)}) %collective-permute-start.14) | collective-permute-done | bytes 1056 | tf_op jit(solution)/shard_map/ppermute | solution.py:450
  95.4 0.7 shard_map.85
  (10 shorter events, 0.1 us)
Async XLA Ops:
  21.8 13.5 %collective-permute-start = (bf16[16,176,128]{2,1,0:T(8,128)(2,1)S(1)}, bf16[16,176,128]{2,1,0:T(8,128)(2,1)S(1)}, u32[]{:S(2)}, u32[]{:S(2)}) collective-permute-start(bf16[16,176,128]{2,1,0:T(8,128)(2,1)S(1)} %all_to_all.10.got_ref.qg_a), channel_id=1, source_target_pairs={{0,16},{16,0},{1,17},{17,1},{2,18},{18,2},{3,19},{19,3},{4,20},{20... | collective-permute-start | bytes 2162696 | tf_op jit(solution)/shard_map/ppermute | solution.py:444
  22.0 8.9 %collective-permute-start.4 = (bf16[144,128]{1,0:T(8,128)(2,1)S(1)}, bf16[144,128]{1,0:T(8,128)(2,1)S(1)}, u32[]{:S(2)}, u32[]{:S(2)}) collective-permute-start(bf16[144,128]{1,0:T(8,128)(2,1)S(1)} %shard_map.74.kv_0), channel_id=1, source_target_pairs={{0,2},{2,0},{4,6},{6,4},{8,10},{10,8},{12,14},{14,12},{1,3},{3,1},... | collective-permute-start | bytes 110600 | tf_op jit(solution)/shard_map/ppermute | solution.py:444
  24.0 9.6 %collective-permute-start.2 = (bf16[144,128]{1,0:T(8,128)(2,1)S(1)}, bf16[144,128]{1,0:T(8,128)(2,1)S(1)}, u32[]{:S(2)}, u32[]{:S(2)}) collective-permute-start(bf16[144,128]{1,0:T(8,128)(2,1)S(1)} %shard_map.74.kv_0), channel_id=1, source_target_pairs={{0,12},{2,14},{4,8},{6,10},{8,4},{10,6},{12,0},{14,2},{1,13},{3,15... | collective-permute-start | bytes 110600 | tf_op jit(solution)/shard_map/ppermute | solution.py:444
  29.4 4.9 %collective-permute-start.1 = (bf16[144,128]{1,0:T(8,128)(2,1)S(1)}, bf16[144,128]{1,0:T(8,128)(2,1)S(1)}, u32[]{:S(2)}, u32[]{:S(2)}) collective-permute-start(bf16[144,128]{1,0:T(8,128)(2,1)S(1)} %shard_map.74.kv_0), channel_id=1, source_target_pairs={{0,4},{2,6},{4,0},{6,2},{8,12},{10,14},{12,8},{14,10},{1,5},{3,7},... | collective-permute-start | bytes 110600 | tf_op jit(solution)/shard_map/ppermute | solution.py:444
  30.8 10.1 %collective-permute-start.5 = (bf16[2,144,128]{2,1,0:T(8,128)(2,1)S(1)}, bf16[2,144,128]{2,1,0:T(8,128)(2,1)S(1)}, u32[]{:S(2)}, u32[]{:S(2)}) collective-permute-start(bf16[2,144,128]{2,1,0:T(8,128)(2,1)S(1)} %pad_maximum_fusion.1), channel_id=1, source_target_pairs={{0,8},{2,10},{4,12},{6,14},{8,0},{10,2},{12,4},{14,6},{1,9},{3,11}... | collective-permute-start | bytes 221192 | tf_op jit(solution)/shard_map/ppermute | solution.py:444
  34.2 6.7 %collective-permute-start.3 = (bf16[2,144,128]{2,1,0:T(8,128)(2,1)S(1)}, bf16[2,144,128]{2,1,0:T(8,128)(2,1)S(1)}, u32[]{:S(2)}, u32[]{:S(2)}) collective-permute-start(bf16[2,144,128]{2,1,0:T(8,128)(2,1)S(1)} %pad_maximum_fusion), channel_id=1, source_target_pairs={{0,2},{2,0},{4,6},{6,4},{8,10},{10,8},{12,14},{14,12},{1,3},{3,1},... | collective-permute-start | bytes 221192 | tf_op jit(solution)/shard_map/ppermute | solution.py:444
  46.6 1.5 %collective-permute-start.6 = (f32[2,16,128]{2,1,0:T(8,128)S(1)}, f32[2,16,128]{2,1,0:T(8,128)S(1)}, u32[]{:S(2)}, u32[]{:S(2)}) collective-permute-start(f32[2,16,128]{2,1,0:T(8,128)S(1)} %shard_map.76.mine_ref), channel_id=1, source_target_pairs={{0,16},{16,0},{1,17},{17,1},{2,18},{18,2},{3,19},{19,3},{4,20},{20... | collective-permute-start | bytes 49160 | tf_op jit(solution)/shard_map/ppermute | solution.py:444
  48.1 18.5 %slice-start = ((s8[7962624]{0:T(1024)(128)(4,1)}), s8[4194304]{0:T(1024)(128)(4,1)S(1)}, s32[]{:S(2)}) async-start(s8[7962624]{0:T(1024)(128)(4,1)} %bitcast.13), calls=%async_computation.2 | async-start | bytes 8388608
  53.3 6.5 %collective-permute-start.7 = (bf16[4,144,128]{2,1,0:T(8,128)(2,1)S(1)}, bf16[4,144,128]{2,1,0:T(8,128)(2,1)S(1)}, u32[]{:S(2)}, u32[]{:S(2)}) collective-permute-start(bf16[4,144,128]{2,1,0:T(8,128)(2,1)S(1)} %get-tuple-element.76), channel_id=1, source_target_pairs={{0,2},{2,0},{4,6},{6,4},{8,10},{10,8},{12,14},{14,12},{1,3},{3,1},... | collective-permute-start | bytes 442376 | tf_op jit(solution)/shard_map/ppermute | solution.py:444
  54.4 12.2 %slice-start.1 = ((s8[7962624]{0:T(1024)(128)(4,1)}), s8[3768320]{0:T(1024)(128)(4,1)S(1)}, s32[]{:S(2)}) async-start(s8[7962624]{0:T(1024)(128)(4,1)} %bitcast.13), calls=%async_computation.3 | async-start | bytes 7536640
  54.4 12.2 %copy-start = (bf16[256,1152]{1,0:T(8,128)(2,1)S(1)}, bf16[256,1152]{1,0:T(8,128)(2,1)}, u32[]{:S(2)}) copy-start(bf16[256,1152]{1,0:T(8,128)(2,1)} %patch_ref) | copy-start | bytes 1769476
  59.8 11.5 %collective-permute-start.8 = (f32[16,96,128]{2,1,0:T(8,128)S(1)}, f32[16,96,128]{2,1,0:T(8,128)S(1)}, u32[]{:S(2)}, u32[]{:S(2)}) collective-permute-start(f32[16,96,128]{2,1,0:T(8,128)S(1)} %get-tuple-element.79), channel_id=1, source_target_pairs={{0,16},{16,0},{1,17},{17,1},{2,18},{18,2},{3,19},{19,3},{4,20},{20... | collective-permute-start | bytes 2359304 | tf_op jit(solution)/shard_map/ppermute | solution.py:444
  60.0 9.3 %collective-permute-start.11 = (bf16[144,128]{1,0:T(8,128)(2,1)S(1)}, bf16[144,128]{1,0:T(8,128)(2,1)S(1)}, u32[]{:S(2)}, u32[]{:S(2)}) collective-permute-start(bf16[144,128]{1,0:T(8,128)(2,1)S(1)} %get-tuple-element.97), channel_id=1, source_target_pairs={{0,8},{2,10},{4,12},{6,14},{8,0},{10,2},{12,4},{14,6},{1,9},{3,11}... | collective-permute-start | bytes 110600 | tf_op jit(solution)/shard_map/ppermute | solution.py:444
  62.8 6.6 %collective-permute-start.10 = (bf16[144,128]{1,0:T(8,128)(2,1)S(1)}, bf16[144,128]{1,0:T(8,128)(2,1)S(1)}, u32[]{:S(2)}, u32[]{:S(2)}) collective-permute-start(bf16[144,128]{1,0:T(8,128)(2,1)S(1)} %get-tuple-element.98), channel_id=1, source_target_pairs={{0,12},{2,14},{4,8},{6,10},{8,4},{10,6},{12,0},{14,2},{1,13},{3,15... | collective-permute-start | bytes 110600 | tf_op jit(solution)/shard_map/ppermute | solution.py:444
  65.2 4.9 %collective-permute-start.9 = (bf16[144,128]{1,0:T(8,128)(2,1)S(1)}, bf16[144,128]{1,0:T(8,128)(2,1)S(1)}, u32[]{:S(2)}, u32[]{:S(2)}) collective-permute-start(bf16[144,128]{1,0:T(8,128)(2,1)S(1)} %get-tuple-element.99), channel_id=1, source_target_pairs={{0,4},{2,6},{4,0},{6,2},{8,12},{10,14},{12,8},{14,10},{1,5},{3,7},... | collective-permute-start | bytes 110600 | tf_op jit(solution)/shard_map/ppermute | solution.py:444
  70.0 1.3 %collective-permute-start.12 = (bf16[144,128]{1,0:T(8,128)(2,1)S(1)}, bf16[144,128]{1,0:T(8,128)(2,1)S(1)}, u32[]{:S(2)}, u32[]{:S(2)}) collective-permute-start(bf16[144,128]{1,0:T(8,128)(2,1)S(1)} %shard_map.81.keys_ref), channel_id=1, source_target_pairs={{0,16},{16,0},{1,17},{17,1},{2,18},{18,2},{3,19},{19,3},{4,20},{20... | collective-permute-start | bytes 110600 | tf_op jit(solution)/shard_map/ppermute | solution.py:444
  87.5 6.5 %collective-permute-start.13 = (f32[4,64]{1,0:T(4,128)S(1)}, f32[4,64]{1,0:T(4,128)S(1)}, u32[]{:S(2)}, u32[]{:S(2)}) collective-permute-start(f32[4,64]{1,0:T(4,128)S(1)} %get-tuple-element.89), channel_id=1, source_target_pairs={{0,1},{1,0},{2,3},{3,2},{4,5},{5,4},{6,7},{7,6},{8,9},{9,8},{10,11... | collective-permute-start | bytes 3080 | tf_op jit(solution)/shard_map/ppermute | solution.py:444
  89.0 6.4 %collective-permute-start.14 = (f32[4,64]{1,0:T(4,128)S(1)}, f32[4,64]{1,0:T(4,128)S(1)}, u32[]{:S(2)}, u32[]{:S(2)}) collective-permute-start(f32[4,64]{1,0:T(4,128)S(1)} %get-tuple-element.90), channel_id=1, source_target_pairs={{1,2},{3,4},{5,6},{7,8},{9,10},{11,12},{13,14},{2,1},{4,3},{6,5},{... | collective-permute-start | bytes 3080 | tf_op jit(solution)/shard_map/ppermute | solution.py:450

commit v14 on v13

--- a/solution.py
+++ b/solution.py
@@ -69,12 +69,21 @@
         k_h = jnp.concatenate([keys[:, part], lanes], axis=1)
         v_h = jnp.concatenate([vals[:, part], lanes], axis=1)
         send_ref[h, 2 * FPAD : 2 * FPAD + 16, :] = jnp.concatenate([k_h, v_h]).astype(bf16)
+    outs = []
+
+    def put(heads, rows):
+        place = (heads, rows)
+        copy = pltpu.make_async_copy(send_ref.at[place], out_ref.at[place], out_sems.at[len(outs)])
+        copy.start()
+        outs.append(copy)
+
+    put(slice(0, HEADS), slice(0, FPAD))
+    put(slice(0, HEADS), slice(2 * FPAD, 2 * FPAD + 16))
     for copy in copies[6:]:
         copy.wait()
     g_t = g_ref[...].astype(f32).T
     prod = g_t * o_ref[...].astype(f32).T
     row = lax.broadcasted_iota(jnp.int32, (8, TOK), 0)
-    outs = []
     for h in range(HEADS):
         part = slice(h * DH, (h + 1) * DH)
         dot = -jnp.sum(prod[part], axis=0, keepdims=True)
@@ -84,10 +93,7 @@
         dots = jnp.where(row == 0, high, jnp.where(row == 1, mid, jnp.where(row == 2, low, 0.0)))
         send_ref[h, FPAD : 2 * FPAD, :] = jnp.concatenate([g_t[part], dots]).astype(bf16)
         if h % 4 == 3:
-            heads = slice(h - 3, h + 1)
-            copy = pltpu.make_async_copy(send_ref.at[heads], out_ref.at[heads], out_sems.at[h // 4])
-            copy.start()
-            outs.append(copy)
+            put(slice(h - 3, h + 1), slice(FPAD, 2 * FPAD))
     for copy in outs:
         copy.wait()
 
@@ -464,7 +470,7 @@
         pack_kernel,
         jax.ShapeDtypeStruct(packed, bf16),
         None,
-        [tokens, tokens, tokens, cells, cells, pltpu.VMEM(packed, bf16), dma((14,)), dma((4,))],
+        [tokens, tokens, tokens, cells, cells, pltpu.VMEM(packed, bf16), dma((14,)), dma((6,))],
         [ANYWHERE] * 5,
         out_specs=ANYWHERE,
     )(

time: 96.4 us -> 96.3 us (level)
  no operation moved by 1% of the time
where the time goes in v14:
time: 96.3 us; the launch traced here: 96 us
  blocking collectives  34 us (35%)
  Pallas kernels  31 us (32%)
  starting transfers between devices  25.9 us (27%)
  waiting for transfers between devices  4.77 us (5%)
    ppermute x14, starting transfers between devices, swapped(): return lax.ppermute(x, axis, [(i, i ^ by) for i in range(peers)])  22.4 us
    all_to_all x1, blocking collectives, on_device(): got = lax.all_to_all(send, HEAD_AXES, 0, 0, tiled=True)  19.4 us
    all_to_all x1, blocking collectives, on_device(): back = lax.all_to_all(send, HEAD_AXES, 0, 0, tiled=True)  14.6 us
    pallas_call x1, Pallas kernels, on_device(): call(second_sums_kernel, sums, 24, [keys], cost_estimate=cost(1))  5.66 us
    pallas_call x1, Pallas kernels, on_device(): call(first_sums_kernel, sums, 24, [keys], cost_estimate=cost(1))  5.58 us
    pallas_call x1, Pallas kernels, on_device(): call(second_kernel, shapes + [jax.ShapeDtypeStruct(block, f32)], 32, scra...  5.37 us
    pallas_call x1, Pallas kernels, on_device(): call(first_kernel, [sums] + dq + [jax.ShapeDtypeStruct(block, bf16)], 32,...  5.26 us
    ppermute x1, starting transfers between devices, neighbours(): lax.ppermute(x, axis, pairs + [(target, source) for source, target in pai...  3.52 us
  transfers between devices with their start and end apart: 15, of which 5 were waited for; matrix products, arithmetic and copies ran while one was open for 0% of the time, Pallas kernels for 16%

profile of v14, /device:TPU:8, one launch (start us, length us, event | category | flops | bytes accessed | tf_op | source)
XLA Modules:
  0.0 96.0 jit_solution(14188325779167640987)
XLA Ops:
  0.0 2.4 %shard_map.73 = bf16[16,176,128]{2,1,0:T(8,128)(2,1)} custom-call(bf16[128,1152]{1,0:T(8,128)(2,1)} %bitcast.19, bf16[128,1152]{1,0:T(8,128)(2,1)} %bitcast.20, bf16[128,1152]{1,0:T(8,128)(2,1)} %bitcast.21, bf16[2,4,1152]{2,1,0:T(4,128)(2,1)} %k_in.1, bf16[2,4,1152]{2,1,0:T(4,128)(2,1)} %v_in.1), custom_call_target="tpu_custom_call" | custom-call | tf_op jit(solution)/shard_map/pallas_call | solution.py:469
  2.4 19.4 %all_to_all.10.got_ref.qg_a = bf16[16,176,128]{2,1,0:T(8,128)(2,1)S(1)} all-to-all(bf16[16,176,128]{2,1,0:T(8,128)(2,1)} %shard_map.73), channel_id=1, replica_groups=mesh['yh'=2,'x'=4,'c'=2,'z'=8,'yl'=2] {'yh','x','yl'}, dimensions={0} | all-to-all | bytes 1441792 | tf_op jit(solution)/shard_map/all_to_all | solution.py:483
  21.8 0.0 collective-permute-start
  21.8 0.1 shard_map.74.kv_0
  21.9 2.0 %collective-permute-start.4 = (bf16[144,128]{1,0:T(8,128)(2,1)S(1)}, bf16[144,128]{1,0:T(8,128)(2,1)S(1)}, u32[]{:S(2)}, u32[]{:S(2)}) collective-permute-start(bf16[144,128]{1,0:T(8,128)(2,1)S(1)} %shard_map.74.kv_0), channel_id=1, source_target_pairs={{0,2},{2,0},{4,6},{6,4},{8,10},{10,8},{12,14},{14,12},{1,3},{3,1},... | collective-permute-start | bytes 110600 | tf_op jit(solution)/shard_map/ppermute | solution.py:450
  23.9 5.4 %collective-permute-start.2 = (bf16[144,128]{1,0:T(8,128)(2,1)S(1)}, bf16[144,128]{1,0:T(8,128)(2,1)S(1)}, u32[]{:S(2)}, u32[]{:S(2)}) collective-permute-start(bf16[144,128]{1,0:T(8,128)(2,1)S(1)} %shard_map.74.kv_0), channel_id=1, source_target_pairs={{0,12},{2,14},{4,8},{6,10},{8,4},{10,6},{12,0},{14,2},{1,13},{3,15... | collective-permute-start | bytes 110600 | tf_op jit(solution)/shard_map/ppermute | solution.py:450
  29.3 1.5 %collective-permute-start.1 = (bf16[144,128]{1,0:T(8,128)(2,1)S(1)}, bf16[144,128]{1,0:T(8,128)(2,1)S(1)}, u32[]{:S(2)}, u32[]{:S(2)}) collective-permute-start(bf16[144,128]{1,0:T(8,128)(2,1)S(1)} %shard_map.74.kv_0), channel_id=1, source_target_pairs={{0,4},{2,6},{4,0},{6,2},{8,12},{10,14},{12,8},{14,10},{1,5},{3,7},... | collective-permute-start | bytes 110600 | tf_op jit(solution)/shard_map/ppermute | solution.py:450
  30.7 0.0 collective-permute-done.4.kv_1
  30.8 2.8 %collective-permute-start.5 = (bf16[2,144,128]{2,1,0:T(8,128)(2,1)S(1)}, bf16[2,144,128]{2,1,0:T(8,128)(2,1)S(1)}, u32[]{:S(2)}, u32[]{:S(2)}) collective-permute-start(bf16[2,144,128]{2,1,0:T(8,128)(2,1)S(1)} %pad_maximum_fusion.1), channel_id=1, source_target_pairs={{0,8},{2,10},{4,12},{6,14},{8,0},{10,2},{12,4},{14,6},{1,9},{3,11}... | collective-permute-start | bytes 221192 | tf_op jit(solution)/shard_map/ppermute | solution.py:450
  33.5 0.0 collective-permute-done.2.kv_6
  33.5 0.6 collective-permute-done.1.kv_2
  34.2 1.1 %collective-permute-start.3 = (bf16[2,144,128]{2,1,0:T(8,128)(2,1)S(1)}, bf16[2,144,128]{2,1,0:T(8,128)(2,1)S(1)}, u32[]{:S(2)}, u32[]{:S(2)}) collective-permute-start(bf16[2,144,128]{2,1,0:T(8,128)(2,1)S(1)} %pad_maximum_fusion), channel_id=1, source_target_pairs={{0,2},{2,0},{4,6},{6,4},{8,10},{10,8},{12,14},{14,12},{1,3},{3,1},... | collective-permute-start | bytes 221192 | tf_op jit(solution)/shard_map/ppermute | solution.py:450
  35.2 0.0 collective-permute-done.qg_b
  35.2 5.6 %shard_map.75.first_ref = f32[2,16,128]{2,1,0:T(8,128)S(1)} custom-call(bf16[16,176,128]{2,1,0:T(8,128)(2,1)S(1)} %all_to_all.10.got_ref.qg_a, bf16[16,176,128]{2,1,0:T(8,128)(2,1)S(1)} %collective-permute-done.qg_b, bf16[144,128]{1,0:T(8,128)(2,1)S(1)} %shard_map.74.kv_0, bf16[144,128]{1,0:T(8,128)(2,1)S(1)} %collective-permute-done.4.kv_1, ...), custom_call_target="tpu_custom_call" | custom-call | flops 1073741824 | bytes 1048576 | tf_op jit(solution)/shard_map/pallas_call | solution.py:497
  40.8 0.0 collective-permute-done.5.kv_45
  40.9 0.0 collective-permute-done.3.kv_37
  40.9 5.7 %shard_map.76.mine_ref = f32[2,16,128]{2,1,0:T(8,128)S(1)} custom-call(bf16[16,176,128]{2,1,0:T(8,128)(2,1)S(1)} %all_to_all.10.got_ref.qg_a, bf16[16,176,128]{2,1,0:T(8,128)(2,1)S(1)} %collective-permute-done.qg_b, bf16[2,144,128]{2,1,0:T(8,128)(2,1)S(1)} %collective-permute-done.3.kv_37, bf16[2,144,128]{2,1,0:T(8,128)(2,1)S(1)} %collective-permute-done.5.kv_45, ...), custom_call_target="tpu_custom_call" | custom-call | flops 1073741824 | bytes 1048576 | tf_op jit(solution)/shard_map/pallas_call | solution.py:499
  46.5 0.3 collective-permute-start.6
  46.8 0.2 shard_map.77
  47.0 0.9 collective-permute-done.6.came_ref
  48.0 0.0 slice-start
  48.0 5.3 %shard_map.78 = (f32[2,16,128]{2,1,0:T(8,128)S(1)}, f32[16,80,128]{2,1,0:T(8,128)S(1)}, f32[16,80,128]{2,1,0:T(8,128)S(1)}, bf16[4,144,128]{2,1,0:T(8,128)(2,1)S(1)}) custom-call(bf16[16,176,128]{2,1,0:T(8,128)(2,1)S(1)} %all_to_all.10.got_ref.qg_a, bf16[16,176,128]{2,1,0:T(8,128)(2,1)S(1)} %collective-permute-done.qg_b, ...), custom_call_target="tpu_custom_call" | custom-call | flops 5368709120 | bytes 1048576 | tf_op jit(solution)/shard_map/pallas_call | solution.py:508
  53.2 1.1 %collective-permute-start.7 = (bf16[4,144,128]{2,1,0:T(8,128)(2,1)S(1)}, bf16[4,144,128]{2,1,0:T(8,128)(2,1)S(1)}, u32[]{:S(2)}, u32[]{:S(2)}) collective-permute-start(bf16[4,144,128]{2,1,0:T(8,128)(2,1)S(1)} %get-tuple-element.76), channel_id=1, source_target_pairs={{0,2},{2,0},{4,6},{6,4},{8,10},{10,8},{12,14},{14,12},{1,3},{3,1},... | collective-permute-start | bytes 442376 | tf_op jit(solution)/shard_map/ppermute | solution.py:450
  54.3 5.4 %shard_map.79 = (f32[16,72,128]{2,1,0:T(8,128)S(1)}, f32[16,24,128]{2,1,0:T(8,128)S(1)}, f32[16,96,128]{2,1,0:T(8,128)S(1)}, f32[4,144,128]{2,1,0:T(8,128)S(1)}) custom-call(bf16[16,176,128]{2,1,0:T(8,128)(2,1)S(1)} %all_to_all.10.got_ref.qg_a, bf16[16,176,128]{2,1,0:T(8,128)(2,1)S(1)} %collective-permute-done.qg_b, ...), custom_call_target="tpu_custom_call" | custom-call | flops 5368709120 | bytes 1048576 | tf_op jit(solution)/shard_map/pallas_call | solution.py:513
  59.7 0.0 collective-permute-done.7
  59.7 0.1 collective-permute-start.8
  59.9 2.8 %collective-permute-start.11 = (bf16[144,128]{1,0:T(8,128)(2,1)S(1)}, bf16[144,128]{1,0:T(8,128)(2,1)S(1)}, u32[]{:S(2)}, u32[]{:S(2)}) collective-permute-start(bf16[144,128]{1,0:T(8,128)(2,1)S(1)} %get-tuple-element.97), channel_id=1, source_target_pairs={{0,8},{2,10},{4,12},{6,14},{8,0},{10,2},{12,4},{14,6},{1,9},{3,11}... | collective-permute-start | bytes 110600 | tf_op jit(solution)/shard_map/ppermute | solution.py:450
  62.7 2.4 %collective-permute-start.10 = (bf16[144,128]{1,0:T(8,128)(2,1)S(1)}, bf16[144,128]{1,0:T(8,128)(2,1)S(1)}, u32[]{:S(2)}, u32[]{:S(2)}) collective-permute-start(bf16[144,128]{1,0:T(8,128)(2,1)S(1)} %get-tuple-element.98), channel_id=1, source_target_pairs={{0,12},{2,14},{4,8},{6,10},{8,4},{10,6},{12,0},{14,2},{1,13},{3,15... | collective-permute-start | bytes 110600 | tf_op jit(solution)/shard_map/ppermute | solution.py:450
  65.1 1.4 %collective-permute-start.9 = (bf16[144,128]{1,0:T(8,128)(2,1)S(1)}, bf16[144,128]{1,0:T(8,128)(2,1)S(1)}, u32[]{:S(2)}, u32[]{:S(2)}) collective-permute-start(bf16[144,128]{1,0:T(8,128)(2,1)S(1)} %get-tuple-element.99), channel_id=1, source_target_pairs={{0,4},{2,6},{4,0},{6,2},{8,12},{10,14},{12,8},{14,10},{1,5},{3,7},... | collective-permute-start | bytes 110600 | tf_op jit(solution)/shard_map/ppermute | solution.py:450
  66.5 0.0 slice-done
  66.5 0.0 slice-done.1
  66.5 0.0 copy-done
  66.5 2.7 %shard_map.80.weights = bf16[512,3456]{1,0:T(8,128)(2,1)S(1)} custom-call(bf16[256,1152]{1,0:T(8,128)(2,1)S(1)} %copy-done, bf16[1152,3456]{1,0:T(8,128)(2,1)S(1)} %bitcast.14), custom_call_target="tpu_custom_call" | custom-call | flops 1048576 | bytes 65536 | tf_op jit(solution)/shard_map/pallas_call | solution.py:526
  69.2 0.0 collective-permute-done.11.came_c
  69.2 0.0 collective-permute-done.10.came_b
  69.2 0.7 collective-permute-done.9.came_a
  69.9 0.1 collective-permute-start.12
  70.0 1.2 %collective-permute-done.12.other_ref = bf16[144,128]{1,0:T(8,128)(2,1)S(1)} collective-permute-done((bf16[144,128]{1,0:T(8,128)(2,1)S(1)}, bf16[144,128]{1,0:T(8,128)(2,1)S(1)}, u32[]{:S(2)}, u32[]{:S(2)}) %collective-permute-start.12) | collective-permute-done | bytes 36896 | tf_op jit(solution)/shard_map/ppermute | solution.py:450
  71.2 0.0 collective-permute-done.8.came_ref
  71.3 0.3 shard_map.82
  71.5 14.6 %all_to_all.11.back_ref = bf16[16,112,128]{2,1,0:T(8,128)(2,1)S(1)} all-to-all(bf16[16,112,128]{2,1,0:T(8,128)(2,1)S(1)} %shard_map.82), channel_id=1, replica_groups=mesh['yh'=2,'x'=4,'c'=2,'z'=8,'yl'=2] {'yh','x','yl'}, dimensions={0} | all-to-all | bytes 917504 | tf_op jit(solution)/shard_map/all_to_all | solution.py:535
  86.1 1.3 %shard_map.83 = (bf16[160,256]{1,0:T(8,128)(2,1)S(1)}, bf16[1152,256]{1,0:T(8,128)(2,1)S(1)}, bf16[2304,128]{1,0:T(8,128)(2,1)S(1)}, f32[4,64]{1,0:T(4,128)S(1)}, f32[4,64]{1,0:T(4,128)S(1)}) custom-call(bf16[16,112,128]{2,1,0:T(8,128)(2,1)S(1)} %all_to_all.11.back_ref, bf16[512,3456]{1,0:T(8,128)(2,1)S(1)} %shard_map.80.weights), custom_call_target="tpu_custom_call" | custom-call | tf_op jit(solution)/shard_map/pallas_call | solution.py:538
  87.4 1.5 %collective-permute-start.13 = (f32[4,64]{1,0:T(4,128)S(1)}, f32[4,64]{1,0:T(4,128)S(1)}, u32[]{:S(2)}, u32[]{:S(2)}) collective-permute-start(f32[4,64]{1,0:T(4,128)S(1)} %get-tuple-element.89), channel_id=1, source_target_pairs={{0,1},{1,0},{2,3},{3,2},{4,5},{5,4},{6,7},{7,6},{8,9},{9,8},{10,11... | collective-permute-start | bytes 3080 | tf_op jit(solution)/shard_map/ppermute | solution.py:450
  88.9 3.5 %collective-permute-start.14 = (f32[4,64]{1,0:T(4,128)S(1)}, f32[4,64]{1,0:T(4,128)S(1)}, u32[]{:S(2)}, u32[]{:S(2)}) collective-permute-start(f32[4,64]{1,0:T(4,128)S(1)} %get-tuple-element.90), channel_id=1, source_target_pairs={{1,2},{3,4},{5,6},{7,8},{9,10},{11,12},{13,14},{2,1},{4,3},{6,5},{... | collective-permute-start | bytes 3080 | tf_op jit(solution)/shard_map/ppermute | solution.py:456
  92.4 1.5 %shard_map.84.center_ref = f32[64,128]{1,0:T(8,128)S(1)} custom-call(bf16[160,256]{1,0:T(8,128)(2,1)S(1)} %get-tuple-element.91.outer_ref, bf16[512,3456]{1,0:T(8,128)(2,1)S(1)} %shard_map.80.weights, bf16[1152,256]{1,0:T(8,128)(2,1)S(1)} %get-tuple-element.92.joined, bf16[2304,128]{1,0:T(8,128)(2,1)S(1)} %get-tuple-element.93.pooled), custom_call_target="tpu_custom_call" | custom-call | flops 1048576 | bytes 65536 | tf_op jit(solution)/shard_map/pallas_call | solution.py:545
  94.0 0.0 collective-permute-done.13.near_ref
  94.0 1.3 %collective-permute-done.14.far_ref = f32[4,64]{1,0:T(4,128)S(1)} collective-permute-done((f32[4,64]{1,0:T(4,128)S(1)}, f32[4,64]{1,0:T(4,128)S(1)}, u32[]{:S(2)}, u32[]{:S(2)}) %collective-permute-start.14) | collective-permute-done | bytes 1056 | tf_op jit(solution)/shard_map/ppermute | solution.py:456
  95.3 0.7 shard_map.85
  (10 shorter events, 0.1 us)
Async XLA Ops:
  21.8 13.5 %collective-permute-start = (bf16[16,176,128]{2,1,0:T(8,128)(2,1)S(1)}, bf16[16,176,128]{2,1,0:T(8,128)(2,1)S(1)}, u32[]{:S(2)}, u32[]{:S(2)}) collective-permute-start(bf16[16,176,128]{2,1,0:T(8,128)(2,1)S(1)} %all_to_all.10.got_ref.qg_a), channel_id=1, source_target_pairs={{0,16},{16,0},{1,17},{17,1},{2,18},{18,2},{3,19},{19,3},{4,20},{20... | collective-permute-start | bytes 2162696 | tf_op jit(solution)/shard_map/ppermute | solution.py:450
  21.9 8.9 %collective-permute-start.4 = (bf16[144,128]{1,0:T(8,128)(2,1)S(1)}, bf16[144,128]{1,0:T(8,128)(2,1)S(1)}, u32[]{:S(2)}, u32[]{:S(2)}) collective-permute-start(bf16[144,128]{1,0:T(8,128)(2,1)S(1)} %shard_map.74.kv_0), channel_id=1, source_target_pairs={{0,2},{2,0},{4,6},{6,4},{8,10},{10,8},{12,14},{14,12},{1,3},{3,1},... | collective-permute-start | bytes 110600 | tf_op jit(solution)/shard_map/ppermute | solution.py:450
  23.9 9.6 %collective-permute-start.2 = (bf16[144,128]{1,0:T(8,128)(2,1)S(1)}, bf16[144,128]{1,0:T(8,128)(2,1)S(1)}, u32[]{:S(2)}, u32[]{:S(2)}) collective-permute-start(bf16[144,128]{1,0:T(8,128)(2,1)S(1)} %shard_map.74.kv_0), channel_id=1, source_target_pairs={{0,12},{2,14},{4,8},{6,10},{8,4},{10,6},{12,0},{14,2},{1,13},{3,15... | collective-permute-start | bytes 110600 | tf_op jit(solution)/shard_map/ppermute | solution.py:450
  29.3 4.9 %collective-permute-start.1 = (bf16[144,128]{1,0:T(8,128)(2,1)S(1)}, bf16[144,128]{1,0:T(8,128)(2,1)S(1)}, u32[]{:S(2)}, u32[]{:S(2)}) collective-permute-start(bf16[144,128]{1,0:T(8,128)(2,1)S(1)} %shard_map.74.kv_0), channel_id=1, source_target_pairs={{0,4},{2,6},{4,0},{6,2},{8,12},{10,14},{12,8},{14,10},{1,5},{3,7},... | collective-permute-start | bytes 110600 | tf_op jit(solution)/shard_map/ppermute | solution.py:450
  30.8 10.1 %collective-permute-start.5 = (bf16[2,144,128]{2,1,0:T(8,128)(2,1)S(1)}, bf16[2,144,128]{2,1,0:T(8,128)(2,1)S(1)}, u32[]{:S(2)}, u32[]{:S(2)}) collective-permute-start(bf16[2,144,128]{2,1,0:T(8,128)(2,1)S(1)} %pad_maximum_fusion.1), channel_id=1, source_target_pairs={{0,8},{2,10},{4,12},{6,14},{8,0},{10,2},{12,4},{14,6},{1,9},{3,11}... | collective-permute-start | bytes 221192 | tf_op jit(solution)/shard_map/ppermute | solution.py:450
  34.2 6.7 %collective-permute-start.3 = (bf16[2,144,128]{2,1,0:T(8,128)(2,1)S(1)}, bf16[2,144,128]{2,1,0:T(8,128)(2,1)S(1)}, u32[]{:S(2)}, u32[]{:S(2)}) collective-permute-start(bf16[2,144,128]{2,1,0:T(8,128)(2,1)S(1)} %pad_maximum_fusion), channel_id=1, source_target_pairs={{0,2},{2,0},{4,6},{6,4},{8,10},{10,8},{12,14},{14,12},{1,3},{3,1},... | collective-permute-start | bytes 221192 | tf_op jit(solution)/shard_map/ppermute | solution.py:450
  46.5 1.5 %collective-permute-start.6 = (f32[2,16,128]{2,1,0:T(8,128)S(1)}, f32[2,16,128]{2,1,0:T(8,128)S(1)}, u32[]{:S(2)}, u32[]{:S(2)}) collective-permute-start(f32[2,16,128]{2,1,0:T(8,128)S(1)} %shard_map.76.mine_ref), channel_id=1, source_target_pairs={{0,16},{16,0},{1,17},{17,1},{2,18},{18,2},{3,19},{19,3},{4,20},{20... | collective-permute-start | bytes 49160 | tf_op jit(solution)/shard_map/ppermute | solution.py:450
  48.0 18.5 %slice-start = ((s8[7962624]{0:T(1024)(128)(4,1)}), s8[4194304]{0:T(1024)(128)(4,1)S(1)}, s32[]{:S(2)}) async-start(s8[7962624]{0:T(1024)(128)(4,1)} %bitcast.13), calls=%async_computation.2 | async-start | bytes 8388608
  53.2 6.5 %collective-permute-start.7 = (bf16[4,144,128]{2,1,0:T(8,128)(2,1)S(1)}, bf16[4,144,128]{2,1,0:T(8,128)(2,1)S(1)}, u32[]{:S(2)}, u32[]{:S(2)}) collective-permute-start(bf16[4,144,128]{2,1,0:T(8,128)(2,1)S(1)} %get-tuple-element.76), channel_id=1, source_target_pairs={{0,2},{2,0},{4,6},{6,4},{8,10},{10,8},{12,14},{14,12},{1,3},{3,1},... | collective-permute-start | bytes 442376 | tf_op jit(solution)/shard_map/ppermute | solution.py:450
  54.3 12.2 %slice-start.1 = ((s8[7962624]{0:T(1024)(128)(4,1)}), s8[3768320]{0:T(1024)(128)(4,1)S(1)}, s32[]{:S(2)}) async-start(s8[7962624]{0:T(1024)(128)(4,1)} %bitcast.13), calls=%async_computation.3 | async-start | bytes 7536640
  54.3 12.2 %copy-start = (bf16[256,1152]{1,0:T(8,128)(2,1)S(1)}, bf16[256,1152]{1,0:T(8,128)(2,1)}, u32[]{:S(2)}) copy-start(bf16[256,1152]{1,0:T(8,128)(2,1)} %patch_ref) | copy-start | bytes 1769476
  59.7 11.5 %collective-permute-start.8 = (f32[16,96,128]{2,1,0:T(8,128)S(1)}, f32[16,96,128]{2,1,0:T(8,128)S(1)}, u32[]{:S(2)}, u32[]{:S(2)}) collective-permute-start(f32[16,96,128]{2,1,0:T(8,128)S(1)} %get-tuple-element.79), channel_id=1, source_target_pairs={{0,16},{16,0},{1,17},{17,1},{2,18},{18,2},{3,19},{19,3},{4,20},{20... | collective-permute-start | bytes 2359304 | tf_op jit(solution)/shard_map/ppermute | solution.py:450
  59.9 9.3 %collective-permute-start.11 = (bf16[144,128]{1,0:T(8,128)(2,1)S(1)}, bf16[144,128]{1,0:T(8,128)(2,1)S(1)}, u32[]{:S(2)}, u32[]{:S(2)}) collective-permute-start(bf16[144,128]{1,0:T(8,128)(2,1)S(1)} %get-tuple-element.97), channel_id=1, source_target_pairs={{0,8},{2,10},{4,12},{6,14},{8,0},{10,2},{12,4},{14,6},{1,9},{3,11}... | collective-permute-start | bytes 110600 | tf_op jit(solution)/shard_map/ppermute | solution.py:450
  62.7 6.6 %collective-permute-start.10 = (bf16[144,128]{1,0:T(8,128)(2,1)S(1)}, bf16[144,128]{1,0:T(8,128)(2,1)S(1)}, u32[]{:S(2)}, u32[]{:S(2)}) collective-permute-start(bf16[144,128]{1,0:T(8,128)(2,1)S(1)} %get-tuple-element.98), channel_id=1, source_target_pairs={{0,12},{2,14},{4,8},{6,10},{8,4},{10,6},{12,0},{14,2},{1,13},{3,15... | collective-permute-start | bytes 110600 | tf_op jit(solution)/shard_map/ppermute | solution.py:450
  65.1 4.9 %collective-permute-start.9 = (bf16[144,128]{1,0:T(8,128)(2,1)S(1)}, bf16[144,128]{1,0:T(8,128)(2,1)S(1)}, u32[]{:S(2)}, u32[]{:S(2)}) collective-permute-start(bf16[144,128]{1,0:T(8,128)(2,1)S(1)} %get-tuple-element.99), channel_id=1, source_target_pairs={{0,4},{2,6},{4,0},{6,2},{8,12},{10,14},{12,8},{14,10},{1,5},{3,7},... | collective-permute-start | bytes 110600 | tf_op jit(solution)/shard_map/ppermute | solution.py:450
  69.9 1.3 %collective-permute-start.12 = (bf16[144,128]{1,0:T(8,128)(2,1)S(1)}, bf16[144,128]{1,0:T(8,128)(2,1)S(1)}, u32[]{:S(2)}, u32[]{:S(2)}) collective-permute-start(bf16[144,128]{1,0:T(8,128)(2,1)S(1)} %shard_map.81.keys_ref), channel_id=1, source_target_pairs={{0,16},{16,0},{1,17},{17,1},{2,18},{18,2},{3,19},{19,3},{4,20},{20... | collective-permute-start | bytes 110600 | tf_op jit(solution)/shard_map/ppermute | solution.py:450
  87.4 6.5 %collective-permute-start.13 = (f32[4,64]{1,0:T(4,128)S(1)}, f32[4,64]{1,0:T(4,128)S(1)}, u32[]{:S(2)}, u32[]{:S(2)}) collective-permute-start(f32[4,64]{1,0:T(4,128)S(1)} %get-tuple-element.89), channel_id=1, source_target_pairs={{0,1},{1,0},{2,3},{3,2},{4,5},{5,4},{6,7},{7,6},{8,9},{9,8},{10,11... | collective-permute-start | bytes 3080 | tf_op jit(solution)/shard_map/ppermute | solution.py:450
  88.9 6.4 %collective-permute-start.14 = (f32[4,64]{1,0:T(4,128)S(1)}, f32[4,64]{1,0:T(4,128)S(1)}, u32[]{:S(2)}, u32[]{:S(2)}) collective-permute-start(f32[4,64]{1,0:T(4,128)S(1)} %get-tuple-element.90), channel_id=1, source_target_pairs={{1,2},{3,4},{5,6},{7,8},{9,10},{11,12},{13,14},{2,1},{4,3},{6,5},{... | collective-permute-start | bytes 3080 | tf_op jit(solution)/shard_map/ppermute | solution.py:456

commit v15 on v14

--- a/solution.py
+++ b/solution.py
@@ -49,11 +49,12 @@
 def pack_kernel(
     q_in, g_in, o_in, k_in, v_in, out_ref, q_ref, g_ref, o_ref, k_ref, v_ref, send_ref, sems, out_sems
 ):
-    pairs = [(k_in, k_ref), (v_in, v_ref)]
+    pairs = []
     quarter = TOK // 4
     for source, target in ((q_in, q_ref), (g_in, g_ref), (o_in, o_ref)):
         for at in range(0, TOK, quarter):
             pairs.append((source.at[at : at + quarter], target.at[at : at + quarter]))
+    pairs[4:4] = [(k_in, k_ref), (v_in, v_ref)]
     copies = [pltpu.make_async_copy(*pair, sems.at[n]) for n, pair in enumerate(pairs)]
     for copy in copies:
         copy.start()
@@ -150,8 +151,8 @@
 
     total = jnp.zeros((1, TILE), f32)
     count = k_s.shape[0]
-    for at in range(0, count, STEP):
-        exps = jnp.exp2(scores(slice(at, at + STEP)) - bound)
+    for at in range(0, count, HALF):
+        exps = jnp.exp2(scores(slice(at, at + HALF)) - bound)
         total = total + jnp.sum(exps, axis=0, keepdims=True)
 
     def again():

time: 96.3 us -> 96.2 us (level)
  no operation moved by 1% of the time
where the time goes in v15:
time: 96.2 us; the launch traced here: 96 us
  blocking collectives  34 us (35%)
  Pallas kernels  31 us (32%)
  starting transfers between devices  25.9 us (27%)
  waiting for transfers between devices  4.75 us (5%)
    ppermute x14, starting transfers between devices, swapped(): return lax.ppermute(x, axis, [(i, i ^ by) for i in range(peers)])  22.4 us
    all_to_all x1, blocking collectives, on_device(): got = lax.all_to_all(send, HEAD_AXES, 0, 0, tiled=True)  19.4 us
    all_to_all x1, blocking collectives, on_device(): back = lax.all_to_all(send, HEAD_AXES, 0, 0, tiled=True)  14.6 us
    pallas_call x1, Pallas kernels, on_device(): call(second_sums_kernel, sums, 24, [keys], cost_estimate=cost(1))  5.65 us
    pallas_call x1, Pallas kernels, on_device(): call(first_sums_kernel, sums, 24, [keys], cost_estimate=cost(1))  5.59 us
    pallas_call x1, Pallas kernels, on_device(): call(second_kernel, shapes + [jax.ShapeDtypeStruct(block, f32)], 32, scra...  5.37 us
    pallas_call x1, Pallas kernels, on_device(): call(first_kernel, [sums] + dq + [jax.ShapeDtypeStruct(block, bf16)], 32,...  5.26 us
    ppermute x1, starting transfers between devices, neighbours(): lax.ppermute(x, axis, pairs + [(target, source) for source, target in pai...  3.5 us
  transfers between devices with their start and end apart: 15, of which 5 were waited for; matrix products, arithmetic and copies ran while one was open for 0% of the time, Pallas kernels for 16%

profile of v15, /device:TPU:8, one launch (start us, length us, event | category | flops | bytes accessed | tf_op | source)
XLA Modules:
  0.0 96.0 jit_solution(1382373219649595076)
XLA Ops:
  0.0 2.4 %shard_map.73 = bf16[16,176,128]{2,1,0:T(8,128)(2,1)} custom-call(bf16[128,1152]{1,0:T(8,128)(2,1)} %bitcast.19, bf16[128,1152]{1,0:T(8,128)(2,1)} %bitcast.20, bf16[128,1152]{1,0:T(8,128)(2,1)} %bitcast.21, bf16[2,4,1152]{2,1,0:T(4,128)(2,1)} %k_in.1, bf16[2,4,1152]{2,1,0:T(4,128)(2,1)} %v_in.1), custom_call_target="tpu_custom_call" | custom-call | tf_op jit(solution)/shard_map/pallas_call | solution.py:470
  2.4 19.4 %all_to_all.10.got_ref.qg_a = bf16[16,176,128]{2,1,0:T(8,128)(2,1)S(1)} all-to-all(bf16[16,176,128]{2,1,0:T(8,128)(2,1)} %shard_map.73), channel_id=1, replica_groups=mesh['yh'=2,'x'=4,'c'=2,'z'=8,'yl'=2] {'yh','x','yl'}, dimensions={0} | all-to-all | bytes 1441792 | tf_op jit(solution)/shard_map/all_to_all | solution.py:484
  21.8 0.0 collective-permute-start
  21.8 0.1 shard_map.74.kv_0
  21.9 2.0 %collective-permute-start.4 = (bf16[144,128]{1,0:T(8,128)(2,1)S(1)}, bf16[144,128]{1,0:T(8,128)(2,1)S(1)}, u32[]{:S(2)}, u32[]{:S(2)}) collective-permute-start(bf16[144,128]{1,0:T(8,128)(2,1)S(1)} %shard_map.74.kv_0), channel_id=1, source_target_pairs={{0,2},{2,0},{4,6},{6,4},{8,10},{10,8},{12,14},{14,12},{1,3},{3,1},... | collective-permute-start | bytes 110600 | tf_op jit(solution)/shard_map/ppermute | solution.py:451
  23.9 5.4 %collective-permute-start.2 = (bf16[144,128]{1,0:T(8,128)(2,1)S(1)}, bf16[144,128]{1,0:T(8,128)(2,1)S(1)}, u32[]{:S(2)}, u32[]{:S(2)}) collective-permute-start(bf16[144,128]{1,0:T(8,128)(2,1)S(1)} %shard_map.74.kv_0), channel_id=1, source_target_pairs={{0,12},{2,14},{4,8},{6,10},{8,4},{10,6},{12,0},{14,2},{1,13},{3,15... | collective-permute-start | bytes 110600 | tf_op jit(solution)/shard_map/ppermute | solution.py:451
  29.3 1.5 %collective-permute-start.1 = (bf16[144,128]{1,0:T(8,128)(2,1)S(1)}, bf16[144,128]{1,0:T(8,128)(2,1)S(1)}, u32[]{:S(2)}, u32[]{:S(2)}) collective-permute-start(bf16[144,128]{1,0:T(8,128)(2,1)S(1)} %shard_map.74.kv_0), channel_id=1, source_target_pairs={{0,4},{2,6},{4,0},{6,2},{8,12},{10,14},{12,8},{14,10},{1,5},{3,7},... | collective-permute-start | bytes 110600 | tf_op jit(solution)/shard_map/ppermute | solution.py:451
  30.7 0.0 collective-permute-done.4.kv_1
  30.8 2.8 %collective-permute-start.5 = (bf16[2,144,128]{2,1,0:T(8,128)(2,1)S(1)}, bf16[2,144,128]{2,1,0:T(8,128)(2,1)S(1)}, u32[]{:S(2)}, u32[]{:S(2)}) collective-permute-start(bf16[2,144,128]{2,1,0:T(8,128)(2,1)S(1)} %pad_maximum_fusion.1), channel_id=1, source_target_pairs={{0,8},{2,10},{4,12},{6,14},{8,0},{10,2},{12,4},{14,6},{1,9},{3,11}... | collective-permute-start | bytes 221192 | tf_op jit(solution)/shard_map/ppermute | solution.py:451
  33.5 0.0 collective-permute-done.2.kv_6
  33.5 0.6 collective-permute-done.1.kv_2
  34.2 1.1 %collective-permute-start.3 = (bf16[2,144,128]{2,1,0:T(8,128)(2,1)S(1)}, bf16[2,144,128]{2,1,0:T(8,128)(2,1)S(1)}, u32[]{:S(2)}, u32[]{:S(2)}) collective-permute-start(bf16[2,144,128]{2,1,0:T(8,128)(2,1)S(1)} %pad_maximum_fusion), channel_id=1, source_target_pairs={{0,2},{2,0},{4,6},{6,4},{8,10},{10,8},{12,14},{14,12},{1,3},{3,1},... | collective-permute-start | bytes 221192 | tf_op jit(solution)/shard_map/ppermute | solution.py:451
  35.3 0.0 collective-permute-done.qg_b
  35.3 5.6 %shard_map.75.first_ref = f32[2,16,128]{2,1,0:T(8,128)S(1)} custom-call(bf16[16,176,128]{2,1,0:T(8,128)(2,1)S(1)} %all_to_all.10.got_ref.qg_a, bf16[16,176,128]{2,1,0:T(8,128)(2,1)S(1)} %collective-permute-done.qg_b, bf16[144,128]{1,0:T(8,128)(2,1)S(1)} %shard_map.74.kv_0, bf16[144,128]{1,0:T(8,128)(2,1)S(1)} %collective-permute-done.4.kv_1, ...), custom_call_target="tpu_custom_call" | custom-call | flops 1073741824 | bytes 1048576 | tf_op jit(solution)/shard_map/pallas_call | solution.py:498
  40.9 0.0 collective-permute-done.5.kv_45
  40.9 0.0 collective-permute-done.3.kv_37
  40.9 5.7 %shard_map.76.mine_ref = f32[2,16,128]{2,1,0:T(8,128)S(1)} custom-call(bf16[16,176,128]{2,1,0:T(8,128)(2,1)S(1)} %all_to_all.10.got_ref.qg_a, bf16[16,176,128]{2,1,0:T(8,128)(2,1)S(1)} %collective-permute-done.qg_b, bf16[2,144,128]{2,1,0:T(8,128)(2,1)S(1)} %collective-permute-done.3.kv_37, bf16[2,144,128]{2,1,0:T(8,128)(2,1)S(1)} %collective-permute-done.5.kv_45, ...), custom_call_target="tpu_custom_call" | custom-call | flops 1073741824 | bytes 1048576 | tf_op jit(solution)/shard_map/pallas_call | solution.py:500
  46.5 0.3 collective-permute-start.6
  46.8 0.2 shard_map.77
  47.0 0.9 collective-permute-done.6.came_ref
  48.0 0.0 slice-start
  48.0 5.3 %shard_map.78 = (f32[2,16,128]{2,1,0:T(8,128)S(1)}, f32[16,80,128]{2,1,0:T(8,128)S(1)}, f32[16,80,128]{2,1,0:T(8,128)S(1)}, bf16[4,144,128]{2,1,0:T(8,128)(2,1)S(1)}) custom-call(bf16[16,176,128]{2,1,0:T(8,128)(2,1)S(1)} %all_to_all.10.got_ref.qg_a, bf16[16,176,128]{2,1,0:T(8,128)(2,1)S(1)} %collective-permute-done.qg_b, ...), custom_call_target="tpu_custom_call" | custom-call | flops 5368709120 | bytes 1048576 | tf_op jit(solution)/shard_map/pallas_call | solution.py:509
  53.2 1.1 %collective-permute-start.7 = (bf16[4,144,128]{2,1,0:T(8,128)(2,1)S(1)}, bf16[4,144,128]{2,1,0:T(8,128)(2,1)S(1)}, u32[]{:S(2)}, u32[]{:S(2)}) collective-permute-start(bf16[4,144,128]{2,1,0:T(8,128)(2,1)S(1)} %get-tuple-element.76), channel_id=1, source_target_pairs={{0,2},{2,0},{4,6},{6,4},{8,10},{10,8},{12,14},{14,12},{1,3},{3,1},... | collective-permute-start | bytes 442376 | tf_op jit(solution)/shard_map/ppermute | solution.py:451
  54.3 5.4 %shard_map.79 = (f32[16,72,128]{2,1,0:T(8,128)S(1)}, f32[16,24,128]{2,1,0:T(8,128)S(1)}, f32[16,96,128]{2,1,0:T(8,128)S(1)}, f32[4,144,128]{2,1,0:T(8,128)S(1)}) custom-call(bf16[16,176,128]{2,1,0:T(8,128)(2,1)S(1)} %all_to_all.10.got_ref.qg_a, bf16[16,176,128]{2,1,0:T(8,128)(2,1)S(1)} %collective-permute-done.qg_b, ...), custom_call_target="tpu_custom_call" | custom-call | flops 5368709120 | bytes 1048576 | tf_op jit(solution)/shard_map/pallas_call | solution.py:514
  59.7 0.0 collective-permute-done.7
  59.7 0.1 collective-permute-start.8
  59.9 2.8 %collective-permute-start.11 = (bf16[144,128]{1,0:T(8,128)(2,1)S(1)}, bf16[144,128]{1,0:T(8,128)(2,1)S(1)}, u32[]{:S(2)}, u32[]{:S(2)}) collective-permute-start(bf16[144,128]{1,0:T(8,128)(2,1)S(1)} %get-tuple-element.97), channel_id=1, source_target_pairs={{0,8},{2,10},{4,12},{6,14},{8,0},{10,2},{12,4},{14,6},{1,9},{3,11}... | collective-permute-start | bytes 110600 | tf_op jit(solution)/shard_map/ppermute | solution.py:451
  62.6 2.4 %collective-permute-start.10 = (bf16[144,128]{1,0:T(8,128)(2,1)S(1)}, bf16[144,128]{1,0:T(8,128)(2,1)S(1)}, u32[]{:S(2)}, u32[]{:S(2)}) collective-permute-start(bf16[144,128]{1,0:T(8,128)(2,1)S(1)} %get-tuple-element.98), channel_id=1, source_target_pairs={{0,12},{2,14},{4,8},{6,10},{8,4},{10,6},{12,0},{14,2},{1,13},{3,15... | collective-permute-start | bytes 110600 | tf_op jit(solution)/shard_map/ppermute | solution.py:451
  65.0 1.5 %collective-permute-start.9 = (bf16[144,128]{1,0:T(8,128)(2,1)S(1)}, bf16[144,128]{1,0:T(8,128)(2,1)S(1)}, u32[]{:S(2)}, u32[]{:S(2)}) collective-permute-start(bf16[144,128]{1,0:T(8,128)(2,1)S(1)} %get-tuple-element.99), channel_id=1, source_target_pairs={{0,4},{2,6},{4,0},{6,2},{8,12},{10,14},{12,8},{14,10},{1,5},{3,7},... | collective-permute-start | bytes 110600 | tf_op jit(solution)/shard_map/ppermute | solution.py:451
  66.5 0.0 slice-done
  66.5 0.0 slice-done.1
  66.5 0.0 copy-done
  66.5 2.7 %shard_map.80.weights = bf16[512,3456]{1,0:T(8,128)(2,1)S(1)} custom-call(bf16[256,1152]{1,0:T(8,128)(2,1)S(1)} %copy-done, bf16[1152,3456]{1,0:T(8,128)(2,1)S(1)} %bitcast.14), custom_call_target="tpu_custom_call" | custom-call | flops 1048576 | bytes 65536 | tf_op jit(solution)/shard_map/pallas_call | solution.py:527
  69.2 0.0 collective-permute-done.11.came_c
  69.2 0.0 collective-permute-done.10.came_b
  69.2 0.6 collective-permute-done.9.came_a
  69.9 0.1 collective-permute-start.12
  70.0 1.2 %collective-permute-done.12.other_ref = bf16[144,128]{1,0:T(8,128)(2,1)S(1)} collective-permute-done((bf16[144,128]{1,0:T(8,128)(2,1)S(1)}, bf16[144,128]{1,0:T(8,128)(2,1)S(1)}, u32[]{:S(2)}, u32[]{:S(2)}) %collective-permute-start.12) | collective-permute-done | bytes 36896 | tf_op jit(solution)/shard_map/ppermute | solution.py:451
  71.2 0.0 collective-permute-done.8.came_ref
  71.2 0.3 shard_map.82
  71.5 14.6 %all_to_all.11.back_ref = bf16[16,112,128]{2,1,0:T(8,128)(2,1)S(1)} all-to-all(bf16[16,112,128]{2,1,0:T(8,128)(2,1)S(1)} %shard_map.82), channel_id=1, replica_groups=mesh['yh'=2,'x'=4,'c'=2,'z'=8,'yl'=2] {'yh','x','yl'}, dimensions={0} | all-to-all | bytes 917504 | tf_op jit(solution)/shard_map/all_to_all | solution.py:536
  86.1 1.3 %shard_map.83 = (bf16[160,256]{1,0:T(8,128)(2,1)S(1)}, bf16[1152,256]{1,0:T(8,128)(2,1)S(1)}, bf16[2304,128]{1,0:T(8,128)(2,1)S(1)}, f32[4,64]{1,0:T(4,128)S(1)}, f32[4,64]{1,0:T(4,128)S(1)}) custom-call(bf16[16,112,128]{2,1,0:T(8,128)(2,1)S(1)} %all_to_all.11.back_ref, bf16[512,3456]{1,0:T(8,128)(2,1)S(1)} %shard_map.80.weights), custom_call_target="tpu_custom_call" | custom-call | tf_op jit(solution)/shard_map/pallas_call | solution.py:539
  87.4 1.5 %collective-permute-start.13 = (f32[4,64]{1,0:T(4,128)S(1)}, f32[4,64]{1,0:T(4,128)S(1)}, u32[]{:S(2)}, u32[]{:S(2)}) collective-permute-start(f32[4,64]{1,0:T(4,128)S(1)} %get-tuple-element.89), channel_id=1, source_target_pairs={{0,1},{1,0},{2,3},{3,2},{4,5},{5,4},{6,7},{7,6},{8,9},{9,8},{10,11... | collective-permute-start | bytes 3080 | tf_op jit(solution)/shard_map/ppermute | solution.py:451
  88.9 3.5 %collective-permute-start.14 = (f32[4,64]{1,0:T(4,128)S(1)}, f32[4,64]{1,0:T(4,128)S(1)}, u32[]{:S(2)}, u32[]{:S(2)}) collective-permute-start(f32[4,64]{1,0:T(4,128)S(1)} %get-tuple-element.90), channel_id=1, source_target_pairs={{1,2},{3,4},{5,6},{7,8},{9,10},{11,12},{13,14},{2,1},{4,3},{6,5},{... | collective-permute-start | bytes 3080 | tf_op jit(solution)/shard_map/ppermute | solution.py:457
  92.4 1.5 %shard_map.84.center_ref = f32[64,128]{1,0:T(8,128)S(1)} custom-call(bf16[160,256]{1,0:T(8,128)(2,1)S(1)} %get-tuple-element.91.outer_ref, bf16[512,3456]{1,0:T(8,128)(2,1)S(1)} %shard_map.80.weights, bf16[1152,256]{1,0:T(8,128)(2,1)S(1)} %get-tuple-element.92.joined, bf16[2304,128]{1,0:T(8,128)(2,1)S(1)} %get-tuple-element.93.pooled), custom_call_target="tpu_custom_call" | custom-call | flops 1048576 | bytes 65536 | tf_op jit(solution)/shard_map/pallas_call | solution.py:546
  93.9 0.0 collective-permute-done.13.near_ref
  93.9 1.3 %collective-permute-done.14.far_ref = f32[4,64]{1,0:T(4,128)S(1)} collective-permute-done((f32[4,64]{1,0:T(4,128)S(1)}, f32[4,64]{1,0:T(4,128)S(1)}, u32[]{:S(2)}, u32[]{:S(2)}) %collective-permute-start.14) | collective-permute-done | bytes 1056 | tf_op jit(solution)/shard_map/ppermute | solution.py:457
  95.3 0.7 shard_map.85
  (10 shorter events, 0.1 us)
Async XLA Ops:
  21.8 13.5 %collective-permute-start = (bf16[16,176,128]{2,1,0:T(8,128)(2,1)S(1)}, bf16[16,176,128]{2,1,0:T(8,128)(2,1)S(1)}, u32[]{:S(2)}, u32[]{:S(2)}) collective-permute-start(bf16[16,176,128]{2,1,0:T(8,128)(2,1)S(1)} %all_to_all.10.got_ref.qg_a), channel_id=1, source_target_pairs={{0,16},{16,0},{1,17},{17,1},{2,18},{18,2},{3,19},{19,3},{4,20},{20... | collective-permute-start | bytes 2162696 | tf_op jit(solution)/shard_map/ppermute | solution.py:451
  21.9 8.9 %collective-permute-start.4 = (bf16[144,128]{1,0:T(8,128)(2,1)S(1)}, bf16[144,128]{1,0:T(8,128)(2,1)S(1)}, u32[]{:S(2)}, u32[]{:S(2)}) collective-permute-start(bf16[144,128]{1,0:T(8,128)(2,1)S(1)} %shard_map.74.kv_0), channel_id=1, source_target_pairs={{0,2},{2,0},{4,6},{6,4},{8,10},{10,8},{12,14},{14,12},{1,3},{3,1},... | collective-permute-start | bytes 110600 | tf_op jit(solution)/shard_map/ppermute | solution.py:451
  23.9 9.6 %collective-permute-start.2 = (bf16[144,128]{1,0:T(8,128)(2,1)S(1)}, bf16[144,128]{1,0:T(8,128)(2,1)S(1)}, u32[]{:S(2)}, u32[]{:S(2)}) collective-permute-start(bf16[144,128]{1,0:T(8,128)(2,1)S(1)} %shard_map.74.kv_0), channel_id=1, source_target_pairs={{0,12},{2,14},{4,8},{6,10},{8,4},{10,6},{12,0},{14,2},{1,13},{3,15... | collective-permute-start | bytes 110600 | tf_op jit(solution)/shard_map/ppermute | solution.py:451
  29.3 4.9 %collective-permute-start.1 = (bf16[144,128]{1,0:T(8,128)(2,1)S(1)}, bf16[144,128]{1,0:T(8,128)(2,1)S(1)}, u32[]{:S(2)}, u32[]{:S(2)}) collective-permute-start(bf16[144,128]{1,0:T(8,128)(2,1)S(1)} %shard_map.74.kv_0), channel_id=1, source_target_pairs={{0,4},{2,6},{4,0},{6,2},{8,12},{10,14},{12,8},{14,10},{1,5},{3,7},... | collective-permute-start | bytes 110600 | tf_op jit(solution)/shard_map/ppermute | solution.py:451
  30.8 10.1 %collective-permute-start.5 = (bf16[2,144,128]{2,1,0:T(8,128)(2,1)S(1)}, bf16[2,144,128]{2,1,0:T(8,128)(2,1)S(1)}, u32[]{:S(2)}, u32[]{:S(2)}) collective-permute-start(bf16[2,144,128]{2,1,0:T(8,128)(2,1)S(1)} %pad_maximum_fusion.1), channel_id=1, source_target_pairs={{0,8},{2,10},{4,12},{6,14},{8,0},{10,2},{12,4},{14,6},{1,9},{3,11}... | collective-permute-start | bytes 221192 | tf_op jit(solution)/shard_map/ppermute | solution.py:451
  34.2 6.7 %collective-permute-start.3 = (bf16[2,144,128]{2,1,0:T(8,128)(2,1)S(1)}, bf16[2,144,128]{2,1,0:T(8,128)(2,1)S(1)}, u32[]{:S(2)}, u32[]{:S(2)}) collective-permute-start(bf16[2,144,128]{2,1,0:T(8,128)(2,1)S(1)} %pad_maximum_fusion), channel_id=1, source_target_pairs={{0,2},{2,0},{4,6},{6,4},{8,10},{10,8},{12,14},{14,12},{1,3},{3,1},... | collective-permute-start | bytes 221192 | tf_op jit(solution)/shard_map/ppermute | solution.py:451
  46.5 1.5 %collective-permute-start.6 = (f32[2,16,128]{2,1,0:T(8,128)S(1)}, f32[2,16,128]{2,1,0:T(8,128)S(1)}, u32[]{:S(2)}, u32[]{:S(2)}) collective-permute-start(f32[2,16,128]{2,1,0:T(8,128)S(1)} %shard_map.76.mine_ref), channel_id=1, source_target_pairs={{0,16},{16,0},{1,17},{17,1},{2,18},{18,2},{3,19},{19,3},{4,20},{20... | collective-permute-start | bytes 49160 | tf_op jit(solution)/shard_map/ppermute | solution.py:451
  48.0 18.5 %slice-start = ((s8[7962624]{0:T(1024)(128)(4,1)}), s8[4194304]{0:T(1024)(128)(4,1)S(1)}, s32[]{:S(2)}) async-start(s8[7962624]{0:T(1024)(128)(4,1)} %bitcast.13), calls=%async_computation.2 | async-start | bytes 8388608
  53.2 6.5 %collective-permute-start.7 = (bf16[4,144,128]{2,1,0:T(8,128)(2,1)S(1)}, bf16[4,144,128]{2,1,0:T(8,128)(2,1)S(1)}, u32[]{:S(2)}, u32[]{:S(2)}) collective-permute-start(bf16[4,144,128]{2,1,0:T(8,128)(2,1)S(1)} %get-tuple-element.76), channel_id=1, source_target_pairs={{0,2},{2,0},{4,6},{6,4},{8,10},{10,8},{12,14},{14,12},{1,3},{3,1},... | collective-permute-start | bytes 442376 | tf_op jit(solution)/shard_map/ppermute | solution.py:451
  54.3 12.2 %slice-start.1 = ((s8[7962624]{0:T(1024)(128)(4,1)}), s8[3768320]{0:T(1024)(128)(4,1)S(1)}, s32[]{:S(2)}) async-start(s8[7962624]{0:T(1024)(128)(4,1)} %bitcast.13), calls=%async_computation.3 | async-start | bytes 7536640
  54.3 12.2 %copy-start = (bf16[256,1152]{1,0:T(8,128)(2,1)S(1)}, bf16[256,1152]{1,0:T(8,128)(2,1)}, u32[]{:S(2)}) copy-start(bf16[256,1152]{1,0:T(8,128)(2,1)} %patch_ref) | copy-start | bytes 1769476
  59.7 11.5 %collective-permute-start.8 = (f32[16,96,128]{2,1,0:T(8,128)S(1)}, f32[16,96,128]{2,1,0:T(8,128)S(1)}, u32[]{:S(2)}, u32[]{:S(2)}) collective-permute-start(f32[16,96,128]{2,1,0:T(8,128)S(1)} %get-tuple-element.79), channel_id=1, source_target_pairs={{0,16},{16,0},{1,17},{17,1},{2,18},{18,2},{3,19},{19,3},{4,20},{20... | collective-permute-start | bytes 2359304 | tf_op jit(solution)/shard_map/ppermute | solution.py:451
  59.9 9.3 %collective-permute-start.11 = (bf16[144,128]{1,0:T(8,128)(2,1)S(1)}, bf16[144,128]{1,0:T(8,128)(2,1)S(1)}, u32[]{:S(2)}, u32[]{:S(2)}) collective-permute-start(bf16[144,128]{1,0:T(8,128)(2,1)S(1)} %get-tuple-element.97), channel_id=1, source_target_pairs={{0,8},{2,10},{4,12},{6,14},{8,0},{10,2},{12,4},{14,6},{1,9},{3,11}... | collective-permute-start | bytes 110600 | tf_op jit(solution)/shard_map/ppermute | solution.py:451
  62.6 6.6 %collective-permute-start.10 = (bf16[144,128]{1,0:T(8,128)(2,1)S(1)}, bf16[144,128]{1,0:T(8,128)(2,1)S(1)}, u32[]{:S(2)}, u32[]{:S(2)}) collective-permute-start(bf16[144,128]{1,0:T(8,128)(2,1)S(1)} %get-tuple-element.98), channel_id=1, source_target_pairs={{0,12},{2,14},{4,8},{6,10},{8,4},{10,6},{12,0},{14,2},{1,13},{3,15... | collective-permute-start | bytes 110600 | tf_op jit(solution)/shard_map/ppermute | solution.py:451
  65.0 4.9 %collective-permute-start.9 = (bf16[144,128]{1,0:T(8,128)(2,1)S(1)}, bf16[144,128]{1,0:T(8,128)(2,1)S(1)}, u32[]{:S(2)}, u32[]{:S(2)}) collective-permute-start(bf16[144,128]{1,0:T(8,128)(2,1)S(1)} %get-tuple-element.99), channel_id=1, source_target_pairs={{0,4},{2,6},{4,0},{6,2},{8,12},{10,14},{12,8},{14,10},{1,5},{3,7},... | collective-permute-start | bytes 110600 | tf_op jit(solution)/shard_map/ppermute | solution.py:451
  69.9 1.3 %collective-permute-start.12 = (bf16[144,128]{1,0:T(8,128)(2,1)S(1)}, bf16[144,128]{1,0:T(8,128)(2,1)S(1)}, u32[]{:S(2)}, u32[]{:S(2)}) collective-permute-start(bf16[144,128]{1,0:T(8,128)(2,1)S(1)} %shard_map.81.keys_ref), channel_id=1, source_target_pairs={{0,16},{16,0},{1,17},{17,1},{2,18},{18,2},{3,19},{19,3},{4,20},{20... | collective-permute-start | bytes 110600 | tf_op jit(solution)/shard_map/ppermute | solution.py:451
  87.4 6.5 %collective-permute-start.13 = (f32[4,64]{1,0:T(4,128)S(1)}, f32[4,64]{1,0:T(4,128)S(1)}, u32[]{:S(2)}, u32[]{:S(2)}) collective-permute-start(f32[4,64]{1,0:T(4,128)S(1)} %get-tuple-element.89), channel_id=1, source_target_pairs={{0,1},{1,0},{2,3},{3,2},{4,5},{5,4},{6,7},{7,6},{8,9},{9,8},{10,11... | collective-permute-start | bytes 3080 | tf_op jit(solution)/shard_map/ppermute | solution.py:451
  88.9 6.4 %collective-permute-start.14 = (f32[4,64]{1,0:T(4,128)S(1)}, f32[4,64]{1,0:T(4,128)S(1)}, u32[]{:S(2)}, u32[]{:S(2)}) collective-permute-start(f32[4,64]{1,0:T(4,128)S(1)} %get-tuple-element.90), channel_id=1, source_target_pairs={{1,2},{3,4},{5,6},{7,8},{9,10},{11,12},{13,14},{2,1},{4,3},{6,5},{... | collective-permute-start | bytes 3080 | tf_op jit(solution)/shard_map/ppermute | solution.py:457
